TPU v7x, 32 devices: a whole 2x2x4 slice. The times are simulated.
32 devices in a mesh: row: 8 (over y, x, core), col: 4 (over z).
Axes of the slice: x: 2, y: 2, z: 4, core: 2. Of those that a mesh axis runs over, the one named last changes fastest.
Arguments:
- vectors: float32 [16, 4096], P(None, ('row', 'col')), may hold values from -6 to 6
- diagonal_energy: float32 [4096], P(('row', 'col')), may hold values from 0.45 to 61
- tiles: float32 [8, 4, 16, 128, 128], P('row', 'col'), may hold values from -0.25 to 0.25
- tile_rows: int32 [8, 4, 16], P('row', 'col'), may hold values from 0 to 3
- tile_cols: int32 [8, 4, 16], P('row', 'col'), may hold values from 0 to 7
- tile_count: int32 [8, 4], P('row', 'col'), may hold values from 1 to 16
Outputs:
- residual: float32 [16, 4096], P(None, ('row', 'col'))
- rayleigh: float32 [16, 16], replicated
- gram: float32 [16, 16], replicated
All inputs are finite; a program needn't handle non-finite values.
Results may differ from a plain program's by a relative error of at most 0.0003.
Values sent between devices are 32-bit elements; how exact they have to be, the bound alone decides.
No kernel may reach another device: no remote copies, remote signals or barrier semaphores. Data moves between devices by JAX's collectives and lax.ppermute only.
A program may use at most 64 MiB of HBM per device.

v0:
```python
import jax
import jax.numpy as jnp
from jax import lax
from jax.sharding import PartitionSpec as P


def per_device(vectors, diagonal_energy, tiles, tile_rows, tile_cols, tile_count):
    hp = lax.Precision.HIGHEST
    tile_set = tiles[0, 0]
    arow = tile_rows[0, 0]
    bcol = tile_cols[0, 0]
    slot_total = arow.shape[0]
    live = (jnp.arange(slot_total, dtype=jnp.int32) < tile_count[0, 0]).astype(jnp.float32)
    group_cols = lax.axis_size("col")
    group_rows = lax.axis_size("row")
    nvec, width = vectors.shape
    x_rows = lax.all_gather(vectors, "col", axis=1, tiled=True).reshape(nvec, group_cols, width)
    x_cols = lax.all_gather(vectors, "row", axis=1, tiled=True).reshape(nvec, group_rows, width)
    pick_a = (arow[:, None] == jnp.arange(group_cols, dtype=jnp.int32)[None, :]).astype(jnp.float32)
    pick_b = (bcol[:, None] == jnp.arange(group_rows, dtype=jnp.int32)[None, :]).astype(jnp.float32)
    own_rows = jnp.einsum("vat,sa->svt", x_rows, pick_a, precision=hp)
    own_cols = jnp.einsum("vbt,sb->svt", x_cols, pick_b, precision=hp)
    forward = jnp.einsum("svk,snk->svn", own_cols, tile_set, precision=hp) * live[:, None, None]
    backward = jnp.einsum("svn,snk->svk", own_rows, tile_set, precision=hp) * live[:, None, None]
    row_terms = jnp.einsum("svn,sa->van", forward, pick_a, precision=hp).reshape(
        nvec, group_cols * width
    )
    from_rows = lax.psum_scatter(row_terms, "col", scatter_dimension=1, tiled=True)
    col_terms = jnp.einsum("svk,sb->vbk", backward, pick_b, precision=hp).reshape(
        nvec, group_rows * width
    )
    from_cols = lax.psum_scatter(col_terms, "row", scatter_dimension=1, tiled=True)
    product = from_rows + from_cols + diagonal_energy[None, :] * vectors
    dim_total = float(group_rows * group_cols * width)
    cross = lax.psum(jnp.dot(vectors, product.T, precision=hp), ("row", "col"))
    rayleigh = cross / dim_total
    residual = product - jnp.dot(rayleigh, vectors, precision=hp)
    gram = lax.psum(jnp.dot(residual, residual.T, precision=hp), ("row", "col")) / dim_total
    return (residual, rayleigh, gram)


def solution(mesh):
    return jax.shard_map(
        per_device,
        mesh=mesh,
        in_specs=(
            P(None, ("row", "col")),
            P(("row", "col")),
            P("row", "col", None, None, None),
            P("row", "col", None),
            P("row", "col", None),
            P("row", "col"),
        ),
        out_specs=(P(None, ("row", "col")), P(), P()),
        check_vma=False,
    )
```

profile of v0, /device:TPU:0, one launch (start us, length us, event | category | flops | bytes accessed | tf_op | source)
XLA Modules:
  0.0 166.0 jit_solution(7668534304483944749)
XLA Ops:
  7.2 0.0 copy-start
  7.2 0.0 reduce-scatter.3.cloned.1.call-start
  7.2 10.8 %all_gather.6 = f32[16,1024]{1,0:T(8,128)S(1)} all-gather(f32[16,128]{1,0:T(8,128)} %param.6), channel_id=1, replica_groups=mesh['row'=8,'col'=4] {'row'}, dimensions={1}, use_global_device_ids=true | all-gather | bytes 73728 | tf_op jit(solution)/shard_map/all_gather | solution.py:18
  18.7 0.0 copy-start.6
  18.7 0.6 copy-done.6
  19.4 0.3 fusion.13
  19.6 0.0 copy-done
  19.6 1.7 %fusion.2 = f32[16,16,128]{2,1,0:T(8,128)S(1)} fusion(f32[1,1,16,128,128]{4,3,2,1,0:T(8,128)S(1)} %copy-done, f32[16,16,128]{2,0,1:T(8,128)S(1)} %fusion.13), kind=kOutput, calls=%fused_computation.4 | convolution fusion | flops 50331648 | bytes 1310720 | tf_op jit(solution)/shard_map/svk,snk->svn/dot_general | solution.py:23
  21.4 0.0 copy-start.5
  21.4 0.7 copy-done.5
  22.0 0.2 fusion.6
  22.3 0.6 copy.31
  22.9 0.0 copy-start.1
  22.9 0.0 reduce-scatter.3.cloned.1.call-update
  22.9 0.0 reduce-scatter.5.cloned.1.call-start
  23.0 0.6 copy-done.1
  23.6 13.3 %all_gather.7 = f32[16,512]{1,0:T(8,128)S(1)} all-gather(f32[16,128]{1,0:T(8,128)S(1)} %copy-done.1), channel_id=1, replica_groups=mesh['row'=8,'col'=4] {'col'}, dimensions={1}, use_global_device_ids=true | all-gather | bytes 40960 | tf_op jit(solution)/shard_map/all_gather | solution.py:17
  37.0 0.3 fusion.19
  37.2 1.0 fusion
  38.2 0.2 fusion.4
  38.5 0.6 copy.30
  39.1 0.0 copy-start.7
  39.1 0.0 reduce-scatter.5.cloned.1.call-update
  39.1 3.0 %reduce-scatter.3.cloned.1.call-done = f32[16,128]{1,0:T(8,128)} async-done(((f32[16,512]{1,0:T(8,128)}), f32[16,128]{1,0:T(8,128)}) %reduce-scatter.3.cloned.1.call-update) | async-done | bytes 8208 | tf_op jit(solution)/shard_map/reduce_scatter | solution.py:28
  42.1 33.0 %reduce-scatter.5.cloned.1.call-done = f32[16,128]{1,0:T(8,128)} async-done(((f32[16,1024]{1,0:T(8,128)}), f32[16,128]{1,0:T(8,128)}) %reduce-scatter.5.cloned.1.call-update) | async-done | bytes 8208 | tf_op jit(solution)/shard_map/reduce_scatter | solution.py:32
  75.1 0.0 copy-done.7
  75.1 0.8 convolution_bitcast_fusion
  75.9 39.4 %psum.14 = f32[16,16]{0,1:T(8,128)S(1)} all-reduce(f32[16,16]{0,1:T(8,128)S(1)} %convolution_bitcast_fusion), channel_id=1, replica_groups=mesh['row'=8,'col'=4] {'row','col'}, use_global_device_ids=true, to_apply=%region_2.0 | all-reduce | flops 256 | bytes 2048 | tf_op jit(solution)/shard_map/psum | solution.py:35
  115.3 0.0 copy-start.3
  115.3 0.0 copy-start.4
  115.3 0.7 copy-done.3
  116.0 0.0 copy-done.4
  116.0 0.2 convolution_subtract_fusion
  116.2 0.0 copy-start.2
  116.2 0.1 fusion.24
  116.4 0.5 copy-done.2
  116.8 41.0 %psum.15 = f32[16,16]{0,1:T(8,128)S(1)} all-reduce(f32[16,16]{0,1:T(8,128)S(1)} %fusion.24), channel_id=1, replica_groups=mesh['row'=8,'col'=4] {'row','col'}, use_global_device_ids=true, to_apply=%region_3.0 | all-reduce | flops 256 | bytes 2048 | tf_op jit(solution)/shard_map/psum | solution.py:38
  157.9 0.7 copy.11
  158.5 0.7 copy.10
  (5 shorter events, 0.0 us)
Async XLA Ops:
  7.2 12.5 %copy-start = (f32[1,1,16,128,128]{4,3,2,1,0:T(8,128)S(1)}, f32[1,1,16,128,128]{4,3,2,1,0:T(8,128)}, u32[]{:S(2)}) copy-start(f32[1,1,16,128,128]{4,3,2,1,0:T(8,128)} %param.8) | copy-start | bytes 3145732
  7.2 35.0 %reduce-scatter.3.cloned.1.call-start = ((), (), s32[]{:S(2)}) async-start(), calls=%async_computation.2 | async-start | bytes 40960 | tf_op jit(solution)/shard_map/reduce_scatter | solution.py:28
  18.7 0.7 copy-start.6
  21.4 0.7 copy-start.5
  22.9 0.7 copy-start.1
  22.9 52.2 %reduce-scatter.5.cloned.1.call-start = ((), (), s32[]{:S(2)}) async-start(), calls=%async_computation.3 | async-start | bytes 73728 | tf_op jit(solution)/shard_map/reduce_scatter | solution.py:32
  39.1 36.0 %copy-start.7 = (f32[128]{0:T(128)S(1)}, f32[128]{0:T(128)}, u32[]{:S(2)}) copy-start(f32[128]{0:T(128)} %param.7) | copy-start | bytes 1540
  115.3 0.7 copy-start.3
  115.3 0.7 copy-start.4
  116.2 0.6 copy-start.2
Sparse Core Ops, SparseCore 0:
  23.1 19.0 reduce-scatter.2
  45.4 29.6 reduce-scatter.4
where the time goes:
time: 167 us; the launch traced here: 166 us
  blocking collectives  105 us (63%)
  waiting for transfers between devices  36 us (22%)
  between operations  14.8 us (9%)
  local copies, waits for them, and re-layouts  5.75 us (3%)
  matrix products  4.9 us (3%)
    psum x1, blocking collectives, per_device(): lax.psum(jnp.dot(residual, residual.T, precision=hp), ('row', 'col'))  41 us
    psum x1, blocking collectives, per_device(): cross = lax.psum(jnp.dot(vectors, product.T, precision=hp), ('row', 'col'))  39.4 us
    reduce_scatter x1, waiting for transfers between devices, per_device(): lax.psum_scatter(col_terms, 'row', scatter_dimension=1, tiled=True)  33 us
    all_gather x1, blocking collectives, per_device(): lax.all_gather(vectors, 'col', axis=1, tiled=True)  13.3 us
    all_gather x1, blocking collectives, per_device(): lax.all_gather(vectors, 'row', axis=1, tiled=True)  10.8 us
    unnamed x21, local copies, waits for them, and re-layouts  5.74 us
  transfers between devices with their start and end apart: 2, of which 2 were waited for; matrix products, arithmetic and copies ran while one was open for 1% of the time, Pallas kernels for 0%

commit v1 on v0

v1 whole, which is shorter than its diff:
```python
import functools

import jax
import jax.numpy as jnp
from jax import lax
from jax.experimental import pallas as pl
from jax.experimental.pallas import tpu as pltpu
from jax.sharding import PartitionSpec as P

HP = lax.Precision.HIGHEST
LAST = (((1,), (1,)), ((), ()))
VMEM = pl.BlockSpec(memory_space=pltpu.VMEM)
SMEM = pl.BlockSpec(memory_space=pltpu.SMEM)


def mult(left, right):
    return lax.dot_general(left, right, (((1,), (0,)), ((), ())), precision=HP, preferred_element_type=jnp.float32)


def mult_last(left, right):
    return lax.dot_general(left, right, LAST, precision=HP, preferred_element_type=jnp.float32)


def shift(value, axis, step):
    size = lax.axis_size(axis)
    return lax.ppermute(value, axis, [(p, (p + step) % size) for p in range(size)])


def around(value, axis):
    return [shift(value, axis, step) for step in range(1, lax.axis_size(axis))]


def products_kernel(n_row, n_col, slots, *refs):
    place, arow, bcol, count, x_ref, d_ref = refs[:6]
    rest = refs[6:]
    from_col, rest = rest[: n_col - 1], rest[n_col - 1 :]
    from_row, rest = rest[: n_row - 1], rest[n_row - 1 :]
    tiles, rest = rest[0], rest[1:]
    to_col, rest = rest[:n_col], rest[n_col:]
    to_row, rest = rest[:n_row], rest[n_row:]
    x_rows, x_cols, row_terms, col_terms = rest
    me_row, me_col = place[0], place[1]
    own = x_ref[...]
    for step in range(n_col):
        x_rows[step] = own if step == 0 else from_col[step - 1][...]
        row_terms[step] = jnp.zeros_like(own)
    for step in range(n_row):
        x_cols[step] = own if step == 0 else from_row[step - 1][...]
        col_terms[step] = jnp.zeros_like(own)
    half = 0.5 * d_ref[...] * own
    row_terms[0] = half
    col_terms[0] = half
    live_total = count[0, 0]
    for slot in range(slots):
        a = arow[0, 0, slot]
        b = bcol[0, 0, slot]
        live = jnp.where(slot < live_total, 1.0, 0.0).astype(jnp.float32)
        tile = tiles[0, 0, slot]
        x_i = x_rows[lax.rem(me_col - a + n_col, n_col)] * live
        x_j = x_cols[lax.rem(me_row - b + n_row, n_row)] * live
        row_terms[lax.rem(a - me_col + n_col, n_col)] += mult_last(x_j, tile)
        col_terms[lax.rem(b - me_row + n_row, n_row)] += mult(x_i, tile)
    total = jnp.zeros((own.shape[0], own.shape[0]), jnp.float32)
    for step in range(n_col):
        total += mult_last(x_rows[(n_col - step) % n_col], row_terms[step])
        to_col[step][...] = row_terms[step]
    for step in range(n_row):
        to_row[step][0] = col_terms[step]
        to_row[step][1, :, : own.shape[0]] = total


def row_sum_kernel(count, *refs):
    out = refs[count]
    nvec = out.shape[0]
    total = refs[0][1, :, :nvec]
    for ref in refs[1:count]:
        total = total + ref[1, :, :nvec]
    out[...] = total


def residual_kernel(n_row, n_col, scale, *refs):
    x_ref, rest = refs[0], refs[1:]
    by_col, rest = rest[:n_col], rest[n_col:]
    by_row, rest = rest[:n_row], rest[n_row:]
    cross, rest = rest[:n_col], rest[n_col:]
    residual, rayleigh, gram = rest
    product = by_col[0][...] + by_row[0][0]
    for ref in by_col[1:]:
        product += ref[...]
    for ref in by_row[1:]:
        product += ref[0]
    half = cross[0][...]
    for ref in cross[1:]:
        half += ref[...]
    ray = (half + half.T) * scale
    rayleigh[...] = ray
    res = product - mult(ray, x_ref[...])
    residual[...] = res
    gram[...] = mult_last(res, res)


def sum_kernel(count, scale, *refs):
    out = refs[count]
    total = refs[0][...]
    for ref in refs[1:count]:
        total = total + ref[...]
    out[...] = total * scale


def per_device(vectors, diagonal_energy, tiles, tile_rows, tile_cols, tile_count):
    n_row = lax.axis_size("row")
    n_col = lax.axis_size("col")
    nvec, width = vectors.shape
    slots = tiles.shape[2]
    scale = 1.0 / float(n_row * n_col * width)
    block = jax.ShapeDtypeStruct((nvec, width), jnp.float32)
    pair = jax.ShapeDtypeStruct((2, nvec, width), jnp.float32)
    square = jax.ShapeDtypeStruct((nvec, nvec), jnp.float32)
    place = jnp.stack([lax.axis_index("row"), lax.axis_index("col")]).astype(jnp.int32)
    with jax.named_scope("share_vectors"):
        from_row = around(vectors, "row")
        from_col = around(vectors, "col")
    with jax.named_scope("tile_products"):
        terms = pl.pallas_call(
            functools.partial(products_kernel, n_row, n_col, slots),
            out_shape=[block] * n_col + [pair] * n_row,
            in_specs=[SMEM] * 4 + [VMEM] * (n_row + n_col + 1),
            out_specs=[VMEM] * (n_row + n_col),
            scratch_shapes=[
                pltpu.VMEM((n_col, nvec, width), jnp.float32),
                pltpu.VMEM((n_row, nvec, width), jnp.float32),
                pltpu.VMEM((n_col, nvec, width), jnp.float32),
                pltpu.VMEM((n_row, nvec, width), jnp.float32),
            ],
            compiler_params=pltpu.CompilerParams(vmem_limit_bytes=16 * 2**20),
            name="tile_products",
        )(place, tile_rows, tile_cols, tile_count, vectors, diagonal_energy.reshape(1, width), *from_col, *from_row, tiles)
    to_col, to_row = terms[:n_col], terms[n_col:]
    with jax.named_scope("return_products"):
        by_row = [to_row[0]] + [shift(to_row[step], "row", step) for step in range(1, n_row)]
        by_col = [to_col[0]] + [shift(to_col[step], "col", step) for step in range(1, n_col)]
    with jax.named_scope("rayleigh_sum"):
        cross = pl.pallas_call(
            functools.partial(row_sum_kernel, n_row),
            out_shape=square,
            in_specs=[VMEM] * n_row,
            out_specs=VMEM,
            name="rayleigh_over_row",
        )(*by_row)
        crosses = [cross] + around(cross, "col")
    with jax.named_scope("residual"):
        residual, rayleigh, part = pl.pallas_call(
            functools.partial(residual_kernel, n_row, n_col, scale),
            out_shape=[block, square, square],
            in_specs=[VMEM] * (1 + n_row + 2 * n_col),
            out_specs=[VMEM] * 3,
            name="residual",
        )(vectors, *by_col, *by_row, *crosses)
    with jax.named_scope("gram_sum"):
        for axis, factor in (("row", 1.0), ("col", scale)):
            size = lax.axis_size(axis)
            part = pl.pallas_call(
                functools.partial(sum_kernel, size, factor),
                out_shape=square,
                in_specs=[VMEM] * size,
                out_specs=VMEM,
                name="gram_over_" + axis,
            )(part, *around(part, axis))
    return (residual, rayleigh, part)


def solution(mesh):
    return jax.shard_map(
        per_device,
        mesh=mesh,
        in_specs=(
            P(None, ("row", "col")),
            P(("row", "col")),
            P("row", "col", None, None, None),
            P("row", "col", None),
            P("row", "col", None),
            P("row", "col"),
        ),
        out_specs=(P(None, ("row", "col")), P(), P()),
        check_vma=False,
    )
```

time: 167 us -> 68.7 us (0.41)
  blocking collectives: 105 us -> 0 us
  starting transfers between devices: 0.08 us -> 36.1 us
  waiting for transfers between devices: 36 us -> 16.8 us
  between operations: 14.8 us -> 1.6 us
  Pallas kernels: 0 us -> 9.42 us
  matrix products: 4.9 us -> 0 us
    psum x2 -> x0, blocking collectives: 80.4 us -> none  [the longest x1 41 us: per_device(): lax.psum(jnp.dot(residual, residual.T, precision=hp), ('row', 'col'))]
    ppermute x0 -> x33, starting transfers between devices: none -> 36.1 us  [shift(): lax.ppermute(value, axis, [(p, (p + step) % size) for p in range(size)])]
    reduce_scatter x2 -> x0, waiting for transfers between devices: 36 us -> none  [the longest x1 33 us: per_device(): lax.psum_scatter(col_terms, 'row', scatter_dimension=1, tiled=True)]
    all_gather x2 -> x0, blocking collectives: 24.1 us -> none  [the longest x1 13.3 us: per_device(): lax.all_gather(vectors, 'col', axis=1, tiled=True)]
    ppermute x0 -> x33, waiting for transfers between devices: none -> 16.8 us  [shift(): lax.ppermute(value, axis, [(p, (p + step) % size) for p in range(size)])]
    pallas_call x0 -> x5, Pallas kernels: none -> 9.42 us  [the longest x1 3.38 us: per_device(): pl.pallas_call(functools.partial(products_kernel, n_row, n_col, slots), o...]
    dot_general x9 -> x0, matrix products: 4.9 us -> none  [the longest x1 1.73 us: per_device(): jnp.einsum('svk,snk->svn', own_cols, tile_set, precision=hp)]
    unnamed x21 -> x60, local copies, waits for them, and re-layouts: 5.74 us -> 4.24 us
  transfers between devices with their start and end apart: 2 -> 33, of which waited for: 2 -> 10; matrix products, arithmetic and copies ran while one was open for 1% -> 0% of each run, Pallas kernels for 0% -> 2%
where the time goes in v1:
time: 68.7 us; the launch traced here: 68.3 us
  starting transfers between devices  36.1 us (53%)
  waiting for transfers between devices  16.8 us (24%)
  Pallas kernels  9.42 us (14%)
  local copies, waits for them, and re-layouts  4.24 us (6%)
  between operations  1.6 us (2%)
    ppermute x33, starting transfers between devices, shift(): lax.ppermute(value, axis, [(p, (p + step) % size) for p in range(size)])  36.1 us
    ppermute x33, waiting for transfers between devices, shift(): lax.ppermute(value, axis, [(p, (p + step) % size) for p in range(size)])  16.8 us
    unnamed x60, local copies, waits for them, and re-layouts  4.24 us
    pallas_call x1, Pallas kernels, per_device(): pl.pallas_call(functools.partial(products_kernel, n_row, n_col, slots), o...  3.38 us
    pallas_call x2, Pallas kernels, per_device(): pl.pallas_call(functools.partial(sum_kernel, size, factor), out_shape=squ...  2.77 us
    pallas_call x1, Pallas kernels, per_device(): pl.pallas_call(functools.partial(residual_kernel, n_row, n_col, scale), o...  1.84 us
    pallas_call x1, Pallas kernels, per_device(): pl.pallas_call(functools.partial(row_sum_kernel, n_row), out_shape=square...  1.44 us
  transfers between devices with their start and end apart: 33, of which 10 were waited for; matrix products, arithmetic and copies ran while one was open for 0% of the time, Pallas kernels for 2%

profile of v1, /device:TPU:0, one launch (start us, length us, event | category | flops | bytes accessed | tf_op | source)
XLA Modules:
  0.0 68.3 jit_solution(8352879926040081201)
XLA Ops:
  0.6 3.4 %collective-permute-start.9 = (f32[16,128]{1,0:T(8,128)}, f32[16,128]{1,0:T(8,128)S(1)}, u32[]{:S(2)}, u32[]{:S(2)}) collective-permute-start(f32[16,128]{1,0:T(8,128)} %refs_0_.1), channel_id=1, source_target_pairs={{0,28},{4,0},{8,4},{12,8},{16,12},{20,16},{24,20},{28,24},{1,29},{... | collective-permute-start | bytes 24584 | tf_op jit(solution)/shard_map/share_vectors/ppermute | solution.py:26
  4.0 0.6 collective-permute-start.8
  4.7 0.3 collective-permute-start.7
  4.9 1.5 %collective-permute-start.6 = (f32[16,128]{1,0:T(8,128)}, f32[16,128]{1,0:T(8,128)S(1)}, u32[]{:S(2)}, u32[]{:S(2)}) collective-permute-start(f32[16,128]{1,0:T(8,128)} %refs_0_.1), channel_id=1, source_target_pairs={{0,16},{4,20},{8,24},{12,28},{16,0},{20,4},{24,8},{28,12},{1,17},{... | collective-permute-start | bytes 24584 | tf_op jit(solution)/shard_map/share_vectors/ppermute | solution.py:26
  6.5 0.2 collective-permute-start.5
  6.6 2.3 %collective-permute-start.4 = (f32[16,128]{1,0:T(8,128)S(1)}, f32[16,128]{1,0:T(8,128)S(1)}, u32[]{:S(2)}, u32[]{:S(2)}) collective-permute-start(f32[16,128]{1,0:T(8,128)S(1)} %copy-done.2), channel_id=1, source_target_pairs={{0,8},{4,12},{8,16},{12,20},{16,24},{20,28},{24,0},{28,4},{1,9},{5... | collective-permute-start | bytes 24584 | tf_op jit(solution)/shard_map/share_vectors/ppermute | solution.py:26
  8.9 3.7 %collective-permute-start.2 = (f32[16,128]{1,0:T(8,128)S(1)}, f32[16,128]{1,0:T(8,128)S(1)}, u32[]{:S(2)}, u32[]{:S(2)}) collective-permute-start(f32[16,128]{1,0:T(8,128)S(1)} %copy-done.2), channel_id=1, source_target_pairs={{0,3},{1,0},{2,1},{3,2},{4,7},{5,4},{6,5},{7,6},{8,11},{9,8},{10,9... | collective-permute-start | bytes 24584 | tf_op jit(solution)/shard_map/share_vectors/ppermute | solution.py:26
  12.6 1.0 %collective-permute-start = (f32[16,128]{1,0:T(8,128)S(1)}, f32[16,128]{1,0:T(8,128)S(1)}, u32[]{:S(2)}, u32[]{:S(2)}) collective-permute-start(f32[16,128]{1,0:T(8,128)S(1)} %copy-done.2), channel_id=1, source_target_pairs={{0,1},{1,2},{2,3},{3,0},{4,5},{5,6},{6,7},{7,4},{8,9},{9,10},{10,1... | collective-permute-start | bytes 24584 | tf_op jit(solution)/shard_map/share_vectors/ppermute | solution.py:26
  13.6 0.1 pad_add_fusion.refs_0_
  14.4 2.7 %collective-permute-done.1.refs_7_ = f32[16,128]{1,0:T(8,128)S(1)} collective-permute-done((f32[16,128]{1,0:T(8,128)S(1)}, f32[16,128]{1,0:T(8,128)S(1)}, u32[]{:S(2)}, u32[]{:S(2)}) %collective-permute-start.1) | collective-permute-done | bytes 8224 | tf_op jit(solution)/shard_map/share_vectors/ppermute | solution.py:26
  17.2 1.0 %collective-permute-done.refs_6_ = f32[16,128]{1,0:T(8,128)S(1)} collective-permute-done((f32[16,128]{1,0:T(8,128)S(1)}, f32[16,128]{1,0:T(8,128)S(1)}, u32[]{:S(2)}, u32[]{:S(2)}) %collective-permute-start) | collective-permute-done | bytes 8224 | tf_op jit(solution)/shard_map/share_vectors/ppermute | solution.py:26
  18.1 1.2 %copy-done = f32[1,1,16,128,128]{4,3,2,1,0:T(8,128)S(1)} copy-done((f32[1,1,16,128,128]{4,3,2,1,0:T(8,128)S(1)}, f32[1,1,16,128,128]{4,3,2,1,0:T(8,128)}, u32[]{:S(2)}) %copy-start) | copy-done | bytes 1048600
  19.4 3.4 %tile_products.1 = (f32[16,128]{1,0:T(8,128)S(1)}, f32[16,128]{1,0:T(8,128)S(1)}, f32[16,128]{1,0:T(8,128)S(1)}, f32[16,128]{1,0:T(8,128)S(1)}, f32[2,16,128]{2,...) custom-call(s32[2]{0:T(128)S(1)} %pad_add_fusion.refs_0_, ...), custom_call_target="tpu_custom_call" | custom-call | tf_op jit(solution)/shard_map/tile_products/tile_products/pallas_call | solution.py:124
  22.7 0.6 copy-done.1
  23.4 1.6 %collective-permute-start.14 = (f32[2,16,128]{2,1,0:T(8,128)S(1)}, f32[2,16,128]{2,1,0:T(8,128)S(1)}, u32[]{:S(2)}, u32[]{:S(2)}) collective-permute-start(f32[2,16,128]{2,1,0:T(8,128)S(1)} %get-tuple-element.24), channel_id=1, source_target_pairs={{0,8},{4,12},{8,16},{12,20},{16,24},{20,28},{24,0},{28,4},{1,9},{5... | collective-permute-start | bytes 49160 | tf_op jit(solution)/shard_map/return_products/ppermute | solution.py:26
  25.0 1.1 %collective-permute-start.15 = (f32[2,16,128]{2,1,0:T(8,128)S(1)}, f32[2,16,128]{2,1,0:T(8,128)S(1)}, u32[]{:S(2)}, u32[]{:S(2)}) collective-permute-start(f32[2,16,128]{2,1,0:T(8,128)S(1)} %get-tuple-element.25), channel_id=1, source_target_pairs={{0,12},{4,16},{8,20},{12,24},{16,28},{20,0},{24,4},{28,8},{1,13},{... | collective-permute-start | bytes 49160 | tf_op jit(solution)/shard_map/return_products/ppermute | solution.py:26
  26.1 1.4 %collective-permute-start.16 = (f32[2,16,128]{2,1,0:T(8,128)S(1)}, f32[2,16,128]{2,1,0:T(8,128)S(1)}, u32[]{:S(2)}, u32[]{:S(2)}) collective-permute-start(f32[2,16,128]{2,1,0:T(8,128)S(1)} %get-tuple-element.26), channel_id=1, source_target_pairs={{0,16},{4,20},{8,24},{12,28},{16,0},{20,4},{24,8},{28,12},{1,17},{... | collective-permute-start | bytes 49160 | tf_op jit(solution)/shard_map/return_products/ppermute | solution.py:26
  27.6 1.7 %collective-permute-start.18 = (f32[2,16,128]{2,1,0:T(8,128)S(1)}, f32[2,16,128]{2,1,0:T(8,128)S(1)}, u32[]{:S(2)}, u32[]{:S(2)}) collective-permute-start(f32[2,16,128]{2,1,0:T(8,128)S(1)} %get-tuple-element.28), channel_id=1, source_target_pairs={{0,24},{4,28},{8,0},{12,4},{16,8},{20,12},{24,16},{28,20},{1,25},{... | collective-permute-start | bytes 49160 | tf_op jit(solution)/shard_map/return_products/ppermute | solution.py:26
  29.3 2.3 %collective-permute-start.19 = (f32[2,16,128]{2,1,0:T(8,128)S(1)}, f32[2,16,128]{2,1,0:T(8,128)S(1)}, u32[]{:S(2)}, u32[]{:S(2)}) collective-permute-start(f32[2,16,128]{2,1,0:T(8,128)S(1)} %get-tuple-element.29), channel_id=1, source_target_pairs={{0,28},{4,0},{8,4},{12,8},{16,12},{20,16},{24,20},{28,24},{1,29},{... | collective-permute-start | bytes 49160 | tf_op jit(solution)/shard_map/return_products/ppermute | solution.py:26
  31.7 1.1 %collective-permute-start.11 = (f32[16,128]{1,0:T(8,128)S(1)}, f32[16,128]{1,0:T(8,128)S(1)}, u32[]{:S(2)}, u32[]{:S(2)}) collective-permute-start(f32[16,128]{1,0:T(8,128)S(1)} %get-tuple-element.20), channel_id=1, source_target_pairs={{0,2},{1,3},{2,0},{3,1},{4,6},{5,7},{6,4},{7,5},{8,10},{9,11},{10,... | collective-permute-start | bytes 24584 | tf_op jit(solution)/shard_map/return_products/ppermute | solution.py:26
  32.8 2.9 %collective-permute-start.12 = (f32[16,128]{1,0:T(8,128)S(1)}, f32[16,128]{1,0:T(8,128)S(1)}, u32[]{:S(2)}, u32[]{:S(2)}) collective-permute-start(f32[16,128]{1,0:T(8,128)S(1)} %get-tuple-element.21), channel_id=1, source_target_pairs={{0,3},{1,0},{2,1},{3,2},{4,7},{5,4},{6,5},{7,6},{8,11},{9,8},{10,9... | collective-permute-start | bytes 24584 | tf_op jit(solution)/shard_map/return_products/ppermute | solution.py:26
  35.8 0.5 copy-done.12
  36.3 1.4 %rayleigh_over_row.1.refs_13_ = f32[16,16]{1,0:T(8,128)} custom-call(f32[2,16,128]{2,1,0:T(8,128)} %copy-done.1, f32[2,16,128]{2,1,0:T(8,128)} %copy-done.7, f32[2,16,128]{2,1,0:T(8,128)} %copy-done.8, f32[2,16,128]{2,1,0:T(8,128)} %copy-done.9, f32[2,16,128]{2,1,0:T(8,128)} %copy-done.10, f32[2,16,128]{2,1,0:T(8,128)} %copy-done.11, ...), custom_call_target="tpu_custom_call" | custom-call | tf_op jit(solution)/shard_map/rayleigh_sum/rayleigh_over_row/pallas_call | solution.py:143
  37.8 0.4 collective-permute-start.22
  38.2 1.4 %collective-permute-start.21 = (f32[16,16]{1,0:T(8,128)}, f32[16,16]{1,0:T(8,128)S(1)}, u32[]{:S(2)}, u32[]{:S(2)}) collective-permute-start(f32[16,16]{1,0:T(8,128)} %rayleigh_over_row.1.refs_13_), channel_id=1, source_target_pairs={{0,2},{1,3},{2,0},{3,1},{4,6},{5,7},{6,4},{7,5},{8,10},{9,11},{10,... | collective-permute-start | bytes 3080 | tf_op jit(solution)/shard_map/rayleigh_sum/ppermute | solution.py:26
  39.7 2.0 %collective-permute-start.20 = (f32[16,16]{1,0:T(8,128)}, f32[16,16]{1,0:T(8,128)S(1)}, u32[]{:S(2)}, u32[]{:S(2)}) collective-permute-start(f32[16,16]{1,0:T(8,128)} %rayleigh_over_row.1.refs_13_), channel_id=1, source_target_pairs={{0,1},{1,2},{2,3},{3,0},{4,5},{5,6},{6,7},{7,4},{8,9},{9,10},{10,1... | collective-permute-start | bytes 3080 | tf_op jit(solution)/shard_map/rayleigh_sum/ppermute | solution.py:26
  41.7 1.3 %collective-permute-done.21.refs_15_ = f32[16,16]{1,0:T(8,128)S(1)} collective-permute-done((f32[16,16]{1,0:T(8,128)}, f32[16,16]{1,0:T(8,128)S(1)}, u32[]{:S(2)}, u32[]{:S(2)}) %collective-permute-start.21) | collective-permute-done | bytes 1056 | tf_op jit(solution)/shard_map/rayleigh_sum/ppermute | solution.py:26
  43.0 2.3 %collective-permute-done.20.refs_14_ = f32[16,16]{1,0:T(8,128)S(1)} collective-permute-done((f32[16,16]{1,0:T(8,128)}, f32[16,16]{1,0:T(8,128)S(1)}, u32[]{:S(2)}, u32[]{:S(2)}) %collective-permute-start.20) | collective-permute-done | bytes 1056 | tf_op jit(solution)/shard_map/rayleigh_sum/ppermute | solution.py:26
  45.3 0.6 copy-done.23
  45.9 1.8 %residual.1 = (f32[16,128]{1,0:T(8,128)}, f32[16,16]{1,0:T(8,128)}, f32[16,16]{1,0:T(8,128)}) custom-call(f32[16,128]{1,0:T(8,128)} %refs_0_.1, f32[16,128]{1,0:T(8,128)} %copy-done.3, f32[16,128]{1,0:T(8,128)} %copy-done.14, f32[16,128]{1,0:T(8,128)} %copy-done.15, f32[16,128]{1,0:T(8,128)} %copy-done.16, f32[2,16,128]{2,1,0:T(8,128)} %copy-done.1, ...), custom_call_target="tpu_custom_call" | custom-call | tf_op jit(solution)/shard_map/residual/residual/pallas_call | solution.py:152
  47.8 0.4 collective-permute-start.28
  48.2 0.3 collective-permute-start.27
  48.5 1.5 %collective-permute-start.26 = (f32[16,16]{1,0:T(8,128)}, f32[16,16]{1,0:T(8,128)S(1)}, u32[]{:S(2)}, u32[]{:S(2)}) collective-permute-start(f32[16,16]{1,0:T(8,128)} %get-tuple-element.32.refs_0_), channel_id=1, source_target_pairs={{0,16},{4,20},{8,24},{12,28},{16,0},{20,4},{24,8},{28,12},{1,17},{... | collective-permute-start | bytes 3080 | tf_op jit(solution)/shard_map/gram_sum/ppermute | solution.py:26
  50.0 0.2 collective-permute-start.25
  50.2 2.5 %collective-permute-start.24 = (f32[16,16]{1,0:T(8,128)}, f32[16,16]{1,0:T(8,128)S(1)}, u32[]{:S(2)}, u32[]{:S(2)}) collective-permute-start(f32[16,16]{1,0:T(8,128)} %get-tuple-element.32.refs_0_), channel_id=1, source_target_pairs={{0,8},{4,12},{8,16},{12,20},{16,24},{20,28},{24,0},{28,4},{1,9},{5... | collective-permute-start | bytes 3080 | tf_op jit(solution)/shard_map/gram_sum/ppermute | solution.py:26
  52.8 0.5 collective-permute-done.25.refs_3_
  53.3 2.3 %collective-permute-done.24.refs_2_ = f32[16,16]{1,0:T(8,128)S(1)} collective-permute-done((f32[16,16]{1,0:T(8,128)}, f32[16,16]{1,0:T(8,128)S(1)}, u32[]{:S(2)}, u32[]{:S(2)}) %collective-permute-start.24) | collective-permute-done | bytes 1056 | tf_op jit(solution)/shard_map/gram_sum/ppermute | solution.py:26
  55.6 1.3 %collective-permute-done.23.refs_1_ = f32[16,16]{1,0:T(8,128)S(1)} collective-permute-done((f32[16,16]{1,0:T(8,128)}, f32[16,16]{1,0:T(8,128)S(1)}, u32[]{:S(2)}, u32[]{:S(2)}) %collective-permute-start.23) | collective-permute-done | bytes 1056 | tf_op jit(solution)/shard_map/gram_sum/ppermute | solution.py:26
  57.0 0.6 copy-done.26
  57.5 1.4 %gram_over_row.1.refs_0_ = f32[16,16]{1,0:T(8,128)} custom-call(f32[16,16]{1,0:T(8,128)} %get-tuple-element.32.refs_0_, f32[16,16]{1,0:T(8,128)} %copy-done.26, f32[16,16]{1,0:T(8,128)} %copy-done.25, f32[16,16]{1,0:T(8,128)} %copy-done.24, f32[16,16]{1,0:T(8,128)} %copy-done.22, f32[16,16]{1,0:T(8,128)} %copy-done.21, f32[16,16]{1,0:T(8,128)} %copy-done.20, ...), custom_call_target="tpu_custom_call" | custom-call | tf_op jit(solution)/shard_map/gram_sum/gram_over_row/pallas_call | solution.py:162
  59.0 0.7 %collective-permute-start.32 = (f32[16,16]{1,0:T(8,128)}, f32[16,16]{1,0:T(8,128)S(1)}, u32[]{:S(2)}, u32[]{:S(2)}) collective-permute-start(f32[16,16]{1,0:T(8,128)} %gram_over_row.1.refs_0_), channel_id=1, source_target_pairs={{0,3},{1,0},{2,1},{3,2},{4,7},{5,4},{6,5},{7,6},{8,11},{9,8},{10,9... | collective-permute-start | bytes 3080 | tf_op jit(solution)/shard_map/gram_sum/ppermute | solution.py:26
  59.7 1.0 %collective-permute-start.31 = (f32[16,16]{1,0:T(8,128)}, f32[16,16]{1,0:T(8,128)S(1)}, u32[]{:S(2)}, u32[]{:S(2)}) collective-permute-start(f32[16,16]{1,0:T(8,128)} %gram_over_row.1.refs_0_), channel_id=1, source_target_pairs={{0,2},{1,3},{2,0},{3,1},{4,6},{5,7},{6,4},{7,5},{8,10},{9,11},{10,... | collective-permute-start | bytes 3080 | tf_op jit(solution)/shard_map/gram_sum/ppermute | solution.py:26
  60.6 0.4 collective-permute-start.30
  61.0 1.8 %collective-permute-done.32.refs_3_ = f32[16,16]{1,0:T(8,128)S(1)} collective-permute-done((f32[16,16]{1,0:T(8,128)}, f32[16,16]{1,0:T(8,128)S(1)}, u32[]{:S(2)}, u32[]{:S(2)}) %collective-permute-start.32) | collective-permute-done | bytes 1056 | tf_op jit(solution)/shard_map/gram_sum/ppermute | solution.py:26
  62.8 1.6 %collective-permute-done.31.refs_2_ = f32[16,16]{1,0:T(8,128)S(1)} collective-permute-done((f32[16,16]{1,0:T(8,128)}, f32[16,16]{1,0:T(8,128)S(1)}, u32[]{:S(2)}, u32[]{:S(2)}) %collective-permute-start.31) | collective-permute-done | bytes 1056 | tf_op jit(solution)/shard_map/gram_sum/ppermute | solution.py:26
  64.5 1.9 %collective-permute-done.30.refs_1_ = f32[16,16]{1,0:T(8,128)S(1)} collective-permute-done((f32[16,16]{1,0:T(8,128)}, f32[16,16]{1,0:T(8,128)S(1)}, u32[]{:S(2)}, u32[]{:S(2)}) %collective-permute-start.30) | collective-permute-done | bytes 1056 | tf_op jit(solution)/shard_map/gram_sum/ppermute | solution.py:26
  66.3 0.6 copy-done.29
  66.9 1.4 %gram_over_col.1 = f32[16,16]{1,0:T(8,128)} custom-call(f32[16,16]{1,0:T(8,128)} %gram_over_row.1.refs_0_, f32[16,16]{1,0:T(8,128)} %copy-done.29, f32[16,16]{1,0:T(8,128)} %copy-done.28, f32[16,16]{1,0:T(8,128)} %copy-done.27), custom_call_target="tpu_custom_call" | custom-call | tf_op jit(solution)/shard_map/gram_sum/gram_over_col/pallas_call | solution.py:162
  (84 shorter events, 0.2 us)
Async XLA Ops:
  0.6 6.0 %copy-start.2 = (f32[16,128]{1,0:T(8,128)S(1)}, f32[16,128]{1,0:T(8,128)}, u32[]{:S(2)}) copy-start(f32[16,128]{1,0:T(8,128)} %refs_0_.1) | copy-start | bytes 24580
  0.6 6.0 %collective-permute-start.9 = (f32[16,128]{1,0:T(8,128)}, f32[16,128]{1,0:T(8,128)S(1)}, u32[]{:S(2)}, u32[]{:S(2)}) collective-permute-start(f32[16,128]{1,0:T(8,128)} %refs_0_.1), channel_id=1, source_target_pairs={{0,28},{4,0},{8,4},{12,8},{16,12},{20,16},{24,20},{28,24},{1,29},{... | collective-permute-start | bytes 24584 | tf_op jit(solution)/shard_map/share_vectors/ppermute | solution.py:26
  4.0 4.9 %collective-permute-start.8 = (f32[16,128]{1,0:T(8,128)}, f32[16,128]{1,0:T(8,128)S(1)}, u32[]{:S(2)}, u32[]{:S(2)}) collective-permute-start(f32[16,128]{1,0:T(8,128)} %refs_0_.1), channel_id=1, source_target_pairs={{0,24},{4,28},{8,0},{12,4},{16,8},{20,12},{24,16},{28,20},{1,25},{... | collective-permute-start | bytes 24584 | tf_op jit(solution)/shard_map/share_vectors/ppermute | solution.py:26
  4.7 4.3 %collective-permute-start.7 = (f32[16,128]{1,0:T(8,128)}, f32[16,128]{1,0:T(8,128)S(1)}, u32[]{:S(2)}, u32[]{:S(2)}) collective-permute-start(f32[16,128]{1,0:T(8,128)} %refs_0_.1), channel_id=1, source_target_pairs={{0,20},{4,24},{8,28},{12,0},{16,4},{20,8},{24,12},{28,16},{1,21},{... | collective-permute-start | bytes 24584 | tf_op jit(solution)/shard_map/share_vectors/ppermute | solution.py:26
  4.9 7.7 %collective-permute-start.6 = (f32[16,128]{1,0:T(8,128)}, f32[16,128]{1,0:T(8,128)S(1)}, u32[]{:S(2)}, u32[]{:S(2)}) collective-permute-start(f32[16,128]{1,0:T(8,128)} %refs_0_.1), channel_id=1, source_target_pairs={{0,16},{4,20},{8,24},{12,28},{16,0},{20,4},{24,8},{28,12},{1,17},{... | collective-permute-start | bytes 24584 | tf_op jit(solution)/shard_map/share_vectors/ppermute | solution.py:26
  6.5 6.2 %collective-permute-start.5 = (f32[16,128]{1,0:T(8,128)}, f32[16,128]{1,0:T(8,128)S(1)}, u32[]{:S(2)}, u32[]{:S(2)}) collective-permute-start(f32[16,128]{1,0:T(8,128)} %refs_0_.1), channel_id=1, source_target_pairs={{0,12},{4,16},{8,20},{12,24},{16,28},{20,0},{24,4},{28,8},{1,13},{... | collective-permute-start | bytes 24584 | tf_op jit(solution)/shard_map/share_vectors/ppermute | solution.py:26
  6.6 7.8 %collective-permute-start.4 = (f32[16,128]{1,0:T(8,128)S(1)}, f32[16,128]{1,0:T(8,128)S(1)}, u32[]{:S(2)}, u32[]{:S(2)}) collective-permute-start(f32[16,128]{1,0:T(8,128)S(1)} %copy-done.2), channel_id=1, source_target_pairs={{0,8},{4,12},{8,16},{12,20},{16,24},{20,28},{24,0},{28,4},{1,9},{5... | collective-permute-start | bytes 24584 | tf_op jit(solution)/shard_map/share_vectors/ppermute | solution.py:26
  8.9 5.5 %collective-permute-start.3 = (f32[16,128]{1,0:T(8,128)S(1)}, f32[16,128]{1,0:T(8,128)S(1)}, u32[]{:S(2)}, u32[]{:S(2)}) collective-permute-start(f32[16,128]{1,0:T(8,128)S(1)} %copy-done.2), channel_id=1, source_target_pairs={{0,4},{4,8},{8,12},{12,16},{16,20},{20,24},{24,28},{28,0},{1,5},{5... | collective-permute-start | bytes 24584 | tf_op jit(solution)/shard_map/share_vectors/ppermute | solution.py:26
  8.9 5.5 %collective-permute-start.2 = (f32[16,128]{1,0:T(8,128)S(1)}, f32[16,128]{1,0:T(8,128)S(1)}, u32[]{:S(2)}, u32[]{:S(2)}) collective-permute-start(f32[16,128]{1,0:T(8,128)S(1)} %copy-done.2), channel_id=1, source_target_pairs={{0,3},{1,0},{2,1},{3,2},{4,7},{5,4},{6,5},{7,6},{8,11},{9,8},{10,9... | collective-permute-start | bytes 24584 | tf_op jit(solution)/shard_map/share_vectors/ppermute | solution.py:26
  12.6 4.6 %collective-permute-start.1 = (f32[16,128]{1,0:T(8,128)S(1)}, f32[16,128]{1,0:T(8,128)S(1)}, u32[]{:S(2)}, u32[]{:S(2)}) collective-permute-start(f32[16,128]{1,0:T(8,128)S(1)} %copy-done.2), channel_id=1, source_target_pairs={{0,2},{1,3},{2,0},{3,1},{4,6},{5,7},{6,4},{7,5},{8,10},{9,11},{10,... | collective-permute-start | bytes 24584 | tf_op jit(solution)/shard_map/share_vectors/ppermute | solution.py:26
  12.6 5.5 %collective-permute-start = (f32[16,128]{1,0:T(8,128)S(1)}, f32[16,128]{1,0:T(8,128)S(1)}, u32[]{:S(2)}, u32[]{:S(2)}) collective-permute-start(f32[16,128]{1,0:T(8,128)S(1)} %copy-done.2), channel_id=1, source_target_pairs={{0,1},{1,2},{2,3},{3,0},{4,5},{5,6},{6,7},{7,4},{8,9},{9,10},{10,1... | collective-permute-start | bytes 24584 | tf_op jit(solution)/shard_map/share_vectors/ppermute | solution.py:26
  14.3 3.8 %copy-start.4 = (s32[1,1,16]{2,1,0:T(1,128)S(1)}, s32[1,1,16]{2,1,0:T(1,128)}, u32[]{:S(2)}) copy-start(s32[1,1,16]{2,1,0:T(1,128)} %refs_1_.1) | copy-start | bytes 196
  14.4 3.8 %copy-start.5 = (s32[1,1,16]{2,1,0:T(1,128)S(1)}, s32[1,1,16]{2,1,0:T(1,128)}, u32[]{:S(2)}) copy-start(s32[1,1,16]{2,1,0:T(1,128)} %refs_2_.1) | copy-start | bytes 196
  14.4 3.7 %copy-start.6 = (f32[128]{0:T(128)S(1)}, f32[128]{0:T(128)}, u32[]{:S(2)}) copy-start(f32[128]{0:T(128)} %param.7) | copy-start | bytes 1540
  23.4 8.3 %copy-start.3 = (f32[16,128]{1,0:T(8,128)}, f32[16,128]{1,0:T(8,128)S(1)}, u32[]{:S(2)}) copy-start(f32[16,128]{1,0:T(8,128)S(1)} %get-tuple-element.18.refs_1_) | copy-start | bytes 24580
  23.4 4.2 %collective-permute-start.13 = (f32[2,16,128]{2,1,0:T(8,128)S(1)}, f32[2,16,128]{2,1,0:T(8,128)S(1)}, u32[]{:S(2)}, u32[]{:S(2)}) collective-permute-start(f32[2,16,128]{2,1,0:T(8,128)S(1)} %get-tuple-element.23), channel_id=1, source_target_pairs={{0,4},{4,8},{8,12},{12,16},{16,20},{20,24},{24,28},{28,0},{1,5},{5... | collective-permute-start | bytes 49160 | tf_op jit(solution)/shard_map/return_products/ppermute | solution.py:26
  23.4 6.0 %collective-permute-start.14 = (f32[2,16,128]{2,1,0:T(8,128)S(1)}, f32[2,16,128]{2,1,0:T(8,128)S(1)}, u32[]{:S(2)}, u32[]{:S(2)}) collective-permute-start(f32[2,16,128]{2,1,0:T(8,128)S(1)} %get-tuple-element.24), channel_id=1, source_target_pairs={{0,8},{4,12},{8,16},{12,20},{16,24},{20,28},{24,0},{28,4},{1,9},{5... | collective-permute-start | bytes 49160 | tf_op jit(solution)/shard_map/return_products/ppermute | solution.py:26
  25.0 6.7 %collective-permute-start.15 = (f32[2,16,128]{2,1,0:T(8,128)S(1)}, f32[2,16,128]{2,1,0:T(8,128)S(1)}, u32[]{:S(2)}, u32[]{:S(2)}) collective-permute-start(f32[2,16,128]{2,1,0:T(8,128)S(1)} %get-tuple-element.25), channel_id=1, source_target_pairs={{0,12},{4,16},{8,20},{12,24},{16,28},{20,0},{24,4},{28,8},{1,13},{... | collective-permute-start | bytes 49160 | tf_op jit(solution)/shard_map/return_products/ppermute | solution.py:26
  26.1 5.6 %collective-permute-start.16 = (f32[2,16,128]{2,1,0:T(8,128)S(1)}, f32[2,16,128]{2,1,0:T(8,128)S(1)}, u32[]{:S(2)}, u32[]{:S(2)}) collective-permute-start(f32[2,16,128]{2,1,0:T(8,128)S(1)} %get-tuple-element.26), channel_id=1, source_target_pairs={{0,16},{4,20},{8,24},{12,28},{16,0},{20,4},{24,8},{28,12},{1,17},{... | collective-permute-start | bytes 49160 | tf_op jit(solution)/shard_map/return_products/ppermute | solution.py:26
  27.5 5.3 %collective-permute-start.17 = (f32[2,16,128]{2,1,0:T(8,128)S(1)}, f32[2,16,128]{2,1,0:T(8,128)S(1)}, u32[]{:S(2)}, u32[]{:S(2)}) collective-permute-start(f32[2,16,128]{2,1,0:T(8,128)S(1)} %get-tuple-element.27), channel_id=1, source_target_pairs={{0,20},{4,24},{8,28},{12,0},{16,4},{20,8},{24,12},{28,16},{1,21},{... | collective-permute-start | bytes 49160 | tf_op jit(solution)/shard_map/return_products/ppermute | solution.py:26
  27.6 8.2 %copy-start.7 = (f32[2,16,128]{2,1,0:T(8,128)}, f32[2,16,128]{2,1,0:T(8,128)S(1)}, u32[]{:S(2)}) copy-start(f32[2,16,128]{2,1,0:T(8,128)S(1)} %collective-permute-done.13.refs_1_.refs_6_) | copy-start | bytes 49156
  27.6 8.2 %collective-permute-start.18 = (f32[2,16,128]{2,1,0:T(8,128)S(1)}, f32[2,16,128]{2,1,0:T(8,128)S(1)}, u32[]{:S(2)}, u32[]{:S(2)}) collective-permute-start(f32[2,16,128]{2,1,0:T(8,128)S(1)} %get-tuple-element.28), channel_id=1, source_target_pairs={{0,24},{4,28},{8,0},{12,4},{16,8},{20,12},{24,16},{28,20},{1,25},{... | collective-permute-start | bytes 49160 | tf_op jit(solution)/shard_map/return_products/ppermute | solution.py:26
  29.3 6.4 %copy-start.8 = (f32[2,16,128]{2,1,0:T(8,128)}, f32[2,16,128]{2,1,0:T(8,128)S(1)}, u32[]{:S(2)}) copy-start(f32[2,16,128]{2,1,0:T(8,128)S(1)} %collective-permute-done.14.refs_2_.refs_7_) | copy-start | bytes 49156
  29.3 6.4 %collective-permute-start.19 = (f32[2,16,128]{2,1,0:T(8,128)S(1)}, f32[2,16,128]{2,1,0:T(8,128)S(1)}, u32[]{:S(2)}, u32[]{:S(2)}) collective-permute-start(f32[2,16,128]{2,1,0:T(8,128)S(1)} %get-tuple-element.29), channel_id=1, source_target_pairs={{0,28},{4,0},{8,4},{12,8},{16,12},{20,16},{24,20},{28,24},{1,29},{... | collective-permute-start | bytes 49160 | tf_op jit(solution)/shard_map/return_products/ppermute | solution.py:26
  31.6 4.1 %copy-start.9 = (f32[2,16,128]{2,1,0:T(8,128)}, f32[2,16,128]{2,1,0:T(8,128)S(1)}, u32[]{:S(2)}) copy-start(f32[2,16,128]{2,1,0:T(8,128)S(1)} %collective-permute-done.15.refs_3_.refs_8_) | copy-start | bytes 49156
  31.6 8.0 %collective-permute-start.10 = (f32[16,128]{1,0:T(8,128)S(1)}, f32[16,128]{1,0:T(8,128)S(1)}, u32[]{:S(2)}, u32[]{:S(2)}) collective-permute-start(f32[16,128]{1,0:T(8,128)S(1)} %get-tuple-element.19), channel_id=1, source_target_pairs={{0,1},{1,2},{2,3},{3,0},{4,5},{5,6},{6,7},{7,4},{8,9},{9,10},{10,1... | collective-permute-start | bytes 24584 | tf_op jit(solution)/shard_map/return_products/ppermute | solution.py:26
  31.7 4.1 %copy-start.10 = (f32[2,16,128]{2,1,0:T(8,128)}, f32[2,16,128]{2,1,0:T(8,128)S(1)}, u32[]{:S(2)}) copy-start(f32[2,16,128]{2,1,0:T(8,128)S(1)} %collective-permute-done.16.refs_4_.refs_9_) | copy-start | bytes 49156
  31.7 10.0 %collective-permute-start.11 = (f32[16,128]{1,0:T(8,128)S(1)}, f32[16,128]{1,0:T(8,128)S(1)}, u32[]{:S(2)}, u32[]{:S(2)}) collective-permute-start(f32[16,128]{1,0:T(8,128)S(1)} %get-tuple-element.20), channel_id=1, source_target_pairs={{0,2},{1,3},{2,0},{3,1},{4,6},{5,7},{6,4},{7,5},{8,10},{9,11},{10,... | collective-permute-start | bytes 24584 | tf_op jit(solution)/shard_map/return_products/ppermute | solution.py:26
  32.8 8.8 %collective-permute-start.12 = (f32[16,128]{1,0:T(8,128)S(1)}, f32[16,128]{1,0:T(8,128)S(1)}, u32[]{:S(2)}, u32[]{:S(2)}) collective-permute-start(f32[16,128]{1,0:T(8,128)S(1)} %get-tuple-element.21), channel_id=1, source_target_pairs={{0,3},{1,0},{2,1},{3,2},{4,7},{5,4},{6,5},{7,6},{8,11},{9,8},{10,9... | collective-permute-start | bytes 24584 | tf_op jit(solution)/shard_map/return_products/ppermute | solution.py:26
  37.8 3.9 %collective-permute-start.22 = (f32[16,16]{1,0:T(8,128)}, f32[16,16]{1,0:T(8,128)S(1)}, u32[]{:S(2)}, u32[]{:S(2)}) collective-permute-start(f32[16,16]{1,0:T(8,128)} %rayleigh_over_row.1.refs_13_), channel_id=1, source_target_pairs={{0,3},{1,0},{2,1},{3,2},{4,7},{5,4},{6,5},{7,6},{8,11},{9,8},{10,9... | collective-permute-start | bytes 3080 | tf_op jit(solution)/shard_map/rayleigh_sum/ppermute | solution.py:26
  38.2 4.8 %collective-permute-start.21 = (f32[16,16]{1,0:T(8,128)}, f32[16,16]{1,0:T(8,128)S(1)}, u32[]{:S(2)}, u32[]{:S(2)}) collective-permute-start(f32[16,16]{1,0:T(8,128)} %rayleigh_over_row.1.refs_13_), channel_id=1, source_target_pairs={{0,2},{1,3},{2,0},{3,1},{4,6},{5,7},{6,4},{7,5},{8,10},{9,11},{10,... | collective-permute-start | bytes 3080 | tf_op jit(solution)/shard_map/rayleigh_sum/ppermute | solution.py:26
  39.7 5.7 %copy-start.14 = (f32[16,128]{1,0:T(8,128)}, f32[16,128]{1,0:T(8,128)S(1)}, u32[]{:S(2)}) copy-start(f32[16,128]{1,0:T(8,128)S(1)} %collective-permute-done.10.refs_2_) | copy-start | bytes 24580
  39.7 5.7 %collective-permute-start.20 = (f32[16,16]{1,0:T(8,128)}, f32[16,16]{1,0:T(8,128)S(1)}, u32[]{:S(2)}, u32[]{:S(2)}) collective-permute-start(f32[16,16]{1,0:T(8,128)} %rayleigh_over_row.1.refs_13_), channel_id=1, source_target_pairs={{0,1},{1,2},{2,3},{3,0},{4,5},{5,6},{6,7},{7,4},{8,9},{9,10},{10,1... | collective-permute-start | bytes 3080 | tf_op jit(solution)/shard_map/rayleigh_sum/ppermute | solution.py:26
  47.7 2.4 %collective-permute-start.29 = (f32[16,16]{1,0:T(8,128)}, f32[16,16]{1,0:T(8,128)S(1)}, u32[]{:S(2)}, u32[]{:S(2)}) collective-permute-start(f32[16,16]{1,0:T(8,128)} %get-tuple-element.32.refs_0_), channel_id=1, source_target_pairs={{0,28},{4,0},{8,4},{12,8},{16,12},{20,16},{24,20},{28,24},{1,29},{... | collective-permute-start | bytes 3080 | tf_op jit(solution)/shard_map/gram_sum/ppermute | solution.py:26
  47.8 5.0 %collective-permute-start.28 = (f32[16,16]{1,0:T(8,128)}, f32[16,16]{1,0:T(8,128)S(1)}, u32[]{:S(2)}, u32[]{:S(2)}) collective-permute-start(f32[16,16]{1,0:T(8,128)} %get-tuple-element.32.refs_0_), channel_id=1, source_target_pairs={{0,24},{4,28},{8,0},{12,4},{16,8},{20,12},{24,16},{28,20},{1,25},{... | collective-permute-start | bytes 3080 | tf_op jit(solution)/shard_map/gram_sum/ppermute | solution.py:26
  48.2 4.6 %collective-permute-start.27 = (f32[16,16]{1,0:T(8,128)}, f32[16,16]{1,0:T(8,128)S(1)}, u32[]{:S(2)}, u32[]{:S(2)}) collective-permute-start(f32[16,16]{1,0:T(8,128)} %get-tuple-element.32.refs_0_), channel_id=1, source_target_pairs={{0,20},{4,24},{8,28},{12,0},{16,4},{20,8},{24,12},{28,16},{1,21},{... | collective-permute-start | bytes 3080 | tf_op jit(solution)/shard_map/gram_sum/ppermute | solution.py:26
  48.5 4.3 %collective-permute-start.26 = (f32[16,16]{1,0:T(8,128)}, f32[16,16]{1,0:T(8,128)S(1)}, u32[]{:S(2)}, u32[]{:S(2)}) collective-permute-start(f32[16,16]{1,0:T(8,128)} %get-tuple-element.32.refs_0_), channel_id=1, source_target_pairs={{0,16},{4,20},{8,24},{12,28},{16,0},{20,4},{24,8},{28,12},{1,17},{... | collective-permute-start | bytes 3080 | tf_op jit(solution)/shard_map/gram_sum/ppermute | solution.py:26
  50.0 3.3 %collective-permute-start.25 = (f32[16,16]{1,0:T(8,128)}, f32[16,16]{1,0:T(8,128)S(1)}, u32[]{:S(2)}, u32[]{:S(2)}) collective-permute-start(f32[16,16]{1,0:T(8,128)} %get-tuple-element.32.refs_0_), channel_id=1, source_target_pairs={{0,12},{4,16},{8,20},{12,24},{16,28},{20,0},{24,4},{28,8},{1,13},{... | collective-permute-start | bytes 3080 | tf_op jit(solution)/shard_map/gram_sum/ppermute | solution.py:26
  50.2 6.7 %copy-start.18 = (f32[16,16]{1,0:T(8,128)}, f32[16,16]{1,0:T(8,128)S(1)}, u32[]{:S(2)}) copy-start(f32[16,16]{1,0:T(8,128)S(1)} %collective-permute-done.29.refs_7_) | copy-start | bytes 3076
  50.2 5.4 %collective-permute-start.24 = (f32[16,16]{1,0:T(8,128)}, f32[16,16]{1,0:T(8,128)S(1)}, u32[]{:S(2)}, u32[]{:S(2)}) collective-permute-start(f32[16,16]{1,0:T(8,128)} %get-tuple-element.32.refs_0_), channel_id=1, source_target_pairs={{0,8},{4,12},{8,16},{12,20},{16,24},{20,28},{24,0},{28,4},{1,9},{5... | collective-permute-start | bytes 3080 | tf_op jit(solution)/shard_map/gram_sum/ppermute | solution.py:26
  52.7 4.2 %copy-start.20 = (f32[16,16]{1,0:T(8,128)}, f32[16,16]{1,0:T(8,128)S(1)}, u32[]{:S(2)}) copy-start(f32[16,16]{1,0:T(8,128)S(1)} %collective-permute-done.28.refs_6_) | copy-start | bytes 3076
  52.7 4.2 %collective-permute-start.23 = (f32[16,16]{1,0:T(8,128)}, f32[16,16]{1,0:T(8,128)S(1)}, u32[]{:S(2)}, u32[]{:S(2)}) collective-permute-start(f32[16,16]{1,0:T(8,128)} %get-tuple-element.32.refs_0_), channel_id=1, source_target_pairs={{0,4},{4,8},{8,12},{12,16},{16,20},{20,24},{24,28},{28,0},{1,5},{5... | collective-permute-start | bytes 3080 | tf_op jit(solution)/shard_map/gram_sum/ppermute | solution.py:26
  52.7 4.2 %copy-start.21 = (f32[16,16]{1,0:T(8,128)}, f32[16,16]{1,0:T(8,128)S(1)}, u32[]{:S(2)}) copy-start(f32[16,16]{1,0:T(8,128)S(1)} %collective-permute-done.27.refs_5_) | copy-start | bytes 3076
  52.8 4.2 %copy-start.22 = (f32[16,16]{1,0:T(8,128)}, f32[16,16]{1,0:T(8,128)S(1)}, u32[]{:S(2)}) copy-start(f32[16,16]{1,0:T(8,128)S(1)} %collective-permute-done.26.refs_4_) | copy-start | bytes 3076
  53.2 3.7 %copy-start.24 = (f32[16,16]{1,0:T(8,128)}, f32[16,16]{1,0:T(8,128)S(1)}, u32[]{:S(2)}) copy-start(f32[16,16]{1,0:T(8,128)S(1)} %collective-permute-done.25.refs_3_) | copy-start | bytes 3076
  59.0 3.9 %collective-permute-start.32 = (f32[16,16]{1,0:T(8,128)}, f32[16,16]{1,0:T(8,128)S(1)}, u32[]{:S(2)}, u32[]{:S(2)}) collective-permute-start(f32[16,16]{1,0:T(8,128)} %gram_over_row.1.refs_0_), channel_id=1, source_target_pairs={{0,3},{1,0},{2,1},{3,2},{4,7},{5,4},{6,5},{7,6},{8,11},{9,8},{10,9... | collective-permute-start | bytes 3080 | tf_op jit(solution)/shard_map/gram_sum/ppermute | solution.py:26
  59.7 4.8 %collective-permute-start.31 = (f32[16,16]{1,0:T(8,128)}, f32[16,16]{1,0:T(8,128)S(1)}, u32[]{:S(2)}, u32[]{:S(2)}) collective-permute-start(f32[16,16]{1,0:T(8,128)} %gram_over_row.1.refs_0_), channel_id=1, source_target_pairs={{0,2},{1,3},{2,0},{3,1},{4,6},{5,7},{6,4},{7,5},{8,10},{9,11},{10,... | collective-permute-start | bytes 3080 | tf_op jit(solution)/shard_map/gram_sum/ppermute | solution.py:26
  60.6 5.7 %collective-permute-start.30 = (f32[16,16]{1,0:T(8,128)}, f32[16,16]{1,0:T(8,128)S(1)}, u32[]{:S(2)}, u32[]{:S(2)}) collective-permute-start(f32[16,16]{1,0:T(8,128)} %gram_over_row.1.refs_0_), channel_id=1, source_target_pairs={{0,1},{1,2},{2,3},{3,0},{4,5},{5,6},{6,7},{7,4},{8,9},{9,10},{10,1... | collective-permute-start | bytes 3080 | tf_op jit(solution)/shard_map/gram_sum/ppermute | solution.py:26
  (15 other events, 27.8 us)

commit v2 on v0

v2 whole, which is shorter than its diff:
```python
import functools

import jax
import jax.numpy as jnp
from jax import lax
from jax.experimental import pallas as pl
from jax.experimental.pallas import tpu as pltpu
from jax.sharding import PartitionSpec as P

HP = lax.Precision.HIGHEST
LAST = (((1,), (1,)), ((), ()))
VMEM = pl.BlockSpec(memory_space=pltpu.VMEM)
SMEM = pl.BlockSpec(memory_space=pltpu.SMEM)


def mult(left, right):
    return lax.dot_general(left, right, (((1,), (0,)), ((), ())), precision=HP, preferred_element_type=jnp.float32)


def mult_last(left, right):
    return lax.dot_general(left, right, LAST, precision=HP, preferred_element_type=jnp.float32)


def swap(blocks, axis):
    return lax.all_to_all(blocks, axis, 0, 0, tiled=True)


def gather(value, axis):
    return swap(jnp.broadcast_to(value[None], (lax.axis_size(axis),) + value.shape), axis)


def products_kernel(n_row, n_col, slots, arow, bcol, count, x_ref, d_ref, x_rows, x_cols, tiles, row_terms, col_terms):
    own = x_ref[...]
    row_terms[...] = jnp.zeros_like(row_terms)
    col_terms[...] = jnp.zeros_like(col_terms)
    live_total = count[0, 0]
    for slot in range(slots):
        a = arow[0, 0, slot]
        b = bcol[0, 0, slot]
        live = jnp.where(slot < live_total, 1.0, 0.0).astype(jnp.float32)
        tile = tiles[0, 0, slot]
        row_terms[a] += mult_last(x_cols[b] * live, tile)
        col_terms[b, 0] += mult(x_rows[a] * live, tile)
    total = mult_last(own, 0.5 * d_ref[...] * own)
    for block in range(n_col):
        total += mult_last(x_rows[block], row_terms[block])
    wide = jnp.concatenate([total, jnp.zeros((own.shape[0], own.shape[1] - own.shape[0]), jnp.float32)], axis=1)
    for block in range(n_row):
        col_terms[block, 1] = wide


def spread(out, square):
    nvec = square.shape[0]
    wide = jnp.concatenate([square, jnp.zeros((nvec, out.shape[2] - nvec), jnp.float32)], axis=1)
    for block in range(out.shape[0]):
        out[block] = wide


def row_sum_kernel(by_row, out):
    out_block = jnp.sum(by_row[:, 1], axis=0)
    for block in range(out.shape[0]):
        out[block] = out_block


def residual_kernel(scale, x_ref, d_ref, by_col, by_row, cross, residual, rayleigh, gram):
    own = x_ref[...]
    nvec = own.shape[0]
    product = jnp.sum(by_col[...], axis=0) + jnp.sum(by_row[:, 0], axis=0) + d_ref[...] * own
    half = jnp.sum(cross[...], axis=0)[:, :nvec]
    ray = (half + half.T) * scale
    rayleigh[...] = ray
    res = product - mult(ray, own)
    residual[...] = res
    spread(gram, mult_last(res, res))


def again_kernel(parts, out):
    total = jnp.sum(parts[...], axis=0)
    for block in range(out.shape[0]):
        out[block] = total


def sum_kernel(scale, parts, out):
    out[...] = jnp.sum(parts[...], axis=0)[:, : out.shape[0]] * scale


def per_device(vectors, diagonal_energy, tiles, tile_rows, tile_cols, tile_count):
    n_row = lax.axis_size("row")
    n_col = lax.axis_size("col")
    nvec, width = vectors.shape
    slots = tiles.shape[2]
    scale = 1.0 / float(n_row * n_col * width)
    block = jax.ShapeDtypeStruct((nvec, width), jnp.float32)
    square = jax.ShapeDtypeStruct((nvec, nvec), jnp.float32)
    per_col = jax.ShapeDtypeStruct((n_col, nvec, width), jnp.float32)
    per_row = jax.ShapeDtypeStruct((n_row, nvec, width), jnp.float32)
    energy = diagonal_energy.reshape(1, width)
    with jax.named_scope("share_vectors"):
        x_cols = gather(vectors, "row")
        x_rows = gather(vectors, "col")
    with jax.named_scope("tile_products"):
        row_terms, col_terms = pl.pallas_call(
            functools.partial(products_kernel, n_row, n_col, slots),
            out_shape=[
                per_col,
                jax.ShapeDtypeStruct((n_row, 2, nvec, width), jnp.float32),
            ],
            in_specs=[SMEM] * 3 + [VMEM] * 5,
            out_specs=[VMEM] * 2,
            compiler_params=pltpu.CompilerParams(vmem_limit_bytes=16 * 2**20),
            name="tile_products",
        )(tile_rows, tile_cols, tile_count, vectors, energy, x_rows, x_cols, tiles)
    with jax.named_scope("return_products"):
        by_row = swap(col_terms, "row")
        by_col = swap(row_terms, "col")
    with jax.named_scope("rayleigh_sum"):
        cross = pl.pallas_call(
            row_sum_kernel, out_shape=per_col, in_specs=[VMEM], out_specs=VMEM, name="rayleigh_over_row"
        )(by_row)
        crosses = swap(cross, "col")
    with jax.named_scope("residual"):
        residual, rayleigh, part = pl.pallas_call(
            functools.partial(residual_kernel, scale),
            out_shape=[block, square, per_row],
            in_specs=[VMEM] * 5,
            out_specs=[VMEM] * 3,
            name="residual",
        )(vectors, energy, by_col, by_row, crosses)
    with jax.named_scope("gram_sum"):
        part = pl.pallas_call(
            again_kernel, out_shape=per_col, in_specs=[VMEM], out_specs=VMEM, name="gram_over_row"
        )(swap(part, "row"))
        gram = pl.pallas_call(
            functools.partial(sum_kernel, scale), out_shape=square, in_specs=[VMEM], out_specs=VMEM, name="gram_over_col"
        )(swap(part, "col"))
    return (residual, rayleigh, gram)


def solution(mesh):
    return jax.shard_map(
        per_device,
        mesh=mesh,
        in_specs=(
            P(None, ("row", "col")),
            P(("row", "col")),
            P("row", "col", None, None, None),
            P("row", "col", None),
            P("row", "col", None),
            P("row", "col"),
        ),
        out_specs=(P(None, ("row", "col")), P(), P()),
        check_vma=False,
    )
```

time: 167 us -> 78.9 us (0.47)
  blocking collectives: 105 us -> 48.6 us
  waiting for transfers between devices: 36 us -> 8.43 us
  between operations: 14.8 us -> 1.33 us
  Pallas kernels: 0 us -> 10.1 us
  starting transfers between devices: 0.08 us -> 6.99 us
  matrix products: 4.9 us -> 0 us
  local copies, waits for them, and re-layouts: 5.75 us -> 2.57 us
    psum x2 -> x0, blocking collectives: 80.4 us -> none  [the longest x1 41 us: per_device(): lax.psum(jnp.dot(residual, residual.T, precision=hp), ('row', 'col'))]
    all_to_all x0 -> x5, blocking collectives: none -> 48.6 us  [swap(): return lax.all_to_all(blocks, axis, 0, 0, tiled=True)]
    reduce_scatter x2 -> x0, waiting for transfers between devices: 36 us -> none  [the longest x1 33 us: per_device(): lax.psum_scatter(col_terms, 'row', scatter_dimension=1, tiled=True)]
    all_gather x2 -> x0, blocking collectives: 24.1 us -> none  [the longest x1 13.3 us: per_device(): lax.all_gather(vectors, 'col', axis=1, tiled=True)]
    pallas_call x0 -> x5, Pallas kernels: none -> 10.1 us  [the longest x1 3.84 us: per_device(): pl.pallas_call(functools.partial(products_kernel, n_row, n_col, slots), o...]
    all_to_all x0 -> x2, waiting for transfers between devices: none -> 8.43 us  [swap(): return lax.all_to_all(blocks, axis, 0, 0, tiled=True)]
    all_to_all x0 -> x2, starting transfers between devices: none -> 6.99 us  [swap(): return lax.all_to_all(blocks, axis, 0, 0, tiled=True)]
    dot_general x9 -> x0, matrix products: 4.9 us -> none  [the longest x1 1.73 us: per_device(): jnp.einsum('svk,snk->svn', own_cols, tile_set, precision=hp)]
  transfers between devices with their start and end apart: 2 -> 2, of which waited for: 2 -> 2; matrix products, arithmetic and copies ran while one was open for 1% -> 0% of each run, Pallas kernels for 0% -> 2%
where the time goes in v2:
time: 78.9 us; the launch traced here: 78 us
  blocking collectives  48.6 us (62%)
  Pallas kernels  10.1 us (13%)
  waiting for transfers between devices  8.43 us (11%)
  starting transfers between devices  6.99 us (9%)
  local copies, waits for them, and re-layouts  2.57 us (3%)
  between operations  1.33 us (2%)
    all_to_all x5, blocking collectives, swap(): return lax.all_to_all(blocks, axis, 0, 0, tiled=True)  48.6 us
    all_to_all x2, waiting for transfers between devices, swap(): return lax.all_to_all(blocks, axis, 0, 0, tiled=True)  8.43 us
    all_to_all x2, starting transfers between devices, swap(): return lax.all_to_all(blocks, axis, 0, 0, tiled=True)  6.99 us
    pallas_call x1, Pallas kernels, per_device(): pl.pallas_call(functools.partial(products_kernel, n_row, n_col, slots), o...  3.84 us
    pallas_call x1, Pallas kernels, per_device(): pl.pallas_call(functools.partial(residual_kernel, scale), out_shape=[bloc...  1.91 us
  transfers between devices with their start and end apart: 2, of which 2 were waited for; matrix products, arithmetic and copies ran while one was open for 0% of the time, Pallas kernels for 2%

profile of v2, /device:TPU:0, one launch (start us, length us, event | category | flops | bytes accessed | tf_op | source)
XLA Modules:
  0.0 78.0 jit_solution(6034520492597388137)
XLA Ops:
  0.6 0.7 broadcast_in_dim.4
  1.3 0.0 copy-start.1
  1.3 11.9 %all_to_all.35.x_rows = f32[4,16,128]{2,1,0:T(8,128)S(1)} all-to-all(f32[4,16,128]{2,1,0:T(8,128)S(1)} %broadcast_in_dim.4), channel_id=1, replica_groups=mesh['row'=8,'col'=4] {'col'}, dimensions={0} | all-to-all | bytes 65536 | tf_op jit(solution)/shard_map/share_vectors/all_to_all | solution.py:25
  13.2 0.0 copy-done.1
  13.2 0.6 broadcast_in_dim.5
  13.9 3.7 %all-to-all-start.1 = ((f32[8,16,128]{2,1,0:T(8,128)}), f32[8,16,128]{2,1,0:T(8,128)S(1)}, u32[]{:S(2)}, u32[]{:S(2)}) async-start(f32[8,16,128]{2,1,0:T(8,128)} %broadcast_in_dim.5), calls=%async_computation.1 | async-start | bytes 131072 | tf_op jit(solution)/shard_map/share_vectors/all_to_all | solution.py:25
  18.2 0.0 copy-start.2
  18.2 0.0 copy-start.3
  18.3 0.0 copy-start.4
  18.3 4.3 %all-to-all-done.1.x_cols = f32[8,16,128]{2,1,0:T(8,128)S(1)} async-done(((f32[8,16,128]{2,1,0:T(8,128)}), f32[8,16,128]{2,1,0:T(8,128)S(1)}, u32[]{:S(2)}, u32[]{:S(2)}) %all-to-all-start.1) | async-done | bytes 65568 | tf_op jit(solution)/shard_map/share_vectors/all_to_all | solution.py:25
  22.6 0.0 copy-done.2
  22.6 0.0 copy-done.3
  22.6 0.0 copy-done.4
  22.6 0.0 copy-start
  22.6 1.2 %copy-done = f32[1,1,16,128,128]{4,3,2,1,0:T(8,128)S(1)} copy-done((f32[1,1,16,128,128]{4,3,2,1,0:T(8,128)S(1)}, f32[1,1,16,128,128]{4,3,2,1,0:T(8,128)}, u32[]{:S(2)}) %copy-start) | copy-done | bytes 1048600
  23.8 3.8 %tile_products.1 = (f32[4,16,128]{2,1,0:T(8,128)}, f32[8,2,16,128]{3,2,1,0:T(8,128)S(1)}) custom-call(s32[1,1,16]{2,1,0:T(1,128)S(1)} %copy-done.3, s32[1,1,16]{2,1,0:T(1,128)S(1)} %copy-done.4, s32[1,1]{1,0:T(1,128)S(6)} %copy.9.count, f32[16,128]{1,0:T(8,128)S(1)} %copy-done.1, f32[1,128]{1,0:T(1,128)S(1)} %bitcast.2, ...), custom_call_target="tpu_custom_call" | custom-call | tf_op jit(solution)/shard_map/tile_products/tile_products/pallas_call | solution.py:102
  27.7 8.6 %all_to_all.36.by_row = f32[8,2,16,128]{3,2,1,0:T(8,128)} all-to-all(f32[8,2,16,128]{3,2,1,0:T(8,128)S(1)} %get-tuple-element.9), channel_id=1, replica_groups=mesh['row'=8,'col'=4] {'row'}, dimensions={0} | all-to-all | bytes 262144 | tf_op jit(solution)/shard_map/return_products/all_to_all | solution.py:25
  36.3 3.3 %all-to-all-start.2 = ((f32[4,16,128]{2,1,0:T(8,128)}), f32[4,16,128]{2,1,0:T(8,128)S(1)}, u32[]{:S(2)}, u32[]{:S(2)}) async-start(f32[4,16,128]{2,1,0:T(8,128)} %get-tuple-element.8), calls=%async_computation.2 | async-start | bytes 65536 | tf_op jit(solution)/shard_map/return_products/all_to_all | solution.py:25
  39.5 1.5 %rayleigh_over_row.1 = f32[4,16,128]{2,1,0:T(8,128)} custom-call(f32[8,2,16,128]{3,2,1,0:T(8,128)} %all_to_all.36.by_row), custom_call_target="tpu_custom_call" | custom-call | tf_op jit(solution)/shard_map/rayleigh_sum/rayleigh_over_row/pallas_call | solution.py:117
  41.1 4.1 %all-to-all-done.2.by_col = f32[4,16,128]{2,1,0:T(8,128)S(1)} async-done(((f32[4,16,128]{2,1,0:T(8,128)}), f32[4,16,128]{2,1,0:T(8,128)S(1)}, u32[]{:S(2)}, u32[]{:S(2)}) %all-to-all-start.2) | async-done | bytes 32800 | tf_op jit(solution)/shard_map/return_products/all_to_all | solution.py:25
  45.2 0.0 copy-start.5
  45.2 9.6 %all_to_all.37.cross = f32[4,16,128]{2,1,0:T(8,128)} all-to-all(f32[4,16,128]{2,1,0:T(8,128)} %rayleigh_over_row.1), channel_id=1, replica_groups=mesh['row'=8,'col'=4] {'col'}, dimensions={0} | all-to-all | bytes 65536 | tf_op jit(solution)/shard_map/rayleigh_sum/all_to_all | solution.py:25
  54.8 0.0 copy-done.5
  54.8 1.9 %residual.1 = (f32[16,128]{1,0:T(8,128)}, f32[16,16]{1,0:T(8,128)}, f32[8,16,128]{2,1,0:T(8,128)}) custom-call(f32[16,128]{1,0:T(8,128)} %x_ref.3, f32[1,128]{1,0:T(1,128)} %bitcast.1, f32[4,16,128]{2,1,0:T(8,128)} %copy-done.5, f32[8,2,16,128]{3,2,1,0:T(8,128)} %all_to_all.36.by_row, f32[4,16,128]{2,1,0:T(8,128)} %all_to_all.37.cross), custom_call_target="tpu_custom_call" | custom-call | tf_op jit(solution)/shard_map/residual/residual/pallas_call | solution.py:122
  56.7 9.0 %all_to_all.38.parts = f32[8,16,128]{2,1,0:T(8,128)} all-to-all(f32[8,16,128]{2,1,0:T(8,128)} %get-tuple-element.12), channel_id=1, replica_groups=mesh['row'=8,'col'=4] {'row'}, dimensions={0} | all-to-all | bytes 131072 | tf_op jit(solution)/shard_map/gram_sum/all_to_all | solution.py:25
  65.6 1.4 %gram_over_row.1 = f32[4,16,128]{2,1,0:T(8,128)} custom-call(f32[8,16,128]{2,1,0:T(8,128)} %all_to_all.38.parts), custom_call_target="tpu_custom_call" | custom-call | tf_op jit(solution)/shard_map/gram_sum/gram_over_row/pallas_call | solution.py:130
  67.1 9.6 %all_to_all.39.parts = f32[4,16,128]{2,1,0:T(8,128)} all-to-all(f32[4,16,128]{2,1,0:T(8,128)} %gram_over_row.1), channel_id=1, replica_groups=mesh['row'=8,'col'=4] {'col'}, dimensions={0} | all-to-all | bytes 65536 | tf_op jit(solution)/shard_map/gram_sum/all_to_all | solution.py:25
  76.7 1.4 %gram_over_col.1 = f32[16,16]{1,0:T(8,128)} custom-call(f32[4,16,128]{2,1,0:T(8,128)} %all_to_all.39.parts), custom_call_target="tpu_custom_call" | custom-call | tf_op jit(solution)/shard_map/gram_sum/gram_over_col/pallas_call | solution.py:133
Async XLA Ops:
  1.3 11.9 %copy-start.1 = (f32[16,128]{1,0:T(8,128)S(1)}, f32[16,128]{1,0:T(8,128)}, u32[]{:S(2)}) copy-start(f32[16,128]{1,0:T(8,128)} %x_ref.3) | copy-start | bytes 24580
  13.9 8.7 %all-to-all-start.1 = ((f32[8,16,128]{2,1,0:T(8,128)}), f32[8,16,128]{2,1,0:T(8,128)S(1)}, u32[]{:S(2)}, u32[]{:S(2)}) async-start(f32[8,16,128]{2,1,0:T(8,128)} %broadcast_in_dim.5), calls=%async_computation.1 | async-start | bytes 131072 | tf_op jit(solution)/shard_map/share_vectors/all_to_all | solution.py:25
  18.2 4.4 %copy-start.2 = (f32[128]{0:T(128)S(1)}, f32[128]{0:T(128)}, u32[]{:S(2)}) copy-start(f32[128]{0:T(128)} %param.7) | copy-start | bytes 1540
  18.2 4.4 %copy-start.3 = (s32[1,1,16]{2,1,0:T(1,128)S(1)}, s32[1,1,16]{2,1,0:T(1,128)}, u32[]{:S(2)}) copy-start(s32[1,1,16]{2,1,0:T(1,128)} %arow.1) | copy-start | bytes 196
  18.3 4.4 %copy-start.4 = (s32[1,1,16]{2,1,0:T(1,128)S(1)}, s32[1,1,16]{2,1,0:T(1,128)}, u32[]{:S(2)}) copy-start(s32[1,1,16]{2,1,0:T(1,128)} %bcol.1) | copy-start | bytes 196
  22.6 1.2 %copy-start = (f32[1,1,16,128,128]{4,3,2,1,0:T(8,128)S(1)}, f32[1,1,16,128,128]{4,3,2,1,0:T(8,128)}, u32[]{:S(2)}) copy-start(f32[1,1,16,128,128]{4,3,2,1,0:T(8,128)} %tiles.1) | copy-start | bytes 3145732
  36.3 8.9 %all-to-all-start.2 = ((f32[4,16,128]{2,1,0:T(8,128)}), f32[4,16,128]{2,1,0:T(8,128)S(1)}, u32[]{:S(2)}, u32[]{:S(2)}) async-start(f32[4,16,128]{2,1,0:T(8,128)} %get-tuple-element.8), calls=%async_computation.2 | async-start | bytes 65536 | tf_op jit(solution)/shard_map/return_products/all_to_all | solution.py:25
  45.2 9.6 %copy-start.5 = (f32[4,16,128]{2,1,0:T(8,128)}, f32[4,16,128]{2,1,0:T(8,128)S(1)}, u32[]{:S(2)}) copy-start(f32[4,16,128]{2,1,0:T(8,128)S(1)} %all-to-all-done.2.by_col) | copy-start | bytes 98308

commit v3 on v0

v3 whole, which is shorter than its diff:
```python
import functools

import jax
import jax.numpy as jnp
from jax import lax
from jax.experimental import pallas as pl
from jax.experimental.pallas import tpu as pltpu
from jax.sharding import PartitionSpec as P

HP = lax.Precision.HIGHEST
VMEM = pl.BlockSpec(memory_space=pltpu.VMEM)
SMEM = pl.BlockSpec(memory_space=pltpu.SMEM)
BOTH = ("row", "col")


def mult(left, right):
    return lax.dot_general(left, right, (((1,), (0,)), ((), ())), precision=HP, preferred_element_type=jnp.float32)


def mult_last(left, right):
    return lax.dot_general(left, right, (((1,), (1,)), ((), ())), precision=HP, preferred_element_type=jnp.float32)


def swap(blocks):
    return lax.all_to_all(blocks, BOTH, 0, 0, tiled=True)


def own_lanes(nvec, width):
    row = lax.broadcasted_iota(jnp.int32, (nvec, width), 0)
    lane = lax.broadcasted_iota(jnp.int32, (nvec, width), 1)
    return lane // nvec == row % (width // nvec)


def packed_gram(left, right):
    nvec, width = left.shape
    per = width // nvec
    wide = mult_last(left, jnp.concatenate([right] * per, axis=0))
    wide = jnp.where(own_lanes(nvec, width), wide, 0.0)
    return jnp.sum(wide.reshape(nvec // per, per, width), axis=1)


def unpack(packed, nvec):
    rows, width = packed.shape
    per = width // nvec
    wide = jnp.concatenate([jnp.broadcast_to(packed[g : g + 1], (per, width)) for g in range(rows)], axis=0)
    wide = jnp.where(own_lanes(nvec, width), wide, 0.0)
    lane = lax.broadcasted_iota(jnp.int32, (width, nvec), 0)
    column = lax.broadcasted_iota(jnp.int32, (width, nvec), 1)
    return mult(wide, (lane % nvec == column).astype(jnp.float32))


def products_kernel(n_row, n_col, slots, place, arow, bcol, count, x_ref, d_ref, x_all, tiles, out, row_terms):
    own = x_ref[...]
    nvec = own.shape[0]
    me_row, me_col = place[0], place[1]
    out[...] = jnp.zeros_like(out)
    half = 0.5 * d_ref[...] * own
    row_terms[...] = jnp.zeros_like(row_terms)
    row_terms[me_col] = half
    out[me_row * n_col + me_col, :nvec] = half
    live_total = count[0, 0]
    for slot in range(slots):
        a = arow[0, 0, slot]
        i = me_row * n_col + a
        j = bcol[0, 0, slot] * n_col + me_col
        live = jnp.where(slot < live_total, 1.0, 0.0).astype(jnp.float32)
        tile = tiles[0, 0, slot]
        row_terms[a] += mult_last(x_all[j] * live, tile)
        out[j, :nvec] += mult(x_all[i] * live, tile)
    left, right = [], []
    for a in range(n_col):
        i = me_row * n_col + a
        terms = row_terms[a]
        out[i, :nvec] += terms
        part = packed_gram(x_all[i], terms)
        total = part if a == 0 else total + part
    for block in range(n_row * n_col):
        out[block, nvec : nvec + total.shape[0]] = total


def residual_kernel(scale, x_ref, parts, residual, rayleigh, out):
    own = x_ref[...]
    nvec = own.shape[0]
    both = jnp.sum(parts[...], axis=0)
    half = unpack(both[nvec : nvec + out.shape[1]], nvec)
    ray = (half + half.T) * scale
    rayleigh[...] = ray
    res = both[:nvec] - mult(ray, own)
    residual[...] = res
    part = packed_gram(res, res)
    for block in range(out.shape[0]):
        out[block] = part


def gram_kernel(scale, parts, out):
    out[...] = unpack(jnp.sum(parts[...], axis=0), out.shape[0]) * scale


def per_device(vectors, diagonal_energy, tiles, tile_rows, tile_cols, tile_count):
    n_row = lax.axis_size("row")
    n_col = lax.axis_size("col")
    devices = n_row * n_col
    nvec, width = vectors.shape
    slots = tiles.shape[2]
    scale = 1.0 / float(devices * width)
    packed_rows = nvec * nvec // width
    padded = nvec + 8 * (-(-packed_rows // 8))
    square = jax.ShapeDtypeStruct((nvec, nvec), jnp.float32)
    place = jnp.stack([lax.axis_index("row"), lax.axis_index("col")]).astype(jnp.int32)
    with jax.named_scope("share_vectors"):
        x_all = swap(jnp.broadcast_to(vectors[None], (devices, nvec, width)))
    with jax.named_scope("tile_products"):
        terms = pl.pallas_call(
            functools.partial(products_kernel, n_row, n_col, slots),
            out_shape=jax.ShapeDtypeStruct((devices, padded, width), jnp.float32),
            in_specs=[SMEM] * 4 + [VMEM] * 4,
            out_specs=VMEM,
            scratch_shapes=[pltpu.VMEM((n_col, nvec, width), jnp.float32)],
            compiler_params=pltpu.CompilerParams(vmem_limit_bytes=40 * 2**20),
            name="tile_products",
        )(place, tile_rows, tile_cols, tile_count, vectors, diagonal_energy.reshape(1, width), x_all, tiles)
    with jax.named_scope("return_products"):
        parts = swap(terms)
    with jax.named_scope("residual"):
        residual, rayleigh, grams = pl.pallas_call(
            functools.partial(residual_kernel, scale),
            out_shape=[
                jax.ShapeDtypeStruct((nvec, width), jnp.float32),
                square,
                jax.ShapeDtypeStruct((devices, packed_rows, width), jnp.float32),
            ],
            in_specs=[VMEM] * 2,
            out_specs=[VMEM] * 3,
            compiler_params=pltpu.CompilerParams(vmem_limit_bytes=40 * 2**20),
            name="residual",
        )(vectors, parts)
    with jax.named_scope("gram_sum"):
        gram = pl.pallas_call(
            functools.partial(gram_kernel, scale), out_shape=square, in_specs=[VMEM], out_specs=VMEM, name="gram_sum"
        )(swap(grams))
    return (residual, rayleigh, gram)


def solution(mesh):
    return jax.shard_map(
        per_device,
        mesh=mesh,
        in_specs=(
            P(None, ("row", "col")),
            P(("row", "col")),
            P("row", "col", None, None, None),
            P("row", "col", None),
            P("row", "col", None),
            P("row", "col"),
        ),
        out_specs=(P(None, ("row", "col")), P(), P()),
        check_vma=False,
    )
```

time: 167 us -> 52.9 us (0.32)
  blocking collectives: 105 us -> 25.4 us
  waiting for transfers between devices: 36 us -> 9.44 us
  between operations: 14.8 us -> 1.34 us
  starting transfers between devices: 0.08 us -> 7.3 us
  Pallas kernels: 0 us -> 6.27 us
  matrix products: 4.9 us -> 0 us
  local copies, waits for them, and re-layouts: 5.75 us -> 2.65 us
    psum x2 -> x0, blocking collectives: 80.4 us -> none  [the longest x1 41 us: per_device(): lax.psum(jnp.dot(residual, residual.T, precision=hp), ('row', 'col'))]
    reduce_scatter x2 -> x0, waiting for transfers between devices: 36 us -> none  [the longest x1 33 us: per_device(): lax.psum_scatter(col_terms, 'row', scatter_dimension=1, tiled=True)]
    all_to_all x0 -> x2, blocking collectives: none -> 25.4 us  [swap(): return lax.all_to_all(blocks, BOTH, 0, 0, tiled=True)]
    all_gather x2 -> x0, blocking collectives: 24.1 us -> none  [the longest x1 13.3 us: per_device(): lax.all_gather(vectors, 'col', axis=1, tiled=True)]
    all_to_all x0 -> x1, waiting for transfers between devices: none -> 9.44 us  [swap(): return lax.all_to_all(blocks, BOTH, 0, 0, tiled=True)]
    all_to_all x0 -> x1, starting transfers between devices: none -> 7.3 us  [swap(): return lax.all_to_all(blocks, BOTH, 0, 0, tiled=True)]
    pallas_call x0 -> x3, Pallas kernels: none -> 6.27 us  [the longest x1 3.67 us: per_device(): pl.pallas_call(functools.partial(products_kernel, n_row, n_col, slots), o...]
    dot_general x9 -> x0, matrix products: 4.9 us -> none  [the longest x1 1.73 us: per_device(): jnp.einsum('svk,snk->svn', own_cols, tile_set, precision=hp)]
  transfers between devices with their start and end apart: 2 -> 1, of which waited for: 2 -> 1; matrix products, arithmetic and copies ran while one was open for 1% -> 0% of each run, Pallas kernels for 0% -> 0%
where the time goes in v3:
time: 52.9 us; the launch traced here: 52.5 us
  blocking collectives  25.4 us (48%)
  waiting for transfers between devices  9.44 us (18%)
  starting transfers between devices  7.3 us (14%)
  Pallas kernels  6.27 us (12%)
  local copies, waits for them, and re-layouts  2.65 us (5%)
  between operations  1.34 us (3%)
    all_to_all x2, blocking collectives, swap(): return lax.all_to_all(blocks, BOTH, 0, 0, tiled=True)  25.4 us
    all_to_all x1, waiting for transfers between devices, swap(): return lax.all_to_all(blocks, BOTH, 0, 0, tiled=True)  9.44 us
    all_to_all x1, starting transfers between devices, swap(): return lax.all_to_all(blocks, BOTH, 0, 0, tiled=True)  7.3 us
    pallas_call x1, Pallas kernels, per_device(): pl.pallas_call(functools.partial(products_kernel, n_row, n_col, slots), o...  3.67 us
    pallas_call x1, Pallas kernels, per_device(): pl.pallas_call(functools.partial(gram_kernel, scale), out_shape=square, i...  1.55 us
    broadcast_in_dim x1, local copies, waits for them, and re-layouts, per_device(): x_all = swap(jnp.broadcast_to(vectors[None], (devices, nvec, width)))  1.41 us
    unnamed x10, local copies, waits for them, and re-layouts  1.24 us
  transfers between devices with their start and end apart: 1, of which 1 were waited for; matrix products, arithmetic and copies ran while one was open for 0% of the time, Pallas kernels for 0%

profile of v3, /device:TPU:0, one launch (start us, length us, event | category | flops | bytes accessed | tf_op | source)
XLA Modules:
  0.0 52.5 jit_solution(14790206309089138769)
XLA Ops:
  0.6 1.4 %broadcast_in_dim.2 = f32[32,16,128]{2,1,0:T(8,128)} broadcast(f32[16,128]{1,0:T(8,128)} %x_ref.3), dimensions={1,2} | broadcast | bytes 270336 | tf_op jit(solution)/shard_map/share_vectors/broadcast_in_dim | solution.py:111
  2.0 7.3 %all-to-all-start = ((f32[32,16,128]{2,1,0:T(8,128)}), f32[32,16,128]{2,1,0:T(8,128)S(1)}, u32[]{:S(2)}, u32[]{:S(2)}) async-start(f32[32,16,128]{2,1,0:T(8,128)} %broadcast_in_dim.2), calls=%async_computation | async-start | bytes 524288 | tf_op jit(solution)/shard_map/share_vectors/all_to_all | solution.py:25
  9.4 0.0 copy-start.1
  10.0 0.1 pad_add_fusion.place
  10.1 0.0 copy-start.2
  10.1 0.0 copy-start.3
  10.1 0.0 copy-start.4
  10.1 9.4 %all-to-all-done.x_all = f32[32,16,128]{2,1,0:T(8,128)S(1)} async-done(((f32[32,16,128]{2,1,0:T(8,128)}), f32[32,16,128]{2,1,0:T(8,128)S(1)}, u32[]{:S(2)}, u32[]{:S(2)}) %all-to-all-start) | async-done | bytes 262176 | tf_op jit(solution)/shard_map/share_vectors/all_to_all | solution.py:25
  19.5 0.0 copy-done.1
  19.5 0.0 copy-done.2
  19.6 0.0 copy-done.3
  19.6 0.0 copy-done.4
  19.6 0.0 copy-start
  19.6 1.2 %copy-done = f32[1,1,16,128,128]{4,3,2,1,0:T(8,128)S(1)} copy-done((f32[1,1,16,128,128]{4,3,2,1,0:T(8,128)S(1)}, f32[1,1,16,128,128]{4,3,2,1,0:T(8,128)}, u32[]{:S(2)}) %copy-start) | copy-done | bytes 1048600
  20.8 3.7 %tile_products.1 = f32[32,24,128]{2,1,0:T(8,128)S(1)} custom-call(s32[2]{0:T(128)S(1)} %pad_add_fusion.place, s32[1,1,16]{2,1,0:T(1,128)S(1)} %copy-done.2, s32[1,1,16]{2,1,0:T(1,128)S(1)} %copy-done.3, s32[1,1]{1,0:T(1,128)S(6)} %copy.9.count, f32[16,128]{1,0:T(8,128)S(1)} %copy-done.1, f32[1,128]{1,0:T(1,128)S(1)} %bitcast.3, ...), custom_call_target="tpu_custom_call" | custom-call | tf_op jit(solution)/shard_map/tile_products/tile_products/pallas_call | solution.py:113
  24.5 14.4 %all_to_all.15.parts = f32[32,24,128]{2,1,0:T(8,128)S(1)} all-to-all(f32[32,24,128]{2,1,0:T(8,128)S(1)} %tile_products.1), channel_id=1, replica_groups=mesh['row'=8,'col'=4] {'row','col'}, dimensions={0} | all-to-all | bytes 786432 | tf_op jit(solution)/shard_map/return_products/all_to_all | solution.py:25
  38.8 1.0 %residual.1 = (f32[16,128]{1,0:T(8,128)}, f32[16,16]{1,0:T(8,128)}, f32[32,2,128]{2,1,0:T(2,128)S(1)}) custom-call(f32[16,128]{1,0:T(8,128)S(1)} %copy-done.1, f32[32,24,128]{2,1,0:T(8,128)S(1)} %all_to_all.15.parts), custom_call_target="tpu_custom_call" | custom-call | tf_op jit(solution)/shard_map/residual/residual/pallas_call | solution.py:125
  39.9 11.1 %all_to_all.16.parts = f32[32,2,128]{2,1,0:T(2,128)} all-to-all(f32[32,2,128]{2,1,0:T(2,128)S(1)} %get-tuple-element.8), channel_id=1, replica_groups=mesh['row'=8,'col'=4] {'row','col'}, dimensions={0} | all-to-all | bytes 65536 | tf_op jit(solution)/shard_map/gram_sum/all_to_all | solution.py:25
  50.9 1.6 %gram_sum.1 = f32[16,16]{1,0:T(8,128)} custom-call(f32[32,2,128]{2,1,0:T(2,128)} %all_to_all.16.parts), custom_call_target="tpu_custom_call" | custom-call | tf_op jit(solution)/shard_map/gram_sum/gram_sum/pallas_call | solution.py:138
Async XLA Ops:
  2.0 17.5 %all-to-all-start = ((f32[32,16,128]{2,1,0:T(8,128)}), f32[32,16,128]{2,1,0:T(8,128)S(1)}, u32[]{:S(2)}, u32[]{:S(2)}) async-start(f32[32,16,128]{2,1,0:T(8,128)} %broadcast_in_dim.2), calls=%async_computation | async-start | bytes 524288 | tf_op jit(solution)/shard_map/share_vectors/all_to_all | solution.py:25
  9.4 10.2 %copy-start.1 = (f32[16,128]{1,0:T(8,128)S(1)}, f32[16,128]{1,0:T(8,128)}, u32[]{:S(2)}) copy-start(f32[16,128]{1,0:T(8,128)} %x_ref.3) | copy-start | bytes 24580
  10.1 9.5 %copy-start.2 = (s32[1,1,16]{2,1,0:T(1,128)S(1)}, s32[1,1,16]{2,1,0:T(1,128)}, u32[]{:S(2)}) copy-start(s32[1,1,16]{2,1,0:T(1,128)} %arow.1) | copy-start | bytes 196
  10.1 9.5 %copy-start.3 = (s32[1,1,16]{2,1,0:T(1,128)S(1)}, s32[1,1,16]{2,1,0:T(1,128)}, u32[]{:S(2)}) copy-start(s32[1,1,16]{2,1,0:T(1,128)} %bcol.1) | copy-start | bytes 196
  10.1 9.5 %copy-start.4 = (f32[128]{0:T(128)S(1)}, f32[128]{0:T(128)}, u32[]{:S(2)}) copy-start(f32[128]{0:T(128)} %param.7) | copy-start | bytes 1540
  19.6 1.2 %copy-start = (f32[1,1,16,128,128]{4,3,2,1,0:T(8,128)S(1)}, f32[1,1,16,128,128]{4,3,2,1,0:T(8,128)}, u32[]{:S(2)}) copy-start(f32[1,1,16,128,128]{4,3,2,1,0:T(8,128)} %tiles.1) | copy-start | bytes 3145732

commit v4 on v3

--- a/solution.py
+++ b/solution.py
@@ -82,14 +82,12 @@
     own = x_ref[...]
     nvec = own.shape[0]
     both = jnp.sum(parts[...], axis=0)
-    half = unpack(both[nvec : nvec + out.shape[1]], nvec)
+    half = unpack(both[nvec : nvec + out.shape[0]], nvec)
     ray = (half + half.T) * scale
     rayleigh[...] = ray
     res = both[:nvec] - mult(ray, own)
     residual[...] = res
-    part = packed_gram(res, res)
-    for block in range(out.shape[0]):
-        out[block] = part
+    out[...] = packed_gram(res, res)
 
 
 def gram_kernel(scale, parts, out):
@@ -108,7 +106,7 @@
     square = jax.ShapeDtypeStruct((nvec, nvec), jnp.float32)
     place = jnp.stack([lax.axis_index("row"), lax.axis_index("col")]).astype(jnp.int32)
     with jax.named_scope("share_vectors"):
-        x_all = swap(jnp.broadcast_to(vectors[None], (devices, nvec, width)))
+        x_all = lax.all_gather(vectors, BOTH)
     with jax.named_scope("tile_products"):
         terms = pl.pallas_call(
             functools.partial(products_kernel, n_row, n_col, slots),
@@ -122,12 +120,12 @@
     with jax.named_scope("return_products"):
         parts = swap(terms)
     with jax.named_scope("residual"):
-        residual, rayleigh, grams = pl.pallas_call(
+        residual, rayleigh, part = pl.pallas_call(
             functools.partial(residual_kernel, scale),
             out_shape=[
                 jax.ShapeDtypeStruct((nvec, width), jnp.float32),
                 square,
-                jax.ShapeDtypeStruct((devices, packed_rows, width), jnp.float32),
+                jax.ShapeDtypeStruct((packed_rows, width), jnp.float32),
             ],
             in_specs=[VMEM] * 2,
             out_specs=[VMEM] * 3,
@@ -137,7 +135,7 @@
     with jax.named_scope("gram_sum"):
         gram = pl.pallas_call(
             functools.partial(gram_kernel, scale), out_shape=square, in_specs=[VMEM], out_specs=VMEM, name="gram_sum"
-        )(swap(grams))
+        )(lax.all_gather(part, BOTH))
     return (residual, rayleigh, gram)
 
 

time: 52.9 us -> 166 us (3.14)
  blocking collectives: 25.4 us -> 156 us
  waiting for transfers between devices: 9.44 us -> 0 us
  starting transfers between devices: 7.3 us -> 0 us
    all_gather x0 -> x2, blocking collectives: none -> 142 us  [the longest x1 71.8 us: per_device(): x_all = lax.all_gather(vectors, BOTH)]
    all_to_all x2 -> x1, blocking collectives: 25.4 us -> 13.5 us  [swap(): return lax.all_to_all(blocks, BOTH, 0, 0, tiled=True)]
    all_to_all x1 -> x0, waiting for transfers between devices: 9.44 us -> none  [swap(): return lax.all_to_all(blocks, BOTH, 0, 0, tiled=True)]
    all_to_all x1 -> x0, starting transfers between devices: 7.3 us -> none  [swap(): return lax.all_to_all(blocks, BOTH, 0, 0, tiled=True)]
  transfers between devices with their start and end apart: 1 -> 0, of which waited for: 1 -> 0; matrix products, arithmetic and copies ran while one was open for 0% -> 0% of each run, Pallas kernels for 0% -> 0%
where the time goes in v4:
time: 166 us
  blocking collectives  156 us (94%)
  Pallas kernels  6.27 us (4%)
  local copies, waits for them, and re-layouts  1.94 us (1%)
    all_gather x1, blocking collectives, per_device(): x_all = lax.all_gather(vectors, BOTH)  71.8 us
    all_gather x1, blocking collectives, per_device(): lax.all_gather(part, BOTH)  70.7 us
    all_to_all x1, blocking collectives, swap(): return lax.all_to_all(blocks, BOTH, 0, 0, tiled=True)  13.5 us
    pallas_call x1, Pallas kernels, per_device(): pl.pallas_call(functools.partial(products_kernel, n_row, n_col, slots), o...  3.67 us

profile of v4, /device:TPU:0, one launch (start us, length us, event | category | flops | bytes accessed | tf_op | source)
XLA Modules:
  0.0 165.6 jit_solution(15566227738632778476)
XLA Ops:
  0.6 0.0 copy-start.1
  1.3 0.0 copy-done.1
  1.3 71.8 %all-gather = f32[512,128]{1,0:T(8,128)S(1)} all-gather(f32[16,128]{1,0:T(8,128)S(1)} %copy-done.1), channel_id=2, replica_groups=mesh['row'=8,'col'=4] {'row','col'}, dimensions={0}, use_global_device_ids=true | all-gather | bytes 270336 | tf_op jit(solution)/shard_map/share_vectors/all_gather | solution.py:109
  73.1 0.1 pad_add_fusion.place
  73.2 0.0 copy-start.2
  73.2 0.0 copy-start.3
  73.2 0.0 copy-start.4
  73.2 0.6 copy-done.2
  73.9 0.0 copy-done.3
  73.9 0.0 copy-done.4
  73.9 0.0 copy-start
  73.9 1.2 copy-done
  75.1 3.7 %tile_products.1 = f32[32,24,128]{2,1,0:T(8,128)S(1)} custom-call(s32[2]{0:T(128)S(1)} %pad_add_fusion.place, s32[1,1,16]{2,1,0:T(1,128)S(1)} %copy-done.2, s32[1,1,16]{2,1,0:T(1,128)S(1)} %copy-done.3, s32[1,1]{1,0:T(1,128)S(6)} %copy.9.count, f32[16,128]{1,0:T(8,128)S(1)} %copy-done.1, f32[1,128]{1,0:T(1,128)S(1)} %bitcast.7, f32[32,16,128]{2,1,0:T(8,128)S(1)} %bitcast.5, ...), custom_call_target="tpu_custom_call" | custom-call | tf_op jit(solution)/shard_map/tile_products/tile_products/pallas_call | solution.py:111
  78.8 13.5 %all_to_all.5.parts = f32[32,24,128]{2,1,0:T(8,128)S(1)} all-to-all(f32[32,24,128]{2,1,0:T(8,128)S(1)} %tile_products.1), channel_id=1, replica_groups=mesh['row'=8,'col'=4] {'row','col'}, dimensions={0} | all-to-all | bytes 786432 | tf_op jit(solution)/shard_map/return_products/all_to_all | solution.py:25
  92.4 1.0 residual.1
  93.4 70.7 %all-gather.2.parts = f32[32,2,128]{2,1,0:T(2,128)} all-gather(f32[1,2,128]{2,1,0:T(2,128)S(1)} %bitcast.6), channel_id=3, replica_groups=mesh['row'=8,'col'=4] {'row','col'}, dimensions={0}, use_global_device_ids=true | all-gather | bytes 33792 | tf_op jit(solution)/shard_map/gram_sum/all_gather | solution.py:138
  164.0 1.6 gram_sum.1
Async XLA Ops:
  0.6 0.7 copy-start.1
  73.2 0.7 copy-start.2
  73.2 0.7 copy-start.3
  73.2 0.7 copy-start.4
  73.9 1.2 copy-start

commit v5 on v3

v5 whole, which is shorter than its diff:
```python
import functools

import jax
import jax.numpy as jnp
from jax import lax
from jax.experimental import pallas as pl
from jax.experimental.pallas import tpu as pltpu
from jax.sharding import PartitionSpec as P

HP = lax.Precision.HIGHEST
VMEM = pl.BlockSpec(memory_space=pltpu.VMEM)
SMEM = pl.BlockSpec(memory_space=pltpu.SMEM)


def mult(left, right):
    return lax.dot_general(left, right, (((1,), (0,)), ((), ())), precision=HP, preferred_element_type=jnp.float32)


def mult_last(left, right):
    return lax.dot_general(left, right, (((1,), (1,)), ((), ())), precision=HP, preferred_element_type=jnp.float32)


def swap(blocks, axis):
    return lax.all_to_all(blocks, axis, 0, 0, tiled=True)


def shift(value, axis, step):
    size = lax.axis_size(axis)
    return lax.ppermute(value, axis, [(p, (p + step) % size) for p in range(size)])


def own_lanes(nvec, width):
    row = lax.broadcasted_iota(jnp.int32, (nvec, width), 0)
    lane = lax.broadcasted_iota(jnp.int32, (nvec, width), 1)
    return lane // nvec == row % (width // nvec)


def packed_gram(left, right):
    nvec, width = left.shape
    per = width // nvec
    wide = mult_last(left, jnp.concatenate([right] * per, axis=0))
    wide = jnp.where(own_lanes(nvec, width), wide, 0.0)
    return jnp.sum(wide.reshape(nvec // per, per, width), axis=1)


def unpack(packed, nvec):
    rows, width = packed.shape
    per = width // nvec
    wide = jnp.concatenate([jnp.broadcast_to(packed[g : g + 1], (per, width)) for g in range(rows)], axis=0)
    wide = jnp.where(own_lanes(nvec, width), wide, 0.0)
    lane = lax.broadcasted_iota(jnp.int32, (width, nvec), 0)
    column = lax.broadcasted_iota(jnp.int32, (width, nvec), 1)
    return mult(wide, (lane % nvec == column).astype(jnp.float32))


def column_kernel(n_row, n_col, slots, place, arow, bcol, count, d_ref, *refs):
    x_rows, (x_cols, tiles, out, rows) = refs[:n_col], refs[n_col:]
    nvec, width = x_rows[0].shape
    me_row, me_col = place[0], place[1]
    for step in range(n_col):
        rows[step] = x_rows[step][...]
    out[...] = jnp.zeros_like(out)
    out[me_row, :nvec] = 0.5 * d_ref[...] * x_rows[0][...]
    for slot in range(slots):
        live = jnp.where(slot < count[0, 0], 1.0, 0.0).astype(jnp.float32)
        behind = lax.rem(me_col - arow[0, 0, slot] + n_col, n_col)
        out[bcol[0, 0, slot], :nvec] += mult(rows[behind] * live, tiles[0, 0, slot])
    total = jnp.zeros((nvec * nvec // width, width), jnp.float32)
    for block in range(n_row):
        total += packed_gram(x_cols[block], out[block, :nvec])
    for block in range(n_row):
        out[block, nvec : nvec + total.shape[0]] = total


def row_kernel(n_col, slots, place, arow, bcol, count, d_ref, x_ref, x_cols, tiles, after, out):
    del after
    out[...] = jnp.zeros_like(out)
    out[0] = 0.5 * d_ref[...] * x_ref[...]
    for slot in range(slots):
        live = jnp.where(slot < count[0, 0], 1.0, 0.0).astype(jnp.float32)
        ahead = lax.rem(arow[0, 0, slot] - place[1] + n_col, n_col)
        out[ahead] += mult_last(x_cols[bcol[0, 0, slot]] * live, tiles[0, 0, slot])


def join_kernel(by_row, terms, *outs):
    nvec = terms.shape[1]
    both = jnp.sum(by_row[...], axis=0)
    outs[0][:nvec] = both[:nvec] + terms[0]
    for step in range(1, len(outs)):
        outs[step][:nvec] = terms[step]
    for out in outs:
        out[nvec:] = both[nvec:]


def residual_kernel(scale, x_ref, *refs):
    parts, (residual, rayleigh, out) = refs[:-3], refs[-3:]
    own = x_ref[...]
    nvec = own.shape[0]
    both = parts[0][...]
    for part in parts[1:]:
        both += part[...]
    half = unpack(both[nvec : nvec + out.shape[1]], nvec)
    ray = (half + half.T) * scale
    rayleigh[...] = ray
    res = both[:nvec] - mult(ray, own)
    residual[...] = res
    part = packed_gram(res, res)
    for block in range(out.shape[0]):
        out[block] = part


def gram_kernel(scale, parts, out):
    out[...] = unpack(jnp.sum(parts[...], axis=0), out.shape[0]) * scale


def per_device(vectors, diagonal_energy, tiles, tile_rows, tile_cols, tile_count):
    n_row = lax.axis_size("row")
    n_col = lax.axis_size("col")
    devices = n_row * n_col
    nvec, width = vectors.shape
    slots = tiles.shape[2]
    scale = 1.0 / float(devices * width)
    packed_rows = nvec * nvec // width
    padded = nvec + 8 * (-(-packed_rows // 8))
    block = jax.ShapeDtypeStruct((nvec, width), jnp.float32)
    joined = jax.ShapeDtypeStruct((padded, width), jnp.float32)
    square = jax.ShapeDtypeStruct((nvec, nvec), jnp.float32)
    place = jnp.stack([lax.axis_index("row"), lax.axis_index("col")]).astype(jnp.int32)
    energy = diagonal_energy.reshape(1, width)
    params = pltpu.CompilerParams(vmem_limit_bytes=24 * 2**20)
    with jax.named_scope("share_vectors"):
        x_cols = swap(jnp.broadcast_to(vectors[None], (n_row, nvec, width)), "row")
        x_rows = [vectors] + [shift(vectors, "col", step) for step in range(1, n_col)]
    with jax.named_scope("column_terms"):
        col_terms = pl.pallas_call(
            functools.partial(column_kernel, n_row, n_col, slots),
            out_shape=jax.ShapeDtypeStruct((n_row, padded, width), jnp.float32),
            in_specs=[SMEM] * 4 + [VMEM] * (n_col + 3),
            out_specs=VMEM,
            scratch_shapes=[pltpu.VMEM((n_col, nvec, width), jnp.float32)],
            compiler_params=params,
            cost_estimate=pl.CostEstimate(flops=12 * slots * nvec * width * width, bytes_accessed=2**20, transcendentals=0),
            name="column_terms",
        )(place, tile_rows, tile_cols, tile_count, energy, *x_rows, x_cols, tiles)
    with jax.named_scope("return_column_terms"):
        by_row = swap(col_terms, "row")
    with jax.named_scope("row_terms"):
        row_terms = pl.pallas_call(
            functools.partial(row_kernel, n_col, slots),
            out_shape=jax.ShapeDtypeStruct((n_col, nvec, width), jnp.float32),
            in_specs=[SMEM] * 4 + [VMEM] * 4 + [pl.BlockSpec(memory_space=pl.ANY)],
            out_specs=VMEM,
            compiler_params=params,
            cost_estimate=pl.CostEstimate(flops=12 * slots * nvec * width * width, bytes_accessed=2**20, transcendentals=0),
            name="row_terms",
        )(place, tile_rows, tile_cols, tile_count, energy, vectors, x_cols, tiles, col_terms)
    with jax.named_scope("return_row_terms"):
        sends = pl.pallas_call(
            join_kernel, out_shape=[joined] * n_col, in_specs=[VMEM] * 2, out_specs=[VMEM] * n_col, name="join"
        )(by_row, row_terms)
        parts = [sends[0]] + [shift(sends[step], "col", step) for step in range(1, n_col)]
    with jax.named_scope("residual"):
        residual, rayleigh, grams = pl.pallas_call(
            functools.partial(residual_kernel, scale),
            out_shape=[block, square, jax.ShapeDtypeStruct((devices, packed_rows, width), jnp.float32)],
            in_specs=[VMEM] * (1 + n_col),
            out_specs=[VMEM] * 3,
            compiler_params=params,
            name="residual",
        )(vectors, *parts)
    with jax.named_scope("gram_sum"):
        gram = pl.pallas_call(
            functools.partial(gram_kernel, scale), out_shape=square, in_specs=[VMEM], out_specs=VMEM, name="gram_sum"
        )(swap(grams, ("row", "col")))
    return (residual, rayleigh, gram)


def solution(mesh):
    return jax.shard_map(
        per_device,
        mesh=mesh,
        in_specs=(
            P(None, ("row", "col")),
            P(("row", "col")),
            P("row", "col", None, None, None),
            P("row", "col", None),
            P("row", "col", None),
            P("row", "col"),
        ),
        out_specs=(P(None, ("row", "col")), P(), P()),
        check_vma=False,
    )
```

time: 52.9 us -> 53.9 us (1.019)
  blocking collectives: 25.4 us -> 10.8 us
  starting transfers between devices: 7.3 us -> 18.1 us
  Pallas kernels: 6.27 us -> 9.45 us
  local copies, waits for them, and re-layouts: 2.65 us -> 4.57 us
    all_to_all x2 -> x1, blocking collectives: 25.4 us -> 10.8 us  [swap(): return lax.all_to_all(blocks, axis, 0, 0, tiled=True)]
    ppermute x0 -> x6, starting transfers between devices: none -> 11 us  [shift(): lax.ppermute(value, axis, [(p, (p + step) % size) for p in range(size)])]
    pallas_call x2 -> x4, Pallas kernels: 4.71 us -> 7.9 us  [the longest x1 3.09 us: per_device(): pl.pallas_call(functools.partial(column_kernel, n_row, n_col, slots), out...]
    all_to_all x1 -> x2, waiting for transfers between devices: 9.44 us -> 6.43 us  [swap(): return lax.all_to_all(blocks, axis, 0, 0, tiled=True)]
    ppermute x0 -> x6, waiting for transfers between devices: none -> 2.55 us  [shift(): lax.ppermute(value, axis, [(p, (p + step) % size) for p in range(size)])]
    unnamed x10 -> x18, local copies, waits for them, and re-layouts: 1.24 us -> 3.23 us
    all_to_all x1 -> x2, starting transfers between devices: 7.3 us -> 7.08 us  [swap(): return lax.all_to_all(blocks, axis, 0, 0, tiled=True)]
  transfers between devices with their start and end apart: 1 -> 8, of which waited for: 1 -> 5; matrix products, arithmetic and copies ran while one was open for 0% -> 3% of each run, Pallas kernels for 0% -> 4%
where the time goes in v5:
time: 53.9 us; the launch traced here: 53.3 us
  starting transfers between devices  18.1 us (34%)
  blocking collectives  10.8 us (20%)
  Pallas kernels  9.45 us (18%)
  waiting for transfers between devices  8.97 us (17%)
  local copies, waits for them, and re-layouts  4.57 us (8%)
  between operations  1.38 us (3%)
    ppermute x6, starting transfers between devices, shift(): lax.ppermute(value, axis, [(p, (p + step) % size) for p in range(size)])  11 us
    all_to_all x1, blocking collectives, swap(): return lax.all_to_all(blocks, axis, 0, 0, tiled=True)  10.8 us
    all_to_all x2, starting transfers between devices, swap(): return lax.all_to_all(blocks, axis, 0, 0, tiled=True)  7.08 us
    all_to_all x2, waiting for transfers between devices, swap(): return lax.all_to_all(blocks, axis, 0, 0, tiled=True)  6.43 us
    unnamed x18, local copies, waits for them, and re-layouts  3.23 us
    pallas_call x1, Pallas kernels, per_device(): pl.pallas_call(functools.partial(column_kernel, n_row, n_col, slots), out...  3.09 us
    ppermute x6, waiting for transfers between devices, shift(): lax.ppermute(value, axis, [(p, (p + step) % size) for p in range(size)])  2.55 us
    pallas_call x1, Pallas kernels, per_device(): pl.pallas_call(functools.partial(row_kernel, n_col, slots), out_shape=jax...  2.27 us
  transfers between devices with their start and end apart: 8, of which 5 were waited for; matrix products, arithmetic and copies ran while one was open for 3% of the time, Pallas kernels for 4%

profile of v5, /device:TPU:0, one launch (start us, length us, event | category | flops | bytes accessed | tf_op | source)
XLA Modules:
  0.0 53.3 jit_solution(10174790239278516027)
XLA Ops:
  0.6 5.1 %collective-permute-start.2 = (f32[16,128]{1,0:T(8,128)}, f32[16,128]{1,0:T(8,128)S(1)}, u32[]{:S(2)}, u32[]{:S(2)}) collective-permute-start(f32[16,128]{1,0:T(8,128)} %x_ref.3), channel_id=1, source_target_pairs={{0,3},{1,0},{2,1},{3,2},{4,7},{5,4},{6,5},{7,6},{8,11},{9,8},{10,9... | collective-permute-start | bytes 24584 | tf_op jit(solution)/shard_map/share_vectors/ppermute | solution.py:29
  5.7 0.0 collective-permute-start.1
  5.7 1.0 %collective-permute-start = (f32[16,128]{1,0:T(8,128)}, f32[16,128]{1,0:T(8,128)S(1)}, u32[]{:S(2)}, u32[]{:S(2)}) collective-permute-start(f32[16,128]{1,0:T(8,128)} %x_ref.3), channel_id=1, source_target_pairs={{0,1},{1,2},{2,3},{3,0},{4,5},{5,6},{6,7},{7,4},{8,9},{9,10},{10,1... | collective-permute-start | bytes 24584 | tf_op jit(solution)/shard_map/share_vectors/ppermute | solution.py:29
  6.7 1.3 %broadcast_in_dim.2 = f32[8,16,128]{2,1,0:T(8,128)} broadcast(f32[16,128]{1,0:T(8,128)} %x_ref.3), dimensions={1,2} | broadcast | bytes 73728 | tf_op jit(solution)/shard_map/share_vectors/broadcast_in_dim | solution.py:132
  8.1 3.7 %all-to-all-start = ((f32[8,16,128]{2,1,0:T(8,128)}), f32[8,16,128]{2,1,0:T(8,128)S(1)}, u32[]{:S(2)}, u32[]{:S(2)}) async-start(f32[8,16,128]{2,1,0:T(8,128)} %broadcast_in_dim.2), calls=%async_computation | async-start | bytes 131072 | tf_op jit(solution)/shard_map/share_vectors/all_to_all | solution.py:24
  11.8 0.0 copy-start.2
  11.8 0.1 pad_add_fusion.place
  12.5 0.0 copy-start.5
  12.6 0.0 copy-start.6
  12.6 0.0 copy-start.7
  12.6 0.0 collective-permute-done.2.refs_3_
  12.6 0.0 collective-permute-done.1.refs_2_
  12.6 0.0 collective-permute-done.refs_1_
  12.6 4.2 %all-to-all-done.refs_4_.x_cols = f32[8,16,128]{2,1,0:T(8,128)S(1)} async-done(((f32[8,16,128]{2,1,0:T(8,128)}), f32[8,16,128]{2,1,0:T(8,128)S(1)}, u32[]{:S(2)}, u32[]{:S(2)}) %all-to-all-start) | async-done | bytes 65568 | tf_op jit(solution)/shard_map/share_vectors/all_to_all | solution.py:24
  16.8 0.0 copy-done.2
  16.8 0.0 copy-done.5
  16.8 0.0 copy-done.6
  16.8 0.0 copy-done.7
  16.9 0.0 copy-start
  16.9 1.2 %copy-done = f32[1,1,16,128,128]{4,3,2,1,0:T(8,128)S(1)} copy-done((f32[1,1,16,128,128]{4,3,2,1,0:T(8,128)S(1)}, f32[1,1,16,128,128]{4,3,2,1,0:T(8,128)}, u32[]{:S(2)}) %copy-start) | copy-done | bytes 1048600
  18.1 0.0 copy-start.1
  18.1 3.1 %column_terms.1.after = f32[8,24,128]{2,1,0:T(8,128)} custom-call(s32[2]{0:T(128)S(1)} %pad_add_fusion.place, s32[1,1,16]{2,1,0:T(1,128)S(1)} %copy-done.5, s32[1,1,16]{2,1,0:T(1,128)S(1)} %copy-done.6, s32[1,1]{1,0:T(1,128)S(6)} %copy.9.count, f32[1,128]{1,0:T(1,128)S(1)} %bitcast.3, f32[16,128]{1,0:T(8,128)S(1)} %copy-done.2, ...), custom_call_target="tpu_custom_call" | custom-call | flops 50331648 | bytes 1048576 | tf_op jit(solution)/shard_map/column_terms/column_terms/pallas_call | solution.py:135
  21.2 3.4 %all-to-all-start.1 = ((f32[8,24,128]{2,1,0:T(8,128)}), f32[8,24,128]{2,1,0:T(8,128)S(1)}, u32[]{:S(2)}, u32[]{:S(2)}) async-start(f32[8,24,128]{2,1,0:T(8,128)} %column_terms.1.after), calls=%async_computation.1 | async-start | bytes 196608 | tf_op jit(solution)/shard_map/return_column_terms/all_to_all | solution.py:24
  24.5 0.0 copy-done.1
  24.6 2.3 %row_terms.1.terms = f32[4,16,128]{2,1,0:T(8,128)S(1)} custom-call(s32[2]{0:T(128)S(1)} %pad_add_fusion.place, s32[1,1,16]{2,1,0:T(1,128)S(1)} %copy-done.5, s32[1,1,16]{2,1,0:T(1,128)S(1)} %copy-done.6, s32[1,1]{1,0:T(1,128)S(6)} %copy.9.count, f32[1,128]{1,0:T(1,128)S(1)} %bitcast.4, f32[16,128]{1,0:T(8,128)S(1)} %copy-done.2, ...), custom_call_target="tpu_custom_call" | custom-call | flops 50331648 | bytes 1048576 | tf_op jit(solution)/shard_map/row_terms/row_terms/pallas_call | solution.py:148
  26.8 0.0 copy-start.3
  26.8 0.6 %copy-done.3 = f32[4,16,128]{2,1,0:T(8,128)} copy-done((f32[4,16,128]{2,1,0:T(8,128)}, f32[4,16,128]{2,1,0:T(8,128)S(1)}, u32[]{:S(2)}) %copy-start.3) | copy-done | bytes 32792
  27.5 2.2 %all-to-all-done.1.by_row = f32[8,24,128]{2,1,0:T(8,128)S(1)} async-done(((f32[8,24,128]{2,1,0:T(8,128)}), f32[8,24,128]{2,1,0:T(8,128)S(1)}, u32[]{:S(2)}, u32[]{:S(2)}) %all-to-all-start.1) | async-done | bytes 98336 | tf_op jit(solution)/shard_map/return_column_terms/all_to_all | solution.py:24
  29.7 0.0 copy-start.8
  29.7 0.6 %copy-done.8 = f32[8,24,128]{2,1,0:T(8,128)} copy-done((f32[8,24,128]{2,1,0:T(8,128)}, f32[8,24,128]{2,1,0:T(8,128)S(1)}, u32[]{:S(2)}) %copy-start.8) | copy-done | bytes 98328
  30.3 1.5 %join.1 = (f32[24,128]{1,0:T(8,128)}, f32[24,128]{1,0:T(8,128)}, f32[24,128]{1,0:T(8,128)}, f32[24,128]{1,0:T(8,128)}) custom-call(f32[8,24,128]{2,1,0:T(8,128)} %copy-done.8, f32[4,16,128]{2,1,0:T(8,128)} %copy-done.3), custom_call_target="tpu_custom_call" | custom-call | tf_op jit(solution)/shard_map/return_row_terms/join/pallas_call | solution.py:158
  31.8 2.5 %collective-permute-start.3 = (f32[24,128]{1,0:T(8,128)}, f32[24,128]{1,0:T(8,128)S(1)}, u32[]{:S(2)}, u32[]{:S(2)}) collective-permute-start(f32[24,128]{1,0:T(8,128)} %get-tuple-element.11), channel_id=1, source_target_pairs={{0,1},{1,2},{2,3},{3,0},{4,5},{5,6},{6,7},{7,4},{8,9},{9,10},{10,1... | collective-permute-start | bytes 36872 | tf_op jit(solution)/shard_map/return_row_terms/ppermute | solution.py:29
  34.3 0.9 %collective-permute-start.4 = (f32[24,128]{1,0:T(8,128)}, f32[24,128]{1,0:T(8,128)S(1)}, u32[]{:S(2)}, u32[]{:S(2)}) collective-permute-start(f32[24,128]{1,0:T(8,128)} %get-tuple-element.12), channel_id=1, source_target_pairs={{0,2},{1,3},{2,0},{3,1},{4,6},{5,7},{6,4},{7,5},{8,10},{9,11},{10,... | collective-permute-start | bytes 36872 | tf_op jit(solution)/shard_map/return_row_terms/ppermute | solution.py:29
  35.2 1.5 %collective-permute-start.5 = (f32[24,128]{1,0:T(8,128)}, f32[24,128]{1,0:T(8,128)S(1)}, u32[]{:S(2)}, u32[]{:S(2)}) collective-permute-start(f32[24,128]{1,0:T(8,128)} %get-tuple-element.13), channel_id=1, source_target_pairs={{0,3},{1,0},{2,1},{3,2},{4,7},{5,4},{6,5},{7,6},{8,11},{9,8},{10,9... | collective-permute-start | bytes 36872 | tf_op jit(solution)/shard_map/return_row_terms/ppermute | solution.py:29
  36.7 0.9 %collective-permute-done.3.refs_1_ = f32[24,128]{1,0:T(8,128)S(1)} collective-permute-done((f32[24,128]{1,0:T(8,128)}, f32[24,128]{1,0:T(8,128)S(1)}, u32[]{:S(2)}, u32[]{:S(2)}) %collective-permute-start.3) | collective-permute-done | bytes 12320 | tf_op jit(solution)/shard_map/return_row_terms/ppermute | solution.py:29
  37.6 1.5 %collective-permute-done.4.refs_2_ = f32[24,128]{1,0:T(8,128)S(1)} collective-permute-done((f32[24,128]{1,0:T(8,128)}, f32[24,128]{1,0:T(8,128)S(1)}, u32[]{:S(2)}, u32[]{:S(2)}) %collective-permute-start.4) | collective-permute-done | bytes 12320 | tf_op jit(solution)/shard_map/return_row_terms/ppermute | solution.py:29
  39.1 0.1 collective-permute-done.5.refs_3_
  39.3 0.0 copy-start.4
  39.3 0.7 %copy-done.4 = f32[24,128]{1,0:T(8,128)S(1)} copy-done((f32[24,128]{1,0:T(8,128)S(1)}, f32[24,128]{1,0:T(8,128)}, u32[]{:S(2)}) %copy-start.4) | copy-done | bytes 12312
  40.0 1.0 %residual.1 = (f32[16,128]{1,0:T(8,128)}, f32[16,16]{1,0:T(8,128)}, f32[32,2,128]{2,1,0:T(2,128)S(1)}) custom-call(f32[16,128]{1,0:T(8,128)S(1)} %copy-done.2, f32[24,128]{1,0:T(8,128)S(1)} %copy-done.4, f32[24,128]{1,0:T(8,128)S(1)} %collective-permute-done.3.refs_1_, f32[24,128]{1,0:T(8,128)S(1)} %collective-permute-done.4.refs_2_, ...), custom_call_target="tpu_custom_call" | custom-call | tf_op jit(solution)/shard_map/residual/residual/pallas_call | solution.py:163
  41.0 10.8 %all_to_all.15.parts = f32[32,2,128]{2,1,0:T(2,128)} all-to-all(f32[32,2,128]{2,1,0:T(2,128)S(1)} %get-tuple-element.16), channel_id=1, replica_groups=mesh['row'=8,'col'=4] {'row','col'}, dimensions={0} | all-to-all | bytes 65536 | tf_op jit(solution)/shard_map/gram_sum/all_to_all | solution.py:24
  51.8 1.6 %gram_sum.1 = f32[16,16]{1,0:T(8,128)} custom-call(f32[32,2,128]{2,1,0:T(2,128)} %all_to_all.15.parts), custom_call_target="tpu_custom_call" | custom-call | tf_op jit(solution)/shard_map/gram_sum/gram_sum/pallas_call | solution.py:172
Async XLA Ops:
  0.6 12.0 %collective-permute-start.2 = (f32[16,128]{1,0:T(8,128)}, f32[16,128]{1,0:T(8,128)S(1)}, u32[]{:S(2)}, u32[]{:S(2)}) collective-permute-start(f32[16,128]{1,0:T(8,128)} %x_ref.3), channel_id=1, source_target_pairs={{0,3},{1,0},{2,1},{3,2},{4,7},{5,4},{6,5},{7,6},{8,11},{9,8},{10,9... | collective-permute-start | bytes 24584 | tf_op jit(solution)/shard_map/share_vectors/ppermute | solution.py:29
  5.7 6.9 %collective-permute-start.1 = (f32[16,128]{1,0:T(8,128)}, f32[16,128]{1,0:T(8,128)S(1)}, u32[]{:S(2)}, u32[]{:S(2)}) collective-permute-start(f32[16,128]{1,0:T(8,128)} %x_ref.3), channel_id=1, source_target_pairs={{0,2},{1,3},{2,0},{3,1},{4,6},{5,7},{6,4},{7,5},{8,10},{9,11},{10,... | collective-permute-start | bytes 24584 | tf_op jit(solution)/shard_map/share_vectors/ppermute | solution.py:29
  5.7 6.9 %collective-permute-start = (f32[16,128]{1,0:T(8,128)}, f32[16,128]{1,0:T(8,128)S(1)}, u32[]{:S(2)}, u32[]{:S(2)}) collective-permute-start(f32[16,128]{1,0:T(8,128)} %x_ref.3), channel_id=1, source_target_pairs={{0,1},{1,2},{2,3},{3,0},{4,5},{5,6},{6,7},{7,4},{8,9},{9,10},{10,1... | collective-permute-start | bytes 24584 | tf_op jit(solution)/shard_map/share_vectors/ppermute | solution.py:29
  8.1 8.7 %all-to-all-start = ((f32[8,16,128]{2,1,0:T(8,128)}), f32[8,16,128]{2,1,0:T(8,128)S(1)}, u32[]{:S(2)}, u32[]{:S(2)}) async-start(f32[8,16,128]{2,1,0:T(8,128)} %broadcast_in_dim.2), calls=%async_computation | async-start | bytes 131072 | tf_op jit(solution)/shard_map/share_vectors/all_to_all | solution.py:24
  11.8 5.0 %copy-start.2 = (f32[16,128]{1,0:T(8,128)S(1)}, f32[16,128]{1,0:T(8,128)}, u32[]{:S(2)}) copy-start(f32[16,128]{1,0:T(8,128)} %x_ref.3) | copy-start | bytes 24580
  12.5 4.3 %copy-start.5 = (s32[1,1,16]{2,1,0:T(1,128)S(1)}, s32[1,1,16]{2,1,0:T(1,128)}, u32[]{:S(2)}) copy-start(s32[1,1,16]{2,1,0:T(1,128)} %arow.3) | copy-start | bytes 196
  12.6 4.3 %copy-start.6 = (s32[1,1,16]{2,1,0:T(1,128)S(1)}, s32[1,1,16]{2,1,0:T(1,128)}, u32[]{:S(2)}) copy-start(s32[1,1,16]{2,1,0:T(1,128)} %bcol.3) | copy-start | bytes 196
  12.6 4.3 %copy-start.7 = (f32[128]{0:T(128)S(1)}, f32[128]{0:T(128)}, u32[]{:S(2)}) copy-start(f32[128]{0:T(128)} %param.7) | copy-start | bytes 1540
  16.9 1.2 %copy-start = (f32[1,1,16,128,128]{4,3,2,1,0:T(8,128)S(1)}, f32[1,1,16,128,128]{4,3,2,1,0:T(8,128)}, u32[]{:S(2)}) copy-start(f32[1,1,16,128,128]{4,3,2,1,0:T(8,128)} %tiles.1) | copy-start | bytes 3145732
  18.1 6.5 %copy-start.1 = (f32[1,1,16,128,128]{4,3,2,1,0:T(8,128)S(1)}, f32[1,1,16,128,128]{4,3,2,1,0:T(8,128)}, u32[]{:S(2)}) copy-start(f32[1,1,16,128,128]{4,3,2,1,0:T(8,128)} %tiles.1) | copy-start | bytes 3145732
  21.2 8.5 %all-to-all-start.1 = ((f32[8,24,128]{2,1,0:T(8,128)}), f32[8,24,128]{2,1,0:T(8,128)S(1)}, u32[]{:S(2)}, u32[]{:S(2)}) async-start(f32[8,24,128]{2,1,0:T(8,128)} %column_terms.1.after), calls=%async_computation.1 | async-start | bytes 196608 | tf_op jit(solution)/shard_map/return_column_terms/all_to_all | solution.py:24
  26.8 0.6 %copy-start.3 = (f32[4,16,128]{2,1,0:T(8,128)}, f32[4,16,128]{2,1,0:T(8,128)S(1)}, u32[]{:S(2)}) copy-start(f32[4,16,128]{2,1,0:T(8,128)S(1)} %row_terms.1.terms) | copy-start | bytes 98308
  29.7 0.6 %copy-start.8 = (f32[8,24,128]{2,1,0:T(8,128)}, f32[8,24,128]{2,1,0:T(8,128)S(1)}, u32[]{:S(2)}) copy-start(f32[8,24,128]{2,1,0:T(8,128)S(1)} %all-to-all-done.1.by_row) | copy-start | bytes 294916
  31.8 5.7 %collective-permute-start.3 = (f32[24,128]{1,0:T(8,128)}, f32[24,128]{1,0:T(8,128)S(1)}, u32[]{:S(2)}, u32[]{:S(2)}) collective-permute-start(f32[24,128]{1,0:T(8,128)} %get-tuple-element.11), channel_id=1, source_target_pairs={{0,1},{1,2},{2,3},{3,0},{4,5},{5,6},{6,7},{7,4},{8,9},{9,10},{10,1... | collective-permute-start | bytes 36872 | tf_op jit(solution)/shard_map/return_row_terms/ppermute | solution.py:29
  34.3 4.8 %collective-permute-start.4 = (f32[24,128]{1,0:T(8,128)}, f32[24,128]{1,0:T(8,128)S(1)}, u32[]{:S(2)}, u32[]{:S(2)}) collective-permute-start(f32[24,128]{1,0:T(8,128)} %get-tuple-element.12), channel_id=1, source_target_pairs={{0,2},{1,3},{2,0},{3,1},{4,6},{5,7},{6,4},{7,5},{8,10},{9,11},{10,... | collective-permute-start | bytes 36872 | tf_op jit(solution)/shard_map/return_row_terms/ppermute | solution.py:29
  35.2 4.0 %collective-permute-start.5 = (f32[24,128]{1,0:T(8,128)}, f32[24,128]{1,0:T(8,128)S(1)}, u32[]{:S(2)}, u32[]{:S(2)}) collective-permute-start(f32[24,128]{1,0:T(8,128)} %get-tuple-element.13), channel_id=1, source_target_pairs={{0,3},{1,0},{2,1},{3,2},{4,7},{5,4},{6,5},{7,6},{8,11},{9,8},{10,9... | collective-permute-start | bytes 36872 | tf_op jit(solution)/shard_map/return_row_terms/ppermute | solution.py:29
  39.3 0.7 %copy-start.4 = (f32[24,128]{1,0:T(8,128)S(1)}, f32[24,128]{1,0:T(8,128)}, u32[]{:S(2)}) copy-start(f32[24,128]{1,0:T(8,128)} %get-tuple-element.10.refs_0_) | copy-start | bytes 36868

commit v6 on v3

--- a/solution.py
+++ b/solution.py
@@ -10,7 +10,6 @@
 HP = lax.Precision.HIGHEST
 VMEM = pl.BlockSpec(memory_space=pltpu.VMEM)
 SMEM = pl.BlockSpec(memory_space=pltpu.SMEM)
-BOTH = ("row", "col")
 
 
 def mult(left, right):
@@ -21,8 +20,13 @@
     return lax.dot_general(left, right, (((1,), (1,)), ((), ())), precision=HP, preferred_element_type=jnp.float32)
 
 
-def swap(blocks):
-    return lax.all_to_all(blocks, BOTH, 0, 0, tiled=True)
+def swap(blocks, axis):
+    return lax.all_to_all(blocks, axis, 0, 0, tiled=True)
+
+
+def shift(value, axis, step):
+    size = lax.axis_size(axis)
+    return lax.ppermute(value, axis, [(p, (p + step) % size) for p in range(size)])
 
 
 def own_lanes(nvec, width):
@@ -49,31 +53,66 @@
     return mult(wide, (lane % nvec == column).astype(jnp.float32))
 
 
-def products_kernel(n_row, n_col, slots, place, arow, bcol, count, x_ref, d_ref, x_all, tiles, out, row_terms):
-    own = x_ref[...]
-    nvec = own.shape[0]
+def split(value):
+    first = value.astype(jnp.bfloat16)
+    rest = value - first.astype(jnp.float32)
+    second = rest.astype(jnp.bfloat16)
+    return first, second, (rest - second.astype(jnp.float32)).astype(jnp.bfloat16)
+
+
+def stack_split(value):
+    return jnp.concatenate(split(value), axis=0)
+
+
+def parts_product(stacked, parts, dims):
+    nvec = stacked.shape[0] // 3
+    total = None
+    for used, part in zip((1, 2, 3), parts[::-1]):
+        wide = lax.dot_general(stacked[: used * nvec], part, dims, preferred_element_type=jnp.float32)
+        for row in reversed(range(used)):
+            piece = wide[row * nvec : (row + 1) * nvec]
+            total = piece if total is None else total + piece
+    return total
+
+
+def column_kernel(n_row, n_col, slots, place, arow, bcol, count, d_ref, *refs):
+    x_rows, (tiles, out, *parts, rows, sums) = refs[:n_col], refs[n_col:]
     me_row, me_col = place[0], place[1]
+    for step in range(n_col):
+        rows[step] = stack_split(x_rows[step][...])
+    sums[...] = jnp.zeros_like(sums)
+    sums[me_row] = 0.5 * d_ref[...] * x_rows[0][...]
+    for slot in range(slots):
+        pieces = split(tiles[0, 0, slot])
+        for part, piece in zip(parts, pieces):
+            part[slot] = piece
+        behind = lax.rem(me_col - arow[0, 0, slot] + n_col, n_col)
+        block = jnp.where(slot < count[0, 0], bcol[0, 0, slot], n_row)
+        sums[block] += parts_product(rows[behind], pieces, (((1,), (0,)), ((), ())))
+    out[...] = sums[:n_row]
+
+
+def row_kernel(n_row, n_col, slots, place, arow, bcol, count, d_ref, *refs):
+    x_rows, (x_cols, col_terms, *parts, out, cols, sums) = refs[:n_col], refs[n_col:]
+    nvec, width = x_rows[0].shape
+    me_row, me_col = place[0], place[1]
+    for block in range(n_row):
+        cols[block] = stack_split(x_cols[block])
+    sums[...] = jnp.zeros_like(sums)
+    sums[0] = 0.5 * d_ref[...] * x_rows[0][...]
+    for slot in range(slots):
+        behind = lax.rem(me_col - arow[0, 0, slot] + n_col, n_col)
+        behind = jnp.where(slot < count[0, 0], behind, n_col)
+        pieces = [part[slot] for part in parts]
+        sums[behind] += parts_product(cols[bcol[0, 0, slot]], pieces, (((1,), (1,)), ((), ())))
+    total = jnp.zeros((nvec * nvec // width, width), jnp.float32)
+    for step in range(n_col):
+        total += packed_gram(x_rows[step][...], sums[step])
     out[...] = jnp.zeros_like(out)
-    half = 0.5 * d_ref[...] * own
-    row_terms[...] = jnp.zeros_like(row_terms)
-    row_terms[me_col] = half
-    out[me_row * n_col + me_col, :nvec] = half
-    live_total = count[0, 0]
-    for slot in range(slots):
-        a = arow[0, 0, slot]
-        i = me_row * n_col + a
-        j = bcol[0, 0, slot] * n_col + me_col
-        live = jnp.where(slot < live_total, 1.0, 0.0).astype(jnp.float32)
-        tile = tiles[0, 0, slot]
-        row_terms[a] += mult_last(x_all[j] * live, tile)
-        out[j, :nvec] += mult(x_all[i] * live, tile)
-    left, right = [], []
-    for a in range(n_col):
-        i = me_row * n_col + a
-        terms = row_terms[a]
-        out[i, :nvec] += terms
-        part = packed_gram(x_all[i], terms)
-        total = part if a == 0 else total + part
+    for block in range(n_row):
+        out[block * n_col + me_col, :nvec] = col_terms[block]
+    for step in range(n_col):
+        out[me_row * n_col + lax.rem(me_col - step + n_col, n_col), :nvec] += sums[step]
     for block in range(n_row * n_col):
         out[block, nvec : nvec + total.shape[0]] = total
 
@@ -105,39 +144,59 @@
     scale = 1.0 / float(devices * width)
     packed_rows = nvec * nvec // width
     padded = nvec + 8 * (-(-packed_rows // 8))
+    block = jax.ShapeDtypeStruct((nvec, width), jnp.float32)
     square = jax.ShapeDtypeStruct((nvec, nvec), jnp.float32)
+    part = jax.ShapeDtypeStruct((slots, width, width), jnp.bfloat16)
     place = jnp.stack([lax.axis_index("row"), lax.axis_index("col")]).astype(jnp.int32)
+    energy = diagonal_energy.reshape(1, width)
+    params = pltpu.CompilerParams(vmem_limit_bytes=40 * 2**20)
+    cost = pl.CostEstimate(flops=12 * slots * nvec * width * width, bytes_accessed=2**20, transcendentals=0)
     with jax.named_scope("share_vectors"):
-        x_all = swap(jnp.broadcast_to(vectors[None], (devices, nvec, width)))
-    with jax.named_scope("tile_products"):
+        x_rows = [vectors] + [shift(vectors, "col", step) for step in range(1, n_col)]
+        x_cols = swap(jnp.broadcast_to(vectors[None], (n_row, nvec, width)), "row")
+    with jax.named_scope("column_terms"):
+        col_terms, *parts = pl.pallas_call(
+            functools.partial(column_kernel, n_row, n_col, slots),
+            out_shape=[jax.ShapeDtypeStruct((n_row, nvec, width), jnp.float32), part, part, part],
+            in_specs=[SMEM] * 4 + [VMEM] * (n_col + 2),
+            out_specs=[VMEM] * 4,
+            scratch_shapes=[
+                pltpu.VMEM((n_col, 3 * nvec, width), jnp.bfloat16),
+                pltpu.VMEM((n_row + 1, nvec, width), jnp.float32),
+            ],
+            compiler_params=params,
+            cost_estimate=cost,
+            name="column_terms",
+        )(place, tile_rows, tile_cols, tile_count, energy, *x_rows, tiles)
+    with jax.named_scope("row_terms"):
         terms = pl.pallas_call(
-            functools.partial(products_kernel, n_row, n_col, slots),
+            functools.partial(row_kernel, n_row, n_col, slots),
             out_shape=jax.ShapeDtypeStruct((devices, padded, width), jnp.float32),
-            in_specs=[SMEM] * 4 + [VMEM] * 4,
+            in_specs=[SMEM] * 4 + [VMEM] * (n_col + 6),
             out_specs=VMEM,
-            scratch_shapes=[pltpu.VMEM((n_col, nvec, width), jnp.float32)],
-            compiler_params=pltpu.CompilerParams(vmem_limit_bytes=40 * 2**20),
-            name="tile_products",
-        )(place, tile_rows, tile_cols, tile_count, vectors, diagonal_energy.reshape(1, width), x_all, tiles)
+            scratch_shapes=[
+                pltpu.VMEM((n_row, 3 * nvec, width), jnp.bfloat16),
+                pltpu.VMEM((n_col + 1, nvec, width), jnp.float32),
+            ],
+            compiler_params=params,
+            cost_estimate=cost,
+            name="row_terms",
+        )(place, tile_rows, tile_cols, tile_count, energy, *x_rows, x_cols, col_terms, *parts)
     with jax.named_scope("return_products"):
-        parts = swap(terms)
+        sums = swap(terms, ("row", "col"))
     with jax.named_scope("residual"):
         residual, rayleigh, grams = pl.pallas_call(
             functools.partial(residual_kernel, scale),
-            out_shape=[
-                jax.ShapeDtypeStruct((nvec, width), jnp.float32),
-                square,
-                jax.ShapeDtypeStruct((devices, packed_rows, width), jnp.float32),
-            ],
+            out_shape=[block, square, jax.ShapeDtypeStruct((devices, packed_rows, width), jnp.float32)],
             in_specs=[VMEM] * 2,
             out_specs=[VMEM] * 3,
-            compiler_params=pltpu.CompilerParams(vmem_limit_bytes=40 * 2**20),
+            compiler_params=params,
             name="residual",
-        )(vectors, parts)
+        )(vectors, sums)
     with jax.named_scope("gram_sum"):
         gram = pl.pallas_call(
             functools.partial(gram_kernel, scale), out_shape=square, in_specs=[VMEM], out_specs=VMEM, name="gram_sum"
-        )(swap(grams))
+        )(swap(grams, ("row", "col")))
     return (residual, rayleigh, gram)
 
 

time: 52.9 us -> 49 us (0.926)
  waiting for transfers between devices: 9.44 us -> 1.27 us
  starting transfers between devices: 7.3 us -> 9.84 us
  blocking collectives: 25.4 us -> 27 us
  local copies, waits for them, and re-layouts: 2.65 us -> 3.2 us
    all_to_all x1, waiting for transfers between devices: 9.44 us -> 1.26 us  [swap(): return lax.all_to_all(blocks, axis, 0, 0, tiled=True)]
    ppermute x0 -> x3, starting transfers between devices: none -> 6.11 us  [shift(): lax.ppermute(value, axis, [(p, (p + step) % size) for p in range(size)])]
    all_to_all x1, starting transfers between devices: 7.3 us -> 3.72 us  [swap(): return lax.all_to_all(blocks, axis, 0, 0, tiled=True)]
    all_to_all x2, blocking collectives: 25.4 us -> 27 us  [swap(): return lax.all_to_all(blocks, axis, 0, 0, tiled=True)]
    unnamed x10, local copies, waits for them, and re-layouts: 1.24 us -> 1.85 us
    pallas_call x2 -> x3, Pallas kernels: 4.71 us -> 4.27 us  [the longest x1 2.13 us: per_device(): pl.pallas_call(functools.partial(row_kernel, n_row, n_col, slots), out_sh...]
  transfers between devices with their start and end apart: 1 -> 4, of which waited for: 1 -> 1; matrix products, arithmetic and copies ran while one was open for 0% -> 3% of each run, Pallas kernels for 0% -> 2%
where the time goes in v6:
time: 49 us; the launch traced here: 48.5 us
  blocking collectives  27 us (55%)
  starting transfers between devices  9.84 us (20%)
  Pallas kernels  5.82 us (12%)
  local copies, waits for them, and re-layouts  3.2 us (7%)
  between operations  1.36 us (3%)
  waiting for transfers between devices  1.27 us (3%)
    all_to_all x2, blocking collectives, swap(): return lax.all_to_all(blocks, axis, 0, 0, tiled=True)  27 us
    ppermute x3, starting transfers between devices, shift(): lax.ppermute(value, axis, [(p, (p + step) % size) for p in range(size)])  6.11 us
    all_to_all x1, starting transfers between devices, swap(): return lax.all_to_all(blocks, axis, 0, 0, tiled=True)  3.72 us
    pallas_call x1, Pallas kernels, per_device(): pl.pallas_call(functools.partial(row_kernel, n_row, n_col, slots), out_sh...  2.13 us
    unnamed x10, local copies, waits for them, and re-layouts  1.85 us
    pallas_call x1, Pallas kernels, per_device(): pl.pallas_call(functools.partial(gram_kernel, scale), out_shape=square, i...  1.55 us
    broadcast_in_dim x1, local copies, waits for them, and re-layouts, per_device(): x_cols = swap(jnp.broadcast_to(vectors[None], (n_row, nvec, width)), 'row')  1.35 us
    all_to_all x1, waiting for transfers between devices, swap(): return lax.all_to_all(blocks, axis, 0, 0, tiled=True)  1.26 us
  transfers between devices with their start and end apart: 4, of which 1 were waited for; matrix products, arithmetic and copies ran while one was open for 3% of the time, Pallas kernels for 2%

profile of v6, /device:TPU:0, one launch (start us, length us, event | category | flops | bytes accessed | tf_op | source)
XLA Modules:
  0.0 48.5 jit_solution(13187548212203605238)
XLA Ops:
  0.6 5.1 %collective-permute-start.2 = (f32[16,128]{1,0:T(8,128)}, f32[16,128]{1,0:T(8,128)S(1)}, u32[]{:S(2)}, u32[]{:S(2)}) collective-permute-start(f32[16,128]{1,0:T(8,128)} %x_ref.1), channel_id=1, source_target_pairs={{0,3},{1,0},{2,1},{3,2},{4,7},{5,4},{6,5},{7,6},{8,11},{9,8},{10,9... | collective-permute-start | bytes 24584 | tf_op jit(solution)/shard_map/share_vectors/ppermute | solution.py:29
  5.7 0.0 collective-permute-start.1
  5.7 1.0 %collective-permute-start = (f32[16,128]{1,0:T(8,128)}, f32[16,128]{1,0:T(8,128)S(1)}, u32[]{:S(2)}, u32[]{:S(2)}) collective-permute-start(f32[16,128]{1,0:T(8,128)} %x_ref.1), channel_id=1, source_target_pairs={{0,1},{1,2},{2,3},{3,0},{4,5},{5,6},{6,7},{7,4},{8,9},{9,10},{10,1... | collective-permute-start | bytes 24584 | tf_op jit(solution)/shard_map/share_vectors/ppermute | solution.py:29
  6.7 1.4 %broadcast_in_dim.2 = f32[8,16,128]{2,1,0:T(8,128)} broadcast(f32[16,128]{1,0:T(8,128)} %x_ref.1), dimensions={1,2} | broadcast | bytes 73728 | tf_op jit(solution)/shard_map/share_vectors/broadcast_in_dim | solution.py:156
  8.1 3.7 %all-to-all-start = ((f32[8,16,128]{2,1,0:T(8,128)}), f32[8,16,128]{2,1,0:T(8,128)S(1)}, u32[]{:S(2)}, u32[]{:S(2)}) async-start(f32[8,16,128]{2,1,0:T(8,128)} %broadcast_in_dim.2), calls=%async_computation | async-start | bytes 131072 | tf_op jit(solution)/shard_map/share_vectors/all_to_all | solution.py:24
  11.8 0.0 copy-start.1
  11.8 0.1 pad_add_fusion.place
  12.6 0.0 copy-start.2
  12.6 0.0 copy-start.3
  12.6 0.0 copy-start.4
  12.6 0.0 collective-permute-done.2.refs_3_
  12.6 0.0 collective-permute-done.1.refs_2_
  12.6 0.0 collective-permute-done.refs_1_
  12.6 0.0 copy-done.1
  12.6 0.6 %copy-done.2 = s32[1,1,16]{2,1,0:T(1,128)S(1)} copy-done((s32[1,1,16]{2,1,0:T(1,128)S(1)}, s32[1,1,16]{2,1,0:T(1,128)}, u32[]{:S(2)}) %copy-start.2) | copy-done | bytes 88
  13.2 0.0 copy-done.3
  13.2 0.0 copy-done.4
  13.2 0.0 copy-start
  13.2 1.2 %copy-done = f32[1,1,16,128,128]{4,3,2,1,0:T(8,128)S(1)} copy-done((f32[1,1,16,128,128]{4,3,2,1,0:T(8,128)S(1)}, f32[1,1,16,128,128]{4,3,2,1,0:T(8,128)}, u32[]{:S(2)}) %copy-start) | copy-done | bytes 1048600
  14.5 1.1 %column_terms.1 = (f32[8,16,128]{2,1,0:T(8,128)S(1)}, bf16[16,128,128]{2,1,0:T(8,128)(2,1)S(1)}, bf16[16,128,128]{2,1,0:T(8,128)(2,1)S(1)}, bf16[16,128,128]{2,1,0:T(8,128)(2,1)S(1)}) custom-call(s32[2]{0:T(128)S(1)} %pad_add_fusion.place, s32[1,1,16]{2,1,0:T(1,128)S(1)} %copy-done.2, s32[1,1,16]{2,1,0:T(1,128)S(1)} %copy-done.3, s32[1,1]{1,0:T(1,128)S(6)} %copy.9.count, ...), custom_call_target="tpu_custom_call" | custom-call | flops 50331648 | bytes 1048576 | tf_op jit(solution)/shard_map/column_terms/column_terms/pallas_call | solution.py:158
  15.6 1.3 %all-to-all-done.refs_4_ = f32[8,16,128]{2,1,0:T(8,128)S(1)} async-done(((f32[8,16,128]{2,1,0:T(8,128)}), f32[8,16,128]{2,1,0:T(8,128)S(1)}, u32[]{:S(2)}, u32[]{:S(2)}) %all-to-all-start) | async-done | bytes 65568 | tf_op jit(solution)/shard_map/share_vectors/all_to_all | solution.py:24
  16.8 2.1 %row_terms.1 = f32[32,24,128]{2,1,0:T(8,128)S(1)} custom-call(s32[2]{0:T(128)S(1)} %pad_add_fusion.place, s32[1,1,16]{2,1,0:T(1,128)S(1)} %copy-done.2, s32[1,1,16]{2,1,0:T(1,128)S(1)} %copy-done.3, s32[1,1]{1,0:T(1,128)S(6)} %copy.9.count, f32[1,128]{1,0:T(1,128)S(1)} %bitcast.4, f32[16,128]{1,0:T(8,128)S(1)} %copy-done.1, ...), custom_call_target="tpu_custom_call" | custom-call | flops 50331648 | bytes 1048576 | tf_op jit(solution)/shard_map/row_terms/row_terms/pallas_call | solution.py:172
  19.0 15.9 %all_to_all.15.parts = f32[32,24,128]{2,1,0:T(8,128)S(1)} all-to-all(f32[32,24,128]{2,1,0:T(8,128)S(1)} %row_terms.1), channel_id=1, replica_groups=mesh['row'=8,'col'=4] {'row','col'}, dimensions={0} | all-to-all | bytes 786432 | tf_op jit(solution)/shard_map/return_products/all_to_all | solution.py:24
  34.9 1.0 %residual.1 = (f32[16,128]{1,0:T(8,128)}, f32[16,16]{1,0:T(8,128)}, f32[32,2,128]{2,1,0:T(2,128)S(1)}) custom-call(f32[16,128]{1,0:T(8,128)S(1)} %copy-done.1, f32[32,24,128]{2,1,0:T(8,128)S(1)} %all_to_all.15.parts), custom_call_target="tpu_custom_call" | custom-call | tf_op jit(solution)/shard_map/residual/residual/pallas_call | solution.py:188
  35.9 11.1 %all_to_all.16.parts = f32[32,2,128]{2,1,0:T(2,128)} all-to-all(f32[32,2,128]{2,1,0:T(2,128)S(1)} %get-tuple-element.16), channel_id=1, replica_groups=mesh['row'=8,'col'=4] {'row','col'}, dimensions={0} | all-to-all | bytes 65536 | tf_op jit(solution)/shard_map/gram_sum/all_to_all | solution.py:24
  47.0 1.6 %gram_sum.1 = f32[16,16]{1,0:T(8,128)} custom-call(f32[32,2,128]{2,1,0:T(2,128)} %all_to_all.16.parts), custom_call_target="tpu_custom_call" | custom-call | tf_op jit(solution)/shard_map/gram_sum/gram_sum/pallas_call | solution.py:197
Async XLA Ops:
  0.6 12.0 %collective-permute-start.2 = (f32[16,128]{1,0:T(8,128)}, f32[16,128]{1,0:T(8,128)S(1)}, u32[]{:S(2)}, u32[]{:S(2)}) collective-permute-start(f32[16,128]{1,0:T(8,128)} %x_ref.1), channel_id=1, source_target_pairs={{0,3},{1,0},{2,1},{3,2},{4,7},{5,4},{6,5},{7,6},{8,11},{9,8},{10,9... | collective-permute-start | bytes 24584 | tf_op jit(solution)/shard_map/share_vectors/ppermute | solution.py:29
  5.7 6.9 %collective-permute-start.1 = (f32[16,128]{1,0:T(8,128)}, f32[16,128]{1,0:T(8,128)S(1)}, u32[]{:S(2)}, u32[]{:S(2)}) collective-permute-start(f32[16,128]{1,0:T(8,128)} %x_ref.1), channel_id=1, source_target_pairs={{0,2},{1,3},{2,0},{3,1},{4,6},{5,7},{6,4},{7,5},{8,10},{9,11},{10,... | collective-permute-start | bytes 24584 | tf_op jit(solution)/shard_map/share_vectors/ppermute | solution.py:29
  5.7 6.9 %collective-permute-start = (f32[16,128]{1,0:T(8,128)}, f32[16,128]{1,0:T(8,128)S(1)}, u32[]{:S(2)}, u32[]{:S(2)}) collective-permute-start(f32[16,128]{1,0:T(8,128)} %x_ref.1), channel_id=1, source_target_pairs={{0,1},{1,2},{2,3},{3,0},{4,5},{5,6},{6,7},{7,4},{8,9},{9,10},{10,1... | collective-permute-start | bytes 24584 | tf_op jit(solution)/shard_map/share_vectors/ppermute | solution.py:29
  8.1 8.7 %all-to-all-start = ((f32[8,16,128]{2,1,0:T(8,128)}), f32[8,16,128]{2,1,0:T(8,128)S(1)}, u32[]{:S(2)}, u32[]{:S(2)}) async-start(f32[8,16,128]{2,1,0:T(8,128)} %broadcast_in_dim.2), calls=%async_computation | async-start | bytes 131072 | tf_op jit(solution)/shard_map/share_vectors/all_to_all | solution.py:24
  11.8 0.8 %copy-start.1 = (f32[16,128]{1,0:T(8,128)S(1)}, f32[16,128]{1,0:T(8,128)}, u32[]{:S(2)}) copy-start(f32[16,128]{1,0:T(8,128)} %x_ref.1) | copy-start | bytes 24580
  12.6 0.7 %copy-start.2 = (s32[1,1,16]{2,1,0:T(1,128)S(1)}, s32[1,1,16]{2,1,0:T(1,128)}, u32[]{:S(2)}) copy-start(s32[1,1,16]{2,1,0:T(1,128)} %arow.3) | copy-start | bytes 196
  12.6 0.7 %copy-start.3 = (s32[1,1,16]{2,1,0:T(1,128)S(1)}, s32[1,1,16]{2,1,0:T(1,128)}, u32[]{:S(2)}) copy-start(s32[1,1,16]{2,1,0:T(1,128)} %bcol.3) | copy-start | bytes 196
  12.6 0.7 %copy-start.4 = (f32[128]{0:T(128)S(1)}, f32[128]{0:T(128)}, u32[]{:S(2)}) copy-start(f32[128]{0:T(128)} %param.7) | copy-start | bytes 1540
  13.2 1.2 %copy-start = (f32[1,1,16,128,128]{4,3,2,1,0:T(8,128)S(1)}, f32[1,1,16,128,128]{4,3,2,1,0:T(8,128)}, u32[]{:S(2)}) copy-start(f32[1,1,16,128,128]{4,3,2,1,0:T(8,128)} %refs_4_.1) | copy-start | bytes 3145732

commit v7 on v6

--- a/solution.py
+++ b/solution.py
@@ -24,9 +24,9 @@
     return lax.all_to_all(blocks, axis, 0, 0, tiled=True)
 
 
-def shift(value, axis, step):
+def trade(value, axis, flip):
     size = lax.axis_size(axis)
-    return lax.ppermute(value, axis, [(p, (p + step) % size) for p in range(size)])
+    return lax.ppermute(value, axis, [(p, p ^ flip) for p in range(size)])
 
 
 def own_lanes(nvec, width):
@@ -75,52 +75,77 @@
     return total
 
 
+def pair_kernel(x_ref, other, out):
+    out[0] = x_ref[...]
+    out[1] = other[...]
+
+
 def column_kernel(n_row, n_col, slots, place, arow, bcol, count, d_ref, *refs):
     x_rows, (tiles, out, *parts, rows, sums) = refs[:n_col], refs[n_col:]
     me_row, me_col = place[0], place[1]
-    for step in range(n_col):
-        rows[step] = stack_split(x_rows[step][...])
+    for flip in range(n_col):
+        rows[flip] = stack_split(x_rows[flip][...])
     sums[...] = jnp.zeros_like(sums)
-    sums[me_row] = 0.5 * d_ref[...] * x_rows[0][...]
+    sums[0] = 0.5 * d_ref[...] * x_rows[0][...]
     for slot in range(slots):
         pieces = split(tiles[0, 0, slot])
         for part, piece in zip(parts, pieces):
             part[slot] = piece
-        behind = lax.rem(me_col - arow[0, 0, slot] + n_col, n_col)
-        block = jnp.where(slot < count[0, 0], bcol[0, 0, slot], n_row)
-        sums[block] += parts_product(rows[behind], pieces, (((1,), (0,)), ((), ())))
+        block = jnp.where(slot < count[0, 0], bcol[0, 0, slot] ^ me_row, n_row)
+        sums[block] += parts_product(rows[arow[0, 0, slot] ^ me_col], pieces, (((1,), (0,)), ((), ())))
     out[...] = sums[:n_row]
 
 
 def row_kernel(n_row, n_col, slots, place, arow, bcol, count, d_ref, *refs):
-    x_rows, (x_cols, col_terms, *parts, out, cols, sums) = refs[:n_col], refs[n_col:]
+    x_rows, refs = refs[:n_col], refs[n_col:]
+    x_pairs, (col_terms, *parts, out, to_core, cols, sums) = refs[: n_row // 2], refs[n_row // 2 :]
     nvec, width = x_rows[0].shape
     me_row, me_col = place[0], place[1]
-    for block in range(n_row):
-        cols[block] = stack_split(x_cols[block])
+    for flip in range(n_row):
+        cols[flip] = stack_split(x_pairs[flip // 2][flip % 2])
     sums[...] = jnp.zeros_like(sums)
     sums[0] = 0.5 * d_ref[...] * x_rows[0][...]
     for slot in range(slots):
-        behind = lax.rem(me_col - arow[0, 0, slot] + n_col, n_col)
-        behind = jnp.where(slot < count[0, 0], behind, n_col)
+        block = jnp.where(slot < count[0, 0], arow[0, 0, slot] ^ me_col, n_col)
         pieces = [part[slot] for part in parts]
-        sums[behind] += parts_product(cols[bcol[0, 0, slot]], pieces, (((1,), (1,)), ((), ())))
-    total = jnp.zeros((nvec * nvec // width, width), jnp.float32)
-    for step in range(n_col):
-        total += packed_gram(x_rows[step][...], sums[step])
-    out[...] = jnp.zeros_like(out)
-    for block in range(n_row):
-        out[block * n_col + me_col, :nvec] = col_terms[block]
-    for step in range(n_col):
-        out[me_row * n_col + lax.rem(me_col - step + n_col, n_col), :nvec] += sums[step]
-    for block in range(n_row * n_col):
-        out[block, nvec : nvec + total.shape[0]] = total
-
-
-def residual_kernel(scale, x_ref, parts, residual, rayleigh, out):
+        sums[block] += parts_product(cols[bcol[0, 0, slot] ^ me_row], pieces, (((1,), (1,)), ((), ())))
+    out[...] = sums[:n_col]
+    for chip in range(n_row // 2):
+        to_core[chip * nvec : (chip + 1) * nvec] = col_terms[2 * chip + 1]
+    total = packed_gram(x_rows[0][...], sums[0])
+    for flip in range(1, n_col):
+        total += packed_gram(x_rows[flip][...], sums[flip])
+    to_core[n_row // 2 * nvec :] = jnp.concatenate([total, jnp.zeros((to_core.shape[0] - n_row // 2 * nvec - total.shape[0], width), jnp.float32)], axis=0)
+
+
+def chip_kernel(col_terms, mine, other, *outs):
+    nvec = col_terms.shape[1]
+    tail = len(outs) * nvec
+    for chip, out in enumerate(outs):
+        out[:nvec] = col_terms[2 * chip] + other[chip * nvec : (chip + 1) * nvec]
+        out[nvec:] = mine[tail:] + other[tail:]
+
+
+def join_kernel(n_chip, *refs):
+    by_row, (terms, *outs) = refs[:n_chip], refs[n_chip:]
+    nvec = terms.shape[1]
+    both = by_row[0][...]
+    for part in by_row[1:]:
+        both += part[...]
+    outs[0][:nvec] = both[:nvec] + terms[0]
+    for flip in range(1, len(outs)):
+        outs[flip][:nvec] = terms[flip]
+    for out in outs:
+        out[nvec:] = both[nvec:]
+
+
+def residual_kernel(scale, x_ref, *refs):
+    parts, (residual, rayleigh, out) = refs[:-3], refs[-3:]
     own = x_ref[...]
     nvec = own.shape[0]
-    both = jnp.sum(parts[...], axis=0)
+    both = parts[0][...]
+    for part in parts[1:]:
+        both += part[...]
     half = unpack(both[nvec : nvec + out.shape[1]], nvec)
     ray = (half + half.T) * scale
     rayleigh[...] = ray
@@ -144,16 +169,26 @@
     scale = 1.0 / float(devices * width)
     packed_rows = nvec * nvec // width
     padded = nvec + 8 * (-(-packed_rows // 8))
+    n_chip = n_row // 2
     block = jax.ShapeDtypeStruct((nvec, width), jnp.float32)
+    joined = jax.ShapeDtypeStruct((padded, width), jnp.float32)
     square = jax.ShapeDtypeStruct((nvec, nvec), jnp.float32)
     part = jax.ShapeDtypeStruct((slots, width, width), jnp.bfloat16)
     place = jnp.stack([lax.axis_index("row"), lax.axis_index("col")]).astype(jnp.int32)
     energy = diagonal_energy.reshape(1, width)
-    params = pltpu.CompilerParams(vmem_limit_bytes=40 * 2**20)
+    params = pltpu.CompilerParams(vmem_limit_bytes=24 * 2**20)
     cost = pl.CostEstimate(flops=12 * slots * nvec * width * width, bytes_accessed=2**20, transcendentals=0)
     with jax.named_scope("share_vectors"):
-        x_rows = [vectors] + [shift(vectors, "col", step) for step in range(1, n_col)]
-        x_cols = swap(jnp.broadcast_to(vectors[None], (n_row, nvec, width)), "row")
+        other = trade(vectors, "row", 1)
+        x_rows = [vectors] + [trade(vectors, "col", flip) for flip in range(1, n_col)]
+        pair = pl.pallas_call(
+            pair_kernel,
+            out_shape=jax.ShapeDtypeStruct((2, nvec, width), jnp.float32),
+            in_specs=[VMEM] * 2,
+            out_specs=VMEM,
+            name="pair",
+        )(vectors, other)
+        x_pairs = [pair] + [trade(pair, "row", 2 * chip) for chip in range(1, n_chip)]
     with jax.named_scope("column_terms"):
         col_terms, *parts = pl.pallas_call(
             functools.partial(column_kernel, n_row, n_col, slots),
@@ -169,11 +204,14 @@
             name="column_terms",
         )(place, tile_rows, tile_cols, tile_count, energy, *x_rows, tiles)
     with jax.named_scope("row_terms"):
-        terms = pl.pallas_call(
+        row_terms, to_core = pl.pallas_call(
             functools.partial(row_kernel, n_row, n_col, slots),
-            out_shape=jax.ShapeDtypeStruct((devices, padded, width), jnp.float32),
-            in_specs=[SMEM] * 4 + [VMEM] * (n_col + 6),
-            out_specs=VMEM,
+            out_shape=[
+                jax.ShapeDtypeStruct((n_col, nvec, width), jnp.float32),
+                jax.ShapeDtypeStruct((n_chip * nvec + padded - nvec, width), jnp.float32),
+            ],
+            in_specs=[SMEM] * 4 + [VMEM] * (1 + n_col + n_chip + 4),
+            out_specs=[VMEM] * 2,
             scratch_shapes=[
                 pltpu.VMEM((n_row, 3 * nvec, width), jnp.bfloat16),
                 pltpu.VMEM((n_col + 1, nvec, width), jnp.float32),
@@ -181,18 +219,29 @@
             compiler_params=params,
             cost_estimate=cost,
             name="row_terms",
-        )(place, tile_rows, tile_cols, tile_count, energy, *x_rows, x_cols, col_terms, *parts)
+        )(place, tile_rows, tile_cols, tile_count, energy, *x_rows, *x_pairs, col_terms, *parts)
     with jax.named_scope("return_products"):
-        sums = swap(terms, ("row", "col"))
+        chips = pl.pallas_call(
+            chip_kernel, out_shape=[joined] * n_chip, in_specs=[VMEM] * 3, out_specs=[VMEM] * n_chip, name="chip_sum"
+        )(col_terms, to_core, trade(to_core, "row", 1))
+        by_row = [chips[0]] + [trade(chips[chip], "row", 2 * chip) for chip in range(1, n_chip)]
+        sends = pl.pallas_call(
+            functools.partial(join_kernel, n_chip),
+            out_shape=[joined] * n_col,
+            in_specs=[VMEM] * (n_chip + 1),
+            out_specs=[VMEM] * n_col,
+            name="row_sum",
+        )(*by_row, row_terms)
+        sums = [sends[0]] + [trade(sends[flip], "col", flip) for flip in range(1, n_col)]
     with jax.named_scope("residual"):
         residual, rayleigh, grams = pl.pallas_call(
             functools.partial(residual_kernel, scale),
             out_shape=[block, square, jax.ShapeDtypeStruct((devices, packed_rows, width), jnp.float32)],
-            in_specs=[VMEM] * 2,
+            in_specs=[VMEM] * (1 + n_col),
             out_specs=[VMEM] * 3,
             compiler_params=params,
             name="residual",
-        )(vectors, sums)
+        )(vectors, *sums)
     with jax.named_scope("gram_sum"):
         gram = pl.pallas_call(
             functools.partial(gram_kernel, scale), out_shape=square, in_specs=[VMEM], out_specs=VMEM, name="gram_sum"

time: 49 us -> 55 us (1.12)
  blocking collectives: 27 us -> 9.65 us
  waiting for transfers between devices: 1.27 us -> 11.2 us
  starting transfers between devices: 9.84 us -> 17.2 us
  Pallas kernels: 5.82 us -> 10.1 us
  local copies, waits for them, and re-layouts: 3.2 us -> 4.97 us
    all_to_all x2 -> x1, blocking collectives: 27 us -> 9.65 us  [swap(): return lax.all_to_all(blocks, axis, 0, 0, tiled=True)]
    ppermute x3 -> x14, waiting for transfers between devices: 0.01 us -> 11.2 us  [trade(): return lax.ppermute(value, axis, [(p, p ^ flip) for p in range(size)])]
    ppermute x3 -> x14, starting transfers between devices: 6.11 us -> 17.2 us  [trade(): return lax.ppermute(value, axis, [(p, p ^ flip) for p in range(size)])]
    pallas_call x0 -> x3, Pallas kernels: none -> 4.27 us  [the longest x1 1.49 us: per_device(): pl.pallas_call(chip_kernel, out_shape=[joined] * n_chip, in_specs=[VMEM]...]
    all_to_all x1 -> x0, starting transfers between devices: 3.72 us -> none  [swap(): return lax.all_to_all(blocks, axis, 0, 0, tiled=True)]
    unnamed x10 -> x30, local copies, waits for them, and re-layouts: 1.85 us -> 4.97 us
    broadcast_in_dim x1 -> x0, local copies, waits for them, and re-layouts: 1.35 us -> none  [per_device(): x_cols = swap(jnp.broadcast_to(vectors[None], (n_row, nvec, width)), 'row')]
    all_to_all x1 -> x0, waiting for transfers between devices: 1.26 us -> none  [swap(): return lax.all_to_all(blocks, axis, 0, 0, tiled=True)]
  transfers between devices with their start and end apart: 4 -> 14, of which waited for: 1 -> 6; matrix products, arithmetic and copies ran while one was open for 3% -> 0% of each run, Pallas kernels for 2% -> 4%
where the time goes in v7:
time: 55 us; the launch traced here: 54.6 us
  starting transfers between devices  17.2 us (31%)
  waiting for transfers between devices  11.2 us (20%)
  Pallas kernels  10.1 us (18%)
  blocking collectives  9.65 us (18%)
  local copies, waits for them, and re-layouts  4.97 us (9%)
  between operations  1.43 us (3%)
    ppermute x14, starting transfers between devices, trade(): return lax.ppermute(value, axis, [(p, p ^ flip) for p in range(size)])  17.2 us
    ppermute x14, waiting for transfers between devices, trade(): return lax.ppermute(value, axis, [(p, p ^ flip) for p in range(size)])  11.2 us
    all_to_all x1, blocking collectives, swap(): return lax.all_to_all(blocks, axis, 0, 0, tiled=True)  9.65 us
    unnamed x30, local copies, waits for them, and re-layouts  4.97 us
    pallas_call x1, Pallas kernels, per_device(): pl.pallas_call(functools.partial(row_kernel, n_row, n_col, slots), out_sh...  2.12 us
    pallas_call x1, Pallas kernels, per_device(): pl.pallas_call(functools.partial(gram_kernel, scale), out_shape=square, i...  1.55 us
    pallas_call x1, Pallas kernels, per_device(): pl.pallas_call(chip_kernel, out_shape=[joined] * n_chip, in_specs=[VMEM]...  1.49 us
    pallas_call x1, Pallas kernels, per_device(): pl.pallas_call(functools.partial(join_kernel, n_chip), out_shape=[joined]...  1.46 us
  transfers between devices with their start and end apart: 14, of which 6 were waited for; matrix products, arithmetic and copies ran while one was open for 0% of the time, Pallas kernels for 4%

profile of v7, /device:TPU:0, one launch (start us, length us, event | category | flops | bytes accessed | tf_op | source)
XLA Modules:
  0.0 54.6 jit_solution(12518059364236387381)
XLA Ops:
  0.6 0.5 collective-permute-start.3
  1.1 4.7 %collective-permute-start.2 = (f32[16,128]{1,0:T(8,128)}, f32[16,128]{1,0:T(8,128)S(1)}, u32[]{:S(2)}, u32[]{:S(2)}) collective-permute-start(f32[16,128]{1,0:T(8,128)} %x_ref.3), channel_id=1, source_target_pairs={{0,3},{1,2},{2,1},{3,0},{4,7},{5,6},{6,5},{7,4},{8,11},{9,10},{10,... | collective-permute-start | bytes 24584 | tf_op jit(solution)/shard_map/share_vectors/ppermute | solution.py:29
  5.8 0.0 collective-permute-start.1
  5.8 0.6 %collective-permute-start = (f32[16,128]{1,0:T(8,128)}, f32[16,128]{1,0:T(8,128)S(1)}, u32[]{:S(2)}, u32[]{:S(2)}) collective-permute-start(f32[16,128]{1,0:T(8,128)} %x_ref.3), channel_id=1, source_target_pairs={{0,1},{1,0},{2,3},{3,2},{4,5},{5,4},{6,7},{7,6},{8,9},{9,8},{10,11... | collective-permute-start | bytes 24584 | tf_op jit(solution)/shard_map/share_vectors/ppermute | solution.py:29
  6.5 0.0 collective-permute-done.3.other
  6.5 0.6 %copy-done.14 = f32[16,128]{1,0:T(8,128)} copy-done((f32[16,128]{1,0:T(8,128)}, f32[16,128]{1,0:T(8,128)S(1)}, u32[]{:S(2)}) %copy-start.14) | copy-done | bytes 8216
  7.1 1.3 %pair.1.refs_4_ = f32[2,16,128]{2,1,0:T(8,128)} custom-call(f32[16,128]{1,0:T(8,128)} %x_ref.3, f32[16,128]{1,0:T(8,128)} %copy-done.14), custom_call_target="tpu_custom_call" | custom-call | tf_op jit(solution)/shard_map/share_vectors/pair/pallas_call | solution.py:184
  8.4 2.6 %collective-permute-start.6 = (f32[2,16,128]{2,1,0:T(8,128)}, f32[2,16,128]{2,1,0:T(8,128)S(1)}, u32[]{:S(2)}, u32[]{:S(2)}) collective-permute-start(f32[2,16,128]{2,1,0:T(8,128)} %pair.1.refs_4_), channel_id=1, source_target_pairs={{0,24},{4,28},{8,16},{12,20},{16,8},{20,12},{24,0},{28,4},{1,25},{... | collective-permute-start | bytes 49160 | tf_op jit(solution)/shard_map/share_vectors/ppermute | solution.py:29
  11.0 0.5 collective-permute-start.5
  11.5 0.0 collective-permute-done.2.refs_3_
  11.5 0.4 collective-permute-start.4
  11.9 0.1 pad_add_fusion.place
  12.6 0.0 copy-start.7
  12.6 0.0 copy-start.8
  12.6 0.0 collective-permute-done.1.refs_2_
  12.7 0.0 collective-permute-done.refs_1_
  12.7 0.6 %copy-done.7 = s32[1,1,16]{2,1,0:T(1,128)S(1)} copy-done((s32[1,1,16]{2,1,0:T(1,128)S(1)}, s32[1,1,16]{2,1,0:T(1,128)}, u32[]{:S(2)}) %copy-start.7) | copy-done | bytes 88
  13.3 0.0 copy-done.8
  13.3 1.2 %copy-done = f32[1,1,16,128,128]{4,3,2,1,0:T(8,128)S(1)} copy-done((f32[1,1,16,128,128]{4,3,2,1,0:T(8,128)S(1)}, f32[1,1,16,128,128]{4,3,2,1,0:T(8,128)}, u32[]{:S(2)}) %copy-start) | copy-done | bytes 1048600
  14.5 1.1 %column_terms.1 = (f32[8,16,128]{2,1,0:T(8,128)S(1)}, bf16[16,128,128]{2,1,0:T(8,128)(2,1)S(1)}, bf16[16,128,128]{2,1,0:T(8,128)(2,1)S(1)}, bf16[16,128,128]{2,1,0:T(8,128)(2,1)S(1)}) custom-call(s32[2]{0:T(128)S(1)} %pad_add_fusion.place, s32[1,1,16]{2,1,0:T(1,128)S(1)} %copy-done.7, s32[1,1,16]{2,1,0:T(1,128)S(1)} %copy-done.8, s32[1,1]{1,0:T(1,128)S(6)} %copy.9.count, ...), custom_call_target="tpu_custom_call" | custom-call | flops 50331648 | bytes 1048576 | tf_op jit(solution)/shard_map/column_terms/column_terms/pallas_call | solution.py:193
  15.6 0.0 collective-permute-done.6.refs_7_
  15.7 0.0 collective-permute-done.5.refs_6_
  15.7 0.0 collective-permute-done.4.refs_5_
  15.7 0.0 copy-done.3
  15.7 2.1 %row_terms.1 = (f32[4,16,128]{2,1,0:T(8,128)S(1)}, f32[72,128]{1,0:T(8,128)S(1)}) custom-call(s32[2]{0:T(128)S(1)} %pad_add_fusion.place, s32[1,1,16]{2,1,0:T(1,128)S(1)} %copy-done.7, s32[1,1,16]{2,1,0:T(1,128)S(1)} %copy-done.8, s32[1,1]{1,0:T(1,128)S(6)} %copy.9.count, f32[1,128]{1,0:T(1,128)S(1)} %bitcast.4, f32[16,128]{1,0:T(8,128)S(1)} %copy-done.2, ...), custom_call_target="tpu_custom_call" | custom-call | flops 50331648 | bytes 1048576 | tf_op jit(solution)/shard_map/row_terms/row_terms/pallas_call | solution.py:207
  17.8 0.6 %copy-done.5 = f32[4,16,128]{2,1,0:T(8,128)} copy-done((f32[4,16,128]{2,1,0:T(8,128)}, f32[4,16,128]{2,1,0:T(8,128)S(1)}, u32[]{:S(2)}) %copy-start.5) | copy-done | bytes 32792
  18.4 0.0 collective-permute-start.7
  18.4 1.2 %collective-permute-done.7.other = f32[72,128]{1,0:T(8,128)S(1)} collective-permute-done((f32[72,128]{1,0:T(8,128)S(1)}, f32[72,128]{1,0:T(8,128)S(1)}, u32[]{:S(2)}, u32[]{:S(2)}) %collective-permute-start.7) | collective-permute-done | bytes 36896 | tf_op jit(solution)/shard_map/return_products/ppermute | solution.py:29
  19.6 0.6 %copy-done.10 = f32[72,128]{1,0:T(8,128)} copy-done((f32[72,128]{1,0:T(8,128)}, f32[72,128]{1,0:T(8,128)S(1)}, u32[]{:S(2)}) %copy-start.10) | copy-done | bytes 36888
  20.3 1.5 %chip_sum.1 = (f32[24,128]{1,0:T(8,128)}, f32[24,128]{1,0:T(8,128)}, f32[24,128]{1,0:T(8,128)}, f32[24,128]{1,0:T(8,128)}) custom-call(f32[8,16,128]{2,1,0:T(8,128)} %copy-done.1, f32[72,128]{1,0:T(8,128)} %copy-done.4, f32[72,128]{1,0:T(8,128)} %copy-done.10), custom_call_target="tpu_custom_call" | custom-call | tf_op jit(solution)/shard_map/return_products/chip_sum/pallas_call | solution.py:224
  21.7 1.6 %collective-permute-start.8 = (f32[24,128]{1,0:T(8,128)}, f32[24,128]{1,0:T(8,128)S(1)}, u32[]{:S(2)}, u32[]{:S(2)}) collective-permute-start(f32[24,128]{1,0:T(8,128)} %get-tuple-element.26), channel_id=1, source_target_pairs={{0,8},{4,12},{8,0},{12,4},{16,24},{20,28},{24,16},{28,20},{1,9},{5... | collective-permute-start | bytes 36872 | tf_op jit(solution)/shard_map/return_products/ppermute | solution.py:29
  23.4 1.5 %collective-permute-start.9 = (f32[24,128]{1,0:T(8,128)}, f32[24,128]{1,0:T(8,128)S(1)}, u32[]{:S(2)}, u32[]{:S(2)}) collective-permute-start(f32[24,128]{1,0:T(8,128)} %get-tuple-element.27), channel_id=1, source_target_pairs={{0,16},{4,20},{8,24},{12,28},{16,0},{20,4},{24,8},{28,12},{1,17},{... | collective-permute-start | bytes 36872 | tf_op jit(solution)/shard_map/return_products/ppermute | solution.py:29
  24.9 0.3 collective-permute-start.10
  25.2 0.4 collective-permute-done.8.refs_1_
  25.7 1.6 %collective-permute-done.9.refs_2_ = f32[24,128]{1,0:T(8,128)S(1)} collective-permute-done((f32[24,128]{1,0:T(8,128)}, f32[24,128]{1,0:T(8,128)S(1)}, u32[]{:S(2)}, u32[]{:S(2)}) %collective-permute-start.9) | collective-permute-done | bytes 12320 | tf_op jit(solution)/shard_map/return_products/ppermute | solution.py:29
  27.3 2.4 %collective-permute-done.10.refs_3_ = f32[24,128]{1,0:T(8,128)S(1)} collective-permute-done((f32[24,128]{1,0:T(8,128)}, f32[24,128]{1,0:T(8,128)S(1)}, u32[]{:S(2)}, u32[]{:S(2)}) %collective-permute-start.10) | collective-permute-done | bytes 12320 | tf_op jit(solution)/shard_map/return_products/ppermute | solution.py:29
  29.7 0.6 %copy-done.13 = f32[24,128]{1,0:T(8,128)} copy-done((f32[24,128]{1,0:T(8,128)}, f32[24,128]{1,0:T(8,128)S(1)}, u32[]{:S(2)}) %copy-start.13) | copy-done | bytes 12312
  30.3 1.5 %row_sum.1 = (f32[24,128]{1,0:T(8,128)}, f32[24,128]{1,0:T(8,128)}, f32[24,128]{1,0:T(8,128)}, f32[24,128]{1,0:T(8,128)}) custom-call(f32[24,128]{1,0:T(8,128)} %get-tuple-element.25.refs_0_, f32[24,128]{1,0:T(8,128)} %copy-done.11, f32[24,128]{1,0:T(8,128)} %copy-done.12, f32[24,128]{1,0:T(8,128)} %copy-done.13, f32[4,16,128]{2,1,0:T(8,128)} %copy-done.5), custom_call_target="tpu_custom_call" | custom-call | tf_op jit(solution)/shard_map/return_products/row_sum/pallas_call | solution.py:228
  31.8 1.2 %collective-permute-start.11 = (f32[24,128]{1,0:T(8,128)}, f32[24,128]{1,0:T(8,128)S(1)}, u32[]{:S(2)}, u32[]{:S(2)}) collective-permute-start(f32[24,128]{1,0:T(8,128)} %get-tuple-element.31), channel_id=1, source_target_pairs={{0,1},{1,0},{2,3},{3,2},{4,5},{5,4},{6,7},{7,6},{8,9},{9,8},{10,11... | collective-permute-start | bytes 36872 | tf_op jit(solution)/shard_map/return_products/ppermute | solution.py:29
  33.0 2.9 %collective-permute-start.12 = (f32[24,128]{1,0:T(8,128)}, f32[24,128]{1,0:T(8,128)S(1)}, u32[]{:S(2)}, u32[]{:S(2)}) collective-permute-start(f32[24,128]{1,0:T(8,128)} %get-tuple-element.32), channel_id=1, source_target_pairs={{0,2},{1,3},{2,0},{3,1},{4,6},{5,7},{6,4},{7,5},{8,10},{9,11},{10,... | collective-permute-start | bytes 36872 | tf_op jit(solution)/shard_map/return_products/ppermute | solution.py:29
  35.9 0.2 collective-permute-start.13
  36.1 0.0 collective-permute-done.11.refs_1_
  36.2 1.7 %collective-permute-done.12.refs_2_ = f32[24,128]{1,0:T(8,128)S(1)} collective-permute-done((f32[24,128]{1,0:T(8,128)}, f32[24,128]{1,0:T(8,128)S(1)}, u32[]{:S(2)}, u32[]{:S(2)}) %collective-permute-start.12) | collective-permute-done | bytes 12320 | tf_op jit(solution)/shard_map/return_products/ppermute | solution.py:29
  37.8 3.8 %collective-permute-done.13.refs_3_ = f32[24,128]{1,0:T(8,128)S(1)} collective-permute-done((f32[24,128]{1,0:T(8,128)}, f32[24,128]{1,0:T(8,128)S(1)}, u32[]{:S(2)}, u32[]{:S(2)}) %collective-permute-start.13) | collective-permute-done | bytes 12320 | tf_op jit(solution)/shard_map/return_products/ppermute | solution.py:29
  41.6 0.7 %copy-done.6 = f32[24,128]{1,0:T(8,128)S(1)} copy-done((f32[24,128]{1,0:T(8,128)S(1)}, f32[24,128]{1,0:T(8,128)}, u32[]{:S(2)}) %copy-start.6) | copy-done | bytes 12312
  42.3 1.0 %residual.1 = (f32[16,128]{1,0:T(8,128)}, f32[16,16]{1,0:T(8,128)}, f32[32,2,128]{2,1,0:T(2,128)S(1)}) custom-call(f32[16,128]{1,0:T(8,128)S(1)} %copy-done.2, f32[24,128]{1,0:T(8,128)S(1)} %copy-done.6, f32[24,128]{1,0:T(8,128)S(1)} %collective-permute-done.11.refs_1_, f32[24,128]{1,0:T(8,128)S(1)} %collective-permute-done.12.refs_2_, ...), custom_call_target="tpu_custom_call" | custom-call | tf_op jit(solution)/shard_map/residual/residual/pallas_call | solution.py:237
  43.4 9.7 %all_to_all.5.parts = f32[32,2,128]{2,1,0:T(2,128)} all-to-all(f32[32,2,128]{2,1,0:T(2,128)S(1)} %get-tuple-element.36), channel_id=1, replica_groups=mesh['row'=8,'col'=4] {'row','col'}, dimensions={0} | all-to-all | bytes 65536 | tf_op jit(solution)/shard_map/gram_sum/all_to_all | solution.py:24
  53.0 1.6 %gram_sum.1 = f32[16,16]{1,0:T(8,128)} custom-call(f32[32,2,128]{2,1,0:T(2,128)} %all_to_all.5.parts), custom_call_target="tpu_custom_call" | custom-call | tf_op jit(solution)/shard_map/gram_sum/gram_sum/pallas_call | solution.py:246
  (19 shorter events, 0.0 us)
Async XLA Ops:
  0.6 5.8 %collective-permute-start.3 = (f32[16,128]{1,0:T(8,128)}, f32[16,128]{1,0:T(8,128)S(1)}, u32[]{:S(2)}, u32[]{:S(2)}) collective-permute-start(f32[16,128]{1,0:T(8,128)} %x_ref.3), channel_id=1, source_target_pairs={{0,4},{4,0},{8,12},{12,8},{16,20},{20,16},{24,28},{28,24},{1,5},{5... | collective-permute-start | bytes 24584 | tf_op jit(solution)/shard_map/share_vectors/ppermute | solution.py:29
  1.1 10.4 %collective-permute-start.2 = (f32[16,128]{1,0:T(8,128)}, f32[16,128]{1,0:T(8,128)S(1)}, u32[]{:S(2)}, u32[]{:S(2)}) collective-permute-start(f32[16,128]{1,0:T(8,128)} %x_ref.3), channel_id=1, source_target_pairs={{0,3},{1,2},{2,1},{3,0},{4,7},{5,6},{6,5},{7,4},{8,11},{9,10},{10,... | collective-permute-start | bytes 24584 | tf_op jit(solution)/shard_map/share_vectors/ppermute | solution.py:29
  5.8 6.8 %collective-permute-start.1 = (f32[16,128]{1,0:T(8,128)}, f32[16,128]{1,0:T(8,128)S(1)}, u32[]{:S(2)}, u32[]{:S(2)}) collective-permute-start(f32[16,128]{1,0:T(8,128)} %x_ref.3), channel_id=1, source_target_pairs={{0,2},{1,3},{2,0},{3,1},{4,6},{5,7},{6,4},{7,5},{8,10},{9,11},{10,... | collective-permute-start | bytes 24584 | tf_op jit(solution)/shard_map/share_vectors/ppermute | solution.py:29
  5.8 6.8 %collective-permute-start = (f32[16,128]{1,0:T(8,128)}, f32[16,128]{1,0:T(8,128)S(1)}, u32[]{:S(2)}, u32[]{:S(2)}) collective-permute-start(f32[16,128]{1,0:T(8,128)} %x_ref.3), channel_id=1, source_target_pairs={{0,1},{1,0},{2,3},{3,2},{4,5},{5,4},{6,7},{7,6},{8,9},{9,8},{10,11... | collective-permute-start | bytes 24584 | tf_op jit(solution)/shard_map/share_vectors/ppermute | solution.py:29
  6.5 0.6 %copy-start.14 = (f32[16,128]{1,0:T(8,128)}, f32[16,128]{1,0:T(8,128)S(1)}, u32[]{:S(2)}) copy-start(f32[16,128]{1,0:T(8,128)S(1)} %collective-permute-done.3.other) | copy-start | bytes 24580
  7.1 5.6 %copy-start.9 = (f32[128]{0:T(128)S(1)}, f32[128]{0:T(128)}, u32[]{:S(2)}) copy-start(f32[128]{0:T(128)} %param.7) | copy-start | bytes 1540
  8.4 4.3 %copy-start.2 = (f32[16,128]{1,0:T(8,128)S(1)}, f32[16,128]{1,0:T(8,128)}, u32[]{:S(2)}) copy-start(f32[16,128]{1,0:T(8,128)} %x_ref.3) | copy-start | bytes 24580
  8.4 7.2 %collective-permute-start.6 = (f32[2,16,128]{2,1,0:T(8,128)}, f32[2,16,128]{2,1,0:T(8,128)S(1)}, u32[]{:S(2)}, u32[]{:S(2)}) collective-permute-start(f32[2,16,128]{2,1,0:T(8,128)} %pair.1.refs_4_), channel_id=1, source_target_pairs={{0,24},{4,28},{8,16},{12,20},{16,8},{20,12},{24,0},{28,4},{1,25},{... | collective-permute-start | bytes 49160 | tf_op jit(solution)/shard_map/share_vectors/ppermute | solution.py:29
  11.0 4.7 %collective-permute-start.5 = (f32[2,16,128]{2,1,0:T(8,128)}, f32[2,16,128]{2,1,0:T(8,128)S(1)}, u32[]{:S(2)}, u32[]{:S(2)}) collective-permute-start(f32[2,16,128]{2,1,0:T(8,128)} %pair.1.refs_4_), channel_id=1, source_target_pairs={{0,16},{4,20},{8,24},{12,28},{16,0},{20,4},{24,8},{28,12},{1,17},{... | collective-permute-start | bytes 49160 | tf_op jit(solution)/shard_map/share_vectors/ppermute | solution.py:29
  11.5 4.2 %collective-permute-start.4 = (f32[2,16,128]{2,1,0:T(8,128)}, f32[2,16,128]{2,1,0:T(8,128)S(1)}, u32[]{:S(2)}, u32[]{:S(2)}) collective-permute-start(f32[2,16,128]{2,1,0:T(8,128)} %pair.1.refs_4_), channel_id=1, source_target_pairs={{0,8},{4,12},{8,0},{12,4},{16,24},{20,28},{24,16},{28,20},{1,9},{5... | collective-permute-start | bytes 49160 | tf_op jit(solution)/shard_map/share_vectors/ppermute | solution.py:29
  12.6 0.7 %copy-start.7 = (s32[1,1,16]{2,1,0:T(1,128)S(1)}, s32[1,1,16]{2,1,0:T(1,128)}, u32[]{:S(2)}) copy-start(s32[1,1,16]{2,1,0:T(1,128)} %arow.3) | copy-start | bytes 196
  12.6 0.7 %copy-start.8 = (s32[1,1,16]{2,1,0:T(1,128)S(1)}, s32[1,1,16]{2,1,0:T(1,128)}, u32[]{:S(2)}) copy-start(s32[1,1,16]{2,1,0:T(1,128)} %bcol.3) | copy-start | bytes 196
  13.3 1.2 %copy-start = (f32[1,1,16,128,128]{4,3,2,1,0:T(8,128)S(1)}, f32[1,1,16,128,128]{4,3,2,1,0:T(8,128)}, u32[]{:S(2)}) copy-start(f32[1,1,16,128,128]{4,3,2,1,0:T(8,128)} %refs_4_.1) | copy-start | bytes 3145732
  14.5 1.2 %copy-start.3 = (f32[2,16,128]{2,1,0:T(8,128)S(1)}, f32[2,16,128]{2,1,0:T(8,128)}, u32[]{:S(2)}) copy-start(f32[2,16,128]{2,1,0:T(8,128)} %pair.1.refs_4_) | copy-start | bytes 49156
  15.6 2.2 %copy-start.1 = (f32[8,16,128]{2,1,0:T(8,128)}, f32[8,16,128]{2,1,0:T(8,128)S(1)}, u32[]{:S(2)}) copy-start(f32[8,16,128]{2,1,0:T(8,128)S(1)} %get-tuple-element.20.refs_8_.col_terms) | copy-start | bytes 196612
  17.8 0.6 %copy-start.5 = (f32[4,16,128]{2,1,0:T(8,128)}, f32[4,16,128]{2,1,0:T(8,128)S(1)}, u32[]{:S(2)}) copy-start(f32[4,16,128]{2,1,0:T(8,128)S(1)} %get-tuple-element.29.refs_4_) | copy-start | bytes 98308
  18.4 1.2 %copy-start.4 = (f32[72,128]{1,0:T(8,128)}, f32[72,128]{1,0:T(8,128)S(1)}, u32[]{:S(2)}) copy-start(f32[72,128]{1,0:T(8,128)S(1)} %get-tuple-element.24.mine) | copy-start | bytes 110596
  18.4 1.2 %collective-permute-start.7 = (f32[72,128]{1,0:T(8,128)S(1)}, f32[72,128]{1,0:T(8,128)S(1)}, u32[]{:S(2)}, u32[]{:S(2)}) collective-permute-start(f32[72,128]{1,0:T(8,128)S(1)} %get-tuple-element.24.mine), channel_id=1, source_target_pairs={{0,4},{4,0},{8,12},{12,8},{16,20},{20,16},{24,28},{28,24},{1,5},{5... | collective-permute-start | bytes 110600 | tf_op jit(solution)/shard_map/return_products/ppermute | solution.py:29
  19.6 0.6 %copy-start.10 = (f32[72,128]{1,0:T(8,128)}, f32[72,128]{1,0:T(8,128)S(1)}, u32[]{:S(2)}) copy-start(f32[72,128]{1,0:T(8,128)S(1)} %collective-permute-done.7.other) | copy-start | bytes 110596
  21.7 3.9 %collective-permute-start.8 = (f32[24,128]{1,0:T(8,128)}, f32[24,128]{1,0:T(8,128)S(1)}, u32[]{:S(2)}, u32[]{:S(2)}) collective-permute-start(f32[24,128]{1,0:T(8,128)} %get-tuple-element.26), channel_id=1, source_target_pairs={{0,8},{4,12},{8,0},{12,4},{16,24},{20,28},{24,16},{28,20},{1,9},{5... | collective-permute-start | bytes 36872 | tf_op jit(solution)/shard_map/return_products/ppermute | solution.py:29
  23.4 3.9 %collective-permute-start.9 = (f32[24,128]{1,0:T(8,128)}, f32[24,128]{1,0:T(8,128)S(1)}, u32[]{:S(2)}, u32[]{:S(2)}) collective-permute-start(f32[24,128]{1,0:T(8,128)} %get-tuple-element.27), channel_id=1, source_target_pairs={{0,16},{4,20},{8,24},{12,28},{16,0},{20,4},{24,8},{28,12},{1,17},{... | collective-permute-start | bytes 36872 | tf_op jit(solution)/shard_map/return_products/ppermute | solution.py:29
  24.9 4.8 %collective-permute-start.10 = (f32[24,128]{1,0:T(8,128)}, f32[24,128]{1,0:T(8,128)S(1)}, u32[]{:S(2)}, u32[]{:S(2)}) collective-permute-start(f32[24,128]{1,0:T(8,128)} %get-tuple-element.28), channel_id=1, source_target_pairs={{0,24},{4,28},{8,16},{12,20},{16,8},{20,12},{24,0},{28,4},{1,25},{... | collective-permute-start | bytes 36872 | tf_op jit(solution)/shard_map/return_products/ppermute | solution.py:29
  25.6 4.1 %copy-start.11 = (f32[24,128]{1,0:T(8,128)}, f32[24,128]{1,0:T(8,128)S(1)}, u32[]{:S(2)}) copy-start(f32[24,128]{1,0:T(8,128)S(1)} %collective-permute-done.8.refs_1_) | copy-start | bytes 36868
  27.3 2.4 %copy-start.12 = (f32[24,128]{1,0:T(8,128)}, f32[24,128]{1,0:T(8,128)S(1)}, u32[]{:S(2)}) copy-start(f32[24,128]{1,0:T(8,128)S(1)} %collective-permute-done.9.refs_2_) | copy-start | bytes 36868
  29.7 0.6 %copy-start.13 = (f32[24,128]{1,0:T(8,128)}, f32[24,128]{1,0:T(8,128)S(1)}, u32[]{:S(2)}) copy-start(f32[24,128]{1,0:T(8,128)S(1)} %collective-permute-done.10.refs_3_) | copy-start | bytes 36868
  31.8 4.4 %collective-permute-start.11 = (f32[24,128]{1,0:T(8,128)}, f32[24,128]{1,0:T(8,128)S(1)}, u32[]{:S(2)}, u32[]{:S(2)}) collective-permute-start(f32[24,128]{1,0:T(8,128)} %get-tuple-element.31), channel_id=1, source_target_pairs={{0,1},{1,0},{2,3},{3,2},{4,5},{5,4},{6,7},{7,6},{8,9},{9,8},{10,11... | collective-permute-start | bytes 36872 | tf_op jit(solution)/shard_map/return_products/ppermute | solution.py:29
  33.0 4.8 %collective-permute-start.12 = (f32[24,128]{1,0:T(8,128)}, f32[24,128]{1,0:T(8,128)S(1)}, u32[]{:S(2)}, u32[]{:S(2)}) collective-permute-start(f32[24,128]{1,0:T(8,128)} %get-tuple-element.32), channel_id=1, source_target_pairs={{0,2},{1,3},{2,0},{3,1},{4,6},{5,7},{6,4},{7,5},{8,10},{9,11},{10,... | collective-permute-start | bytes 36872 | tf_op jit(solution)/shard_map/return_products/ppermute | solution.py:29
  35.9 5.7 %collective-permute-start.13 = (f32[24,128]{1,0:T(8,128)}, f32[24,128]{1,0:T(8,128)S(1)}, u32[]{:S(2)}, u32[]{:S(2)}) collective-permute-start(f32[24,128]{1,0:T(8,128)} %get-tuple-element.33), channel_id=1, source_target_pairs={{0,3},{1,2},{2,1},{3,0},{4,7},{5,6},{6,5},{7,4},{8,11},{9,10},{10,... | collective-permute-start | bytes 36872 | tf_op jit(solution)/shard_map/return_products/ppermute | solution.py:29
  41.6 0.7 %copy-start.6 = (f32[24,128]{1,0:T(8,128)S(1)}, f32[24,128]{1,0:T(8,128)}, u32[]{:S(2)}) copy-start(f32[24,128]{1,0:T(8,128)} %get-tuple-element.30.refs_0_) | copy-start | bytes 36868

commit v8 on v7

--- a/solution.py
+++ b/solution.py
@@ -80,49 +80,48 @@
     out[1] = other[...]
 
 
-def column_kernel(n_row, n_col, slots, place, arow, bcol, count, d_ref, *refs):
-    x_rows, (tiles, out, *parts, rows, sums) = refs[:n_col], refs[n_col:]
+def products_kernel(n_row, n_col, slots, place, arow, bcol, count, d_ref, *refs):
+    x_rows, refs = refs[:n_col], refs[n_col:]
+    x_pairs, refs = refs[: n_row // 2], refs[n_row // 2 :]
+    tiles, row_out, col_out, to_core, rows, cols, row_sums, col_sums, held, sems = refs
+    nvec, width = x_rows[0].shape
     me_row, me_col = place[0], place[1]
+    copies = [pltpu.make_async_copy(tiles.at[0, 0, slot], held.at[slot], sems.at[slot]) for slot in range(slots)]
+    for copy in copies:
+        copy.start()
     for flip in range(n_col):
         rows[flip] = stack_split(x_rows[flip][...])
-    sums[...] = jnp.zeros_like(sums)
-    sums[0] = 0.5 * d_ref[...] * x_rows[0][...]
-    for slot in range(slots):
-        pieces = split(tiles[0, 0, slot])
-        for part, piece in zip(parts, pieces):
-            part[slot] = piece
-        block = jnp.where(slot < count[0, 0], bcol[0, 0, slot] ^ me_row, n_row)
-        sums[block] += parts_product(rows[arow[0, 0, slot] ^ me_col], pieces, (((1,), (0,)), ((), ())))
-    out[...] = sums[:n_row]
-
-
-def row_kernel(n_row, n_col, slots, place, arow, bcol, count, d_ref, *refs):
-    x_rows, refs = refs[:n_col], refs[n_col:]
-    x_pairs, (col_terms, *parts, out, to_core, cols, sums) = refs[: n_row // 2], refs[n_row // 2 :]
-    nvec, width = x_rows[0].shape
-    me_row, me_col = place[0], place[1]
     for flip in range(n_row):
         cols[flip] = stack_split(x_pairs[flip // 2][flip % 2])
-    sums[...] = jnp.zeros_like(sums)
-    sums[0] = 0.5 * d_ref[...] * x_rows[0][...]
+    half = 0.5 * d_ref[...] * x_rows[0][...]
+    row_sums[...] = jnp.zeros_like(row_sums)
+    col_sums[...] = jnp.zeros_like(col_sums)
+    row_sums[0] = half
+    col_sums[0] = half
     for slot in range(slots):
-        block = jnp.where(slot < count[0, 0], arow[0, 0, slot] ^ me_col, n_col)
-        pieces = [part[slot] for part in parts]
-        sums[block] += parts_product(cols[bcol[0, 0, slot] ^ me_row], pieces, (((1,), (1,)), ((), ())))
-    out[...] = sums[:n_col]
+        live = slot < count[0, 0]
+        i = arow[0, 0, slot] ^ me_col
+        j = bcol[0, 0, slot] ^ me_row
+        copies[slot].wait()
+        pieces = split(held[slot])
+        row_sums[jnp.where(live, i, n_col)] += parts_product(cols[j], pieces, (((1,), (1,)), ((), ())))
+        col_sums[jnp.where(live, j, n_row)] += parts_product(rows[i], pieces, (((1,), (0,)), ((), ())))
+    total = packed_gram(x_rows[0][...], row_sums[0])
+    for flip in range(1, n_col):
+        total += packed_gram(x_rows[flip][...], row_sums[flip])
+    row_out[...] = row_sums[:n_col]
     for chip in range(n_row // 2):
-        to_core[chip * nvec : (chip + 1) * nvec] = col_terms[2 * chip + 1]
-    total = packed_gram(x_rows[0][...], sums[0])
-    for flip in range(1, n_col):
-        total += packed_gram(x_rows[flip][...], sums[flip])
-    to_core[n_row // 2 * nvec :] = jnp.concatenate([total, jnp.zeros((to_core.shape[0] - n_row // 2 * nvec - total.shape[0], width), jnp.float32)], axis=0)
+        col_out[chip] = col_sums[2 * chip]
+        to_core[chip * nvec : (chip + 1) * nvec] = col_sums[2 * chip + 1]
+    rest = jnp.zeros((to_core.shape[0] - n_row // 2 * nvec - total.shape[0], width), jnp.float32)
+    to_core[n_row // 2 * nvec :] = jnp.concatenate([total, rest], axis=0)
 
 
 def chip_kernel(col_terms, mine, other, *outs):
     nvec = col_terms.shape[1]
     tail = len(outs) * nvec
     for chip, out in enumerate(outs):
-        out[:nvec] = col_terms[2 * chip] + other[chip * nvec : (chip + 1) * nvec]
+        out[:nvec] = col_terms[chip] + other[chip * nvec : (chip + 1) * nvec]
         out[nvec:] = mine[tail:] + other[tail:]
 
 
@@ -173,11 +172,9 @@
     block = jax.ShapeDtypeStruct((nvec, width), jnp.float32)
     joined = jax.ShapeDtypeStruct((padded, width), jnp.float32)
     square = jax.ShapeDtypeStruct((nvec, nvec), jnp.float32)
-    part = jax.ShapeDtypeStruct((slots, width, width), jnp.bfloat16)
     place = jnp.stack([lax.axis_index("row"), lax.axis_index("col")]).astype(jnp.int32)
     energy = diagonal_energy.reshape(1, width)
-    params = pltpu.CompilerParams(vmem_limit_bytes=24 * 2**20)
-    cost = pl.CostEstimate(flops=12 * slots * nvec * width * width, bytes_accessed=2**20, transcendentals=0)
+    params = pltpu.CompilerParams(vmem_limit_bytes=16 * 2**20)
     with jax.named_scope("share_vectors"):
         other = trade(vectors, "row", 1)
         x_rows = [vectors] + [trade(vectors, "col", flip) for flip in range(1, n_col)]
@@ -186,43 +183,40 @@
             out_shape=jax.ShapeDtypeStruct((2, nvec, width), jnp.float32),
             in_specs=[VMEM] * 2,
             out_specs=VMEM,
+            compiler_params=params,
             name="pair",
         )(vectors, other)
         x_pairs = [pair] + [trade(pair, "row", 2 * chip) for chip in range(1, n_chip)]
-    with jax.named_scope("column_terms"):
-        col_terms, *parts = pl.pallas_call(
-            functools.partial(column_kernel, n_row, n_col, slots),
-            out_shape=[jax.ShapeDtypeStruct((n_row, nvec, width), jnp.float32), part, part, part],
-            in_specs=[SMEM] * 4 + [VMEM] * (n_col + 2),
-            out_specs=[VMEM] * 4,
+    with jax.named_scope("tile_products"):
+        row_terms, col_terms, to_core = pl.pallas_call(
+            functools.partial(products_kernel, n_row, n_col, slots),
+            out_shape=[
+                jax.ShapeDtypeStruct((n_col, nvec, width), jnp.float32),
+                jax.ShapeDtypeStruct((n_chip, nvec, width), jnp.float32),
+                jax.ShapeDtypeStruct((n_chip * nvec + padded - nvec, width), jnp.float32),
+            ],
+            in_specs=[SMEM] * 4 + [VMEM] * (1 + n_col + n_chip) + [pl.BlockSpec(memory_space=pl.ANY)],
+            out_specs=[VMEM] * 3,
             scratch_shapes=[
                 pltpu.VMEM((n_col, 3 * nvec, width), jnp.bfloat16),
-                pltpu.VMEM((n_row + 1, nvec, width), jnp.float32),
-            ],
-            compiler_params=params,
-            cost_estimate=cost,
-            name="column_terms",
-        )(place, tile_rows, tile_cols, tile_count, energy, *x_rows, tiles)
-    with jax.named_scope("row_terms"):
-        row_terms, to_core = pl.pallas_call(
-            functools.partial(row_kernel, n_row, n_col, slots),
-            out_shape=[
-                jax.ShapeDtypeStruct((n_col, nvec, width), jnp.float32),
-                jax.ShapeDtypeStruct((n_chip * nvec + padded - nvec, width), jnp.float32),
-            ],
-            in_specs=[SMEM] * 4 + [VMEM] * (1 + n_col + n_chip + 4),
-            out_specs=[VMEM] * 2,
-            scratch_shapes=[
                 pltpu.VMEM((n_row, 3 * nvec, width), jnp.bfloat16),
                 pltpu.VMEM((n_col + 1, nvec, width), jnp.float32),
+                pltpu.VMEM((n_row + 1, nvec, width), jnp.float32),
+                pltpu.VMEM((slots, width, width), jnp.float32),
+                pltpu.SemaphoreType.DMA((slots,)),
             ],
-            compiler_params=params,
-            cost_estimate=cost,
-            name="row_terms",
-        )(place, tile_rows, tile_cols, tile_count, energy, *x_rows, *x_pairs, col_terms, *parts)
+            compiler_params=pltpu.CompilerParams(vmem_limit_bytes=53 * 2**20),
+            cost_estimate=pl.CostEstimate(flops=24 * slots * nvec * width * width, bytes_accessed=2**20, transcendentals=0),
+            name="tile_products",
+        )(place, tile_rows, tile_cols, tile_count, energy, *x_rows, *x_pairs, tiles)
     with jax.named_scope("return_products"):
         chips = pl.pallas_call(
-            chip_kernel, out_shape=[joined] * n_chip, in_specs=[VMEM] * 3, out_specs=[VMEM] * n_chip, name="chip_sum"
+            chip_kernel,
+            out_shape=[joined] * n_chip,
+            in_specs=[VMEM] * 3,
+            out_specs=[VMEM] * n_chip,
+            compiler_params=params,
+            name="chip_sum",
         )(col_terms, to_core, trade(to_core, "row", 1))
         by_row = [chips[0]] + [trade(chips[chip], "row", 2 * chip) for chip in range(1, n_chip)]
         sends = pl.pallas_call(
@@ -230,6 +224,7 @@
             out_shape=[joined] * n_col,
             in_specs=[VMEM] * (n_chip + 1),
             out_specs=[VMEM] * n_col,
+            compiler_params=params,
             name="row_sum",
         )(*by_row, row_terms)
         sums = [sends[0]] + [trade(sends[flip], "col", flip) for flip in range(1, n_col)]
@@ -244,7 +239,12 @@
         )(vectors, *sums)
     with jax.named_scope("gram_sum"):
         gram = pl.pallas_call(
-            functools.partial(gram_kernel, scale), out_shape=square, in_specs=[VMEM], out_specs=VMEM, name="gram_sum"
+            functools.partial(gram_kernel, scale),
+            out_shape=square,
+            in_specs=[VMEM],
+            out_specs=VMEM,
+            compiler_params=params,
+            name="gram_sum",
         )(swap(grams, ("row", "col")))
     return (residual, rayleigh, gram)
 

time: 55 us -> 47.6 us (0.87)
  local copies, waits for them, and re-layouts: 4.97 us -> 0.02 us
  Pallas kernels: 10.1 us -> 7.38 us
  waiting for transfers between devices: 11.2 us -> 12.2 us
  blocking collectives: 9.65 us -> 8.97 us
    unnamed x30 -> x8, local copies, waits for them, and re-layouts: 4.97 us -> 0.02 us
    pallas_call x2 -> x1, Pallas kernels: 3.22 us -> 5.55 us  [per_device(): pl.pallas_call(functools.partial(products_kernel, n_row, n_col, slots), o...]
    pallas_call x1, Pallas kernels: 1.49 us -> 0.01 us  [per_device(): pl.pallas_call(chip_kernel, out_shape=[joined] * n_chip, in_specs=[VMEM]...]
    pallas_call x1, Pallas kernels: 1.46 us -> 0.01 us  [per_device(): pl.pallas_call(functools.partial(join_kernel, n_chip), out_shape=[joined]...]
    pallas_call x1, Pallas kernels: 1.32 us -> 0.01 us  [per_device(): pl.pallas_call(pair_kernel, out_shape=jax.ShapeDtypeStruct((2, nvec, widt...]
    ppermute x14, waiting for transfers between devices: 11.2 us -> 12.2 us  [trade(): return lax.ppermute(value, axis, [(p, p ^ flip) for p in range(size)])]
    pallas_call x1, Pallas kernels: 1.55 us -> 0.8 us  [per_device(): pl.pallas_call(functools.partial(gram_kernel, scale), out_shape=square, i...]
    all_to_all x1, blocking collectives: 9.65 us -> 8.97 us  [swap(): return lax.all_to_all(blocks, axis, 0, 0, tiled=True)]
  transfers between devices with their start and end apart: 14 -> 14, of which waited for: 6 -> 9; matrix products, arithmetic and copies ran while one was open for 0% -> 0% of each run, Pallas kernels for 4% -> 0%
where the time goes in v8:
time: 47.6 us; the launch traced here: 47.4 us
  starting transfers between devices  17.4 us (37%)
  waiting for transfers between devices  12.2 us (26%)
  blocking collectives  8.97 us (19%)
  Pallas kernels  7.38 us (16%)
  between operations  1.37 us (3%)
    ppermute x14, starting transfers between devices, trade(): return lax.ppermute(value, axis, [(p, p ^ flip) for p in range(size)])  17.4 us
    ppermute x14, waiting for transfers between devices, trade(): return lax.ppermute(value, axis, [(p, p ^ flip) for p in range(size)])  12.2 us
    all_to_all x1, blocking collectives, swap(): return lax.all_to_all(blocks, axis, 0, 0, tiled=True)  8.97 us
    pallas_call x1, Pallas kernels, per_device(): pl.pallas_call(functools.partial(products_kernel, n_row, n_col, slots), o...  5.55 us
    pallas_call x1, Pallas kernels, per_device(): pl.pallas_call(functools.partial(residual_kernel, scale), out_shape=[bloc...  1.01 us
  transfers between devices with their start and end apart: 14, of which 9 were waited for; matrix products, arithmetic and copies ran while one was open for 0% of the time, Pallas kernels for 0%

profile of v8, /device:TPU:0, one launch (start us, length us, event | category | flops | bytes accessed | tf_op | source)
XLA Modules:
  0.0 47.4 jit_solution(4233738841555698939)
XLA Ops:
  0.6 0.0 copy-start
  0.6 0.5 %collective-permute-start.3 = (f32[16,128]{1,0:T(8,128)}, f32[16,128]{1,0:T(8,128)S(1)}, u32[]{:S(2)}, u32[]{:S(2)}) collective-permute-start(f32[16,128]{1,0:T(8,128)} %x_ref.3), channel_id=1, source_target_pairs={{0,4},{4,0},{8,12},{12,8},{16,20},{20,16},{24,28},{28,24},{1,5},{5... | collective-permute-start | bytes 24584 | tf_op jit(solution)/shard_map/share_vectors/ppermute | solution.py:29
  1.2 4.7 %collective-permute-start.2 = (f32[16,128]{1,0:T(8,128)}, f32[16,128]{1,0:T(8,128)S(1)}, u32[]{:S(2)}, u32[]{:S(2)}) collective-permute-start(f32[16,128]{1,0:T(8,128)} %x_ref.3), channel_id=1, source_target_pairs={{0,3},{1,2},{2,1},{3,0},{4,7},{5,6},{6,5},{7,4},{8,11},{9,10},{10,... | collective-permute-start | bytes 24584 | tf_op jit(solution)/shard_map/share_vectors/ppermute | solution.py:29
  5.8 0.0 collective-permute-start.1
  5.8 0.7 %collective-permute-start = (f32[16,128]{1,0:T(8,128)}, f32[16,128]{1,0:T(8,128)S(1)}, u32[]{:S(2)}, u32[]{:S(2)}) collective-permute-start(f32[16,128]{1,0:T(8,128)} %x_ref.3), channel_id=1, source_target_pairs={{0,1},{1,0},{2,3},{3,2},{4,5},{5,4},{6,7},{7,6},{8,9},{9,8},{10,11... | collective-permute-start | bytes 24584 | tf_op jit(solution)/shard_map/share_vectors/ppermute | solution.py:29
  6.5 0.0 collective-permute-done.3.other
  6.5 0.0 copy-done
  6.5 2.6 %collective-permute-start.6 = (f32[2,16,128]{2,1,0:T(8,128)S(1)}, f32[2,16,128]{2,1,0:T(8,128)S(1)}, u32[]{:S(2)}, u32[]{:S(2)}) collective-permute-start(f32[2,16,128]{2,1,0:T(8,128)S(1)} %pair.1.refs_4_), channel_id=1, source_target_pairs={{0,24},{4,28},{8,16},{12,20},{16,8},{20,12},{24,0},{28,4},{1,25},{... | collective-permute-start | bytes 49160 | tf_op jit(solution)/shard_map/share_vectors/ppermute | solution.py:29
  9.1 0.5 %collective-permute-start.5 = (f32[2,16,128]{2,1,0:T(8,128)S(1)}, f32[2,16,128]{2,1,0:T(8,128)S(1)}, u32[]{:S(2)}, u32[]{:S(2)}) collective-permute-start(f32[2,16,128]{2,1,0:T(8,128)S(1)} %pair.1.refs_4_), channel_id=1, source_target_pairs={{0,16},{4,20},{8,24},{12,28},{16,0},{20,4},{24,8},{28,12},{1,17},{... | collective-permute-start | bytes 49160 | tf_op jit(solution)/shard_map/share_vectors/ppermute | solution.py:29
  9.6 0.0 collective-permute-done.2.refs_3_
  9.7 0.4 collective-permute-start.4
  10.1 0.1 pad_add_fusion.place
  10.8 0.0 copy-start.1
  10.8 0.0 copy-start.2
  10.8 0.0 copy-start.3
  10.8 0.0 collective-permute-done.1.refs_2_
  10.8 0.0 collective-permute-done.refs_1_
  10.8 0.4 collective-permute-done.6.refs_7_
  11.2 1.7 %collective-permute-done.5.refs_6_ = f32[2,16,128]{2,1,0:T(8,128)S(1)} collective-permute-done((f32[2,16,128]{2,1,0:T(8,128)S(1)}, f32[2,16,128]{2,1,0:T(8,128)S(1)}, u32[]{:S(2)}, u32[]{:S(2)}) %collective-permute-start.5) | collective-permute-done | bytes 16416 | tf_op jit(solution)/shard_map/share_vectors/ppermute | solution.py:29
  12.9 0.5 %collective-permute-done.4.refs_5_ = f32[2,16,128]{2,1,0:T(8,128)S(1)} collective-permute-done((f32[2,16,128]{2,1,0:T(8,128)S(1)}, f32[2,16,128]{2,1,0:T(8,128)S(1)}, u32[]{:S(2)}, u32[]{:S(2)}) %collective-permute-start.4) | collective-permute-done | bytes 16416 | tf_op jit(solution)/shard_map/share_vectors/ppermute | solution.py:29
  13.4 0.0 copy-done.1
  13.4 0.0 copy-done.2
  13.4 0.0 copy-done.3
  13.4 5.5 %tile_products.1 = (f32[4,16,128]{2,1,0:T(8,128)S(1)}, f32[4,16,128]{2,1,0:T(8,128)S(1)}, f32[72,128]{1,0:T(8,128)S(1)}) custom-call(s32[2]{0:T(128)S(1)} %pad_add_fusion.place, s32[1,1,16]{2,1,0:T(1,128)S(1)} %copy-done.1, s32[1,1,16]{2,1,0:T(1,128)S(1)} %copy-done.2, s32[1,1]{1,0:T(1,128)S(6)} %copy.9.count, f32[1,128]{1,0:T(1,128)S(1)} %bitcast.3, ...), custom_call_target="tpu_custom_call" | custom-call | flops 100663296 | bytes 1048576 | tf_op jit(solution)/shard_map/tile_products/tile_products/pallas_call | solution.py:191
  19.0 0.1 collective-permute-start.7
  19.0 1.2 %collective-permute-done.7.other = f32[72,128]{1,0:T(8,128)S(1)} collective-permute-done((f32[72,128]{1,0:T(8,128)S(1)}, f32[72,128]{1,0:T(8,128)S(1)}, u32[]{:S(2)}, u32[]{:S(2)}) %collective-permute-start.7) | collective-permute-done | bytes 36896 | tf_op jit(solution)/shard_map/return_products/ppermute | solution.py:29
  20.2 0.4 collective-permute-start.8
  20.7 1.6 %collective-permute-start.9 = (f32[24,128]{1,0:T(8,128)S(1)}, f32[24,128]{1,0:T(8,128)S(1)}, u32[]{:S(2)}, u32[]{:S(2)}) collective-permute-start(f32[24,128]{1,0:T(8,128)S(1)} %get-tuple-element.21), channel_id=1, source_target_pairs={{0,16},{4,20},{8,24},{12,28},{16,0},{20,4},{24,8},{28,12},{1,17},{... | collective-permute-start | bytes 36872 | tf_op jit(solution)/shard_map/return_products/ppermute | solution.py:29
  22.3 1.4 %collective-permute-start.10 = (f32[24,128]{1,0:T(8,128)S(1)}, f32[24,128]{1,0:T(8,128)S(1)}, u32[]{:S(2)}, u32[]{:S(2)}) collective-permute-start(f32[24,128]{1,0:T(8,128)S(1)} %get-tuple-element.22), channel_id=1, source_target_pairs={{0,24},{4,28},{8,16},{12,20},{16,8},{20,12},{24,0},{28,4},{1,25},{... | collective-permute-start | bytes 36872 | tf_op jit(solution)/shard_map/return_products/ppermute | solution.py:29
  23.7 0.2 collective-permute-done.8.refs_1_
  23.9 0.4 collective-permute-done.9.refs_2_
  24.3 2.5 %collective-permute-done.10.refs_3_ = f32[24,128]{1,0:T(8,128)S(1)} collective-permute-done((f32[24,128]{1,0:T(8,128)S(1)}, f32[24,128]{1,0:T(8,128)S(1)}, u32[]{:S(2)}, u32[]{:S(2)}) %collective-permute-start.10) | collective-permute-done | bytes 12320 | tf_op jit(solution)/shard_map/return_products/ppermute | solution.py:29
  26.9 1.3 %collective-permute-start.11 = (f32[24,128]{1,0:T(8,128)S(1)}, f32[24,128]{1,0:T(8,128)S(1)}, u32[]{:S(2)}, u32[]{:S(2)}) collective-permute-start(f32[24,128]{1,0:T(8,128)S(1)} %get-tuple-element.25), channel_id=1, source_target_pairs={{0,1},{1,0},{2,3},{3,2},{4,5},{5,4},{6,7},{7,6},{8,9},{9,8},{10,11... | collective-permute-start | bytes 36872 | tf_op jit(solution)/shard_map/return_products/ppermute | solution.py:29
  28.2 2.9 %collective-permute-start.12 = (f32[24,128]{1,0:T(8,128)S(1)}, f32[24,128]{1,0:T(8,128)S(1)}, u32[]{:S(2)}, u32[]{:S(2)}) collective-permute-start(f32[24,128]{1,0:T(8,128)S(1)} %get-tuple-element.26), channel_id=1, source_target_pairs={{0,2},{1,3},{2,0},{3,1},{4,6},{5,7},{6,4},{7,5},{8,10},{9,11},{10,... | collective-permute-start | bytes 36872 | tf_op jit(solution)/shard_map/return_products/ppermute | solution.py:29
  31.1 0.2 collective-permute-start.13
  31.4 0.0 collective-permute-done.11.refs_1_
  31.4 1.4 %collective-permute-done.12.refs_2_ = f32[24,128]{1,0:T(8,128)S(1)} collective-permute-done((f32[24,128]{1,0:T(8,128)S(1)}, f32[24,128]{1,0:T(8,128)S(1)}, u32[]{:S(2)}, u32[]{:S(2)}) %collective-permute-start.12) | collective-permute-done | bytes 12320 | tf_op jit(solution)/shard_map/return_products/ppermute | solution.py:29
  32.8 3.8 %collective-permute-done.13.refs_3_ = f32[24,128]{1,0:T(8,128)S(1)} collective-permute-done((f32[24,128]{1,0:T(8,128)S(1)}, f32[24,128]{1,0:T(8,128)S(1)}, u32[]{:S(2)}, u32[]{:S(2)}) %collective-permute-start.13) | collective-permute-done | bytes 12320 | tf_op jit(solution)/shard_map/return_products/ppermute | solution.py:29
  36.6 1.0 %residual.1 = (f32[16,128]{1,0:T(8,128)}, f32[16,16]{1,0:T(8,128)}, f32[32,2,128]{2,1,0:T(2,128)S(1)}) custom-call(f32[16,128]{1,0:T(8,128)S(1)} %copy-done, f32[24,128]{1,0:T(8,128)S(1)} %get-tuple-element.24.refs_0_, f32[24,128]{1,0:T(8,128)S(1)} %collective-permute-done.11.refs_1_, f32[24,128]{1,0:T(8,128)S(1)} %collective-permute-done.12.refs_2_, ...), custom_call_target="tpu_custom_call" | custom-call | tf_op jit(solution)/shard_map/residual/residual/pallas_call | solution.py:232
  37.6 9.0 %all_to_all.5.parts = f32[32,2,128]{2,1,0:T(2,128)S(1)} all-to-all(f32[32,2,128]{2,1,0:T(2,128)S(1)} %get-tuple-element.30), channel_id=1, replica_groups=mesh['row'=8,'col'=4] {'row','col'}, dimensions={0} | all-to-all | bytes 65536 | tf_op jit(solution)/shard_map/gram_sum/all_to_all | solution.py:24
  46.6 0.8 %gram_sum.1 = f32[16,16]{1,0:T(8,128)} custom-call(f32[32,2,128]{2,1,0:T(2,128)S(1)} %all_to_all.5.parts), custom_call_target="tpu_custom_call" | custom-call | tf_op jit(solution)/shard_map/gram_sum/gram_sum/pallas_call | solution.py:241
  (3 shorter events, 0.0 us)
Async XLA Ops:
  0.6 5.9 %copy-start = (f32[16,128]{1,0:T(8,128)S(1)}, f32[16,128]{1,0:T(8,128)}, u32[]{:S(2)}) copy-start(f32[16,128]{1,0:T(8,128)} %x_ref.3) | copy-start | bytes 24580
  0.6 5.9 %collective-permute-start.3 = (f32[16,128]{1,0:T(8,128)}, f32[16,128]{1,0:T(8,128)S(1)}, u32[]{:S(2)}, u32[]{:S(2)}) collective-permute-start(f32[16,128]{1,0:T(8,128)} %x_ref.3), channel_id=1, source_target_pairs={{0,4},{4,0},{8,12},{12,8},{16,20},{20,16},{24,28},{28,24},{1,5},{5... | collective-permute-start | bytes 24584 | tf_op jit(solution)/shard_map/share_vectors/ppermute | solution.py:29
  1.2 8.5 %collective-permute-start.2 = (f32[16,128]{1,0:T(8,128)}, f32[16,128]{1,0:T(8,128)S(1)}, u32[]{:S(2)}, u32[]{:S(2)}) collective-permute-start(f32[16,128]{1,0:T(8,128)} %x_ref.3), channel_id=1, source_target_pairs={{0,3},{1,2},{2,1},{3,0},{4,7},{5,6},{6,5},{7,4},{8,11},{9,10},{10,... | collective-permute-start | bytes 24584 | tf_op jit(solution)/shard_map/share_vectors/ppermute | solution.py:29
  5.8 5.0 %collective-permute-start.1 = (f32[16,128]{1,0:T(8,128)}, f32[16,128]{1,0:T(8,128)S(1)}, u32[]{:S(2)}, u32[]{:S(2)}) collective-permute-start(f32[16,128]{1,0:T(8,128)} %x_ref.3), channel_id=1, source_target_pairs={{0,2},{1,3},{2,0},{3,1},{4,6},{5,7},{6,4},{7,5},{8,10},{9,11},{10,... | collective-permute-start | bytes 24584 | tf_op jit(solution)/shard_map/share_vectors/ppermute | solution.py:29
  5.8 5.0 %collective-permute-start = (f32[16,128]{1,0:T(8,128)}, f32[16,128]{1,0:T(8,128)S(1)}, u32[]{:S(2)}, u32[]{:S(2)}) collective-permute-start(f32[16,128]{1,0:T(8,128)} %x_ref.3), channel_id=1, source_target_pairs={{0,1},{1,0},{2,3},{3,2},{4,5},{5,4},{6,7},{7,6},{8,9},{9,8},{10,11... | collective-permute-start | bytes 24584 | tf_op jit(solution)/shard_map/share_vectors/ppermute | solution.py:29
  6.5 4.7 %collective-permute-start.6 = (f32[2,16,128]{2,1,0:T(8,128)S(1)}, f32[2,16,128]{2,1,0:T(8,128)S(1)}, u32[]{:S(2)}, u32[]{:S(2)}) collective-permute-start(f32[2,16,128]{2,1,0:T(8,128)S(1)} %pair.1.refs_4_), channel_id=1, source_target_pairs={{0,24},{4,28},{8,16},{12,20},{16,8},{20,12},{24,0},{28,4},{1,25},{... | collective-permute-start | bytes 49160 | tf_op jit(solution)/shard_map/share_vectors/ppermute | solution.py:29
  9.1 3.7 %collective-permute-start.5 = (f32[2,16,128]{2,1,0:T(8,128)S(1)}, f32[2,16,128]{2,1,0:T(8,128)S(1)}, u32[]{:S(2)}, u32[]{:S(2)}) collective-permute-start(f32[2,16,128]{2,1,0:T(8,128)S(1)} %pair.1.refs_4_), channel_id=1, source_target_pairs={{0,16},{4,20},{8,24},{12,28},{16,0},{20,4},{24,8},{28,12},{1,17},{... | collective-permute-start | bytes 49160 | tf_op jit(solution)/shard_map/share_vectors/ppermute | solution.py:29
  9.7 3.7 %collective-permute-start.4 = (f32[2,16,128]{2,1,0:T(8,128)S(1)}, f32[2,16,128]{2,1,0:T(8,128)S(1)}, u32[]{:S(2)}, u32[]{:S(2)}) collective-permute-start(f32[2,16,128]{2,1,0:T(8,128)S(1)} %pair.1.refs_4_), channel_id=1, source_target_pairs={{0,8},{4,12},{8,0},{12,4},{16,24},{20,28},{24,16},{28,20},{1,9},{5... | collective-permute-start | bytes 49160 | tf_op jit(solution)/shard_map/share_vectors/ppermute | solution.py:29
  10.8 2.6 %copy-start.1 = (s32[1,1,16]{2,1,0:T(1,128)S(1)}, s32[1,1,16]{2,1,0:T(1,128)}, u32[]{:S(2)}) copy-start(s32[1,1,16]{2,1,0:T(1,128)} %arow.1) | copy-start | bytes 196
  10.8 2.6 %copy-start.2 = (s32[1,1,16]{2,1,0:T(1,128)S(1)}, s32[1,1,16]{2,1,0:T(1,128)}, u32[]{:S(2)}) copy-start(s32[1,1,16]{2,1,0:T(1,128)} %bcol.1) | copy-start | bytes 196
  10.8 2.6 %copy-start.3 = (f32[128]{0:T(128)S(1)}, f32[128]{0:T(128)}, u32[]{:S(2)}) copy-start(f32[128]{0:T(128)} %param.7) | copy-start | bytes 1540
  19.0 1.3 %collective-permute-start.7 = (f32[72,128]{1,0:T(8,128)S(1)}, f32[72,128]{1,0:T(8,128)S(1)}, u32[]{:S(2)}, u32[]{:S(2)}) collective-permute-start(f32[72,128]{1,0:T(8,128)S(1)} %get-tuple-element.18.mine), channel_id=1, source_target_pairs={{0,4},{4,0},{8,12},{12,8},{16,20},{20,16},{24,28},{28,24},{1,5},{5... | collective-permute-start | bytes 110600 | tf_op jit(solution)/shard_map/return_products/ppermute | solution.py:29
  20.2 3.7 %collective-permute-start.8 = (f32[24,128]{1,0:T(8,128)S(1)}, f32[24,128]{1,0:T(8,128)S(1)}, u32[]{:S(2)}, u32[]{:S(2)}) collective-permute-start(f32[24,128]{1,0:T(8,128)S(1)} %get-tuple-element.20), channel_id=1, source_target_pairs={{0,8},{4,12},{8,0},{12,4},{16,24},{20,28},{24,16},{28,20},{1,9},{5... | collective-permute-start | bytes 36872 | tf_op jit(solution)/shard_map/return_products/ppermute | solution.py:29
  20.7 3.7 %collective-permute-start.9 = (f32[24,128]{1,0:T(8,128)S(1)}, f32[24,128]{1,0:T(8,128)S(1)}, u32[]{:S(2)}, u32[]{:S(2)}) collective-permute-start(f32[24,128]{1,0:T(8,128)S(1)} %get-tuple-element.21), channel_id=1, source_target_pairs={{0,16},{4,20},{8,24},{12,28},{16,0},{20,4},{24,8},{28,12},{1,17},{... | collective-permute-start | bytes 36872 | tf_op jit(solution)/shard_map/return_products/ppermute | solution.py:29
  22.3 4.6 %collective-permute-start.10 = (f32[24,128]{1,0:T(8,128)S(1)}, f32[24,128]{1,0:T(8,128)S(1)}, u32[]{:S(2)}, u32[]{:S(2)}) collective-permute-start(f32[24,128]{1,0:T(8,128)S(1)} %get-tuple-element.22), channel_id=1, source_target_pairs={{0,24},{4,28},{8,16},{12,20},{16,8},{20,12},{24,0},{28,4},{1,25},{... | collective-permute-start | bytes 36872 | tf_op jit(solution)/shard_map/return_products/ppermute | solution.py:29
  26.9 4.5 %collective-permute-start.11 = (f32[24,128]{1,0:T(8,128)S(1)}, f32[24,128]{1,0:T(8,128)S(1)}, u32[]{:S(2)}, u32[]{:S(2)}) collective-permute-start(f32[24,128]{1,0:T(8,128)S(1)} %get-tuple-element.25), channel_id=1, source_target_pairs={{0,1},{1,0},{2,3},{3,2},{4,5},{5,4},{6,7},{7,6},{8,9},{9,8},{10,11... | collective-permute-start | bytes 36872 | tf_op jit(solution)/shard_map/return_products/ppermute | solution.py:29
  28.2 4.6 %collective-permute-start.12 = (f32[24,128]{1,0:T(8,128)S(1)}, f32[24,128]{1,0:T(8,128)S(1)}, u32[]{:S(2)}, u32[]{:S(2)}) collective-permute-start(f32[24,128]{1,0:T(8,128)S(1)} %get-tuple-element.26), channel_id=1, source_target_pairs={{0,2},{1,3},{2,0},{3,1},{4,6},{5,7},{6,4},{7,5},{8,10},{9,11},{10,... | collective-permute-start | bytes 36872 | tf_op jit(solution)/shard_map/return_products/ppermute | solution.py:29
  31.1 5.5 %collective-permute-start.13 = (f32[24,128]{1,0:T(8,128)S(1)}, f32[24,128]{1,0:T(8,128)S(1)}, u32[]{:S(2)}, u32[]{:S(2)}) collective-permute-start(f32[24,128]{1,0:T(8,128)S(1)} %get-tuple-element.27), channel_id=1, source_target_pairs={{0,3},{1,2},{2,1},{3,0},{4,7},{5,6},{6,5},{7,4},{8,11},{9,10},{10,... | collective-permute-start | bytes 36872 | tf_op jit(solution)/shard_map/return_products/ppermute | solution.py:29

commit v9 on v8

--- a/solution.py
+++ b/solution.py
@@ -10,6 +10,7 @@
 HP = lax.Precision.HIGHEST
 VMEM = pl.BlockSpec(memory_space=pltpu.VMEM)
 SMEM = pl.BlockSpec(memory_space=pltpu.SMEM)
+CHUNKS = 4
 
 
 def mult(left, right):
@@ -36,9 +37,10 @@
 
 
 def packed_gram(left, right):
-    nvec, width = left.shape
+    nvec, width = left[0].shape
     per = width // nvec
-    wide = mult_last(left, jnp.concatenate([right] * per, axis=0))
+    right = jnp.concatenate(right, axis=1)
+    wide = mult_last(jnp.concatenate(left, axis=1), jnp.concatenate([right] * per, axis=0))
     wide = jnp.where(own_lanes(nvec, width), wide, 0.0)
     return jnp.sum(wide.reshape(nvec // per, per, width), axis=1)
 
@@ -86,7 +88,11 @@
     tiles, row_out, col_out, to_core, rows, cols, row_sums, col_sums, held, sems = refs
     nvec, width = x_rows[0].shape
     me_row, me_col = place[0], place[1]
-    copies = [pltpu.make_async_copy(tiles.at[0, 0, slot], held.at[slot], sems.at[slot]) for slot in range(slots)]
+    group = slots // CHUNKS
+    copies = [
+        pltpu.make_async_copy(tiles.at[0, 0, pl.ds(k * group, group)], held.at[pl.ds(k * group, group)], sems.at[k])
+        for k in range(CHUNKS)
+    ]
     for copy in copies:
         copy.start()
     for flip in range(n_col):
@@ -102,13 +108,12 @@
         live = slot < count[0, 0]
         i = arow[0, 0, slot] ^ me_col
         j = bcol[0, 0, slot] ^ me_row
-        copies[slot].wait()
+        if slot % group == 0:
+            copies[slot // group].wait()
         pieces = split(held[slot])
         row_sums[jnp.where(live, i, n_col)] += parts_product(cols[j], pieces, (((1,), (1,)), ((), ())))
         col_sums[jnp.where(live, j, n_row)] += parts_product(rows[i], pieces, (((1,), (0,)), ((), ())))
-    total = packed_gram(x_rows[0][...], row_sums[0])
-    for flip in range(1, n_col):
-        total += packed_gram(x_rows[flip][...], row_sums[flip])
+    total = packed_gram([x[...] for x in x_rows], [row_sums[flip] for flip in range(n_col)])
     row_out[...] = row_sums[:n_col]
     for chip in range(n_row // 2):
         col_out[chip] = col_sums[2 * chip]
@@ -150,7 +155,7 @@
     rayleigh[...] = ray
     res = both[:nvec] - mult(ray, own)
     residual[...] = res
-    part = packed_gram(res, res)
+    part = packed_gram([res], [res])
     for block in range(out.shape[0]):
         out[block] = part
 
@@ -203,7 +208,7 @@
                 pltpu.VMEM((n_col + 1, nvec, width), jnp.float32),
                 pltpu.VMEM((n_row + 1, nvec, width), jnp.float32),
                 pltpu.VMEM((slots, width, width), jnp.float32),
-                pltpu.SemaphoreType.DMA((slots,)),
+                pltpu.SemaphoreType.DMA((CHUNKS,)),
             ],
             compiler_params=pltpu.CompilerParams(vmem_limit_bytes=53 * 2**20),
             cost_estimate=pl.CostEstimate(flops=24 * slots * nvec * width * width, bytes_accessed=2**20, transcendentals=0),

time: 47.6 us -> 46 us (0.966)
  Pallas kernels: 7.38 us -> 5.84 us
    pallas_call x1, Pallas kernels: 5.55 us -> 4.01 us  [per_device(): pl.pallas_call(functools.partial(products_kernel, n_row, n_col, slots), o...]
where the time goes in v9:
time: 46 us; the launch traced here: 45.9 us
  starting transfers between devices  17.4 us (38%)
  waiting for transfers between devices  12.2 us (27%)
  blocking collectives  8.97 us (20%)
  Pallas kernels  5.84 us (13%)
  between operations  1.37 us (3%)
    ppermute x14, starting transfers between devices, trade(): return lax.ppermute(value, axis, [(p, p ^ flip) for p in range(size)])  17.4 us
    ppermute x14, waiting for transfers between devices, trade(): return lax.ppermute(value, axis, [(p, p ^ flip) for p in range(size)])  12.2 us
    all_to_all x1, blocking collectives, swap(): return lax.all_to_all(blocks, axis, 0, 0, tiled=True)  8.97 us
    pallas_call x1, Pallas kernels, per_device(): pl.pallas_call(functools.partial(products_kernel, n_row, n_col, slots), o...  4.01 us
    pallas_call x1, Pallas kernels, per_device(): pl.pallas_call(functools.partial(residual_kernel, scale), out_shape=[bloc...  1.01 us
  transfers between devices with their start and end apart: 14, of which 9 were waited for; matrix products, arithmetic and copies ran while one was open for 0% of the time, Pallas kernels for 0%

profile of v9, /device:TPU:0, one launch (start us, length us, event | category | flops | bytes accessed | tf_op | source)
XLA Modules:
  0.0 45.9 jit_solution(2774725043749725882)
XLA Ops:
  0.6 0.0 copy-start
  0.6 0.5 %collective-permute-start.3 = (f32[16,128]{1,0:T(8,128)}, f32[16,128]{1,0:T(8,128)S(1)}, u32[]{:S(2)}, u32[]{:S(2)}) collective-permute-start(f32[16,128]{1,0:T(8,128)} %x_ref.3), channel_id=1, source_target_pairs={{0,4},{4,0},{8,12},{12,8},{16,20},{20,16},{24,28},{28,24},{1,5},{5... | collective-permute-start | bytes 24584 | tf_op jit(solution)/shard_map/share_vectors/ppermute | solution.py:30
  1.2 4.7 %collective-permute-start.2 = (f32[16,128]{1,0:T(8,128)}, f32[16,128]{1,0:T(8,128)S(1)}, u32[]{:S(2)}, u32[]{:S(2)}) collective-permute-start(f32[16,128]{1,0:T(8,128)} %x_ref.3), channel_id=1, source_target_pairs={{0,3},{1,2},{2,1},{3,0},{4,7},{5,6},{6,5},{7,4},{8,11},{9,10},{10,... | collective-permute-start | bytes 24584 | tf_op jit(solution)/shard_map/share_vectors/ppermute | solution.py:30
  5.8 0.0 collective-permute-start.1
  5.8 0.7 %collective-permute-start = (f32[16,128]{1,0:T(8,128)}, f32[16,128]{1,0:T(8,128)S(1)}, u32[]{:S(2)}, u32[]{:S(2)}) collective-permute-start(f32[16,128]{1,0:T(8,128)} %x_ref.3), channel_id=1, source_target_pairs={{0,1},{1,0},{2,3},{3,2},{4,5},{5,4},{6,7},{7,6},{8,9},{9,8},{10,11... | collective-permute-start | bytes 24584 | tf_op jit(solution)/shard_map/share_vectors/ppermute | solution.py:30
  6.5 0.0 collective-permute-done.3.other
  6.5 0.0 copy-done
  6.5 2.6 %collective-permute-start.6 = (f32[2,16,128]{2,1,0:T(8,128)S(1)}, f32[2,16,128]{2,1,0:T(8,128)S(1)}, u32[]{:S(2)}, u32[]{:S(2)}) collective-permute-start(f32[2,16,128]{2,1,0:T(8,128)S(1)} %pair.1.refs_4_), channel_id=1, source_target_pairs={{0,24},{4,28},{8,16},{12,20},{16,8},{20,12},{24,0},{28,4},{1,25},{... | collective-permute-start | bytes 49160 | tf_op jit(solution)/shard_map/share_vectors/ppermute | solution.py:30
  9.1 0.5 %collective-permute-start.5 = (f32[2,16,128]{2,1,0:T(8,128)S(1)}, f32[2,16,128]{2,1,0:T(8,128)S(1)}, u32[]{:S(2)}, u32[]{:S(2)}) collective-permute-start(f32[2,16,128]{2,1,0:T(8,128)S(1)} %pair.1.refs_4_), channel_id=1, source_target_pairs={{0,16},{4,20},{8,24},{12,28},{16,0},{20,4},{24,8},{28,12},{1,17},{... | collective-permute-start | bytes 49160 | tf_op jit(solution)/shard_map/share_vectors/ppermute | solution.py:30
  9.6 0.0 collective-permute-done.2.refs_3_
  9.7 0.4 collective-permute-start.4
  10.1 0.1 pad_add_fusion.place
  10.8 0.0 copy-start.1
  10.8 0.0 copy-start.2
  10.8 0.0 copy-start.3
  10.8 0.0 collective-permute-done.1.refs_2_
  10.8 0.0 collective-permute-done.refs_1_
  10.8 0.4 collective-permute-done.6.refs_7_
  11.2 1.7 %collective-permute-done.5.refs_6_ = f32[2,16,128]{2,1,0:T(8,128)S(1)} collective-permute-done((f32[2,16,128]{2,1,0:T(8,128)S(1)}, f32[2,16,128]{2,1,0:T(8,128)S(1)}, u32[]{:S(2)}, u32[]{:S(2)}) %collective-permute-start.5) | collective-permute-done | bytes 16416 | tf_op jit(solution)/shard_map/share_vectors/ppermute | solution.py:30
  12.9 0.5 %collective-permute-done.4.refs_5_ = f32[2,16,128]{2,1,0:T(8,128)S(1)} collective-permute-done((f32[2,16,128]{2,1,0:T(8,128)S(1)}, f32[2,16,128]{2,1,0:T(8,128)S(1)}, u32[]{:S(2)}, u32[]{:S(2)}) %collective-permute-start.4) | collective-permute-done | bytes 16416 | tf_op jit(solution)/shard_map/share_vectors/ppermute | solution.py:30
  13.4 0.0 copy-done.1
  13.4 0.0 copy-done.2
  13.4 0.0 copy-done.3
  13.4 4.0 %tile_products.1 = (f32[4,16,128]{2,1,0:T(8,128)S(1)}, f32[4,16,128]{2,1,0:T(8,128)S(1)}, f32[72,128]{1,0:T(8,128)S(1)}) custom-call(s32[2]{0:T(128)S(1)} %pad_add_fusion.place, s32[1,1,16]{2,1,0:T(1,128)S(1)} %copy-done.1, s32[1,1,16]{2,1,0:T(1,128)S(1)} %copy-done.2, s32[1,1]{1,0:T(1,128)S(6)} %copy.9.count, f32[1,128]{1,0:T(1,128)S(1)} %bitcast.3, ...), custom_call_target="tpu_custom_call" | custom-call | flops 100663296 | bytes 1048576 | tf_op jit(solution)/shard_map/tile_products/tile_products/pallas_call | solution.py:196
  17.4 0.1 collective-permute-start.7
  17.5 1.2 %collective-permute-done.7.other = f32[72,128]{1,0:T(8,128)S(1)} collective-permute-done((f32[72,128]{1,0:T(8,128)S(1)}, f32[72,128]{1,0:T(8,128)S(1)}, u32[]{:S(2)}, u32[]{:S(2)}) %collective-permute-start.7) | collective-permute-done | bytes 36896 | tf_op jit(solution)/shard_map/return_products/ppermute | solution.py:30
  18.7 0.4 collective-permute-start.8
  19.1 1.6 %collective-permute-start.9 = (f32[24,128]{1,0:T(8,128)S(1)}, f32[24,128]{1,0:T(8,128)S(1)}, u32[]{:S(2)}, u32[]{:S(2)}) collective-permute-start(f32[24,128]{1,0:T(8,128)S(1)} %get-tuple-element.21), channel_id=1, source_target_pairs={{0,16},{4,20},{8,24},{12,28},{16,0},{20,4},{24,8},{28,12},{1,17},{... | collective-permute-start | bytes 36872 | tf_op jit(solution)/shard_map/return_products/ppermute | solution.py:30
  20.8 1.4 %collective-permute-start.10 = (f32[24,128]{1,0:T(8,128)S(1)}, f32[24,128]{1,0:T(8,128)S(1)}, u32[]{:S(2)}, u32[]{:S(2)}) collective-permute-start(f32[24,128]{1,0:T(8,128)S(1)} %get-tuple-element.22), channel_id=1, source_target_pairs={{0,24},{4,28},{8,16},{12,20},{16,8},{20,12},{24,0},{28,4},{1,25},{... | collective-permute-start | bytes 36872 | tf_op jit(solution)/shard_map/return_products/ppermute | solution.py:30
  22.2 0.2 collective-permute-done.8.refs_1_
  22.4 0.4 collective-permute-done.9.refs_2_
  22.8 2.5 %collective-permute-done.10.refs_3_ = f32[24,128]{1,0:T(8,128)S(1)} collective-permute-done((f32[24,128]{1,0:T(8,128)S(1)}, f32[24,128]{1,0:T(8,128)S(1)}, u32[]{:S(2)}, u32[]{:S(2)}) %collective-permute-start.10) | collective-permute-done | bytes 12320 | tf_op jit(solution)/shard_map/return_products/ppermute | solution.py:30
  25.4 1.3 %collective-permute-start.11 = (f32[24,128]{1,0:T(8,128)S(1)}, f32[24,128]{1,0:T(8,128)S(1)}, u32[]{:S(2)}, u32[]{:S(2)}) collective-permute-start(f32[24,128]{1,0:T(8,128)S(1)} %get-tuple-element.25), channel_id=1, source_target_pairs={{0,1},{1,0},{2,3},{3,2},{4,5},{5,4},{6,7},{7,6},{8,9},{9,8},{10,11... | collective-permute-start | bytes 36872 | tf_op jit(solution)/shard_map/return_products/ppermute | solution.py:30
  26.7 2.9 %collective-permute-start.12 = (f32[24,128]{1,0:T(8,128)S(1)}, f32[24,128]{1,0:T(8,128)S(1)}, u32[]{:S(2)}, u32[]{:S(2)}) collective-permute-start(f32[24,128]{1,0:T(8,128)S(1)} %get-tuple-element.26), channel_id=1, source_target_pairs={{0,2},{1,3},{2,0},{3,1},{4,6},{5,7},{6,4},{7,5},{8,10},{9,11},{10,... | collective-permute-start | bytes 36872 | tf_op jit(solution)/shard_map/return_products/ppermute | solution.py:30
  29.6 0.2 collective-permute-start.13
  29.8 0.0 collective-permute-done.11.refs_1_
  29.8 1.4 %collective-permute-done.12.refs_2_ = f32[24,128]{1,0:T(8,128)S(1)} collective-permute-done((f32[24,128]{1,0:T(8,128)S(1)}, f32[24,128]{1,0:T(8,128)S(1)}, u32[]{:S(2)}, u32[]{:S(2)}) %collective-permute-start.12) | collective-permute-done | bytes 12320 | tf_op jit(solution)/shard_map/return_products/ppermute | solution.py:30
  31.3 3.8 %collective-permute-done.13.refs_3_ = f32[24,128]{1,0:T(8,128)S(1)} collective-permute-done((f32[24,128]{1,0:T(8,128)S(1)}, f32[24,128]{1,0:T(8,128)S(1)}, u32[]{:S(2)}, u32[]{:S(2)}) %collective-permute-start.13) | collective-permute-done | bytes 12320 | tf_op jit(solution)/shard_map/return_products/ppermute | solution.py:30
  35.1 1.0 %residual.1 = (f32[16,128]{1,0:T(8,128)}, f32[16,16]{1,0:T(8,128)}, f32[32,2,128]{2,1,0:T(2,128)S(1)}) custom-call(f32[16,128]{1,0:T(8,128)S(1)} %copy-done, f32[24,128]{1,0:T(8,128)S(1)} %get-tuple-element.24.refs_0_, f32[24,128]{1,0:T(8,128)S(1)} %collective-permute-done.11.refs_1_, f32[24,128]{1,0:T(8,128)S(1)} %collective-permute-done.12.refs_2_, ...), custom_call_target="tpu_custom_call" | custom-call | tf_op jit(solution)/shard_map/residual/residual/pallas_call | solution.py:237
  36.1 9.0 %all_to_all.5.parts = f32[32,2,128]{2,1,0:T(2,128)S(1)} all-to-all(f32[32,2,128]{2,1,0:T(2,128)S(1)} %get-tuple-element.30), channel_id=1, replica_groups=mesh['row'=8,'col'=4] {'row','col'}, dimensions={0} | all-to-all | bytes 65536 | tf_op jit(solution)/shard_map/gram_sum/all_to_all | solution.py:25
  45.1 0.8 %gram_sum.1 = f32[16,16]{1,0:T(8,128)} custom-call(f32[32,2,128]{2,1,0:T(2,128)S(1)} %all_to_all.5.parts), custom_call_target="tpu_custom_call" | custom-call | tf_op jit(solution)/shard_map/gram_sum/gram_sum/pallas_call | solution.py:246
  (3 shorter events, 0.0 us)
Async XLA Ops:
  0.6 5.9 %copy-start = (f32[16,128]{1,0:T(8,128)S(1)}, f32[16,128]{1,0:T(8,128)}, u32[]{:S(2)}) copy-start(f32[16,128]{1,0:T(8,128)} %x_ref.3) | copy-start | bytes 24580
  0.6 5.9 %collective-permute-start.3 = (f32[16,128]{1,0:T(8,128)}, f32[16,128]{1,0:T(8,128)S(1)}, u32[]{:S(2)}, u32[]{:S(2)}) collective-permute-start(f32[16,128]{1,0:T(8,128)} %x_ref.3), channel_id=1, source_target_pairs={{0,4},{4,0},{8,12},{12,8},{16,20},{20,16},{24,28},{28,24},{1,5},{5... | collective-permute-start | bytes 24584 | tf_op jit(solution)/shard_map/share_vectors/ppermute | solution.py:30
  1.2 8.5 %collective-permute-start.2 = (f32[16,128]{1,0:T(8,128)}, f32[16,128]{1,0:T(8,128)S(1)}, u32[]{:S(2)}, u32[]{:S(2)}) collective-permute-start(f32[16,128]{1,0:T(8,128)} %x_ref.3), channel_id=1, source_target_pairs={{0,3},{1,2},{2,1},{3,0},{4,7},{5,6},{6,5},{7,4},{8,11},{9,10},{10,... | collective-permute-start | bytes 24584 | tf_op jit(solution)/shard_map/share_vectors/ppermute | solution.py:30
  5.8 5.0 %collective-permute-start.1 = (f32[16,128]{1,0:T(8,128)}, f32[16,128]{1,0:T(8,128)S(1)}, u32[]{:S(2)}, u32[]{:S(2)}) collective-permute-start(f32[16,128]{1,0:T(8,128)} %x_ref.3), channel_id=1, source_target_pairs={{0,2},{1,3},{2,0},{3,1},{4,6},{5,7},{6,4},{7,5},{8,10},{9,11},{10,... | collective-permute-start | bytes 24584 | tf_op jit(solution)/shard_map/share_vectors/ppermute | solution.py:30
  5.8 5.0 %collective-permute-start = (f32[16,128]{1,0:T(8,128)}, f32[16,128]{1,0:T(8,128)S(1)}, u32[]{:S(2)}, u32[]{:S(2)}) collective-permute-start(f32[16,128]{1,0:T(8,128)} %x_ref.3), channel_id=1, source_target_pairs={{0,1},{1,0},{2,3},{3,2},{4,5},{5,4},{6,7},{7,6},{8,9},{9,8},{10,11... | collective-permute-start | bytes 24584 | tf_op jit(solution)/shard_map/share_vectors/ppermute | solution.py:30
  6.5 4.7 %collective-permute-start.6 = (f32[2,16,128]{2,1,0:T(8,128)S(1)}, f32[2,16,128]{2,1,0:T(8,128)S(1)}, u32[]{:S(2)}, u32[]{:S(2)}) collective-permute-start(f32[2,16,128]{2,1,0:T(8,128)S(1)} %pair.1.refs_4_), channel_id=1, source_target_pairs={{0,24},{4,28},{8,16},{12,20},{16,8},{20,12},{24,0},{28,4},{1,25},{... | collective-permute-start | bytes 49160 | tf_op jit(solution)/shard_map/share_vectors/ppermute | solution.py:30
  9.1 3.7 %collective-permute-start.5 = (f32[2,16,128]{2,1,0:T(8,128)S(1)}, f32[2,16,128]{2,1,0:T(8,128)S(1)}, u32[]{:S(2)}, u32[]{:S(2)}) collective-permute-start(f32[2,16,128]{2,1,0:T(8,128)S(1)} %pair.1.refs_4_), channel_id=1, source_target_pairs={{0,16},{4,20},{8,24},{12,28},{16,0},{20,4},{24,8},{28,12},{1,17},{... | collective-permute-start | bytes 49160 | tf_op jit(solution)/shard_map/share_vectors/ppermute | solution.py:30
  9.7 3.7 %collective-permute-start.4 = (f32[2,16,128]{2,1,0:T(8,128)S(1)}, f32[2,16,128]{2,1,0:T(8,128)S(1)}, u32[]{:S(2)}, u32[]{:S(2)}) collective-permute-start(f32[2,16,128]{2,1,0:T(8,128)S(1)} %pair.1.refs_4_), channel_id=1, source_target_pairs={{0,8},{4,12},{8,0},{12,4},{16,24},{20,28},{24,16},{28,20},{1,9},{5... | collective-permute-start | bytes 49160 | tf_op jit(solution)/shard_map/share_vectors/ppermute | solution.py:30
  10.8 2.6 %copy-start.1 = (s32[1,1,16]{2,1,0:T(1,128)S(1)}, s32[1,1,16]{2,1,0:T(1,128)}, u32[]{:S(2)}) copy-start(s32[1,1,16]{2,1,0:T(1,128)} %arow.1) | copy-start | bytes 196
  10.8 2.6 %copy-start.2 = (s32[1,1,16]{2,1,0:T(1,128)S(1)}, s32[1,1,16]{2,1,0:T(1,128)}, u32[]{:S(2)}) copy-start(s32[1,1,16]{2,1,0:T(1,128)} %bcol.1) | copy-start | bytes 196
  10.8 2.6 %copy-start.3 = (f32[128]{0:T(128)S(1)}, f32[128]{0:T(128)}, u32[]{:S(2)}) copy-start(f32[128]{0:T(128)} %param.7) | copy-start | bytes 1540
  17.4 1.3 %collective-permute-start.7 = (f32[72,128]{1,0:T(8,128)S(1)}, f32[72,128]{1,0:T(8,128)S(1)}, u32[]{:S(2)}, u32[]{:S(2)}) collective-permute-start(f32[72,128]{1,0:T(8,128)S(1)} %get-tuple-element.18.mine), channel_id=1, source_target_pairs={{0,4},{4,0},{8,12},{12,8},{16,20},{20,16},{24,28},{28,24},{1,5},{5... | collective-permute-start | bytes 110600 | tf_op jit(solution)/shard_map/return_products/ppermute | solution.py:30
  18.7 3.7 %collective-permute-start.8 = (f32[24,128]{1,0:T(8,128)S(1)}, f32[24,128]{1,0:T(8,128)S(1)}, u32[]{:S(2)}, u32[]{:S(2)}) collective-permute-start(f32[24,128]{1,0:T(8,128)S(1)} %get-tuple-element.20), channel_id=1, source_target_pairs={{0,8},{4,12},{8,0},{12,4},{16,24},{20,28},{24,16},{28,20},{1,9},{5... | collective-permute-start | bytes 36872 | tf_op jit(solution)/shard_map/return_products/ppermute | solution.py:30
  19.1 3.7 %collective-permute-start.9 = (f32[24,128]{1,0:T(8,128)S(1)}, f32[24,128]{1,0:T(8,128)S(1)}, u32[]{:S(2)}, u32[]{:S(2)}) collective-permute-start(f32[24,128]{1,0:T(8,128)S(1)} %get-tuple-element.21), channel_id=1, source_target_pairs={{0,16},{4,20},{8,24},{12,28},{16,0},{20,4},{24,8},{28,12},{1,17},{... | collective-permute-start | bytes 36872 | tf_op jit(solution)/shard_map/return_products/ppermute | solution.py:30
  20.8 4.6 %collective-permute-start.10 = (f32[24,128]{1,0:T(8,128)S(1)}, f32[24,128]{1,0:T(8,128)S(1)}, u32[]{:S(2)}, u32[]{:S(2)}) collective-permute-start(f32[24,128]{1,0:T(8,128)S(1)} %get-tuple-element.22), channel_id=1, source_target_pairs={{0,24},{4,28},{8,16},{12,20},{16,8},{20,12},{24,0},{28,4},{1,25},{... | collective-permute-start | bytes 36872 | tf_op jit(solution)/shard_map/return_products/ppermute | solution.py:30
  25.4 4.5 %collective-permute-start.11 = (f32[24,128]{1,0:T(8,128)S(1)}, f32[24,128]{1,0:T(8,128)S(1)}, u32[]{:S(2)}, u32[]{:S(2)}) collective-permute-start(f32[24,128]{1,0:T(8,128)S(1)} %get-tuple-element.25), channel_id=1, source_target_pairs={{0,1},{1,0},{2,3},{3,2},{4,5},{5,4},{6,7},{7,6},{8,9},{9,8},{10,11... | collective-permute-start | bytes 36872 | tf_op jit(solution)/shard_map/return_products/ppermute | solution.py:30
  26.7 4.6 %collective-permute-start.12 = (f32[24,128]{1,0:T(8,128)S(1)}, f32[24,128]{1,0:T(8,128)S(1)}, u32[]{:S(2)}, u32[]{:S(2)}) collective-permute-start(f32[24,128]{1,0:T(8,128)S(1)} %get-tuple-element.26), channel_id=1, source_target_pairs={{0,2},{1,3},{2,0},{3,1},{4,6},{5,7},{6,4},{7,5},{8,10},{9,11},{10,... | collective-permute-start | bytes 36872 | tf_op jit(solution)/shard_map/return_products/ppermute | solution.py:30
  29.6 5.5 %collective-permute-start.13 = (f32[24,128]{1,0:T(8,128)S(1)}, f32[24,128]{1,0:T(8,128)S(1)}, u32[]{:S(2)}, u32[]{:S(2)}) collective-permute-start(f32[24,128]{1,0:T(8,128)S(1)} %get-tuple-element.27), channel_id=1, source_target_pairs={{0,3},{1,2},{2,1},{3,0},{4,7},{5,6},{6,5},{7,4},{8,11},{9,10},{10,... | collective-permute-start | bytes 36872 | tf_op jit(solution)/shard_map/return_products/ppermute | solution.py:30

commit v10 on v7

--- a/solution.py
+++ b/solution.py
@@ -36,9 +36,10 @@
 
 
 def packed_gram(left, right):
-    nvec, width = left.shape
+    nvec, width = left[0].shape
     per = width // nvec
-    wide = mult_last(left, jnp.concatenate([right] * per, axis=0))
+    right = jnp.concatenate(right, axis=1)
+    wide = mult_last(jnp.concatenate(left, axis=1), jnp.concatenate([right] * per, axis=0))
     wide = jnp.where(own_lanes(nvec, width), wide, 0.0)
     return jnp.sum(wide.reshape(nvec // per, per, width), axis=1)
 
@@ -112,10 +113,9 @@
     out[...] = sums[:n_col]
     for chip in range(n_row // 2):
         to_core[chip * nvec : (chip + 1) * nvec] = col_terms[2 * chip + 1]
-    total = packed_gram(x_rows[0][...], sums[0])
-    for flip in range(1, n_col):
-        total += packed_gram(x_rows[flip][...], sums[flip])
-    to_core[n_row // 2 * nvec :] = jnp.concatenate([total, jnp.zeros((to_core.shape[0] - n_row // 2 * nvec - total.shape[0], width), jnp.float32)], axis=0)
+    total = packed_gram([x[...] for x in x_rows], [sums[flip] for flip in range(n_col)])
+    rest = jnp.zeros((to_core.shape[0] - n_row // 2 * nvec - total.shape[0], width), jnp.float32)
+    to_core[n_row // 2 * nvec :] = jnp.concatenate([total, rest], axis=0)
 
 
 def chip_kernel(col_terms, mine, other, *outs):
@@ -151,7 +151,7 @@
     rayleigh[...] = ray
     res = both[:nvec] - mult(ray, own)
     residual[...] = res
-    part = packed_gram(res, res)
+    part = packed_gram([res], [res])
     for block in range(out.shape[0]):
         out[block] = part
 
@@ -173,10 +173,10 @@
     block = jax.ShapeDtypeStruct((nvec, width), jnp.float32)
     joined = jax.ShapeDtypeStruct((padded, width), jnp.float32)
     square = jax.ShapeDtypeStruct((nvec, nvec), jnp.float32)
-    part = jax.ShapeDtypeStruct((slots, width, width), jnp.bfloat16)
     place = jnp.stack([lax.axis_index("row"), lax.axis_index("col")]).astype(jnp.int32)
     energy = diagonal_energy.reshape(1, width)
-    params = pltpu.CompilerParams(vmem_limit_bytes=24 * 2**20)
+    part = jax.ShapeDtypeStruct((slots, width, width), jnp.bfloat16)
+    params = pltpu.CompilerParams(vmem_limit_bytes=16 * 2**20)
     cost = pl.CostEstimate(flops=12 * slots * nvec * width * width, bytes_accessed=2**20, transcendentals=0)
     with jax.named_scope("share_vectors"):
         other = trade(vectors, "row", 1)
@@ -186,6 +186,7 @@
             out_shape=jax.ShapeDtypeStruct((2, nvec, width), jnp.float32),
             in_specs=[VMEM] * 2,
             out_specs=VMEM,
+            compiler_params=params,
             name="pair",
         )(vectors, other)
         x_pairs = [pair] + [trade(pair, "row", 2 * chip) for chip in range(1, n_chip)]
@@ -222,7 +223,12 @@
         )(place, tile_rows, tile_cols, tile_count, energy, *x_rows, *x_pairs, col_terms, *parts)
     with jax.named_scope("return_products"):
         chips = pl.pallas_call(
-            chip_kernel, out_shape=[joined] * n_chip, in_specs=[VMEM] * 3, out_specs=[VMEM] * n_chip, name="chip_sum"
+            chip_kernel,
+            out_shape=[joined] * n_chip,
+            in_specs=[VMEM] * 3,
+            out_specs=[VMEM] * n_chip,
+            compiler_params=params,
+            name="chip_sum",
         )(col_terms, to_core, trade(to_core, "row", 1))
         by_row = [chips[0]] + [trade(chips[chip], "row", 2 * chip) for chip in range(1, n_chip)]
         sends = pl.pallas_call(
@@ -230,6 +236,7 @@
             out_shape=[joined] * n_col,
             in_specs=[VMEM] * (n_chip + 1),
             out_specs=[VMEM] * n_col,
+            compiler_params=params,
             name="row_sum",
         )(*by_row, row_terms)
         sums = [sends[0]] + [trade(sends[flip], "col", flip) for flip in range(1, n_col)]
@@ -244,7 +251,12 @@
         )(vectors, *sums)
     with jax.named_scope("gram_sum"):
         gram = pl.pallas_call(
-            functools.partial(gram_kernel, scale), out_shape=square, in_specs=[VMEM], out_specs=VMEM, name="gram_sum"
+            functools.partial(gram_kernel, scale),
+            out_shape=square,
+            in_specs=[VMEM],
+            out_specs=VMEM,
+            compiler_params=params,
+            name="gram_sum",
         )(swap(grams, ("row", "col")))
     return (residual, rayleigh, gram)
 

time: 55 us -> 45.8 us (0.83)
  Pallas kernels: 10.1 us -> 5.11 us
  local copies, waits for them, and re-layouts: 4.97 us -> 1.87 us
  blocking collectives: 9.65 us -> 8.97 us
    unnamed x30 -> x10, local copies, waits for them, and re-layouts: 4.97 us -> 1.87 us
    pallas_call x1, Pallas kernels: 1.49 us -> 0.01 us  [per_device(): pl.pallas_call(chip_kernel, out_shape=[joined] * n_chip, in_specs=[VMEM]...]
    pallas_call x1, Pallas kernels: 1.46 us -> 0.01 us  [per_device(): pl.pallas_call(functools.partial(join_kernel, n_chip), out_shape=[joined]...]
    pallas_call x1, Pallas kernels: 1.32 us -> 0.01 us  [per_device(): pl.pallas_call(pair_kernel, out_shape=jax.ShapeDtypeStruct((2, nvec, widt...]
    pallas_call x1, Pallas kernels: 1.55 us -> 0.8 us  [per_device(): pl.pallas_call(functools.partial(gram_kernel, scale), out_shape=square, i...]
    all_to_all x1, blocking collectives: 9.65 us -> 8.97 us  [swap(): return lax.all_to_all(blocks, axis, 0, 0, tiled=True)]
  transfers between devices with their start and end apart: 14 -> 14, of which waited for: 6 -> 6; matrix products, arithmetic and copies ran while one was open for 0% -> 0% of each run, Pallas kernels for 4% -> 2%
where the time goes in v10:
time: 45.8 us; the launch traced here: 45.6 us
  starting transfers between devices  17.4 us (38%)
  waiting for transfers between devices  10.7 us (23%)
  blocking collectives  8.97 us (20%)
  Pallas kernels  5.11 us (11%)
  local copies, waits for them, and re-layouts  1.87 us (4%)
  between operations  1.41 us (3%)
    ppermute x14, starting transfers between devices, trade(): return lax.ppermute(value, axis, [(p, p ^ flip) for p in range(size)])  17.4 us
    ppermute x14, waiting for transfers between devices, trade(): return lax.ppermute(value, axis, [(p, p ^ flip) for p in range(size)])  10.7 us
    all_to_all x1, blocking collectives, swap(): return lax.all_to_all(blocks, axis, 0, 0, tiled=True)  8.97 us
    pallas_call x1, Pallas kernels, per_device(): pl.pallas_call(functools.partial(row_kernel, n_row, n_col, slots), out_sh...  2.19 us
    unnamed x10, local copies, waits for them, and re-layouts  1.87 us
    pallas_call x1, Pallas kernels, per_device(): pl.pallas_call(functools.partial(column_kernel, n_row, n_col, slots), out...  1.1 us
    pallas_call x1, Pallas kernels, per_device(): pl.pallas_call(functools.partial(residual_kernel, scale), out_shape=[bloc...  1.01 us
  transfers between devices with their start and end apart: 14, of which 6 were waited for; matrix products, arithmetic and copies ran while one was open for 0% of the time, Pallas kernels for 2%

profile of v10, /device:TPU:0, one launch (start us, length us, event | category | flops | bytes accessed | tf_op | source)
XLA Modules:
  0.0 45.6 jit_solution(5824287624604503835)
XLA Ops:
  0.6 0.0 copy-start.1
  0.6 0.5 %collective-permute-start.3 = (f32[16,128]{1,0:T(8,128)}, f32[16,128]{1,0:T(8,128)S(1)}, u32[]{:S(2)}, u32[]{:S(2)}) collective-permute-start(f32[16,128]{1,0:T(8,128)} %x_ref.3), channel_id=1, source_target_pairs={{0,4},{4,0},{8,12},{12,8},{16,20},{20,16},{24,28},{28,24},{1,5},{5... | collective-permute-start | bytes 24584 | tf_op jit(solution)/shard_map/share_vectors/ppermute | solution.py:29
  1.2 4.7 %collective-permute-start.2 = (f32[16,128]{1,0:T(8,128)}, f32[16,128]{1,0:T(8,128)S(1)}, u32[]{:S(2)}, u32[]{:S(2)}) collective-permute-start(f32[16,128]{1,0:T(8,128)} %x_ref.3), channel_id=1, source_target_pairs={{0,3},{1,2},{2,1},{3,0},{4,7},{5,6},{6,5},{7,4},{8,11},{9,10},{10,... | collective-permute-start | bytes 24584 | tf_op jit(solution)/shard_map/share_vectors/ppermute | solution.py:29
  5.8 0.0 collective-permute-start.1
  5.8 0.7 %collective-permute-start = (f32[16,128]{1,0:T(8,128)}, f32[16,128]{1,0:T(8,128)S(1)}, u32[]{:S(2)}, u32[]{:S(2)}) collective-permute-start(f32[16,128]{1,0:T(8,128)} %x_ref.3), channel_id=1, source_target_pairs={{0,1},{1,0},{2,3},{3,2},{4,5},{5,4},{6,7},{7,6},{8,9},{9,8},{10,11... | collective-permute-start | bytes 24584 | tf_op jit(solution)/shard_map/share_vectors/ppermute | solution.py:29
  6.5 0.0 collective-permute-done.3.other
  6.5 0.0 copy-done.1
  6.5 2.6 %collective-permute-start.6 = (f32[2,16,128]{2,1,0:T(8,128)S(1)}, f32[2,16,128]{2,1,0:T(8,128)S(1)}, u32[]{:S(2)}, u32[]{:S(2)}) collective-permute-start(f32[2,16,128]{2,1,0:T(8,128)S(1)} %pair.1.refs_4_), channel_id=1, source_target_pairs={{0,24},{4,28},{8,16},{12,20},{16,8},{20,12},{24,0},{28,4},{1,25},{... | collective-permute-start | bytes 49160 | tf_op jit(solution)/shard_map/share_vectors/ppermute | solution.py:29
  9.1 0.5 %collective-permute-start.5 = (f32[2,16,128]{2,1,0:T(8,128)S(1)}, f32[2,16,128]{2,1,0:T(8,128)S(1)}, u32[]{:S(2)}, u32[]{:S(2)}) collective-permute-start(f32[2,16,128]{2,1,0:T(8,128)S(1)} %pair.1.refs_4_), channel_id=1, source_target_pairs={{0,16},{4,20},{8,24},{12,28},{16,0},{20,4},{24,8},{28,12},{1,17},{... | collective-permute-start | bytes 49160 | tf_op jit(solution)/shard_map/share_vectors/ppermute | solution.py:29
  9.6 0.0 collective-permute-done.2.refs_3_
  9.7 0.4 collective-permute-start.4
  10.1 0.1 pad_add_fusion.place
  10.8 0.0 copy-start.2
  10.8 0.0 copy-start.3
  10.8 0.0 copy-start.4
  10.8 0.0 collective-permute-done.1.refs_2_
  10.8 0.0 collective-permute-done.refs_1_
  10.8 0.6 %copy-done.2 = s32[1,1,16]{2,1,0:T(1,128)S(1)} copy-done((s32[1,1,16]{2,1,0:T(1,128)S(1)}, s32[1,1,16]{2,1,0:T(1,128)}, u32[]{:S(2)}) %copy-start.2) | copy-done | bytes 88
  11.4 0.0 copy-done.3
  11.5 0.0 copy-done.4
  11.5 0.0 copy-start
  11.5 1.2 %copy-done = f32[1,1,16,128,128]{4,3,2,1,0:T(8,128)S(1)} copy-done((f32[1,1,16,128,128]{4,3,2,1,0:T(8,128)S(1)}, f32[1,1,16,128,128]{4,3,2,1,0:T(8,128)}, u32[]{:S(2)}) %copy-start) | copy-done | bytes 1048600
  12.7 1.1 %column_terms.1 = (f32[8,16,128]{2,1,0:T(8,128)S(1)}, bf16[16,128,128]{2,1,0:T(8,128)(2,1)S(1)}, bf16[16,128,128]{2,1,0:T(8,128)(2,1)S(1)}, bf16[16,128,128]{2,1,0:T(8,128)(2,1)S(1)}) custom-call(s32[2]{0:T(128)S(1)} %pad_add_fusion.place, s32[1,1,16]{2,1,0:T(1,128)S(1)} %copy-done.2, s32[1,1,16]{2,1,0:T(1,128)S(1)} %copy-done.3, s32[1,1]{1,0:T(1,128)S(6)} %copy.9.count, ...), custom_call_target="tpu_custom_call" | custom-call | flops 50331648 | bytes 1048576 | tf_op jit(solution)/shard_map/column_terms/column_terms/pallas_call | solution.py:194
  13.8 0.0 collective-permute-done.6.refs_7_
  13.8 0.0 collective-permute-done.5.refs_6_
  13.8 0.0 collective-permute-done.4.refs_5_
  13.8 2.2 %row_terms.1 = (f32[4,16,128]{2,1,0:T(8,128)S(1)}, f32[72,128]{1,0:T(8,128)S(1)}) custom-call(s32[2]{0:T(128)S(1)} %pad_add_fusion.place, s32[1,1,16]{2,1,0:T(1,128)S(1)} %copy-done.2, s32[1,1,16]{2,1,0:T(1,128)S(1)} %copy-done.3, s32[1,1]{1,0:T(1,128)S(6)} %copy.9.count, f32[1,128]{1,0:T(1,128)S(1)} %bitcast.4, f32[16,128]{1,0:T(8,128)S(1)} %copy-done.1, ...), custom_call_target="tpu_custom_call" | custom-call | flops 50331648 | bytes 1048576 | tf_op jit(solution)/shard_map/row_terms/row_terms/pallas_call | solution.py:208
  16.0 0.1 collective-permute-start.7
  16.1 1.2 %collective-permute-done.7.other = f32[72,128]{1,0:T(8,128)S(1)} collective-permute-done((f32[72,128]{1,0:T(8,128)S(1)}, f32[72,128]{1,0:T(8,128)S(1)}, u32[]{:S(2)}, u32[]{:S(2)}) %collective-permute-start.7) | collective-permute-done | bytes 36896 | tf_op jit(solution)/shard_map/return_products/ppermute | solution.py:29
  17.3 1.6 %collective-permute-start.8 = (f32[24,128]{1,0:T(8,128)S(1)}, f32[24,128]{1,0:T(8,128)S(1)}, u32[]{:S(2)}, u32[]{:S(2)}) collective-permute-start(f32[24,128]{1,0:T(8,128)S(1)} %get-tuple-element.26), channel_id=1, source_target_pairs={{0,8},{4,12},{8,0},{12,4},{16,24},{20,28},{24,16},{28,20},{1,9},{5... | collective-permute-start | bytes 36872 | tf_op jit(solution)/shard_map/return_products/ppermute | solution.py:29
  19.0 1.5 %collective-permute-start.9 = (f32[24,128]{1,0:T(8,128)S(1)}, f32[24,128]{1,0:T(8,128)S(1)}, u32[]{:S(2)}, u32[]{:S(2)}) collective-permute-start(f32[24,128]{1,0:T(8,128)S(1)} %get-tuple-element.27), channel_id=1, source_target_pairs={{0,16},{4,20},{8,24},{12,28},{16,0},{20,4},{24,8},{28,12},{1,17},{... | collective-permute-start | bytes 36872 | tf_op jit(solution)/shard_map/return_products/ppermute | solution.py:29
  20.5 0.3 collective-permute-start.10
  20.8 0.2 collective-permute-done.8.refs_1_
  21.0 1.6 %collective-permute-done.9.refs_2_ = f32[24,128]{1,0:T(8,128)S(1)} collective-permute-done((f32[24,128]{1,0:T(8,128)S(1)}, f32[24,128]{1,0:T(8,128)S(1)}, u32[]{:S(2)}, u32[]{:S(2)}) %collective-permute-start.9) | collective-permute-done | bytes 12320 | tf_op jit(solution)/shard_map/return_products/ppermute | solution.py:29
  22.7 2.4 %collective-permute-done.10.refs_3_ = f32[24,128]{1,0:T(8,128)S(1)} collective-permute-done((f32[24,128]{1,0:T(8,128)S(1)}, f32[24,128]{1,0:T(8,128)S(1)}, u32[]{:S(2)}, u32[]{:S(2)}) %collective-permute-start.10) | collective-permute-done | bytes 12320 | tf_op jit(solution)/shard_map/return_products/ppermute | solution.py:29
  25.1 1.3 %collective-permute-start.11 = (f32[24,128]{1,0:T(8,128)S(1)}, f32[24,128]{1,0:T(8,128)S(1)}, u32[]{:S(2)}, u32[]{:S(2)}) collective-permute-start(f32[24,128]{1,0:T(8,128)S(1)} %get-tuple-element.31), channel_id=1, source_target_pairs={{0,1},{1,0},{2,3},{3,2},{4,5},{5,4},{6,7},{7,6},{8,9},{9,8},{10,11... | collective-permute-start | bytes 36872 | tf_op jit(solution)/shard_map/return_products/ppermute | solution.py:29
  26.4 2.9 %collective-permute-start.12 = (f32[24,128]{1,0:T(8,128)S(1)}, f32[24,128]{1,0:T(8,128)S(1)}, u32[]{:S(2)}, u32[]{:S(2)}) collective-permute-start(f32[24,128]{1,0:T(8,128)S(1)} %get-tuple-element.32), channel_id=1, source_target_pairs={{0,2},{1,3},{2,0},{3,1},{4,6},{5,7},{6,4},{7,5},{8,10},{9,11},{10,... | collective-permute-start | bytes 36872 | tf_op jit(solution)/shard_map/return_products/ppermute | solution.py:29
  29.3 0.2 collective-permute-start.13
  29.5 0.0 collective-permute-done.11.refs_1_
  29.5 1.4 %collective-permute-done.12.refs_2_ = f32[24,128]{1,0:T(8,128)S(1)} collective-permute-done((f32[24,128]{1,0:T(8,128)S(1)}, f32[24,128]{1,0:T(8,128)S(1)}, u32[]{:S(2)}, u32[]{:S(2)}) %collective-permute-start.12) | collective-permute-done | bytes 12320 | tf_op jit(solution)/shard_map/return_products/ppermute | solution.py:29
  31.0 3.8 %collective-permute-done.13.refs_3_ = f32[24,128]{1,0:T(8,128)S(1)} collective-permute-done((f32[24,128]{1,0:T(8,128)S(1)}, f32[24,128]{1,0:T(8,128)S(1)}, u32[]{:S(2)}, u32[]{:S(2)}) %collective-permute-start.13) | collective-permute-done | bytes 12320 | tf_op jit(solution)/shard_map/return_products/ppermute | solution.py:29
  34.8 1.0 %residual.1 = (f32[16,128]{1,0:T(8,128)}, f32[16,16]{1,0:T(8,128)}, f32[32,2,128]{2,1,0:T(2,128)S(1)}) custom-call(f32[16,128]{1,0:T(8,128)S(1)} %copy-done.1, f32[24,128]{1,0:T(8,128)S(1)} %get-tuple-element.30.refs_0_, f32[24,128]{1,0:T(8,128)S(1)} %collective-permute-done.11.refs_1_, f32[24,128]{1,0:T(8,128)S(1)} %collective-permute-done.12.refs_2_, ...), custom_call_target="tpu_custom_call" | custom-call | tf_op jit(solution)/shard_map/residual/residual/pallas_call | solution.py:244
  35.8 9.0 %all_to_all.5.parts = f32[32,2,128]{2,1,0:T(2,128)S(1)} all-to-all(f32[32,2,128]{2,1,0:T(2,128)S(1)} %get-tuple-element.36), channel_id=1, replica_groups=mesh['row'=8,'col'=4] {'row','col'}, dimensions={0} | all-to-all | bytes 65536 | tf_op jit(solution)/shard_map/gram_sum/all_to_all | solution.py:24
  44.8 0.8 %gram_sum.1 = f32[16,16]{1,0:T(8,128)} custom-call(f32[32,2,128]{2,1,0:T(2,128)S(1)} %all_to_all.5.parts), custom_call_target="tpu_custom_call" | custom-call | tf_op jit(solution)/shard_map/gram_sum/gram_sum/pallas_call | solution.py:253
  (3 shorter events, 0.0 us)
Async XLA Ops:
  0.6 5.9 %copy-start.1 = (f32[16,128]{1,0:T(8,128)S(1)}, f32[16,128]{1,0:T(8,128)}, u32[]{:S(2)}) copy-start(f32[16,128]{1,0:T(8,128)} %x_ref.3) | copy-start | bytes 24580
  0.6 5.9 %collective-permute-start.3 = (f32[16,128]{1,0:T(8,128)}, f32[16,128]{1,0:T(8,128)S(1)}, u32[]{:S(2)}, u32[]{:S(2)}) collective-permute-start(f32[16,128]{1,0:T(8,128)} %x_ref.3), channel_id=1, source_target_pairs={{0,4},{4,0},{8,12},{12,8},{16,20},{20,16},{24,28},{28,24},{1,5},{5... | collective-permute-start | bytes 24584 | tf_op jit(solution)/shard_map/share_vectors/ppermute | solution.py:29
  1.2 8.5 %collective-permute-start.2 = (f32[16,128]{1,0:T(8,128)}, f32[16,128]{1,0:T(8,128)S(1)}, u32[]{:S(2)}, u32[]{:S(2)}) collective-permute-start(f32[16,128]{1,0:T(8,128)} %x_ref.3), channel_id=1, source_target_pairs={{0,3},{1,2},{2,1},{3,0},{4,7},{5,6},{6,5},{7,4},{8,11},{9,10},{10,... | collective-permute-start | bytes 24584 | tf_op jit(solution)/shard_map/share_vectors/ppermute | solution.py:29
  5.8 5.0 %collective-permute-start.1 = (f32[16,128]{1,0:T(8,128)}, f32[16,128]{1,0:T(8,128)S(1)}, u32[]{:S(2)}, u32[]{:S(2)}) collective-permute-start(f32[16,128]{1,0:T(8,128)} %x_ref.3), channel_id=1, source_target_pairs={{0,2},{1,3},{2,0},{3,1},{4,6},{5,7},{6,4},{7,5},{8,10},{9,11},{10,... | collective-permute-start | bytes 24584 | tf_op jit(solution)/shard_map/share_vectors/ppermute | solution.py:29
  5.8 5.0 %collective-permute-start = (f32[16,128]{1,0:T(8,128)}, f32[16,128]{1,0:T(8,128)S(1)}, u32[]{:S(2)}, u32[]{:S(2)}) collective-permute-start(f32[16,128]{1,0:T(8,128)} %x_ref.3), channel_id=1, source_target_pairs={{0,1},{1,0},{2,3},{3,2},{4,5},{5,4},{6,7},{7,6},{8,9},{9,8},{10,11... | collective-permute-start | bytes 24584 | tf_op jit(solution)/shard_map/share_vectors/ppermute | solution.py:29
  6.5 7.3 %collective-permute-start.6 = (f32[2,16,128]{2,1,0:T(8,128)S(1)}, f32[2,16,128]{2,1,0:T(8,128)S(1)}, u32[]{:S(2)}, u32[]{:S(2)}) collective-permute-start(f32[2,16,128]{2,1,0:T(8,128)S(1)} %pair.1.refs_4_), channel_id=1, source_target_pairs={{0,24},{4,28},{8,16},{12,20},{16,8},{20,12},{24,0},{28,4},{1,25},{... | collective-permute-start | bytes 49160 | tf_op jit(solution)/shard_map/share_vectors/ppermute | solution.py:29
  9.1 4.7 %collective-permute-start.5 = (f32[2,16,128]{2,1,0:T(8,128)S(1)}, f32[2,16,128]{2,1,0:T(8,128)S(1)}, u32[]{:S(2)}, u32[]{:S(2)}) collective-permute-start(f32[2,16,128]{2,1,0:T(8,128)S(1)} %pair.1.refs_4_), channel_id=1, source_target_pairs={{0,16},{4,20},{8,24},{12,28},{16,0},{20,4},{24,8},{28,12},{1,17},{... | collective-permute-start | bytes 49160 | tf_op jit(solution)/shard_map/share_vectors/ppermute | solution.py:29
  9.7 4.2 %collective-permute-start.4 = (f32[2,16,128]{2,1,0:T(8,128)S(1)}, f32[2,16,128]{2,1,0:T(8,128)S(1)}, u32[]{:S(2)}, u32[]{:S(2)}) collective-permute-start(f32[2,16,128]{2,1,0:T(8,128)S(1)} %pair.1.refs_4_), channel_id=1, source_target_pairs={{0,8},{4,12},{8,0},{12,4},{16,24},{20,28},{24,16},{28,20},{1,9},{5... | collective-permute-start | bytes 49160 | tf_op jit(solution)/shard_map/share_vectors/ppermute | solution.py:29
  10.8 0.7 %copy-start.2 = (s32[1,1,16]{2,1,0:T(1,128)S(1)}, s32[1,1,16]{2,1,0:T(1,128)}, u32[]{:S(2)}) copy-start(s32[1,1,16]{2,1,0:T(1,128)} %arow.3) | copy-start | bytes 196
  10.8 0.7 %copy-start.3 = (s32[1,1,16]{2,1,0:T(1,128)S(1)}, s32[1,1,16]{2,1,0:T(1,128)}, u32[]{:S(2)}) copy-start(s32[1,1,16]{2,1,0:T(1,128)} %bcol.3) | copy-start | bytes 196
  10.8 0.7 %copy-start.4 = (f32[128]{0:T(128)S(1)}, f32[128]{0:T(128)}, u32[]{:S(2)}) copy-start(f32[128]{0:T(128)} %param.7) | copy-start | bytes 1540
  11.5 1.2 %copy-start = (f32[1,1,16,128,128]{4,3,2,1,0:T(8,128)S(1)}, f32[1,1,16,128,128]{4,3,2,1,0:T(8,128)}, u32[]{:S(2)}) copy-start(f32[1,1,16,128,128]{4,3,2,1,0:T(8,128)} %refs_4_.1) | copy-start | bytes 3145732
  16.0 1.3 %collective-permute-start.7 = (f32[72,128]{1,0:T(8,128)S(1)}, f32[72,128]{1,0:T(8,128)S(1)}, u32[]{:S(2)}, u32[]{:S(2)}) collective-permute-start(f32[72,128]{1,0:T(8,128)S(1)} %get-tuple-element.24.mine), channel_id=1, source_target_pairs={{0,4},{4,0},{8,12},{12,8},{16,20},{20,16},{24,28},{28,24},{1,5},{5... | collective-permute-start | bytes 110600 | tf_op jit(solution)/shard_map/return_products/ppermute | solution.py:29
  17.3 3.7 %collective-permute-start.8 = (f32[24,128]{1,0:T(8,128)S(1)}, f32[24,128]{1,0:T(8,128)S(1)}, u32[]{:S(2)}, u32[]{:S(2)}) collective-permute-start(f32[24,128]{1,0:T(8,128)S(1)} %get-tuple-element.26), channel_id=1, source_target_pairs={{0,8},{4,12},{8,0},{12,4},{16,24},{20,28},{24,16},{28,20},{1,9},{5... | collective-permute-start | bytes 36872 | tf_op jit(solution)/shard_map/return_products/ppermute | solution.py:29
  19.0 3.7 %collective-permute-start.9 = (f32[24,128]{1,0:T(8,128)S(1)}, f32[24,128]{1,0:T(8,128)S(1)}, u32[]{:S(2)}, u32[]{:S(2)}) collective-permute-start(f32[24,128]{1,0:T(8,128)S(1)} %get-tuple-element.27), channel_id=1, source_target_pairs={{0,16},{4,20},{8,24},{12,28},{16,0},{20,4},{24,8},{28,12},{1,17},{... | collective-permute-start | bytes 36872 | tf_op jit(solution)/shard_map/return_products/ppermute | solution.py:29
  20.5 4.6 %collective-permute-start.10 = (f32[24,128]{1,0:T(8,128)S(1)}, f32[24,128]{1,0:T(8,128)S(1)}, u32[]{:S(2)}, u32[]{:S(2)}) collective-permute-start(f32[24,128]{1,0:T(8,128)S(1)} %get-tuple-element.28), channel_id=1, source_target_pairs={{0,24},{4,28},{8,16},{12,20},{16,8},{20,12},{24,0},{28,4},{1,25},{... | collective-permute-start | bytes 36872 | tf_op jit(solution)/shard_map/return_products/ppermute | solution.py:29
  25.1 4.5 %collective-permute-start.11 = (f32[24,128]{1,0:T(8,128)S(1)}, f32[24,128]{1,0:T(8,128)S(1)}, u32[]{:S(2)}, u32[]{:S(2)}) collective-permute-start(f32[24,128]{1,0:T(8,128)S(1)} %get-tuple-element.31), channel_id=1, source_target_pairs={{0,1},{1,0},{2,3},{3,2},{4,5},{5,4},{6,7},{7,6},{8,9},{9,8},{10,11... | collective-permute-start | bytes 36872 | tf_op jit(solution)/shard_map/return_products/ppermute | solution.py:29
  26.4 4.6 %collective-permute-start.12 = (f32[24,128]{1,0:T(8,128)S(1)}, f32[24,128]{1,0:T(8,128)S(1)}, u32[]{:S(2)}, u32[]{:S(2)}) collective-permute-start(f32[24,128]{1,0:T(8,128)S(1)} %get-tuple-element.32), channel_id=1, source_target_pairs={{0,2},{1,3},{2,0},{3,1},{4,6},{5,7},{6,4},{7,5},{8,10},{9,11},{10,... | collective-permute-start | bytes 36872 | tf_op jit(solution)/shard_map/return_products/ppermute | solution.py:29
  29.3 5.5 %collective-permute-start.13 = (f32[24,128]{1,0:T(8,128)S(1)}, f32[24,128]{1,0:T(8,128)S(1)}, u32[]{:S(2)}, u32[]{:S(2)}) collective-permute-start(f32[24,128]{1,0:T(8,128)S(1)} %get-tuple-element.33), channel_id=1, source_target_pairs={{0,3},{1,2},{2,1},{3,0},{4,7},{5,6},{6,5},{7,4},{8,11},{9,10},{10,... | collective-permute-start | bytes 36872 | tf_op jit(solution)/shard_map/return_products/ppermute | solution.py:29

commit v11 on v10

v11 whole, which is shorter than its diff:
```python
import functools

import jax
import jax.numpy as jnp
from jax import lax
from jax.experimental import pallas as pl
from jax.experimental.pallas import tpu as pltpu
from jax.sharding import PartitionSpec as P

HP = lax.Precision.HIGHEST
VMEM = pl.BlockSpec(memory_space=pltpu.VMEM)
SMEM = pl.BlockSpec(memory_space=pltpu.SMEM)


def mult(left, right):
    return lax.dot_general(left, right, (((1,), (0,)), ((), ())), precision=HP, preferred_element_type=jnp.float32)


def mult_last(left, right):
    return lax.dot_general(left, right, (((1,), (1,)), ((), ())), precision=HP, preferred_element_type=jnp.float32)


def swap(blocks, axis):
    return lax.all_to_all(blocks, axis, 0, 0, tiled=True)


def trade(value, axis, flip):
    size = lax.axis_size(axis)
    return lax.ppermute(value, axis, [(p, p ^ flip) for p in range(size)])


def own_lanes(nvec, width):
    row = lax.broadcasted_iota(jnp.int32, (nvec, width), 0)
    lane = lax.broadcasted_iota(jnp.int32, (nvec, width), 1)
    return lane // nvec == row % (width // nvec)


def packed_gram(left, right):
    nvec, width = right.shape
    per = width // nvec
    wide = mult_last(left, jnp.concatenate([right] * per, axis=0))
    mask = own_lanes(nvec, width)
    squares = []
    for first in range(0, left.shape[0], nvec):
        own = jnp.where(mask, wide[first : first + nvec], 0.0)
        squares.append(jnp.sum(own.reshape(nvec // per, per, width), axis=1))
    return squares


def unpack(packed, nvec):
    rows, width = packed[0].shape
    per = width // nvec
    lane = lax.broadcasted_iota(jnp.int32, (width, nvec), 0)
    column = lax.broadcasted_iota(jnp.int32, (width, nvec), 1)
    mask = own_lanes(nvec, width)
    wide = []
    for square in packed:
        spread = jnp.concatenate([jnp.broadcast_to(square[g : g + 1], (per, width)) for g in range(rows)], axis=0)
        wide.append(jnp.where(mask, spread, 0.0))
    return mult(jnp.concatenate(wide, axis=0), (lane % nvec == column).astype(jnp.float32))


def split(value):
    first = value.astype(jnp.bfloat16)
    rest = value - first.astype(jnp.float32)
    second = rest.astype(jnp.bfloat16)
    return first, second, (rest - second.astype(jnp.float32)).astype(jnp.bfloat16)


def stack_split(value):
    return jnp.concatenate(split(value), axis=0)


def parts_product(stacked, parts, dims):
    nvec = stacked.shape[0] // 3
    total = None
    for used, part in zip((1, 2, 3), parts[::-1]):
        wide = lax.dot_general(stacked[: used * nvec], part, dims, preferred_element_type=jnp.float32)
        for row in reversed(range(used)):
            piece = wide[row * nvec : (row + 1) * nvec]
            total = piece if total is None else total + piece
    return total


def pair_kernel(x_ref, other, out):
    out[0] = x_ref[...]
    out[1] = other[...]


def column_kernel(n_row, n_col, slots, place, arow, bcol, count, d_ref, *refs):
    x_rows, (tiles, keep, to_core, *parts, rows, sums) = refs[:n_col], refs[n_col:]
    me_row, me_col = place[0], place[1]
    for flip in range(n_col):
        rows[flip] = stack_split(x_rows[flip][...])
    sums[...] = jnp.zeros_like(sums)
    sums[0] = d_ref[...] * x_rows[0][...]
    for slot in range(slots):
        pieces = split(tiles[0, 0, slot])
        for part, piece in zip(parts, pieces):
            part[slot] = piece
        block = jnp.where(slot < count[0, 0], bcol[0, 0, slot] ^ me_row, n_row)
        sums[block] += parts_product(rows[arow[0, 0, slot] ^ me_col], pieces, (((1,), (0,)), ((), ())))
    for chip in range(n_row // 2):
        keep[chip] = sums[2 * chip]
        to_core[chip] = sums[2 * chip + 1]


def row_kernel(n_row, n_col, slots, place, arow, bcol, count, *refs):
    x_pairs, refs = refs[: n_row // 2], refs[n_row // 2 :]
    parts, outs, (cols, sums) = refs[:3], refs[3:-2], refs[-2:]
    me_row, me_col = place[0], place[1]
    for flip in range(n_row):
        cols[flip] = stack_split(x_pairs[flip // 2][flip % 2])
    sums[...] = jnp.zeros_like(sums)
    for slot in range(slots):
        block = jnp.where(slot < count[0, 0], arow[0, 0, slot] ^ me_col, n_col)
        pieces = [part[slot] for part in parts]
        sums[block] += parts_product(cols[bcol[0, 0, slot] ^ me_row], pieces, (((1,), (1,)), ((), ())))
    for flip, out in enumerate(outs):
        out[...] = sums[flip]


def chip_kernel(mine, other, *outs):
    for chip, out in enumerate(outs):
        out[...] = mine[chip] + other[chip]


def product_kernel(x_ref, *refs):
    parts, (product, out) = refs[:-2], refs[-2:]
    own = x_ref[...]
    total = parts[0][...]
    for part in parts[1:]:
        total += part[...]
    product[...] = total
    squares = packed_gram(jnp.concatenate([own, total], axis=0), total) + packed_gram(own, own)
    for block in range(out.shape[0]):
        for which, square in enumerate(squares):
            out[block, which] = square


def result_kernel(scale, x_ref, product, parts, residual, rayleigh, gram, sound):
    own = x_ref[...]
    nvec = own.shape[0]
    sums = jnp.sum(parts[...], axis=0)
    squares = unpack([sums[which] for which in range(3)], nvec) * scale
    ray, outer, inner = squares[:nvec], squares[nvec : 2 * nvec], squares[2 * nvec :]
    rayleigh[...] = ray
    residual[...] = product[...] - mult(ray, own)
    twice = mult(ray, ray)
    lifted = mult_last(mult(ray, inner), ray)
    result = outer - (twice + twice.T) + lifted
    gram[...] = result
    diagonal = lax.broadcasted_iota(jnp.int32, (nvec, nvec), 0) == lax.broadcasted_iota(jnp.int32, (nvec, nvec), 1)
    margin = jnp.sum(jnp.where(diagonal, 64.0 * result - (outer + lifted), 0.0))
    sound[0, 0] = (margin >= 0.0).astype(jnp.int32)


def gram_parts_kernel(residual, out):
    square = packed_gram(residual[...], residual[...])[0]
    for block in range(out.shape[0]):
        out[block] = square


def gram_kernel(scale, parts, out):
    out[...] = unpack([jnp.sum(parts[...], axis=0)], out.shape[0]) * scale


def per_device(vectors, diagonal_energy, tiles, tile_rows, tile_cols, tile_count):
    n_row = lax.axis_size("row")
    n_col = lax.axis_size("col")
    devices = n_row * n_col
    nvec, width = vectors.shape
    slots = tiles.shape[2]
    scale = 1.0 / float(devices * width)
    n_chip = n_row // 2
    packed_rows = nvec * nvec // width
    block = jax.ShapeDtypeStruct((nvec, width), jnp.float32)
    blocks = jax.ShapeDtypeStruct((n_chip, nvec, width), jnp.float32)
    square = jax.ShapeDtypeStruct((nvec, nvec), jnp.float32)
    part = jax.ShapeDtypeStruct((slots, width, width), jnp.bfloat16)
    place = jnp.stack([lax.axis_index("row"), lax.axis_index("col")]).astype(jnp.int32)
    energy = diagonal_energy.reshape(1, width)
    params = pltpu.CompilerParams(vmem_limit_bytes=16 * 2**20)
    cost = pl.CostEstimate(flops=12 * slots * nvec * width * width, bytes_accessed=2**20, transcendentals=0)
    with jax.named_scope("share_vectors"):
        other = trade(vectors, "row", 1)
        x_rows = [vectors] + [trade(vectors, "col", flip) for flip in range(1, n_col)]
        pair = pl.pallas_call(
            pair_kernel,
            out_shape=jax.ShapeDtypeStruct((2, nvec, width), jnp.float32),
            in_specs=[VMEM] * 2,
            out_specs=VMEM,
            compiler_params=params,
            name="pair",
        )(vectors, other)
        x_pairs = [pair] + [trade(pair, "row", 2 * chip) for chip in range(1, n_chip)]
    with jax.named_scope("column_terms"):
        keep, to_core, *parts = pl.pallas_call(
            functools.partial(column_kernel, n_row, n_col, slots),
            out_shape=[blocks, blocks, part, part, part],
            in_specs=[SMEM] * 4 + [VMEM] * (n_col + 2),
            out_specs=[VMEM] * 5,
            scratch_shapes=[
                pltpu.VMEM((n_col, 3 * nvec, width), jnp.bfloat16),
                pltpu.VMEM((n_row + 1, nvec, width), jnp.float32),
            ],
            compiler_params=params,
            cost_estimate=cost,
            name="column_terms",
        )(place, tile_rows, tile_cols, tile_count, energy, *x_rows, tiles)
        from_core = trade(to_core, "row", 1)
    with jax.named_scope("row_terms"):
        row_terms = pl.pallas_call(
            functools.partial(row_kernel, n_row, n_col, slots),
            out_shape=[block] * n_col,
            in_specs=[SMEM] * 4 + [VMEM] * (n_chip + 3),
            out_specs=[VMEM] * n_col,
            scratch_shapes=[
                pltpu.VMEM((n_row, 3 * nvec, width), jnp.bfloat16),
                pltpu.VMEM((n_col + 1, nvec, width), jnp.float32),
            ],
            compiler_params=params,
            cost_estimate=cost,
            name="row_terms",
        )(place, tile_rows, tile_cols, tile_count, *x_pairs, *parts)
    with jax.named_scope("return_products"):
        sums = [row_terms[0]] + [trade(row_terms[flip], "col", flip) for flip in range(1, n_col)]
        chips = pl.pallas_call(
            chip_kernel,
            out_shape=[block] * n_chip,
            in_specs=[VMEM] * 2,
            out_specs=[VMEM] * n_chip,
            compiler_params=params,
            name="chip_sum",
        )(keep, from_core)
        sums += [chips[0]] + [trade(chips[chip], "row", 2 * chip) for chip in range(1, n_chip)]
    with jax.named_scope("product"):
        product, squares = pl.pallas_call(
            product_kernel,
            out_shape=[block, jax.ShapeDtypeStruct((devices, 3, packed_rows, width), jnp.float32)],
            in_specs=[VMEM] * (1 + n_col + n_chip),
            out_specs=[VMEM] * 2,
            compiler_params=params,
            name="product",
        )(vectors, *sums)
    with jax.named_scope("results"):
        residual, rayleigh, gram, sound = pl.pallas_call(
            functools.partial(result_kernel, scale),
            out_shape=[block, square, square, jax.ShapeDtypeStruct((1, 1), jnp.int32)],
            in_specs=[VMEM] * 3,
            out_specs=[VMEM] * 3 + [SMEM],
            compiler_params=params,
            name="results",
        )(vectors, product, swap(squares, ("row", "col")))

    def from_residual(residual, gram):
        parts = pl.pallas_call(
            gram_parts_kernel,
            out_shape=jax.ShapeDtypeStruct((devices, packed_rows, width), jnp.float32),
            in_specs=[VMEM],
            out_specs=VMEM,
            compiler_params=params,
            name="gram_parts",
        )(residual)
        return pl.pallas_call(
            functools.partial(gram_kernel, scale),
            out_shape=square,
            in_specs=[VMEM],
            out_specs=VMEM,
            compiler_params=params,
            name="gram_sum",
        )(swap(parts, ("row", "col")))

    with jax.named_scope("gram"):
        gram = lax.cond(sound[0, 0] > 0, lambda residual, gram: gram, from_residual, residual, gram)
    return (residual, rayleigh, gram)


def solution(mesh):
    return jax.shard_map(
        per_device,
        mesh=mesh,
        in_specs=(
            P(None, ("row", "col")),
            P(("row", "col")),
            P("row", "col", None, None, None),
            P("row", "col", None),
            P("row", "col", None),
            P("row", "col"),
        ),
        out_specs=(P(None, ("row", "col")), P(), P()),
        check_vma=False,
    )
```

time: 45.8 us -> 46.1 us (level)
  blocking collectives: 8.97 us -> 10.6 us
  waiting for transfers between devices: 10.7 us -> 9.67 us
  Pallas kernels: 5.11 us -> 4.26 us
  between operations: 1.41 us -> 2.08 us
    all_to_all x1, blocking collectives: 8.97 us -> 10.6 us  [swap(): return lax.all_to_all(blocks, axis, 0, 0, tiled=True)]
    ppermute x14, waiting for transfers between devices: 10.7 us -> 9.67 us  [trade(): return lax.ppermute(value, axis, [(p, p ^ flip) for p in range(size)])]
    pallas_call x1, Pallas kernels: 2.19 us -> 1.58 us  [per_device(): pl.pallas_call(functools.partial(row_kernel, n_row, n_col, slots), out_sh...]
    pallas_call x4 -> x3, Pallas kernels: 1.83 us -> 1.56 us  [the longest x1 1.21 us: per_device(): pl.pallas_call(functools.partial(result_kernel, scale), out_shape=[block,...]
    unnamed x10 -> x12, local copies, waits for them, and re-layouts: 1.87 us -> 1.84 us
  transfers between devices with their start and end apart: 14 -> 14, of which waited for: 6 -> 8; matrix products, arithmetic and copies ran while one was open for 0% -> 0% of each run, Pallas kernels for 2% -> 6%
where the time goes in v11:
time: 46.1 us; the launch traced here: 45.9 us
  starting transfers between devices  17.4 us (38%)
  blocking collectives  10.6 us (23%)
  waiting for transfers between devices  9.67 us (21%)
  Pallas kernels  4.26 us (9%)
  between operations  2.08 us (5%)
  local copies, waits for them, and re-layouts  1.84 us (4%)
    ppermute x14, starting transfers between devices, trade(): return lax.ppermute(value, axis, [(p, p ^ flip) for p in range(size)])  17.4 us
    all_to_all x1, blocking collectives, swap(): return lax.all_to_all(blocks, axis, 0, 0, tiled=True)  10.6 us
    ppermute x14, waiting for transfers between devices, trade(): return lax.ppermute(value, axis, [(p, p ^ flip) for p in range(size)])  9.67 us
    unnamed x12, local copies, waits for them, and re-layouts  1.84 us
    pallas_call x1, Pallas kernels, per_device(): pl.pallas_call(functools.partial(row_kernel, n_row, n_col, slots), out_sh...  1.58 us
    pallas_call x1, Pallas kernels, per_device(): pl.pallas_call(functools.partial(result_kernel, scale), out_shape=[block,...  1.21 us
    pallas_call x1, Pallas kernels, per_device(): pl.pallas_call(functools.partial(column_kernel, n_row, n_col, slots), out...  1.11 us
  transfers between devices with their start and end apart: 14, of which 8 were waited for; matrix products, arithmetic and copies ran while one was open for 0% of the time, Pallas kernels for 6%

profile of v11, /device:TPU:0, one launch (start us, length us, event | category | flops | bytes accessed | tf_op | source)
XLA Modules:
  0.0 45.9 jit_solution(12956842901949646419)
XLA Ops:
  0.6 5.1 %collective-permute-start.6 = (f32[16,128]{1,0:T(8,128)}, f32[16,128]{1,0:T(8,128)S(1)}, u32[]{:S(2)}, u32[]{:S(2)}) collective-permute-start(f32[16,128]{1,0:T(8,128)} %x_ref.5), channel_id=1, source_target_pairs={{0,3},{1,2},{2,1},{3,0},{4,7},{5,6},{6,5},{7,4},{8,11},{9,10},{10,... | collective-permute-start | bytes 24584 | tf_op jit(solution)/shard_map/share_vectors/ppermute | solution.py:29
  5.7 0.0 collective-permute-start.5
  5.7 0.6 %collective-permute-start.4 = (f32[16,128]{1,0:T(8,128)}, f32[16,128]{1,0:T(8,128)S(1)}, u32[]{:S(2)}, u32[]{:S(2)}) collective-permute-start(f32[16,128]{1,0:T(8,128)} %x_ref.5), channel_id=1, source_target_pairs={{0,1},{1,0},{2,3},{3,2},{4,5},{5,4},{6,7},{7,6},{8,9},{9,8},{10,11... | collective-permute-start | bytes 24584 | tf_op jit(solution)/shard_map/share_vectors/ppermute | solution.py:29
  6.4 0.0 collective-permute-start
  6.4 0.0 copy-start.1
  6.4 0.1 pad_add_fusion.place
  7.1 0.0 copy-start.2
  7.1 0.0 copy-start.3
  7.1 0.0 copy-start.4
  7.2 0.4 collective-permute-done.6.refs_3_
  7.6 2.9 %collective-permute-done.5.refs_2_ = f32[16,128]{1,0:T(8,128)S(1)} collective-permute-done((f32[16,128]{1,0:T(8,128)}, f32[16,128]{1,0:T(8,128)S(1)}, u32[]{:S(2)}, u32[]{:S(2)}) %collective-permute-start.5) | collective-permute-done | bytes 8224 | tf_op jit(solution)/shard_map/share_vectors/ppermute | solution.py:29
  10.5 0.0 collective-permute-done.4.refs_1_
  10.5 0.0 copy-done.1
  10.5 0.0 copy-done.2
  10.5 0.0 copy-done.3
  10.5 0.0 copy-done.4
  10.5 0.0 copy-start
  10.5 1.2 %copy-done = f32[1,1,16,128,128]{4,3,2,1,0:T(8,128)S(1)} copy-done((f32[1,1,16,128,128]{4,3,2,1,0:T(8,128)S(1)}, f32[1,1,16,128,128]{4,3,2,1,0:T(8,128)}, u32[]{:S(2)}) %copy-start) | copy-done | bytes 1048600
  11.8 1.1 %column_terms.1 = (f32[4,16,128]{2,1,0:T(8,128)S(1)}, f32[4,16,128]{2,1,0:T(8,128)S(1)}, bf16[16,128,128]{2,1,0:T(8,128)(2,1)S(1)}, bf16[16,128,128]{2,1,0:T(8,128)(2,1)S(1)}, bf16[16,128,128]{2,1,0:T(8,128)(2,1)S(1)}) custom-call(s32[2]{0:T(128)S(1)} %pad_add_fusion.place, s32[1,1,16]{2,1,0:T(1,128)S(1)} %copy-done.2, s32[1,1,16]{2,1,0:T(1,128)S(1)} %copy-done.3, ...), custom_call_target="tpu_custom_call" | custom-call | flops 50331648 | bytes 1048576 | tf_op jit(solution)/shard_map/column_terms/column_terms/pallas_call | solution.py:198
  12.9 0.1 collective-permute-start.10
  13.0 0.0 collective-permute-done.other
  13.0 2.5 %collective-permute-start.3 = (f32[2,16,128]{2,1,0:T(8,128)S(1)}, f32[2,16,128]{2,1,0:T(8,128)S(1)}, u32[]{:S(2)}, u32[]{:S(2)}) collective-permute-start(f32[2,16,128]{2,1,0:T(8,128)S(1)} %pair.1.refs_0_), channel_id=1, source_target_pairs={{0,24},{4,28},{8,16},{12,20},{16,8},{20,12},{24,0},{28,4},{1,25},{... | collective-permute-start | bytes 49160 | tf_op jit(solution)/shard_map/share_vectors/ppermute | solution.py:29
  15.5 0.5 %collective-permute-start.2 = (f32[2,16,128]{2,1,0:T(8,128)S(1)}, f32[2,16,128]{2,1,0:T(8,128)S(1)}, u32[]{:S(2)}, u32[]{:S(2)}) collective-permute-start(f32[2,16,128]{2,1,0:T(8,128)S(1)} %pair.1.refs_0_), channel_id=1, source_target_pairs={{0,16},{4,20},{8,24},{12,28},{16,0},{20,4},{24,8},{28,12},{1,17},{... | collective-permute-start | bytes 49160 | tf_op jit(solution)/shard_map/share_vectors/ppermute | solution.py:29
  16.0 0.5 %collective-permute-start.1 = (f32[2,16,128]{2,1,0:T(8,128)S(1)}, f32[2,16,128]{2,1,0:T(8,128)S(1)}, u32[]{:S(2)}, u32[]{:S(2)}) collective-permute-start(f32[2,16,128]{2,1,0:T(8,128)S(1)} %pair.1.refs_0_), channel_id=1, source_target_pairs={{0,8},{4,12},{8,0},{12,4},{16,24},{20,28},{24,16},{28,20},{1,9},{5... | collective-permute-start | bytes 49160 | tf_op jit(solution)/shard_map/share_vectors/ppermute | solution.py:29
  16.5 1.1 %collective-permute-done.3.refs_3_ = f32[2,16,128]{2,1,0:T(8,128)S(1)} collective-permute-done((f32[2,16,128]{2,1,0:T(8,128)S(1)}, f32[2,16,128]{2,1,0:T(8,128)S(1)}, u32[]{:S(2)}, u32[]{:S(2)}) %collective-permute-start.3) | collective-permute-done | bytes 16416 | tf_op jit(solution)/shard_map/share_vectors/ppermute | solution.py:29
  17.7 1.5 %collective-permute-done.2.refs_2_ = f32[2,16,128]{2,1,0:T(8,128)S(1)} collective-permute-done((f32[2,16,128]{2,1,0:T(8,128)S(1)}, f32[2,16,128]{2,1,0:T(8,128)S(1)}, u32[]{:S(2)}, u32[]{:S(2)}) %collective-permute-start.2) | collective-permute-done | bytes 16416 | tf_op jit(solution)/shard_map/share_vectors/ppermute | solution.py:29
  19.2 0.5 %collective-permute-done.1.refs_1_ = f32[2,16,128]{2,1,0:T(8,128)S(1)} collective-permute-done((f32[2,16,128]{2,1,0:T(8,128)S(1)}, f32[2,16,128]{2,1,0:T(8,128)S(1)}, u32[]{:S(2)}, u32[]{:S(2)}) %collective-permute-start.1) | collective-permute-done | bytes 16416 | tf_op jit(solution)/shard_map/share_vectors/ppermute | solution.py:29
  19.7 1.6 %row_terms.1 = (f32[16,128]{1,0:T(8,128)S(1)}, f32[16,128]{1,0:T(8,128)S(1)}, f32[16,128]{1,0:T(8,128)S(1)}, f32[16,128]{1,0:T(8,128)S(1)}) custom-call(s32[2]{0:T(128)S(1)} %pad_add_fusion.place, s32[1,1,16]{2,1,0:T(1,128)S(1)} %copy-done.2, s32[1,1,16]{2,1,0:T(1,128)S(1)} %copy-done.3, s32[1,1]{1,0:T(1,128)S(6)} %copy.11.count, ...), custom_call_target="tpu_custom_call" | custom-call | flops 50331648 | bytes 1048576 | tf_op jit(solution)/shard_map/row_terms/row_terms/pallas_call | solution.py:213
  21.3 0.1 collective-permute-start.7
  21.4 2.1 %collective-permute-start.8 = (f32[16,128]{1,0:T(8,128)S(1)}, f32[16,128]{1,0:T(8,128)S(1)}, u32[]{:S(2)}, u32[]{:S(2)}) collective-permute-start(f32[16,128]{1,0:T(8,128)S(1)} %get-tuple-element.32), channel_id=1, source_target_pairs={{0,2},{1,3},{2,0},{3,1},{4,6},{5,7},{6,4},{7,5},{8,10},{9,11},{10,... | collective-permute-start | bytes 24584 | tf_op jit(solution)/shard_map/return_products/ppermute | solution.py:29
  23.5 2.3 %collective-permute-start.9 = (f32[16,128]{1,0:T(8,128)S(1)}, f32[16,128]{1,0:T(8,128)S(1)}, u32[]{:S(2)}, u32[]{:S(2)}) collective-permute-start(f32[16,128]{1,0:T(8,128)S(1)} %get-tuple-element.33), channel_id=1, source_target_pairs={{0,3},{1,2},{2,1},{3,0},{4,7},{5,6},{6,5},{7,4},{8,11},{9,10},{10,... | collective-permute-start | bytes 24584 | tf_op jit(solution)/shard_map/return_products/ppermute | solution.py:29
  25.8 0.0 collective-permute-done.10.other
  25.8 0.6 %collective-permute-start.11 = (f32[16,128]{1,0:T(8,128)S(1)}, f32[16,128]{1,0:T(8,128)S(1)}, u32[]{:S(2)}, u32[]{:S(2)}) collective-permute-start(f32[16,128]{1,0:T(8,128)S(1)} %get-tuple-element.37), channel_id=1, source_target_pairs={{0,8},{4,12},{8,0},{12,4},{16,24},{20,28},{24,16},{28,20},{1,9},{5... | collective-permute-start | bytes 24584 | tf_op jit(solution)/shard_map/return_products/ppermute | solution.py:29
  26.4 1.5 %collective-permute-start.12 = (f32[16,128]{1,0:T(8,128)S(1)}, f32[16,128]{1,0:T(8,128)S(1)}, u32[]{:S(2)}, u32[]{:S(2)}) collective-permute-start(f32[16,128]{1,0:T(8,128)S(1)} %get-tuple-element.38), channel_id=1, source_target_pairs={{0,16},{4,20},{8,24},{12,28},{16,0},{20,4},{24,8},{28,12},{1,17},{... | collective-permute-start | bytes 24584 | tf_op jit(solution)/shard_map/return_products/ppermute | solution.py:29
  27.9 0.0 collective-permute-done.7.refs_1_
  27.9 1.4 %collective-permute-start.13 = (f32[16,128]{1,0:T(8,128)S(1)}, f32[16,128]{1,0:T(8,128)S(1)}, u32[]{:S(2)}, u32[]{:S(2)}) collective-permute-start(f32[16,128]{1,0:T(8,128)S(1)} %get-tuple-element.39), channel_id=1, source_target_pairs={{0,24},{4,28},{8,16},{12,20},{16,8},{20,12},{24,0},{28,4},{1,25},{... | collective-permute-start | bytes 24584 | tf_op jit(solution)/shard_map/return_products/ppermute | solution.py:29
  29.4 0.0 collective-permute-done.8.refs_2_
  29.4 0.0 collective-permute-done.9.refs_3_
  29.4 0.2 collective-permute-done.11.refs_5_
  29.5 0.5 %collective-permute-done.12.refs_6_ = f32[16,128]{1,0:T(8,128)S(1)} collective-permute-done((f32[16,128]{1,0:T(8,128)S(1)}, f32[16,128]{1,0:T(8,128)S(1)}, u32[]{:S(2)}, u32[]{:S(2)}) %collective-permute-start.12) | collective-permute-done | bytes 8224 | tf_op jit(solution)/shard_map/return_products/ppermute | solution.py:29
  30.1 2.4 %collective-permute-done.13.refs_7_ = f32[16,128]{1,0:T(8,128)S(1)} collective-permute-done((f32[16,128]{1,0:T(8,128)S(1)}, f32[16,128]{1,0:T(8,128)S(1)}, u32[]{:S(2)}, u32[]{:S(2)}) %collective-permute-start.13) | collective-permute-done | bytes 8224 | tf_op jit(solution)/shard_map/return_products/ppermute | solution.py:29
  32.5 0.3 product.1
  32.8 10.6 %all_to_all.10.parts = f32[32,3,2,128]{3,2,1,0:T(2,128)S(1)} all-to-all(f32[32,3,2,128]{3,2,1,0:T(2,128)S(1)} %get-tuple-element.41), channel_id=1, replica_groups=mesh['row'=8,'col'=4] {'row','col'}, dimensions={0} | all-to-all | bytes 196608 | tf_op jit(solution)/shard_map/results/all_to_all | solution.py:24
  43.4 1.2 %results.1 = (f32[16,128]{1,0:T(8,128)}, f32[16,16]{1,0:T(8,128)}, f32[16,16]{1,0:T(8,128)S(1)}, s32[1,1]{1,0:T(1,128)}) custom-call(f32[16,128]{1,0:T(8,128)S(1)} %copy-done.1, f32[16,128]{1,0:T(8,128)S(1)} %get-tuple-element.40.product, f32[32,3,2,128]{3,2,1,0:T(2,128)S(1)} %all_to_all.10.parts), custom_call_target="tpu_custom_call" | custom-call | tf_op jit(solution)/shard_map/results/results/pallas_call | solution.py:247
  45.3 0.0 copy-start.5
  45.3 0.6 %copy-done.5 = f32[16,16]{1,0:T(8,128)} copy-done((f32[16,16]{1,0:T(8,128)}, f32[16,16]{1,0:T(8,128)S(1)}, u32[]{:S(2)}) %copy-start.5) | copy-done | bytes 1048
  (3 shorter events, 0.0 us)
Async XLA Ops:
  0.6 7.0 %collective-permute-start.6 = (f32[16,128]{1,0:T(8,128)}, f32[16,128]{1,0:T(8,128)S(1)}, u32[]{:S(2)}, u32[]{:S(2)}) collective-permute-start(f32[16,128]{1,0:T(8,128)} %x_ref.5), channel_id=1, source_target_pairs={{0,3},{1,2},{2,1},{3,0},{4,7},{5,6},{6,5},{7,4},{8,11},{9,10},{10,... | collective-permute-start | bytes 24584 | tf_op jit(solution)/shard_map/share_vectors/ppermute | solution.py:29
  5.7 4.8 %collective-permute-start.5 = (f32[16,128]{1,0:T(8,128)}, f32[16,128]{1,0:T(8,128)S(1)}, u32[]{:S(2)}, u32[]{:S(2)}) collective-permute-start(f32[16,128]{1,0:T(8,128)} %x_ref.5), channel_id=1, source_target_pairs={{0,2},{1,3},{2,0},{3,1},{4,6},{5,7},{6,4},{7,5},{8,10},{9,11},{10,... | collective-permute-start | bytes 24584 | tf_op jit(solution)/shard_map/share_vectors/ppermute | solution.py:29
  5.7 4.8 %collective-permute-start.4 = (f32[16,128]{1,0:T(8,128)}, f32[16,128]{1,0:T(8,128)S(1)}, u32[]{:S(2)}, u32[]{:S(2)}) collective-permute-start(f32[16,128]{1,0:T(8,128)} %x_ref.5), channel_id=1, source_target_pairs={{0,1},{1,0},{2,3},{3,2},{4,5},{5,4},{6,7},{7,6},{8,9},{9,8},{10,11... | collective-permute-start | bytes 24584 | tf_op jit(solution)/shard_map/share_vectors/ppermute | solution.py:29
  6.4 6.6 %collective-permute-start = (f32[16,128]{1,0:T(8,128)}, f32[16,128]{1,0:T(8,128)S(1)}, u32[]{:S(2)}, u32[]{:S(2)}) collective-permute-start(f32[16,128]{1,0:T(8,128)} %x_ref.5), channel_id=1, source_target_pairs={{0,4},{4,0},{8,12},{12,8},{16,20},{20,16},{24,28},{28,24},{1,5},{5... | collective-permute-start | bytes 24584 | tf_op jit(solution)/shard_map/share_vectors/ppermute | solution.py:29
  6.4 4.1 %copy-start.1 = (f32[16,128]{1,0:T(8,128)S(1)}, f32[16,128]{1,0:T(8,128)}, u32[]{:S(2)}) copy-start(f32[16,128]{1,0:T(8,128)} %x_ref.5) | copy-start | bytes 24580
  7.1 3.4 %copy-start.2 = (s32[1,1,16]{2,1,0:T(1,128)S(1)}, s32[1,1,16]{2,1,0:T(1,128)}, u32[]{:S(2)}) copy-start(s32[1,1,16]{2,1,0:T(1,128)} %arow.3) | copy-start | bytes 196
  7.1 3.4 %copy-start.3 = (s32[1,1,16]{2,1,0:T(1,128)S(1)}, s32[1,1,16]{2,1,0:T(1,128)}, u32[]{:S(2)}) copy-start(s32[1,1,16]{2,1,0:T(1,128)} %bcol.3) | copy-start | bytes 196
  7.1 3.4 %copy-start.4 = (f32[128]{0:T(128)S(1)}, f32[128]{0:T(128)}, u32[]{:S(2)}) copy-start(f32[128]{0:T(128)} %param.9) | copy-start | bytes 1540
  10.5 1.2 %copy-start = (f32[1,1,16,128,128]{4,3,2,1,0:T(8,128)S(1)}, f32[1,1,16,128,128]{4,3,2,1,0:T(8,128)}, u32[]{:S(2)}) copy-start(f32[1,1,16,128,128]{4,3,2,1,0:T(8,128)} %refs_4_.1) | copy-start | bytes 3145732
  12.9 12.9 %collective-permute-start.10 = (f32[4,16,128]{2,1,0:T(8,128)S(1)}, f32[4,16,128]{2,1,0:T(8,128)S(1)}, u32[]{:S(2)}, u32[]{:S(2)}) collective-permute-start(f32[4,16,128]{2,1,0:T(8,128)S(1)} %get-tuple-element.35), channel_id=1, source_target_pairs={{0,4},{4,0},{8,12},{12,8},{16,20},{20,16},{24,28},{28,24},{1,5},{5... | collective-permute-start | bytes 98312 | tf_op jit(solution)/shard_map/column_terms/ppermute | solution.py:29
  13.0 4.7 %collective-permute-start.3 = (f32[2,16,128]{2,1,0:T(8,128)S(1)}, f32[2,16,128]{2,1,0:T(8,128)S(1)}, u32[]{:S(2)}, u32[]{:S(2)}) collective-permute-start(f32[2,16,128]{2,1,0:T(8,128)S(1)} %pair.1.refs_0_), channel_id=1, source_target_pairs={{0,24},{4,28},{8,16},{12,20},{16,8},{20,12},{24,0},{28,4},{1,25},{... | collective-permute-start | bytes 49160 | tf_op jit(solution)/shard_map/share_vectors/ppermute | solution.py:29
  15.5 3.7 %collective-permute-start.2 = (f32[2,16,128]{2,1,0:T(8,128)S(1)}, f32[2,16,128]{2,1,0:T(8,128)S(1)}, u32[]{:S(2)}, u32[]{:S(2)}) collective-permute-start(f32[2,16,128]{2,1,0:T(8,128)S(1)} %pair.1.refs_0_), channel_id=1, source_target_pairs={{0,16},{4,20},{8,24},{12,28},{16,0},{20,4},{24,8},{28,12},{1,17},{... | collective-permute-start | bytes 49160 | tf_op jit(solution)/shard_map/share_vectors/ppermute | solution.py:29
  16.0 3.7 %collective-permute-start.1 = (f32[2,16,128]{2,1,0:T(8,128)S(1)}, f32[2,16,128]{2,1,0:T(8,128)S(1)}, u32[]{:S(2)}, u32[]{:S(2)}) collective-permute-start(f32[2,16,128]{2,1,0:T(8,128)S(1)} %pair.1.refs_0_), channel_id=1, source_target_pairs={{0,8},{4,12},{8,0},{12,4},{16,24},{20,28},{24,16},{28,20},{1,9},{5... | collective-permute-start | bytes 49160 | tf_op jit(solution)/shard_map/share_vectors/ppermute | solution.py:29
  21.3 6.6 %collective-permute-start.7 = (f32[16,128]{1,0:T(8,128)S(1)}, f32[16,128]{1,0:T(8,128)S(1)}, u32[]{:S(2)}, u32[]{:S(2)}) collective-permute-start(f32[16,128]{1,0:T(8,128)S(1)} %get-tuple-element.31), channel_id=1, source_target_pairs={{0,1},{1,0},{2,3},{3,2},{4,5},{5,4},{6,7},{7,6},{8,9},{9,8},{10,11... | collective-permute-start | bytes 24584 | tf_op jit(solution)/shard_map/return_products/ppermute | solution.py:29
  21.4 7.9 %collective-permute-start.8 = (f32[16,128]{1,0:T(8,128)S(1)}, f32[16,128]{1,0:T(8,128)S(1)}, u32[]{:S(2)}, u32[]{:S(2)}) collective-permute-start(f32[16,128]{1,0:T(8,128)S(1)} %get-tuple-element.32), channel_id=1, source_target_pairs={{0,2},{1,3},{2,0},{3,1},{4,6},{5,7},{6,4},{7,5},{8,10},{9,11},{10,... | collective-permute-start | bytes 24584 | tf_op jit(solution)/shard_map/return_products/ppermute | solution.py:29
  23.5 5.9 %collective-permute-start.9 = (f32[16,128]{1,0:T(8,128)S(1)}, f32[16,128]{1,0:T(8,128)S(1)}, u32[]{:S(2)}, u32[]{:S(2)}) collective-permute-start(f32[16,128]{1,0:T(8,128)S(1)} %get-tuple-element.33), channel_id=1, source_target_pairs={{0,3},{1,2},{2,1},{3,0},{4,7},{5,6},{6,5},{7,4},{8,11},{9,10},{10,... | collective-permute-start | bytes 24584 | tf_op jit(solution)/shard_map/return_products/ppermute | solution.py:29
  25.8 3.7 %collective-permute-start.11 = (f32[16,128]{1,0:T(8,128)S(1)}, f32[16,128]{1,0:T(8,128)S(1)}, u32[]{:S(2)}, u32[]{:S(2)}) collective-permute-start(f32[16,128]{1,0:T(8,128)S(1)} %get-tuple-element.37), channel_id=1, source_target_pairs={{0,8},{4,12},{8,0},{12,4},{16,24},{20,28},{24,16},{28,20},{1,9},{5... | collective-permute-start | bytes 24584 | tf_op jit(solution)/shard_map/return_products/ppermute | solution.py:29
  26.4 3.7 %collective-permute-start.12 = (f32[16,128]{1,0:T(8,128)S(1)}, f32[16,128]{1,0:T(8,128)S(1)}, u32[]{:S(2)}, u32[]{:S(2)}) collective-permute-start(f32[16,128]{1,0:T(8,128)S(1)} %get-tuple-element.38), channel_id=1, source_target_pairs={{0,16},{4,20},{8,24},{12,28},{16,0},{20,4},{24,8},{28,12},{1,17},{... | collective-permute-start | bytes 24584 | tf_op jit(solution)/shard_map/return_products/ppermute | solution.py:29
  27.9 4.6 %collective-permute-start.13 = (f32[16,128]{1,0:T(8,128)S(1)}, f32[16,128]{1,0:T(8,128)S(1)}, u32[]{:S(2)}, u32[]{:S(2)}) collective-permute-start(f32[16,128]{1,0:T(8,128)S(1)} %get-tuple-element.39), channel_id=1, source_target_pairs={{0,24},{4,28},{8,16},{12,20},{16,8},{20,12},{24,0},{28,4},{1,25},{... | collective-permute-start | bytes 24584 | tf_op jit(solution)/shard_map/return_products/ppermute | solution.py:29
  45.3 0.6 %copy-start.5 = (f32[16,16]{1,0:T(8,128)}, f32[16,16]{1,0:T(8,128)S(1)}, u32[]{:S(2)}) copy-start(f32[16,16]{1,0:T(8,128)S(1)} %get-tuple-element.46) | copy-start | bytes 3076

commit v12 on v11

--- a/solution.py
+++ b/solution.py
@@ -88,7 +88,7 @@
 
 
 def column_kernel(n_row, n_col, slots, place, arow, bcol, count, d_ref, *refs):
-    x_rows, (tiles, keep, to_core, *parts, rows, sums) = refs[:n_col], refs[n_col:]
+    x_rows, (tiles, even, odd, *parts, rows, sums) = refs[:n_col], refs[n_col:]
     me_row, me_col = place[0], place[1]
     for flip in range(n_col):
         rows[flip] = stack_split(x_rows[flip][...])
@@ -101,13 +101,14 @@
         block = jnp.where(slot < count[0, 0], bcol[0, 0, slot] ^ me_row, n_row)
         sums[block] += parts_product(rows[arow[0, 0, slot] ^ me_col], pieces, (((1,), (0,)), ((), ())))
     for chip in range(n_row // 2):
-        keep[chip] = sums[2 * chip]
-        to_core[chip] = sums[2 * chip + 1]
+        even[chip] = sums[2 * chip]
+        odd[chip] = sums[2 * chip + 1]
 
 
 def row_kernel(n_row, n_col, slots, place, arow, bcol, count, *refs):
     x_pairs, refs = refs[: n_row // 2], refs[n_row // 2 :]
-    parts, outs, (cols, sums) = refs[:3], refs[3:-2], refs[-2:]
+    (odd, *parts), (to_core, *outs), (cols, sums) = refs[:4], refs[4:-2], refs[-2:]
+    to_core[...] = odd[...]
     me_row, me_col = place[0], place[1]
     for flip in range(n_row):
         cols[flip] = stack_split(x_pairs[flip // 2][flip % 2])
@@ -195,7 +196,7 @@
         )(vectors, other)
         x_pairs = [pair] + [trade(pair, "row", 2 * chip) for chip in range(1, n_chip)]
     with jax.named_scope("column_terms"):
-        keep, to_core, *parts = pl.pallas_call(
+        even, odd, *parts = pl.pallas_call(
             functools.partial(column_kernel, n_row, n_col, slots),
             out_shape=[blocks, blocks, part, part, part],
             in_specs=[SMEM] * 4 + [VMEM] * (n_col + 2),
@@ -208,13 +209,12 @@
             cost_estimate=cost,
             name="column_terms",
         )(place, tile_rows, tile_cols, tile_count, energy, *x_rows, tiles)
-        from_core = trade(to_core, "row", 1)
     with jax.named_scope("row_terms"):
-        row_terms = pl.pallas_call(
+        to_core, *row_terms = pl.pallas_call(
             functools.partial(row_kernel, n_row, n_col, slots),
-            out_shape=[block] * n_col,
-            in_specs=[SMEM] * 4 + [VMEM] * (n_chip + 3),
-            out_specs=[VMEM] * n_col,
+            out_shape=[blocks] + [block] * n_col,
+            in_specs=[SMEM] * 4 + [VMEM] * (n_chip + 4),
+            out_specs=[VMEM] * (1 + n_col),
             scratch_shapes=[
                 pltpu.VMEM((n_row, 3 * nvec, width), jnp.bfloat16),
                 pltpu.VMEM((n_col + 1, nvec, width), jnp.float32),
@@ -222,8 +222,9 @@
             compiler_params=params,
             cost_estimate=cost,
             name="row_terms",
-        )(place, tile_rows, tile_cols, tile_count, *x_pairs, *parts)
+        )(place, tile_rows, tile_cols, tile_count, *x_pairs, odd, *parts)
     with jax.named_scope("return_products"):
+        from_core = trade(to_core, "row", 1)
         sums = [row_terms[0]] + [trade(row_terms[flip], "col", flip) for flip in range(1, n_col)]
         chips = pl.pallas_call(
             chip_kernel,
@@ -232,7 +233,7 @@
             out_specs=[VMEM] * n_chip,
             compiler_params=params,
             name="chip_sum",
-        )(keep, from_core)
+        )(even, from_core)
         sums += [chips[0]] + [trade(chips[chip], "row", 2 * chip) for chip in range(1, n_chip)]
     with jax.named_scope("product"):
         product, squares = pl.pallas_call(
@@ -253,7 +254,7 @@
             name="results",
         )(vectors, product, swap(squares, ("row", "col")))
 
-    def from_residual(residual, gram):
+    def from_residual(_):
         parts = pl.pallas_call(
             gram_parts_kernel,
             out_shape=jax.ShapeDtypeStruct((devices, packed_rows, width), jnp.float32),
@@ -262,7 +263,7 @@
             compiler_params=params,
             name="gram_parts",
         )(residual)
-        return pl.pallas_call(
+        gram = pl.pallas_call(
             functools.partial(gram_kernel, scale),
             out_shape=square,
             in_specs=[VMEM],
@@ -270,9 +271,10 @@
             compiler_params=params,
             name="gram_sum",
         )(swap(parts, ("row", "col")))
+        return jnp.int32(1), gram
 
     with jax.named_scope("gram"):
-        gram = lax.cond(sound[0, 0] > 0, lambda residual, gram: gram, from_residual, residual, gram)
+        _, gram = lax.while_loop(lambda state: state[0] == 0, from_residual, (sound[0, 0], gram))
     return (residual, rayleigh, gram)
 
 

time: 46.1 us -> 42.5 us (0.922)
  waiting for transfers between devices: 9.67 us -> 4.23 us
  blocking collectives: 10.6 us -> 11.7 us
  between operations: 2.08 us -> 1.43 us
  loops' own time: 0.01 us -> 0.65 us
  local copies, waits for them, and re-layouts: 1.84 us -> 2.47 us
    ppermute x14, waiting for transfers between devices: 9.67 us -> 4.23 us  [trade(): return lax.ppermute(value, axis, [(p, p ^ flip) for p in range(size)])]
    all_to_all x1, blocking collectives: 10.6 us -> 11.7 us  [swap(): return lax.all_to_all(blocks, axis, 0, 0, tiled=True)]
    another operation x1, loops' own time: 0.01 us -> 0.65 us  [per_device(): lax.while_loop(lambda state: state[0] == 0, from_residual, (sound[0, 0],...]
    unnamed x12, local copies, waits for them, and re-layouts: 1.84 us -> 2.47 us
  transfers between devices with their start and end apart: 14 -> 14, of which waited for: 8 -> 2; matrix products, arithmetic and copies ran while one was open for 0% -> 0% of each run, Pallas kernels for 6% -> 3%
where the time goes in v12:
time: 42.5 us; the launch traced here: 42.3 us
  starting transfers between devices  17.5 us (41%)
  blocking collectives  11.7 us (28%)
  Pallas kernels  4.26 us (10%)
  waiting for transfers between devices  4.23 us (10%)
  local copies, waits for them, and re-layouts  2.47 us (6%)
  between operations  1.43 us (3%)
  loops' own time  0.65 us (2%)
    ppermute x14, starting transfers between devices, trade(): return lax.ppermute(value, axis, [(p, p ^ flip) for p in range(size)])  17.5 us
    all_to_all x1, blocking collectives, swap(): return lax.all_to_all(blocks, axis, 0, 0, tiled=True)  11.7 us
    ppermute x14, waiting for transfers between devices, trade(): return lax.ppermute(value, axis, [(p, p ^ flip) for p in range(size)])  4.23 us
    unnamed x12, local copies, waits for them, and re-layouts  2.47 us
    pallas_call x1, Pallas kernels, per_device(): pl.pallas_call(functools.partial(row_kernel, n_row, n_col, slots), out_sh...  1.59 us
    pallas_call x1, Pallas kernels, per_device(): pl.pallas_call(functools.partial(result_kernel, scale), out_shape=[block,...  1.21 us
    pallas_call x1, Pallas kernels, per_device(): pl.pallas_call(functools.partial(column_kernel, n_row, n_col, slots), out...  1.11 us
  transfers between devices with their start and end apart: 14, of which 2 were waited for; matrix products, arithmetic and copies ran while one was open for 0% of the time, Pallas kernels for 3%

profile of v12, /device:TPU:0, one launch (start us, length us, event | category | flops | bytes accessed | tf_op | source)
XLA Modules:
  0.0 42.3 jit_solution(15462984239243678990)
XLA Ops:
  0.6 0.0 copy-start.1
  0.6 0.5 %collective-permute-start = (f32[16,128]{1,0:T(8,128)}, f32[16,128]{1,0:T(8,128)S(1)}, u32[]{:S(2)}, u32[]{:S(2)}) collective-permute-start(f32[16,128]{1,0:T(8,128)} %x_ref.5), channel_id=1, source_target_pairs={{0,4},{4,0},{8,12},{12,8},{16,20},{20,16},{24,28},{28,24},{1,5},{5... | collective-permute-start | bytes 24584 | tf_op jit(solution)/shard_map/share_vectors/ppermute | solution.py:29
  1.2 4.7 %collective-permute-start.6 = (f32[16,128]{1,0:T(8,128)}, f32[16,128]{1,0:T(8,128)S(1)}, u32[]{:S(2)}, u32[]{:S(2)}) collective-permute-start(f32[16,128]{1,0:T(8,128)} %x_ref.5), channel_id=1, source_target_pairs={{0,3},{1,2},{2,1},{3,0},{4,7},{5,6},{6,5},{7,4},{8,11},{9,10},{10,... | collective-permute-start | bytes 24584 | tf_op jit(solution)/shard_map/share_vectors/ppermute | solution.py:29
  5.8 0.0 collective-permute-start.5
  5.8 0.7 %collective-permute-start.4 = (f32[16,128]{1,0:T(8,128)}, f32[16,128]{1,0:T(8,128)S(1)}, u32[]{:S(2)}, u32[]{:S(2)}) collective-permute-start(f32[16,128]{1,0:T(8,128)} %x_ref.5), channel_id=1, source_target_pairs={{0,1},{1,0},{2,3},{3,2},{4,5},{5,4},{6,7},{7,6},{8,9},{9,8},{10,11... | collective-permute-start | bytes 24584 | tf_op jit(solution)/shard_map/share_vectors/ppermute | solution.py:29
  6.5 0.0 collective-permute-done.other
  6.5 0.0 copy-done.1
  6.5 2.6 %collective-permute-start.3 = (f32[2,16,128]{2,1,0:T(8,128)S(1)}, f32[2,16,128]{2,1,0:T(8,128)S(1)}, u32[]{:S(2)}, u32[]{:S(2)}) collective-permute-start(f32[2,16,128]{2,1,0:T(8,128)S(1)} %pair.1.refs_0_), channel_id=1, source_target_pairs={{0,24},{4,28},{8,16},{12,20},{16,8},{20,12},{24,0},{28,4},{1,25},{... | collective-permute-start | bytes 49160 | tf_op jit(solution)/shard_map/share_vectors/ppermute | solution.py:29
  9.1 0.5 %collective-permute-start.2 = (f32[2,16,128]{2,1,0:T(8,128)S(1)}, f32[2,16,128]{2,1,0:T(8,128)S(1)}, u32[]{:S(2)}, u32[]{:S(2)}) collective-permute-start(f32[2,16,128]{2,1,0:T(8,128)S(1)} %pair.1.refs_0_), channel_id=1, source_target_pairs={{0,16},{4,20},{8,24},{12,28},{16,0},{20,4},{24,8},{28,12},{1,17},{... | collective-permute-start | bytes 49160 | tf_op jit(solution)/shard_map/share_vectors/ppermute | solution.py:29
  9.6 0.0 collective-permute-done.6.refs_3_
  9.7 0.4 collective-permute-start.1
  10.1 0.1 pad_add_fusion.place
  10.8 0.0 copy-start.2
  10.8 0.0 copy-start.3
  10.8 0.0 copy-start.4
  10.8 0.0 collective-permute-done.5.refs_2_
  10.8 0.0 collective-permute-done.4.refs_1_
  10.8 0.6 %copy-done.2 = s32[1,1,16]{2,1,0:T(1,128)S(1)} copy-done((s32[1,1,16]{2,1,0:T(1,128)S(1)}, s32[1,1,16]{2,1,0:T(1,128)}, u32[]{:S(2)}) %copy-start.2) | copy-done | bytes 88
  11.4 0.0 copy-done.3
  11.5 0.0 copy-done.4
  11.5 0.0 copy-start
  11.5 1.2 %copy-done = f32[1,1,16,128,128]{4,3,2,1,0:T(8,128)S(1)} copy-done((f32[1,1,16,128,128]{4,3,2,1,0:T(8,128)S(1)}, f32[1,1,16,128,128]{4,3,2,1,0:T(8,128)}, u32[]{:S(2)}) %copy-start) | copy-done | bytes 1048600
  12.7 1.1 %column_terms.1 = (f32[4,16,128]{2,1,0:T(8,128)S(1)}, f32[4,16,128]{2,1,0:T(8,128)S(1)}, bf16[16,128,128]{2,1,0:T(8,128)(2,1)S(1)}, bf16[16,128,128]{2,1,0:T(8,128)(2,1)S(1)}, bf16[16,128,128]{2,1,0:T(8,128)(2,1)S(1)}) custom-call(s32[2]{0:T(128)S(1)} %pad_add_fusion.place, s32[1,1,16]{2,1,0:T(1,128)S(1)} %copy-done.2, s32[1,1,16]{2,1,0:T(1,128)S(1)} %copy-done.3, ...), custom_call_target="tpu_custom_call" | custom-call | flops 50331648 | bytes 1048576 | tf_op jit(solution)/shard_map/column_terms/column_terms/pallas_call | solution.py:199
  13.8 0.0 collective-permute-done.3.refs_3_
  13.8 0.0 collective-permute-done.2.refs_2_
  13.8 0.0 collective-permute-done.1.refs_1_
  13.9 1.6 %row_terms.1 = (f32[4,16,128]{2,1,0:T(8,128)S(1)}, f32[16,128]{1,0:T(8,128)S(1)}, f32[16,128]{1,0:T(8,128)S(1)}, f32[16,128]{1,0:T(8,128)S(1)}, f32[16,128]{1,0:T(8,128)S(1)}) custom-call(s32[2]{0:T(128)S(1)} %pad_add_fusion.place, s32[1,1,16]{2,1,0:T(1,128)S(1)} %copy-done.2, s32[1,1,16]{2,1,0:T(1,128)S(1)} %copy-done.3, s32[1,1]{1,0:T(1,128)S(6)} %copy.16.count, ...), custom_call_target="tpu_custom_call" | custom-call | flops 50331648 | bytes 1048576 | tf_op jit(solution)/shard_map/row_terms/row_terms/pallas_call | solution.py:213
  15.4 0.1 collective-permute-start.10
  15.5 1.4 %collective-permute-start.7 = (f32[16,128]{1,0:T(8,128)S(1)}, f32[16,128]{1,0:T(8,128)S(1)}, u32[]{:S(2)}, u32[]{:S(2)}) collective-permute-start(f32[16,128]{1,0:T(8,128)S(1)} %get-tuple-element.43), channel_id=1, source_target_pairs={{0,1},{1,0},{2,3},{3,2},{4,5},{5,4},{6,7},{7,6},{8,9},{9,8},{10,11... | collective-permute-start | bytes 24584 | tf_op jit(solution)/shard_map/return_products/ppermute | solution.py:29
  17.0 2.9 %collective-permute-start.8 = (f32[16,128]{1,0:T(8,128)S(1)}, f32[16,128]{1,0:T(8,128)S(1)}, u32[]{:S(2)}, u32[]{:S(2)}) collective-permute-start(f32[16,128]{1,0:T(8,128)S(1)} %get-tuple-element.44), channel_id=1, source_target_pairs={{0,2},{1,3},{2,0},{3,1},{4,6},{5,7},{6,4},{7,5},{8,10},{9,11},{10,... | collective-permute-start | bytes 24584 | tf_op jit(solution)/shard_map/return_products/ppermute | solution.py:29
  19.9 0.1 collective-permute-start.9
  20.0 0.0 collective-permute-done.10.other
  20.0 1.7 %collective-permute-start.11 = (f32[16,128]{1,0:T(8,128)S(1)}, f32[16,128]{1,0:T(8,128)S(1)}, u32[]{:S(2)}, u32[]{:S(2)}) collective-permute-start(f32[16,128]{1,0:T(8,128)S(1)} %get-tuple-element.49), channel_id=1, source_target_pairs={{0,8},{4,12},{8,0},{12,4},{16,24},{20,28},{24,16},{28,20},{1,9},{5... | collective-permute-start | bytes 24584 | tf_op jit(solution)/shard_map/return_products/ppermute | solution.py:29
  21.7 1.5 %collective-permute-start.12 = (f32[16,128]{1,0:T(8,128)S(1)}, f32[16,128]{1,0:T(8,128)S(1)}, u32[]{:S(2)}, u32[]{:S(2)}) collective-permute-start(f32[16,128]{1,0:T(8,128)S(1)} %get-tuple-element.50), channel_id=1, source_target_pairs={{0,16},{4,20},{8,24},{12,28},{16,0},{20,4},{24,8},{28,12},{1,17},{... | collective-permute-start | bytes 24584 | tf_op jit(solution)/shard_map/return_products/ppermute | solution.py:29
  23.2 0.0 collective-permute-done.7.refs_1_
  23.2 0.3 collective-permute-start.13
  23.6 0.0 collective-permute-done.8.refs_2_
  23.6 1.8 %collective-permute-done.9.refs_3_ = f32[16,128]{1,0:T(8,128)S(1)} collective-permute-done((f32[16,128]{1,0:T(8,128)S(1)}, f32[16,128]{1,0:T(8,128)S(1)}, u32[]{:S(2)}, u32[]{:S(2)}) %collective-permute-start.9) | collective-permute-done | bytes 8224 | tf_op jit(solution)/shard_map/return_products/ppermute | solution.py:29
  25.3 0.0 collective-permute-done.11.refs_5_
  25.4 0.0 collective-permute-done.12.refs_6_
  25.4 2.4 %collective-permute-done.13.refs_7_ = f32[16,128]{1,0:T(8,128)S(1)} collective-permute-done((f32[16,128]{1,0:T(8,128)S(1)}, f32[16,128]{1,0:T(8,128)S(1)}, u32[]{:S(2)}, u32[]{:S(2)}) %collective-permute-start.13) | collective-permute-done | bytes 8224 | tf_op jit(solution)/shard_map/return_products/ppermute | solution.py:29
  27.8 0.3 product.1
  28.1 11.7 %all_to_all.9.parts = f32[32,3,2,128]{3,2,1,0:T(2,128)S(1)} all-to-all(f32[32,3,2,128]{3,2,1,0:T(2,128)S(1)} %get-tuple-element.53), channel_id=1, replica_groups=mesh['row'=8,'col'=4] {'row','col'}, dimensions={0} | all-to-all | bytes 196608 | tf_op jit(solution)/shard_map/results/all_to_all | solution.py:24
  39.8 1.2 %results.1 = (f32[16,128]{1,0:T(8,128)S(1)}, f32[16,16]{1,0:T(8,128)}, f32[16,16]{1,0:T(8,128)}, s32[1,1]{1,0:T(1,128)}) custom-call(f32[16,128]{1,0:T(8,128)S(1)} %copy-done.1, f32[16,128]{1,0:T(8,128)S(1)} %get-tuple-element.52.product, f32[32,3,2,128]{3,2,1,0:T(2,128)S(1)} %all_to_all.9.parts), custom_call_target="tpu_custom_call" | custom-call | tf_op jit(solution)/shard_map/results/results/pallas_call | solution.py:248
  41.0 0.7 %while.9 = (s32[]{:T(128)}, f32[16,16]{1,0:T(8,128)}, f32[16,128]{1,0:T(8,128)S(1)}) while((s32[]{:T(128)}, f32[16,16]{1,0:T(8,128)}, f32[16,128]{1,0:T(8,128)S(1)}) %tuple.17), condition=%region_1.0_spmd, body=%region_0.0_spmd | while | flops 1 | bytes 98377 | solution.py:277
  41.7 0.0 copy-start.5
  41.7 0.6 %copy-done.5 = f32[16,128]{1,0:T(8,128)} copy-done((f32[16,128]{1,0:T(8,128)}, f32[16,128]{1,0:T(8,128)S(1)}, u32[]{:S(2)}) %copy-start.5) | copy-done | bytes 8216
  (2 shorter events, 0.0 us)
Async XLA Ops:
  0.6 5.9 %copy-start.1 = (f32[16,128]{1,0:T(8,128)S(1)}, f32[16,128]{1,0:T(8,128)}, u32[]{:S(2)}) copy-start(f32[16,128]{1,0:T(8,128)} %x_ref.5) | copy-start | bytes 24580
  0.6 5.9 %collective-permute-start = (f32[16,128]{1,0:T(8,128)}, f32[16,128]{1,0:T(8,128)S(1)}, u32[]{:S(2)}, u32[]{:S(2)}) collective-permute-start(f32[16,128]{1,0:T(8,128)} %x_ref.5), channel_id=1, source_target_pairs={{0,4},{4,0},{8,12},{12,8},{16,20},{20,16},{24,28},{28,24},{1,5},{5... | collective-permute-start | bytes 24584 | tf_op jit(solution)/shard_map/share_vectors/ppermute | solution.py:29
  1.2 8.5 %collective-permute-start.6 = (f32[16,128]{1,0:T(8,128)}, f32[16,128]{1,0:T(8,128)S(1)}, u32[]{:S(2)}, u32[]{:S(2)}) collective-permute-start(f32[16,128]{1,0:T(8,128)} %x_ref.5), channel_id=1, source_target_pairs={{0,3},{1,2},{2,1},{3,0},{4,7},{5,6},{6,5},{7,4},{8,11},{9,10},{10,... | collective-permute-start | bytes 24584 | tf_op jit(solution)/shard_map/share_vectors/ppermute | solution.py:29
  5.8 5.0 %collective-permute-start.5 = (f32[16,128]{1,0:T(8,128)}, f32[16,128]{1,0:T(8,128)S(1)}, u32[]{:S(2)}, u32[]{:S(2)}) collective-permute-start(f32[16,128]{1,0:T(8,128)} %x_ref.5), channel_id=1, source_target_pairs={{0,2},{1,3},{2,0},{3,1},{4,6},{5,7},{6,4},{7,5},{8,10},{9,11},{10,... | collective-permute-start | bytes 24584 | tf_op jit(solution)/shard_map/share_vectors/ppermute | solution.py:29
  5.8 5.0 %collective-permute-start.4 = (f32[16,128]{1,0:T(8,128)}, f32[16,128]{1,0:T(8,128)S(1)}, u32[]{:S(2)}, u32[]{:S(2)}) collective-permute-start(f32[16,128]{1,0:T(8,128)} %x_ref.5), channel_id=1, source_target_pairs={{0,1},{1,0},{2,3},{3,2},{4,5},{5,4},{6,7},{7,6},{8,9},{9,8},{10,11... | collective-permute-start | bytes 24584 | tf_op jit(solution)/shard_map/share_vectors/ppermute | solution.py:29
  6.5 7.3 %collective-permute-start.3 = (f32[2,16,128]{2,1,0:T(8,128)S(1)}, f32[2,16,128]{2,1,0:T(8,128)S(1)}, u32[]{:S(2)}, u32[]{:S(2)}) collective-permute-start(f32[2,16,128]{2,1,0:T(8,128)S(1)} %pair.1.refs_0_), channel_id=1, source_target_pairs={{0,24},{4,28},{8,16},{12,20},{16,8},{20,12},{24,0},{28,4},{1,25},{... | collective-permute-start | bytes 49160 | tf_op jit(solution)/shard_map/share_vectors/ppermute | solution.py:29
  9.1 4.7 %collective-permute-start.2 = (f32[2,16,128]{2,1,0:T(8,128)S(1)}, f32[2,16,128]{2,1,0:T(8,128)S(1)}, u32[]{:S(2)}, u32[]{:S(2)}) collective-permute-start(f32[2,16,128]{2,1,0:T(8,128)S(1)} %pair.1.refs_0_), channel_id=1, source_target_pairs={{0,16},{4,20},{8,24},{12,28},{16,0},{20,4},{24,8},{28,12},{1,17},{... | collective-permute-start | bytes 49160 | tf_op jit(solution)/shard_map/share_vectors/ppermute | solution.py:29
  9.7 4.2 %collective-permute-start.1 = (f32[2,16,128]{2,1,0:T(8,128)S(1)}, f32[2,16,128]{2,1,0:T(8,128)S(1)}, u32[]{:S(2)}, u32[]{:S(2)}) collective-permute-start(f32[2,16,128]{2,1,0:T(8,128)S(1)} %pair.1.refs_0_), channel_id=1, source_target_pairs={{0,8},{4,12},{8,0},{12,4},{16,24},{20,28},{24,16},{28,20},{1,9},{5... | collective-permute-start | bytes 49160 | tf_op jit(solution)/shard_map/share_vectors/ppermute | solution.py:29
  10.8 0.7 %copy-start.2 = (s32[1,1,16]{2,1,0:T(1,128)S(1)}, s32[1,1,16]{2,1,0:T(1,128)}, u32[]{:S(2)}) copy-start(s32[1,1,16]{2,1,0:T(1,128)} %arow.3) | copy-start | bytes 196
  10.8 0.7 %copy-start.3 = (s32[1,1,16]{2,1,0:T(1,128)S(1)}, s32[1,1,16]{2,1,0:T(1,128)}, u32[]{:S(2)}) copy-start(s32[1,1,16]{2,1,0:T(1,128)} %bcol.3) | copy-start | bytes 196
  10.8 0.7 %copy-start.4 = (f32[128]{0:T(128)S(1)}, f32[128]{0:T(128)}, u32[]{:S(2)}) copy-start(f32[128]{0:T(128)} %param.9) | copy-start | bytes 1540
  11.5 1.2 %copy-start = (f32[1,1,16,128,128]{4,3,2,1,0:T(8,128)S(1)}, f32[1,1,16,128,128]{4,3,2,1,0:T(8,128)}, u32[]{:S(2)}) copy-start(f32[1,1,16,128,128]{4,3,2,1,0:T(8,128)} %refs_4_.1) | copy-start | bytes 3145732
  15.4 4.5 %collective-permute-start.10 = (f32[4,16,128]{2,1,0:T(8,128)S(1)}, f32[4,16,128]{2,1,0:T(8,128)S(1)}, u32[]{:S(2)}, u32[]{:S(2)}) collective-permute-start(f32[4,16,128]{2,1,0:T(8,128)S(1)} %get-tuple-element.47), channel_id=1, source_target_pairs={{0,4},{4,0},{8,12},{12,8},{16,20},{20,16},{24,28},{28,24},{1,5},{5... | collective-permute-start | bytes 98312 | tf_op jit(solution)/shard_map/return_products/ppermute | solution.py:29
  15.5 7.7 %collective-permute-start.7 = (f32[16,128]{1,0:T(8,128)S(1)}, f32[16,128]{1,0:T(8,128)S(1)}, u32[]{:S(2)}, u32[]{:S(2)}) collective-permute-start(f32[16,128]{1,0:T(8,128)S(1)} %get-tuple-element.43), channel_id=1, source_target_pairs={{0,1},{1,0},{2,3},{3,2},{4,5},{5,4},{6,7},{7,6},{8,9},{9,8},{10,11... | collective-permute-start | bytes 24584 | tf_op jit(solution)/shard_map/return_products/ppermute | solution.py:29
  17.0 6.6 %collective-permute-start.8 = (f32[16,128]{1,0:T(8,128)S(1)}, f32[16,128]{1,0:T(8,128)S(1)}, u32[]{:S(2)}, u32[]{:S(2)}) collective-permute-start(f32[16,128]{1,0:T(8,128)S(1)} %get-tuple-element.44), channel_id=1, source_target_pairs={{0,2},{1,3},{2,0},{3,1},{4,6},{5,7},{6,4},{7,5},{8,10},{9,11},{10,... | collective-permute-start | bytes 24584 | tf_op jit(solution)/shard_map/return_products/ppermute | solution.py:29
  19.9 5.4 %collective-permute-start.9 = (f32[16,128]{1,0:T(8,128)S(1)}, f32[16,128]{1,0:T(8,128)S(1)}, u32[]{:S(2)}, u32[]{:S(2)}) collective-permute-start(f32[16,128]{1,0:T(8,128)S(1)} %get-tuple-element.45), channel_id=1, source_target_pairs={{0,3},{1,2},{2,1},{3,0},{4,7},{5,6},{6,5},{7,4},{8,11},{9,10},{10,... | collective-permute-start | bytes 24584 | tf_op jit(solution)/shard_map/return_products/ppermute | solution.py:29
  20.0 5.4 %collective-permute-start.11 = (f32[16,128]{1,0:T(8,128)S(1)}, f32[16,128]{1,0:T(8,128)S(1)}, u32[]{:S(2)}, u32[]{:S(2)}) collective-permute-start(f32[16,128]{1,0:T(8,128)S(1)} %get-tuple-element.49), channel_id=1, source_target_pairs={{0,8},{4,12},{8,0},{12,4},{16,24},{20,28},{24,16},{28,20},{1,9},{5... | collective-permute-start | bytes 24584 | tf_op jit(solution)/shard_map/return_products/ppermute | solution.py:29
  21.7 3.7 %collective-permute-start.12 = (f32[16,128]{1,0:T(8,128)S(1)}, f32[16,128]{1,0:T(8,128)S(1)}, u32[]{:S(2)}, u32[]{:S(2)}) collective-permute-start(f32[16,128]{1,0:T(8,128)S(1)} %get-tuple-element.50), channel_id=1, source_target_pairs={{0,16},{4,20},{8,24},{12,28},{16,0},{20,4},{24,8},{28,12},{1,17},{... | collective-permute-start | bytes 24584 | tf_op jit(solution)/shard_map/return_products/ppermute | solution.py:29
  23.2 4.6 %collective-permute-start.13 = (f32[16,128]{1,0:T(8,128)S(1)}, f32[16,128]{1,0:T(8,128)S(1)}, u32[]{:S(2)}, u32[]{:S(2)}) collective-permute-start(f32[16,128]{1,0:T(8,128)S(1)} %get-tuple-element.51), channel_id=1, source_target_pairs={{0,24},{4,28},{8,16},{12,20},{16,8},{20,12},{24,0},{28,4},{1,25},{... | collective-permute-start | bytes 24584 | tf_op jit(solution)/shard_map/return_products/ppermute | solution.py:29
  41.7 0.6 %copy-start.5 = (f32[16,128]{1,0:T(8,128)}, f32[16,128]{1,0:T(8,128)S(1)}, u32[]{:S(2)}) copy-start(f32[16,128]{1,0:T(8,128)S(1)} %get-tuple-element.106) | copy-start | bytes 24580

commit v13 on v12

--- a/solution.py
+++ b/solution.py
@@ -82,56 +82,60 @@
     return total
 
 
-def pair_kernel(x_ref, other, out):
-    out[0] = x_ref[...]
-    out[1] = other[...]
-
-
-def column_kernel(n_row, n_col, slots, place, arow, bcol, count, d_ref, *refs):
-    x_rows, (tiles, even, odd, *parts, rows, sums) = refs[:n_col], refs[n_col:]
+def join_kernel(mine, other, out):
+    half = mine.shape[0]
+    out[:half] = mine[...]
+    out[half:] = other[...]
+
+
+def part_blocks(sums, total, send, keep):
+    for block in range(total // 2):
+        keep[block] = sums[2 * block]
+        send[block] = sums[2 * block + 1]
+
+
+def column_kernel(n_row, n_col, slots, place, arow, bcol, count, d_ref, near, far, tiles, send, keep, *refs):
+    *parts, rows, sums = refs
     me_row, me_col = place[0], place[1]
+    half = n_col // 2
     for flip in range(n_col):
-        rows[flip] = stack_split(x_rows[flip][...])
+        rows[flip] = stack_split(near[flip] if flip < half else far[flip - half])
     sums[...] = jnp.zeros_like(sums)
-    sums[0] = d_ref[...] * x_rows[0][...]
+    sums[0] = d_ref[...] * near[0]
     for slot in range(slots):
         pieces = split(tiles[0, 0, slot])
         for part, piece in zip(parts, pieces):
             part[slot] = piece
         block = jnp.where(slot < count[0, 0], bcol[0, 0, slot] ^ me_row, n_row)
         sums[block] += parts_product(rows[arow[0, 0, slot] ^ me_col], pieces, (((1,), (0,)), ((), ())))
-    for chip in range(n_row // 2):
-        even[chip] = sums[2 * chip]
-        odd[chip] = sums[2 * chip + 1]
-
-
-def row_kernel(n_row, n_col, slots, place, arow, bcol, count, *refs):
-    x_pairs, refs = refs[: n_row // 2], refs[n_row // 2 :]
-    (odd, *parts), (to_core, *outs), (cols, sums) = refs[:4], refs[4:-2], refs[-2:]
-    to_core[...] = odd[...]
+    part_blocks(sums, n_row, send, keep)
+
+
+def row_kernel(n_row, n_col, slots, place, arow, bcol, count, near, far, early, *refs):
+    *parts, late, send, keep, cols, sums = refs
     me_row, me_col = place[0], place[1]
+    late[...] = early[...]
+    half = n_row // 2
     for flip in range(n_row):
-        cols[flip] = stack_split(x_pairs[flip // 2][flip % 2])
+        cols[flip] = stack_split(near[flip] if flip < half else far[flip - half])
     sums[...] = jnp.zeros_like(sums)
     for slot in range(slots):
         block = jnp.where(slot < count[0, 0], arow[0, 0, slot] ^ me_col, n_col)
         pieces = [part[slot] for part in parts]
         sums[block] += parts_product(cols[bcol[0, 0, slot] ^ me_row], pieces, (((1,), (1,)), ((), ())))
-    for flip, out in enumerate(outs):
-        out[...] = sums[flip]
-
-
-def chip_kernel(mine, other, *outs):
-    for chip, out in enumerate(outs):
-        out[...] = mine[chip] + other[chip]
+    part_blocks(sums, n_col, send, keep)
+
+
+def halve_kernel(mine, other, send, keep):
+    part_blocks([mine[block] + other[block] for block in range(mine.shape[0])], mine.shape[0], send, keep)
 
 
 def product_kernel(x_ref, *refs):
     parts, (product, out) = refs[:-2], refs[-2:]
     own = x_ref[...]
-    total = parts[0][...]
+    total = parts[0][0]
     for part in parts[1:]:
-        total += part[...]
+        total += part[0]
     product[...] = total
     squares = packed_gram(jnp.concatenate([own, total], axis=0), total) + packed_gram(own, own)
     for block in range(out.shape[0]):
@@ -139,12 +143,16 @@
             out[block, which] = square
 
 
+def summed_squares(scale, parts, nvec):
+    sums = jnp.sum(parts[...], axis=0)
+    squares = unpack([sums[which] for which in range(3)], nvec) * scale
+    return squares[:nvec], squares[nvec : 2 * nvec], squares[2 * nvec :]
+
+
 def result_kernel(scale, x_ref, product, parts, residual, rayleigh, gram, sound):
     own = x_ref[...]
     nvec = own.shape[0]
-    sums = jnp.sum(parts[...], axis=0)
-    squares = unpack([sums[which] for which in range(3)], nvec) * scale
-    ray, outer, inner = squares[:nvec], squares[nvec : 2 * nvec], squares[2 * nvec :]
+    ray, outer, inner = summed_squares(scale, parts, nvec)
     rayleigh[...] = ray
     residual[...] = product[...] - mult(ray, own)
     twice = mult(ray, ray)
@@ -156,8 +164,11 @@
     sound[0, 0] = (margin >= 0.0).astype(jnp.int32)
 
 
-def gram_parts_kernel(residual, out):
-    square = packed_gram(residual[...], residual[...])[0]
+def gram_parts_kernel(scale, x_ref, product, parts, out):
+    own = x_ref[...]
+    ray, _, _ = summed_squares(scale, parts, own.shape[0])
+    residual = product[...] - mult(ray, own)
+    square = packed_gram(residual, residual)[0]
     for block in range(out.shape[0]):
         out[block] = square
 
@@ -173,33 +184,59 @@
     nvec, width = vectors.shape
     slots = tiles.shape[2]
     scale = 1.0 / float(devices * width)
-    n_chip = n_row // 2
     packed_rows = nvec * nvec // width
     block = jax.ShapeDtypeStruct((nvec, width), jnp.float32)
-    blocks = jax.ShapeDtypeStruct((n_chip, nvec, width), jnp.float32)
     square = jax.ShapeDtypeStruct((nvec, nvec), jnp.float32)
     part = jax.ShapeDtypeStruct((slots, width, width), jnp.bfloat16)
     place = jnp.stack([lax.axis_index("row"), lax.axis_index("col")]).astype(jnp.int32)
     energy = diagonal_energy.reshape(1, width)
     params = pltpu.CompilerParams(vmem_limit_bytes=16 * 2**20)
     cost = pl.CostEstimate(flops=12 * slots * nvec * width * width, bytes_accessed=2**20, transcendentals=0)
+
+    def blocks(total):
+        return jax.ShapeDtypeStruct((total, nvec, width), jnp.float32)
+
+    def gather(axis):
+        size = lax.axis_size(axis)
+        near = vectors[None]
+        far = trade(near, axis, 1)
+        reach = 2
+        while reach < size:
+            near = pl.pallas_call(
+                join_kernel,
+                out_shape=blocks(reach),
+                in_specs=[VMEM] * 2,
+                out_specs=VMEM,
+                compiler_params=params,
+                name="join_" + axis,
+            )(near, far)
+            far = trade(near, axis, reach)
+            reach *= 2
+        return near, far
+
+    def halve(send, keep, axis):
+        flip = 1
+        while keep.shape[0] > 1:
+            half = keep.shape[0] // 2
+            send, keep = pl.pallas_call(
+                halve_kernel,
+                out_shape=[blocks(half)] * 2,
+                in_specs=[VMEM] * 2,
+                out_specs=[VMEM] * 2,
+                compiler_params=params,
+                name="halve_" + axis,
+            )(keep, trade(send, axis, flip))
+            flip *= 2
+        return keep, trade(send, axis, flip)
+
     with jax.named_scope("share_vectors"):
-        other = trade(vectors, "row", 1)
-        x_rows = [vectors] + [trade(vectors, "col", flip) for flip in range(1, n_col)]
-        pair = pl.pallas_call(
-            pair_kernel,
-            out_shape=jax.ShapeDtypeStruct((2, nvec, width), jnp.float32),
-            in_specs=[VMEM] * 2,
-            out_specs=VMEM,
-            compiler_params=params,
-            name="pair",
-        )(vectors, other)
-        x_pairs = [pair] + [trade(pair, "row", 2 * chip) for chip in range(1, n_chip)]
+        x_row = gather("row")
+        x_col = gather("col")
     with jax.named_scope("column_terms"):
-        even, odd, *parts = pl.pallas_call(
+        col_send, col_keep, *parts = pl.pallas_call(
             functools.partial(column_kernel, n_row, n_col, slots),
-            out_shape=[blocks, blocks, part, part, part],
-            in_specs=[SMEM] * 4 + [VMEM] * (n_col + 2),
+            out_shape=[blocks(n_row // 2)] * 2 + [part] * 3,
+            in_specs=[SMEM] * 4 + [VMEM] * 4,
             out_specs=[VMEM] * 5,
             scratch_shapes=[
                 pltpu.VMEM((n_col, 3 * nvec, width), jnp.bfloat16),
@@ -208,13 +245,13 @@
             compiler_params=params,
             cost_estimate=cost,
             name="column_terms",
-        )(place, tile_rows, tile_cols, tile_count, energy, *x_rows, tiles)
+        )(place, tile_rows, tile_cols, tile_count, energy, *x_col, tiles)
     with jax.named_scope("row_terms"):
-        to_core, *row_terms = pl.pallas_call(
+        col_send, row_send, row_keep = pl.pallas_call(
             functools.partial(row_kernel, n_row, n_col, slots),
-            out_shape=[blocks] + [block] * n_col,
-            in_specs=[SMEM] * 4 + [VMEM] * (n_chip + 4),
-            out_specs=[VMEM] * (1 + n_col),
+            out_shape=[blocks(n_row // 2)] + [blocks(n_col // 2)] * 2,
+            in_specs=[SMEM] * 4 + [VMEM] * 6,
+            out_specs=[VMEM] * 3,
             scratch_shapes=[
                 pltpu.VMEM((n_row, 3 * nvec, width), jnp.bfloat16),
                 pltpu.VMEM((n_col + 1, nvec, width), jnp.float32),
@@ -222,28 +259,19 @@
             compiler_params=params,
             cost_estimate=cost,
             name="row_terms",
-        )(place, tile_rows, tile_cols, tile_count, *x_pairs, odd, *parts)
+        )(place, tile_rows, tile_cols, tile_count, *x_row, col_send, *parts)
     with jax.named_scope("return_products"):
-        from_core = trade(to_core, "row", 1)
-        sums = [row_terms[0]] + [trade(row_terms[flip], "col", flip) for flip in range(1, n_col)]
-        chips = pl.pallas_call(
-            chip_kernel,
-            out_shape=[block] * n_chip,
-            in_specs=[VMEM] * 2,
-            out_specs=[VMEM] * n_chip,
-            compiler_params=params,
-            name="chip_sum",
-        )(even, from_core)
-        sums += [chips[0]] + [trade(chips[chip], "row", 2 * chip) for chip in range(1, n_chip)]
+        sums = halve(col_send, col_keep, "row") + halve(row_send, row_keep, "col")
     with jax.named_scope("product"):
         product, squares = pl.pallas_call(
             product_kernel,
             out_shape=[block, jax.ShapeDtypeStruct((devices, 3, packed_rows, width), jnp.float32)],
-            in_specs=[VMEM] * (1 + n_col + n_chip),
+            in_specs=[VMEM] * 5,
             out_specs=[VMEM] * 2,
             compiler_params=params,
             name="product",
         )(vectors, *sums)
+        squares = swap(squares, ("row", "col"))
     with jax.named_scope("results"):
         residual, rayleigh, gram, sound = pl.pallas_call(
             functools.partial(result_kernel, scale),
@@ -252,17 +280,17 @@
             out_specs=[VMEM] * 3 + [SMEM],
             compiler_params=params,
             name="results",
-        )(vectors, product, swap(squares, ("row", "col")))
+        )(vectors, product, squares)
 
     def from_residual(_):
         parts = pl.pallas_call(
-            gram_parts_kernel,
+            functools.partial(gram_parts_kernel, scale),
             out_shape=jax.ShapeDtypeStruct((devices, packed_rows, width), jnp.float32),
-            in_specs=[VMEM],
+            in_specs=[VMEM] * 3,
             out_specs=VMEM,
             compiler_params=params,
             name="gram_parts",
-        )(residual)
+        )(vectors, product, squares)
         gram = pl.pallas_call(
             functools.partial(gram_kernel, scale),
             out_shape=square,

time: 42.5 us -> 41.8 us (0.984)
  starting transfers between devices: 17.5 us -> 14.6 us
  waiting for transfers between devices: 4.23 us -> 6.81 us
  Pallas kernels: 4.26 us -> 4.97 us
  local copies, waits for them, and re-layouts: 2.47 us -> 1.88 us
  blocking collectives: 11.7 us -> 11.2 us
    ppermute x14 -> x10, starting transfers between devices: 17.5 us -> 14.6 us  [trade(): return lax.ppermute(value, axis, [(p, p ^ flip) for p in range(size)])]
    ppermute x14 -> x10, waiting for transfers between devices: 4.23 us -> 6.81 us  [trade(): return lax.ppermute(value, axis, [(p, p ^ flip) for p in range(size)])]
    pallas_call x2 -> x6, Pallas kernels: 0.01 us -> 0.72 us  [the longest x3 0.7 us: gather(): pl.pallas_call(join_kernel, out_shape=blocks(reach), in_specs=[VMEM] * 2,...]
    unnamed x12 -> x10, local copies, waits for them, and re-layouts: 2.47 us -> 1.88 us
    all_to_all x1, blocking collectives: 11.7 us -> 11.2 us  [swap(): return lax.all_to_all(blocks, axis, 0, 0, tiled=True)]
  transfers between devices with their start and end apart: 14 -> 10, of which waited for: 2 -> 5; matrix products, arithmetic and copies ran while one was open for 0% -> 0% of each run, Pallas kernels for 3% -> 3%
where the time goes in v13:
time: 41.8 us; the launch traced here: 41.5 us
  starting transfers between devices  14.6 us (35%)
  blocking collectives  11.2 us (27%)
  waiting for transfers between devices  6.81 us (16%)
  Pallas kernels  4.97 us (12%)
  local copies, waits for them, and re-layouts  1.88 us (4%)
  between operations  1.39 us (3%)
  loops' own time  0.58 us (1%)
    ppermute x10, starting transfers between devices, trade(): return lax.ppermute(value, axis, [(p, p ^ flip) for p in range(size)])  14.6 us
    all_to_all x1, blocking collectives, swap(): return lax.all_to_all(blocks, axis, 0, 0, tiled=True)  11.2 us
    ppermute x10, waiting for transfers between devices, trade(): return lax.ppermute(value, axis, [(p, p ^ flip) for p in range(size)])  6.81 us
    unnamed x10, local copies, waits for them, and re-layouts  1.88 us
    pallas_call x1, Pallas kernels, per_device(): pl.pallas_call(functools.partial(row_kernel, n_row, n_col, slots), out_sh...  1.59 us
    pallas_call x1, Pallas kernels, per_device(): pl.pallas_call(functools.partial(result_kernel, scale), out_shape=[block,...  1.21 us
    pallas_call x1, Pallas kernels, per_device(): pl.pallas_call(functools.partial(column_kernel, n_row, n_col, slots), out...  1.11 us
  transfers between devices with their start and end apart: 10, of which 5 were waited for; matrix products, arithmetic and copies ran while one was open for 0% of the time, Pallas kernels for 3%

profile of v13, /device:TPU:0, one launch (start us, length us, event | category | flops | bytes accessed | tf_op | source)
XLA Modules:
  0.0 41.5 jit_solution(5204100268099590371)
XLA Ops:
  0.6 0.0 copy-start.4
  0.6 0.5 %collective-permute-start.2 = (f32[1,16,128]{2,1,0:T(8,128)}, f32[1,16,128]{2,1,0:T(8,128)S(1)}, u32[]{:S(2)}, u32[]{:S(2)}) collective-permute-start(f32[1,16,128]{2,1,0:T(8,128)} %bitcast.6), channel_id=1, source_target_pairs={{0,4},{4,0},{8,12},{12,8},{16,20},{20,16},{24,28},{28,24},{1,5},{5... | collective-permute-start | bytes 24584 | tf_op jit(solution)/shard_map/share_vectors/ppermute | solution.py:29
  1.2 1.0 %collective-permute-done.2.other = f32[1,16,128]{2,1,0:T(8,128)S(1)} collective-permute-done((f32[1,16,128]{2,1,0:T(8,128)}, f32[1,16,128]{2,1,0:T(8,128)S(1)}, u32[]{:S(2)}, u32[]{:S(2)}) %collective-permute-start.2) | collective-permute-done | bytes 8224 | tf_op jit(solution)/shard_map/share_vectors/ppermute | solution.py:29
  2.2 0.7 %join_row.2.mine = f32[2,16,128]{2,1,0:T(8,128)S(1)} custom-call(f32[1,16,128]{2,1,0:T(8,128)} %bitcast.7, f32[1,16,128]{2,1,0:T(8,128)S(1)} %collective-permute-done.2.other), custom_call_target="tpu_custom_call" | custom-call | tf_op jit(solution)/shard_map/share_vectors/join_row/pallas_call | solution.py:205
  2.9 2.8 %collective-permute-start.3 = (f32[2,16,128]{2,1,0:T(8,128)S(1)}, f32[2,16,128]{2,1,0:T(8,128)S(1)}, u32[]{:S(2)}, u32[]{:S(2)}) collective-permute-start(f32[2,16,128]{2,1,0:T(8,128)S(1)} %join_row.2.mine), channel_id=1, source_target_pairs={{0,8},{4,12},{8,0},{12,4},{16,24},{20,28},{24,16},{28,20},{1,9},{5... | collective-permute-start | bytes 49160 | tf_op jit(solution)/shard_map/share_vectors/ppermute | solution.py:29
  5.7 0.0 copy-done.4
  5.7 1.6 %collective-permute-start = (f32[1,16,128]{2,1,0:T(8,128)S(1)}, f32[1,16,128]{2,1,0:T(8,128)S(1)}, u32[]{:S(2)}, u32[]{:S(2)}) collective-permute-start(f32[1,16,128]{2,1,0:T(8,128)S(1)} %bitcast.8), channel_id=1, source_target_pairs={{0,1},{1,0},{2,3},{3,2},{4,5},{5,4},{6,7},{7,6},{8,9},{9,8},{10,11... | collective-permute-start | bytes 24584 | tf_op jit(solution)/shard_map/share_vectors/ppermute | solution.py:29
  7.3 2.1 %collective-permute-done.other = f32[1,16,128]{2,1,0:T(8,128)S(1)} collective-permute-done((f32[1,16,128]{2,1,0:T(8,128)S(1)}, f32[1,16,128]{2,1,0:T(8,128)S(1)}, u32[]{:S(2)}, u32[]{:S(2)}) %collective-permute-start) | collective-permute-done | bytes 8224 | tf_op jit(solution)/shard_map/share_vectors/ppermute | solution.py:29
  9.4 2.6 %collective-permute-start.1 = (f32[2,16,128]{2,1,0:T(8,128)S(1)}, f32[2,16,128]{2,1,0:T(8,128)S(1)}, u32[]{:S(2)}, u32[]{:S(2)}) collective-permute-start(f32[2,16,128]{2,1,0:T(8,128)S(1)} %join_col.1.near), channel_id=1, source_target_pairs={{0,2},{1,3},{2,0},{3,1},{4,6},{5,7},{6,4},{7,5},{8,10},{9,11},{10,... | collective-permute-start | bytes 49160 | tf_op jit(solution)/shard_map/share_vectors/ppermute | solution.py:29
  12.0 0.0 collective-permute-done.3.other
  12.0 1.5 %collective-permute-start.4 = (f32[4,16,128]{2,1,0:T(8,128)S(1)}, f32[4,16,128]{2,1,0:T(8,128)S(1)}, u32[]{:S(2)}, u32[]{:S(2)}) collective-permute-start(f32[4,16,128]{2,1,0:T(8,128)S(1)} %join_row.3.near), channel_id=1, source_target_pairs={{0,16},{4,20},{8,24},{12,28},{16,0},{20,4},{24,8},{28,12},{1,17},{... | collective-permute-start | bytes 98312 | tf_op jit(solution)/shard_map/share_vectors/ppermute | solution.py:29
  13.5 0.1 pad_add_fusion.place
  14.2 0.0 copy-start.1
  14.2 0.0 copy-start.2
  14.3 0.0 copy-start.3
  14.3 0.0 collective-permute-done.1.far
  14.3 0.6 %copy-done.1 = s32[1,1,16]{2,1,0:T(1,128)S(1)} copy-done((s32[1,1,16]{2,1,0:T(1,128)S(1)}, s32[1,1,16]{2,1,0:T(1,128)}, u32[]{:S(2)}) %copy-start.1) | copy-done | bytes 88
  14.9 0.0 copy-done.2
  14.9 0.0 copy-done.3
  14.9 0.0 copy-start
  14.9 1.2 %copy-done = f32[1,1,16,128,128]{4,3,2,1,0:T(8,128)S(1)} copy-done((f32[1,1,16,128,128]{4,3,2,1,0:T(8,128)S(1)}, f32[1,1,16,128,128]{4,3,2,1,0:T(8,128)}, u32[]{:S(2)}) %copy-start) | copy-done | bytes 1048600
  16.1 1.1 %column_terms.1 = (f32[4,16,128]{2,1,0:T(8,128)S(1)}, f32[4,16,128]{2,1,0:T(8,128)S(1)}, bf16[16,128,128]{2,1,0:T(8,128)(2,1)S(1)}, bf16[16,128,128]{2,1,0:T(8,128)(2,1)S(1)}, bf16[16,128,128]{2,1,0:T(8,128)(2,1)S(1)}) custom-call(s32[2]{0:T(128)S(1)} %pad_add_fusion.place, s32[1,1,16]{2,1,0:T(1,128)S(1)} %copy-done.1, s32[1,1,16]{2,1,0:T(1,128)S(1)} %copy-done.2, ...), custom_call_target="tpu_custom_call" | custom-call | flops 50331648 | bytes 1048576 | tf_op jit(solution)/shard_map/column_terms/column_terms/pallas_call | solution.py:236
  17.3 0.0 collective-permute-done.4.far
  17.3 1.6 %row_terms.1 = (f32[4,16,128]{2,1,0:T(8,128)S(1)}, f32[2,16,128]{2,1,0:T(8,128)S(1)}, f32[2,16,128]{2,1,0:T(8,128)S(1)}) custom-call(s32[2]{0:T(128)S(1)} %pad_add_fusion.place, s32[1,1,16]{2,1,0:T(1,128)S(1)} %copy-done.1, s32[1,1,16]{2,1,0:T(1,128)S(1)} %copy-done.2, s32[1,1]{1,0:T(1,128)S(6)} %copy.16.count, f32[4,16,128]{2,1,0:T(8,128)S(1)} %join_row.3.near, ...), custom_call_target="tpu_custom_call" | custom-call | flops 50331648 | bytes 1048576 | tf_op jit(solution)/shard_map/row_terms/row_terms/pallas_call | solution.py:250
  18.9 0.1 collective-permute-start.5
  18.9 1.6 %collective-permute-start.8 = (f32[2,16,128]{2,1,0:T(8,128)S(1)}, f32[2,16,128]{2,1,0:T(8,128)S(1)}, u32[]{:S(2)}, u32[]{:S(2)}) collective-permute-start(f32[2,16,128]{2,1,0:T(8,128)S(1)} %get-tuple-element.59), channel_id=1, source_target_pairs={{0,1},{1,0},{2,3},{3,2},{4,5},{5,4},{6,7},{7,6},{8,9},{9,8},{10,11... | collective-permute-start | bytes 49160 | tf_op jit(solution)/shard_map/return_products/ppermute | solution.py:29
  20.6 0.0 collective-permute-done.5.other
  20.6 0.6 %collective-permute-start.6 = (f32[2,16,128]{2,1,0:T(8,128)S(1)}, f32[2,16,128]{2,1,0:T(8,128)S(1)}, u32[]{:S(2)}, u32[]{:S(2)}) collective-permute-start(f32[2,16,128]{2,1,0:T(8,128)S(1)} %get-tuple-element.55), channel_id=1, source_target_pairs={{0,8},{4,12},{8,0},{12,4},{16,24},{20,28},{24,16},{28,20},{1,9},{5... | collective-permute-start | bytes 49160 | tf_op jit(solution)/shard_map/return_products/ppermute | solution.py:29
  21.2 1.5 %collective-permute-done.8.other = f32[2,16,128]{2,1,0:T(8,128)S(1)} collective-permute-done((f32[2,16,128]{2,1,0:T(8,128)S(1)}, f32[2,16,128]{2,1,0:T(8,128)S(1)}, u32[]{:S(2)}, u32[]{:S(2)}) %collective-permute-start.8) | collective-permute-done | bytes 16416 | tf_op jit(solution)/shard_map/return_products/ppermute | solution.py:29
  22.8 1.7 %collective-permute-start.9 = (f32[1,16,128]{2,1,0:T(8,128)S(1)}, f32[1,16,128]{2,1,0:T(8,128)S(1)}, u32[]{:S(2)}, u32[]{:S(2)}) collective-permute-start(f32[1,16,128]{2,1,0:T(8,128)S(1)} %get-tuple-element.61), channel_id=1, source_target_pairs={{0,2},{1,3},{2,0},{3,1},{4,6},{5,7},{6,4},{7,5},{8,10},{9,11},{10,... | collective-permute-start | bytes 24584 | tf_op jit(solution)/shard_map/return_products/ppermute | solution.py:29
  24.5 0.0 collective-permute-done.6.other
  24.5 1.6 %collective-permute-start.7 = (f32[1,16,128]{2,1,0:T(8,128)S(1)}, f32[1,16,128]{2,1,0:T(8,128)S(1)}, u32[]{:S(2)}, u32[]{:S(2)}) collective-permute-start(f32[1,16,128]{2,1,0:T(8,128)S(1)} %get-tuple-element.57), channel_id=1, source_target_pairs={{0,16},{4,20},{8,24},{12,28},{16,0},{20,4},{24,8},{28,12},{1,17},{... | collective-permute-start | bytes 24584 | tf_op jit(solution)/shard_map/return_products/ppermute | solution.py:29
  26.1 1.2 %collective-permute-done.9.refs_3_ = f32[1,16,128]{2,1,0:T(8,128)S(1)} collective-permute-done((f32[1,16,128]{2,1,0:T(8,128)S(1)}, f32[1,16,128]{2,1,0:T(8,128)S(1)}, u32[]{:S(2)}, u32[]{:S(2)}) %collective-permute-start.9) | collective-permute-done | bytes 8224 | tf_op jit(solution)/shard_map/return_products/ppermute | solution.py:29
  27.3 0.9 %collective-permute-done.7.refs_1_ = f32[1,16,128]{2,1,0:T(8,128)S(1)} collective-permute-done((f32[1,16,128]{2,1,0:T(8,128)S(1)}, f32[1,16,128]{2,1,0:T(8,128)S(1)}, u32[]{:S(2)}, u32[]{:S(2)}) %collective-permute-start.7) | collective-permute-done | bytes 8224 | tf_op jit(solution)/shard_map/return_products/ppermute | solution.py:29
  28.2 0.3 product.1
  28.5 11.2 %all_to_all.9.parts = f32[32,3,2,128]{3,2,1,0:T(2,128)S(1)} all-to-all(f32[32,3,2,128]{3,2,1,0:T(2,128)S(1)} %get-tuple-element.63), channel_id=1, replica_groups=mesh['row'=8,'col'=4] {'row','col'}, dimensions={0} | all-to-all | bytes 196608 | tf_op jit(solution)/shard_map/product/all_to_all | solution.py:24
  39.8 1.2 %results.1 = (f32[16,128]{1,0:T(8,128)}, f32[16,16]{1,0:T(8,128)}, f32[16,16]{1,0:T(8,128)}, s32[1,1]{1,0:T(1,128)}) custom-call(f32[16,128]{1,0:T(8,128)S(1)} %copy-done.4, f32[16,128]{1,0:T(8,128)S(1)} %get-tuple-element.87.product, f32[32,3,2,128]{3,2,1,0:T(2,128)S(1)} %all_to_all.9.parts), custom_call_target="tpu_custom_call" | custom-call | tf_op jit(solution)/shard_map/results/results/pallas_call | solution.py:276
  41.0 0.6 %while.9 = (s32[]{:T(128)}, f32[16,16]{1,0:T(8,128)}, f32[16,128]{1,0:T(8,128)S(1)}, f32[16,128]{1,0:T(8,128)S(1)}, f32[32,3,2,128]{3,2,1,0:T(2,128)S(1)}) while((s32[]{:T(128)}, f32[16,16]{1,0:T(8,128)}, f32[16,128]{1,0:T(8,128)S(1)}, f32[16,128]{1,0:T(8,128)S(1)}, f32[32,3,2,128]{3,2,1,0:T(2,128)S(1)}) %tuple.20), condition=%region_1.0_spmd, body=%region_0.0_spmd | while | flops 1 | bytes 98393 | solution.py:305
  (5 shorter events, 0.0 us)
Async XLA Ops:
  0.6 5.1 %copy-start.4 = (f32[16,128]{1,0:T(8,128)S(1)}, f32[16,128]{1,0:T(8,128)}, u32[]{:S(2)}) copy-start(f32[16,128]{1,0:T(8,128)} %x_ref.3) | copy-start | bytes 24580
  0.6 1.6 %collective-permute-start.2 = (f32[1,16,128]{2,1,0:T(8,128)}, f32[1,16,128]{2,1,0:T(8,128)S(1)}, u32[]{:S(2)}, u32[]{:S(2)}) collective-permute-start(f32[1,16,128]{2,1,0:T(8,128)} %bitcast.6), channel_id=1, source_target_pairs={{0,4},{4,0},{8,12},{12,8},{16,20},{20,16},{24,28},{28,24},{1,5},{5... | collective-permute-start | bytes 24584 | tf_op jit(solution)/shard_map/share_vectors/ppermute | solution.py:29
  2.9 9.1 %collective-permute-start.3 = (f32[2,16,128]{2,1,0:T(8,128)S(1)}, f32[2,16,128]{2,1,0:T(8,128)S(1)}, u32[]{:S(2)}, u32[]{:S(2)}) collective-permute-start(f32[2,16,128]{2,1,0:T(8,128)S(1)} %join_row.2.mine), channel_id=1, source_target_pairs={{0,8},{4,12},{8,0},{12,4},{16,24},{20,28},{24,16},{28,20},{1,9},{5... | collective-permute-start | bytes 49160 | tf_op jit(solution)/shard_map/share_vectors/ppermute | solution.py:29
  5.7 3.7 %collective-permute-start = (f32[1,16,128]{2,1,0:T(8,128)S(1)}, f32[1,16,128]{2,1,0:T(8,128)S(1)}, u32[]{:S(2)}, u32[]{:S(2)}) collective-permute-start(f32[1,16,128]{2,1,0:T(8,128)S(1)} %bitcast.8), channel_id=1, source_target_pairs={{0,1},{1,0},{2,3},{3,2},{4,5},{5,4},{6,7},{7,6},{8,9},{9,8},{10,11... | collective-permute-start | bytes 24584 | tf_op jit(solution)/shard_map/share_vectors/ppermute | solution.py:29
  9.4 4.9 %collective-permute-start.1 = (f32[2,16,128]{2,1,0:T(8,128)S(1)}, f32[2,16,128]{2,1,0:T(8,128)S(1)}, u32[]{:S(2)}, u32[]{:S(2)}) collective-permute-start(f32[2,16,128]{2,1,0:T(8,128)S(1)} %join_col.1.near), channel_id=1, source_target_pairs={{0,2},{1,3},{2,0},{3,1},{4,6},{5,7},{6,4},{7,5},{8,10},{9,11},{10,... | collective-permute-start | bytes 49160 | tf_op jit(solution)/shard_map/share_vectors/ppermute | solution.py:29
  12.0 5.3 %collective-permute-start.4 = (f32[4,16,128]{2,1,0:T(8,128)S(1)}, f32[4,16,128]{2,1,0:T(8,128)S(1)}, u32[]{:S(2)}, u32[]{:S(2)}) collective-permute-start(f32[4,16,128]{2,1,0:T(8,128)S(1)} %join_row.3.near), channel_id=1, source_target_pairs={{0,16},{4,20},{8,24},{12,28},{16,0},{20,4},{24,8},{28,12},{1,17},{... | collective-permute-start | bytes 98312 | tf_op jit(solution)/shard_map/share_vectors/ppermute | solution.py:29
  14.2 0.7 %copy-start.1 = (s32[1,1,16]{2,1,0:T(1,128)S(1)}, s32[1,1,16]{2,1,0:T(1,128)}, u32[]{:S(2)}) copy-start(s32[1,1,16]{2,1,0:T(1,128)} %arow.3) | copy-start | bytes 196
  14.2 0.7 %copy-start.2 = (s32[1,1,16]{2,1,0:T(1,128)S(1)}, s32[1,1,16]{2,1,0:T(1,128)}, u32[]{:S(2)}) copy-start(s32[1,1,16]{2,1,0:T(1,128)} %bcol.3) | copy-start | bytes 196
  14.3 0.7 %copy-start.3 = (f32[128]{0:T(128)S(1)}, f32[128]{0:T(128)}, u32[]{:S(2)}) copy-start(f32[128]{0:T(128)} %param.9) | copy-start | bytes 1540
  14.9 1.2 %copy-start = (f32[1,1,16,128,128]{4,3,2,1,0:T(8,128)S(1)}, f32[1,1,16,128,128]{4,3,2,1,0:T(8,128)}, u32[]{:S(2)}) copy-start(f32[1,1,16,128,128]{4,3,2,1,0:T(8,128)} %tiles.1) | copy-start | bytes 3145732
  18.9 1.7 %collective-permute-start.5 = (f32[4,16,128]{2,1,0:T(8,128)S(1)}, f32[4,16,128]{2,1,0:T(8,128)S(1)}, u32[]{:S(2)}, u32[]{:S(2)}) collective-permute-start(f32[4,16,128]{2,1,0:T(8,128)S(1)} %get-tuple-element.53), channel_id=1, source_target_pairs={{0,4},{4,0},{8,12},{12,8},{16,20},{20,16},{24,28},{28,24},{1,5},{5... | collective-permute-start | bytes 98312 | tf_op jit(solution)/shard_map/return_products/ppermute | solution.py:29
  18.9 3.8 %collective-permute-start.8 = (f32[2,16,128]{2,1,0:T(8,128)S(1)}, f32[2,16,128]{2,1,0:T(8,128)S(1)}, u32[]{:S(2)}, u32[]{:S(2)}) collective-permute-start(f32[2,16,128]{2,1,0:T(8,128)S(1)} %get-tuple-element.59), channel_id=1, source_target_pairs={{0,1},{1,0},{2,3},{3,2},{4,5},{5,4},{6,7},{7,6},{8,9},{9,8},{10,11... | collective-permute-start | bytes 49160 | tf_op jit(solution)/shard_map/return_products/ppermute | solution.py:29
  20.6 3.9 %collective-permute-start.6 = (f32[2,16,128]{2,1,0:T(8,128)S(1)}, f32[2,16,128]{2,1,0:T(8,128)S(1)}, u32[]{:S(2)}, u32[]{:S(2)}) collective-permute-start(f32[2,16,128]{2,1,0:T(8,128)S(1)} %get-tuple-element.55), channel_id=1, source_target_pairs={{0,8},{4,12},{8,0},{12,4},{16,24},{20,28},{24,16},{28,20},{1,9},{5... | collective-permute-start | bytes 49160 | tf_op jit(solution)/shard_map/return_products/ppermute | solution.py:29
  22.8 4.5 %collective-permute-start.9 = (f32[1,16,128]{2,1,0:T(8,128)S(1)}, f32[1,16,128]{2,1,0:T(8,128)S(1)}, u32[]{:S(2)}, u32[]{:S(2)}) collective-permute-start(f32[1,16,128]{2,1,0:T(8,128)S(1)} %get-tuple-element.61), channel_id=1, source_target_pairs={{0,2},{1,3},{2,0},{3,1},{4,6},{5,7},{6,4},{7,5},{8,10},{9,11},{10,... | collective-permute-start | bytes 24584 | tf_op jit(solution)/shard_map/return_products/ppermute | solution.py:29
  24.5 3.7 %collective-permute-start.7 = (f32[1,16,128]{2,1,0:T(8,128)S(1)}, f32[1,16,128]{2,1,0:T(8,128)S(1)}, u32[]{:S(2)}, u32[]{:S(2)}) collective-permute-start(f32[1,16,128]{2,1,0:T(8,128)S(1)} %get-tuple-element.57), channel_id=1, source_target_pairs={{0,16},{4,20},{8,24},{12,28},{16,0},{20,4},{24,8},{28,12},{1,17},{... | collective-permute-start | bytes 24584 | tf_op jit(solution)/shard_map/return_products/ppermute | solution.py:29

commit v14 on v13

--- a/solution.py
+++ b/solution.py
@@ -82,10 +82,18 @@
     return total
 
 
-def join_kernel(mine, other, out):
-    half = mine.shape[0]
-    out[:half] = mine[...]
-    out[half:] = other[...]
+def join_kernel(axes, *refs):
+    for which, out in enumerate(refs[-axes:]):
+        mine, other = refs[2 * which : 2 * which + 2]
+        half = mine.shape[0]
+        out[:half] = mine[...]
+        out[half:] = other[...]
+
+
+def split_kernel(slots, tiles, *parts):
+    for slot in range(slots):
+        for part, piece in zip(parts, split(tiles[0, 0, slot])):
+            part[slot] = piece
 
 
 def part_blocks(sums, total, send, keep):
@@ -94,8 +102,8 @@
         send[block] = sums[2 * block + 1]
 
 
-def column_kernel(n_row, n_col, slots, place, arow, bcol, count, d_ref, near, far, tiles, send, keep, *refs):
-    *parts, rows, sums = refs
+def column_kernel(n_row, n_col, slots, place, arow, bcol, count, d_ref, near, far, *refs):
+    *parts, send, keep, rows, sums = refs
     me_row, me_col = place[0], place[1]
     half = n_col // 2
     for flip in range(n_col):
@@ -103,9 +111,7 @@
     sums[...] = jnp.zeros_like(sums)
     sums[0] = d_ref[...] * near[0]
     for slot in range(slots):
-        pieces = split(tiles[0, 0, slot])
-        for part, piece in zip(parts, pieces):
-            part[slot] = piece
+        pieces = [part[slot] for part in parts]
         block = jnp.where(slot < count[0, 0], bcol[0, 0, slot] ^ me_row, n_row)
         sums[block] += parts_product(rows[arow[0, 0, slot] ^ me_col], pieces, (((1,), (0,)), ((), ())))
     part_blocks(sums, n_row, send, keep)
@@ -196,23 +202,25 @@
     def blocks(total):
         return jax.ShapeDtypeStruct((total, nvec, width), jnp.float32)
 
-    def gather(axis):
-        size = lax.axis_size(axis)
-        near = vectors[None]
-        far = trade(near, axis, 1)
+    def gather(axes, after):
+        near = [vectors[None]] * len(axes)
+        far = [trade(vectors[None], axis, 1) for axis in axes]
         reach = 2
-        while reach < size:
-            near = pl.pallas_call(
-                join_kernel,
-                out_shape=blocks(reach),
-                in_specs=[VMEM] * 2,
-                out_specs=VMEM,
+        while any(reach < lax.axis_size(axis) for axis in axes):
+            going = [which for which, axis in enumerate(axes) if reach < lax.axis_size(axis)]
+            joined = pl.pallas_call(
+                functools.partial(join_kernel, len(going)),
+                out_shape=[blocks(reach)] * len(going),
+                in_specs=[VMEM] * (2 * len(going)) + [pl.BlockSpec(memory_space=pl.ANY)] * len(after),
+                out_specs=[VMEM] * len(going),
                 compiler_params=params,
-                name="join_" + axis,
-            )(near, far)
-            far = trade(near, axis, reach)
+                name="join",
+            )(*[half for which in going for half in (near[which], far[which])], *after)
+            for which, half in zip(going, joined):
+                near[which], far[which] = half, trade(half, axes[which], reach)
             reach *= 2
-        return near, far
+            after = ()
+        return list(zip(near, far))
 
     def halve(send, keep, axis):
         flip = 1
@@ -229,15 +237,24 @@
             flip *= 2
         return keep, trade(send, axis, flip)
 
+    with jax.named_scope("split_tiles"):
+        parts = pl.pallas_call(
+            functools.partial(split_kernel, slots),
+            out_shape=[part] * 3,
+            in_specs=[VMEM],
+            out_specs=[VMEM] * 3,
+            compiler_params=params,
+            cost_estimate=pl.CostEstimate(flops=0, bytes_accessed=5 * slots * width * width, transcendentals=0),
+            name="split_tiles",
+        )(tiles)
     with jax.named_scope("share_vectors"):
-        x_row = gather("row")
-        x_col = gather("col")
+        x_row, x_col = gather(("row", "col"), parts[:1])
     with jax.named_scope("column_terms"):
-        col_send, col_keep, *parts = pl.pallas_call(
+        col_send, col_keep = pl.pallas_call(
             functools.partial(column_kernel, n_row, n_col, slots),
-            out_shape=[blocks(n_row // 2)] * 2 + [part] * 3,
-            in_specs=[SMEM] * 4 + [VMEM] * 4,
-            out_specs=[VMEM] * 5,
+            out_shape=[blocks(n_row // 2)] * 2,
+            in_specs=[SMEM] * 4 + [VMEM] * 6,
+            out_specs=[VMEM] * 2,
             scratch_shapes=[
                 pltpu.VMEM((n_col, 3 * nvec, width), jnp.bfloat16),
                 pltpu.VMEM((n_row + 1, nvec, width), jnp.float32),
@@ -245,7 +262,7 @@
             compiler_params=params,
             cost_estimate=cost,
             name="column_terms",
-        )(place, tile_rows, tile_cols, tile_count, energy, *x_col, tiles)
+        )(place, tile_rows, tile_cols, tile_count, energy, *x_col, *parts)
     with jax.named_scope("row_terms"):
         col_send, row_send, row_keep = pl.pallas_call(
             functools.partial(row_kernel, n_row, n_col, slots),

time: 41.8 us -> 40.1 us (0.959)
  waiting for transfers between devices: 6.81 us -> 3.51 us
  starting transfers between devices: 14.6 us -> 16 us
  blocking collectives: 11.2 us -> 11.8 us
  Pallas kernels: 4.97 us -> 4.44 us
    ppermute x10, waiting for transfers between devices: 6.81 us -> 3.51 us  [trade(): return lax.ppermute(value, axis, [(p, p ^ flip) for p in range(size)])]
    ppermute x10, starting transfers between devices: 14.6 us -> 16 us  [trade(): return lax.ppermute(value, axis, [(p, p ^ flip) for p in range(size)])]
    all_to_all x1, blocking collectives: 11.2 us -> 11.8 us  [swap(): return lax.all_to_all(blocks, axis, 0, 0, tiled=True)]
    pallas_call x3, Pallas kernels: 0.7 us -> 0.2 us  [the longest x1 0.19 us: per_device(): pl.pallas_call(functools.partial(split_kernel, slots), out_shape=[part] *...]
  transfers between devices with their start and end apart: 10 -> 10, of which waited for: 5 -> 4; matrix products, arithmetic and copies ran while one was open for 0% -> 0% of each run, Pallas kernels for 3% -> 3%
where the time goes in v14:
time: 40.1 us; the launch traced here: 39.9 us
  starting transfers between devices  16 us (40%)
  blocking collectives  11.8 us (29%)
  Pallas kernels  4.44 us (11%)
  waiting for transfers between devices  3.51 us (9%)
  local copies, waits for them, and re-layouts  1.97 us (5%)
  between operations  1.38 us (3%)
  loops' own time  0.69 us (2%)
    ppermute x10, starting transfers between devices, trade(): return lax.ppermute(value, axis, [(p, p ^ flip) for p in range(size)])  16 us
    all_to_all x1, blocking collectives, swap(): return lax.all_to_all(blocks, axis, 0, 0, tiled=True)  11.8 us
    ppermute x10, waiting for transfers between devices, trade(): return lax.ppermute(value, axis, [(p, p ^ flip) for p in range(size)])  3.51 us
    unnamed x10, local copies, waits for them, and re-layouts  1.97 us
    pallas_call x1, Pallas kernels, per_device(): pl.pallas_call(functools.partial(row_kernel, n_row, n_col, slots), out_sh...  1.59 us
    pallas_call x1, Pallas kernels, per_device(): pl.pallas_call(functools.partial(result_kernel, scale), out_shape=[block,...  1.21 us
    pallas_call x1, Pallas kernels, per_device(): pl.pallas_call(functools.partial(column_kernel, n_row, n_col, slots), out...  1.1 us
  transfers between devices with their start and end apart: 10, of which 4 were waited for; matrix products, arithmetic and copies ran while one was open for 0% of the time, Pallas kernels for 3%

profile of v14, /device:TPU:0, one launch (start us, length us, event | category | flops | bytes accessed | tf_op | source)
XLA Modules:
  0.0 39.9 jit_solution(14310287002316655580)
XLA Ops:
  0.6 3.1 %collective-permute-start.1 = (f32[1,16,128]{2,1,0:T(8,128)}, f32[1,16,128]{2,1,0:T(8,128)S(1)}, u32[]{:S(2)}, u32[]{:S(2)}) collective-permute-start(f32[1,16,128]{2,1,0:T(8,128)} %bitcast.6), channel_id=1, source_target_pairs={{0,1},{1,0},{2,3},{3,2},{4,5},{5,4},{6,7},{7,6},{8,9},{9,8},{10,11... | collective-permute-start | bytes 24584 | tf_op jit(solution)/shard_map/share_vectors/ppermute | solution.py:29
  3.7 0.0 collective-permute-start
  3.7 0.0 copy-start
  3.7 1.2 %copy-done = f32[1,1,16,128,128]{4,3,2,1,0:T(8,128)S(1)} copy-done((f32[1,1,16,128,128]{4,3,2,1,0:T(8,128)S(1)}, f32[1,1,16,128,128]{4,3,2,1,0:T(8,128)}, u32[]{:S(2)}) %copy-start) | copy-done | bytes 1048600
  4.9 0.0 copy-start.4
  5.0 0.2 split_tiles.1
  5.1 0.4 %collective-permute-done.1.refs_3_ = f32[1,16,128]{2,1,0:T(8,128)S(1)} collective-permute-done((f32[1,16,128]{2,1,0:T(8,128)}, f32[1,16,128]{2,1,0:T(8,128)S(1)}, u32[]{:S(2)}, u32[]{:S(2)}) %collective-permute-start.1) | collective-permute-done | bytes 8224 | tf_op jit(solution)/shard_map/share_vectors/ppermute | solution.py:29
  5.6 0.0 collective-permute-done.refs_1_
  5.6 0.1 copy-done.4
  5.6 1.9 %collective-permute-start.3 = (f32[2,16,128]{2,1,0:T(8,128)S(1)}, f32[2,16,128]{2,1,0:T(8,128)S(1)}, u32[]{:S(2)}, u32[]{:S(2)}) collective-permute-start(f32[2,16,128]{2,1,0:T(8,128)S(1)} %get-tuple-element.55.refs_0_), channel_id=1, source_target_pairs={{0,8},{4,12},{8,0},{12,4},{16,24},{20,28},{24,16},{28,20},{1,9},{5... | collective-permute-start | bytes 49160 | tf_op jit(solution)/shard_map/share_vectors/ppermute | solution.py:29
  7.6 2.6 %collective-permute-start.2 = (f32[2,16,128]{2,1,0:T(8,128)S(1)}, f32[2,16,128]{2,1,0:T(8,128)S(1)}, u32[]{:S(2)}, u32[]{:S(2)}) collective-permute-start(f32[2,16,128]{2,1,0:T(8,128)S(1)} %get-tuple-element.51.near), channel_id=1, source_target_pairs={{0,2},{1,3},{2,0},{3,1},{4,6},{5,7},{6,4},{7,5},{8,10},{9,11},{10,... | collective-permute-start | bytes 49160 | tf_op jit(solution)/shard_map/share_vectors/ppermute | solution.py:29
  10.2 0.0 collective-permute-done.3.refs_1_
  10.2 1.5 %collective-permute-start.4 = (f32[4,16,128]{2,1,0:T(8,128)S(1)}, f32[4,16,128]{2,1,0:T(8,128)S(1)}, u32[]{:S(2)}, u32[]{:S(2)}) collective-permute-start(f32[4,16,128]{2,1,0:T(8,128)S(1)} %join.3.near), channel_id=1, source_target_pairs={{0,16},{4,20},{8,24},{12,28},{16,0},{20,4},{24,8},{28,12},{1,17},{... | collective-permute-start | bytes 98312 | tf_op jit(solution)/shard_map/share_vectors/ppermute | solution.py:29
  11.7 0.1 pad_add_fusion.place
  12.4 0.0 collective-permute-done.2.far
  12.4 0.0 copy-start.1
  12.4 0.0 copy-start.2
  12.5 0.0 copy-start.3
  12.5 0.6 %copy-done.1 = s32[1,1,16]{2,1,0:T(1,128)S(1)} copy-done((s32[1,1,16]{2,1,0:T(1,128)S(1)}, s32[1,1,16]{2,1,0:T(1,128)}, u32[]{:S(2)}) %copy-start.1) | copy-done | bytes 88
  13.1 0.0 copy-done.2
  13.1 0.0 copy-done.3
  13.1 1.1 %column_terms.1 = (f32[4,16,128]{2,1,0:T(8,128)S(1)}, f32[4,16,128]{2,1,0:T(8,128)S(1)}) custom-call(s32[2]{0:T(128)S(1)} %pad_add_fusion.place, s32[1,1,16]{2,1,0:T(1,128)S(1)} %copy-done.1, s32[1,1,16]{2,1,0:T(1,128)S(1)} %copy-done.2, s32[1,1]{1,0:T(1,128)S(6)} %copy.16.count, f32[1,128]{1,0:T(1,128)S(1)} %bitcast.5, ...), custom_call_target="tpu_custom_call" | custom-call | flops 50331648 | bytes 1048576 | tf_op jit(solution)/shard_map/column_terms/column_terms/pallas_call | solution.py:253
  14.2 0.0 collective-permute-done.4.far
  14.2 1.6 %row_terms.1 = (f32[4,16,128]{2,1,0:T(8,128)S(1)}, f32[2,16,128]{2,1,0:T(8,128)S(1)}, f32[2,16,128]{2,1,0:T(8,128)S(1)}) custom-call(s32[2]{0:T(128)S(1)} %pad_add_fusion.place, s32[1,1,16]{2,1,0:T(1,128)S(1)} %copy-done.1, s32[1,1,16]{2,1,0:T(1,128)S(1)} %copy-done.2, s32[1,1]{1,0:T(1,128)S(6)} %copy.16.count, f32[4,16,128]{2,1,0:T(8,128)S(1)} %join.3.near, ...), custom_call_target="tpu_custom_call" | custom-call | flops 50331648 | bytes 1048576 | tf_op jit(solution)/shard_map/row_terms/row_terms/pallas_call | solution.py:267
  15.8 0.1 collective-permute-start.5
  15.9 1.6 %collective-permute-start.8 = (f32[2,16,128]{2,1,0:T(8,128)S(1)}, f32[2,16,128]{2,1,0:T(8,128)S(1)}, u32[]{:S(2)}, u32[]{:S(2)}) collective-permute-start(f32[2,16,128]{2,1,0:T(8,128)S(1)} %get-tuple-element.63), channel_id=1, source_target_pairs={{0,1},{1,0},{2,3},{3,2},{4,5},{5,4},{6,7},{7,6},{8,9},{9,8},{10,11... | collective-permute-start | bytes 49160 | tf_op jit(solution)/shard_map/return_products/ppermute | solution.py:29
  17.5 0.0 collective-permute-done.5.other
  17.6 1.2 %collective-permute-start.6 = (f32[2,16,128]{2,1,0:T(8,128)S(1)}, f32[2,16,128]{2,1,0:T(8,128)S(1)}, u32[]{:S(2)}, u32[]{:S(2)}) collective-permute-start(f32[2,16,128]{2,1,0:T(8,128)S(1)} %get-tuple-element.59), channel_id=1, source_target_pairs={{0,8},{4,12},{8,0},{12,4},{16,24},{20,28},{24,16},{28,20},{1,9},{5... | collective-permute-start | bytes 49160 | tf_op jit(solution)/shard_map/return_products/ppermute | solution.py:29
  18.8 0.9 %collective-permute-done.8.other = f32[2,16,128]{2,1,0:T(8,128)S(1)} collective-permute-done((f32[2,16,128]{2,1,0:T(8,128)S(1)}, f32[2,16,128]{2,1,0:T(8,128)S(1)}, u32[]{:S(2)}, u32[]{:S(2)}) %collective-permute-start.8) | collective-permute-done | bytes 16416 | tf_op jit(solution)/shard_map/return_products/ppermute | solution.py:29
  19.7 2.4 %collective-permute-start.9 = (f32[1,16,128]{2,1,0:T(8,128)S(1)}, f32[1,16,128]{2,1,0:T(8,128)S(1)}, u32[]{:S(2)}, u32[]{:S(2)}) collective-permute-start(f32[1,16,128]{2,1,0:T(8,128)S(1)} %get-tuple-element.65), channel_id=1, source_target_pairs={{0,2},{1,3},{2,0},{3,1},{4,6},{5,7},{6,4},{7,5},{8,10},{9,11},{10,... | collective-permute-start | bytes 24584 | tf_op jit(solution)/shard_map/return_products/ppermute | solution.py:29
  22.1 0.0 collective-permute-done.6.other
  22.1 1.6 %collective-permute-start.7 = (f32[1,16,128]{2,1,0:T(8,128)S(1)}, f32[1,16,128]{2,1,0:T(8,128)S(1)}, u32[]{:S(2)}, u32[]{:S(2)}) collective-permute-start(f32[1,16,128]{2,1,0:T(8,128)S(1)} %get-tuple-element.61), channel_id=1, source_target_pairs={{0,16},{4,20},{8,24},{12,28},{16,0},{20,4},{24,8},{28,12},{1,17},{... | collective-permute-start | bytes 24584 | tf_op jit(solution)/shard_map/return_products/ppermute | solution.py:29
  23.7 0.6 %collective-permute-done.9.refs_3_ = f32[1,16,128]{2,1,0:T(8,128)S(1)} collective-permute-done((f32[1,16,128]{2,1,0:T(8,128)S(1)}, f32[1,16,128]{2,1,0:T(8,128)S(1)}, u32[]{:S(2)}, u32[]{:S(2)}) %collective-permute-start.9) | collective-permute-done | bytes 8224 | tf_op jit(solution)/shard_map/return_products/ppermute | solution.py:29
  24.3 1.5 %collective-permute-done.7.refs_1_ = f32[1,16,128]{2,1,0:T(8,128)S(1)} collective-permute-done((f32[1,16,128]{2,1,0:T(8,128)S(1)}, f32[1,16,128]{2,1,0:T(8,128)S(1)}, u32[]{:S(2)}, u32[]{:S(2)}) %collective-permute-start.7) | collective-permute-done | bytes 8224 | tf_op jit(solution)/shard_map/return_products/ppermute | solution.py:29
  25.8 0.3 product.1
  26.2 11.8 %all_to_all.9.parts = f32[32,3,2,128]{3,2,1,0:T(2,128)S(1)} all-to-all(f32[32,3,2,128]{3,2,1,0:T(2,128)S(1)} %get-tuple-element.67), channel_id=1, replica_groups=mesh['row'=8,'col'=4] {'row','col'}, dimensions={0} | all-to-all | bytes 196608 | tf_op jit(solution)/shard_map/product/all_to_all | solution.py:24
  38.0 1.2 %results.1 = (f32[16,128]{1,0:T(8,128)}, f32[16,16]{1,0:T(8,128)}, f32[16,16]{1,0:T(8,128)}, s32[1,1]{1,0:T(1,128)}) custom-call(f32[16,128]{1,0:T(8,128)S(1)} %copy-done.4, f32[16,128]{1,0:T(8,128)S(1)} %get-tuple-element.91.product, f32[32,3,2,128]{3,2,1,0:T(2,128)S(1)} %all_to_all.9.parts), custom_call_target="tpu_custom_call" | custom-call | tf_op jit(solution)/shard_map/results/results/pallas_call | solution.py:293
  39.2 0.7 %while.9 = (s32[]{:T(128)}, f32[16,16]{1,0:T(8,128)}, f32[16,128]{1,0:T(8,128)S(1)}, f32[16,128]{1,0:T(8,128)S(1)}, f32[32,3,2,128]{3,2,1,0:T(2,128)S(1)}) while((s32[]{:T(128)}, f32[16,16]{1,0:T(8,128)}, f32[16,128]{1,0:T(8,128)S(1)}, f32[16,128]{1,0:T(8,128)S(1)}, f32[32,3,2,128]{3,2,1,0:T(2,128)S(1)}) %tuple.20), condition=%region_1.0_spmd, body=%region_0.0_spmd | while | flops 1 | bytes 98393 | solution.py:322
  (5 shorter events, 0.0 us)
Async XLA Ops:
  0.6 4.9 %collective-permute-start.1 = (f32[1,16,128]{2,1,0:T(8,128)}, f32[1,16,128]{2,1,0:T(8,128)S(1)}, u32[]{:S(2)}, u32[]{:S(2)}) collective-permute-start(f32[1,16,128]{2,1,0:T(8,128)} %bitcast.6), channel_id=1, source_target_pairs={{0,1},{1,0},{2,3},{3,2},{4,5},{5,4},{6,7},{7,6},{8,9},{9,8},{10,11... | collective-permute-start | bytes 24584 | tf_op jit(solution)/shard_map/share_vectors/ppermute | solution.py:29
  3.7 1.8 %collective-permute-start = (f32[1,16,128]{2,1,0:T(8,128)}, f32[1,16,128]{2,1,0:T(8,128)S(1)}, u32[]{:S(2)}, u32[]{:S(2)}) collective-permute-start(f32[1,16,128]{2,1,0:T(8,128)} %bitcast.7), channel_id=1, source_target_pairs={{0,4},{4,0},{8,12},{12,8},{16,20},{20,16},{24,28},{28,24},{1,5},{5... | collective-permute-start | bytes 24584 | tf_op jit(solution)/shard_map/share_vectors/ppermute | solution.py:29
  3.7 1.2 %copy-start = (f32[1,1,16,128,128]{4,3,2,1,0:T(8,128)S(1)}, f32[1,1,16,128,128]{4,3,2,1,0:T(8,128)}, u32[]{:S(2)}) copy-start(f32[1,1,16,128,128]{4,3,2,1,0:T(8,128)} %tiles.1) | copy-start | bytes 3145732
  4.9 0.7 %copy-start.4 = (f32[16,128]{1,0:T(8,128)S(1)}, f32[16,128]{1,0:T(8,128)}, u32[]{:S(2)}) copy-start(f32[16,128]{1,0:T(8,128)} %x_ref.3) | copy-start | bytes 24580
  5.6 4.5 %collective-permute-start.3 = (f32[2,16,128]{2,1,0:T(8,128)S(1)}, f32[2,16,128]{2,1,0:T(8,128)S(1)}, u32[]{:S(2)}, u32[]{:S(2)}) collective-permute-start(f32[2,16,128]{2,1,0:T(8,128)S(1)} %get-tuple-element.55.refs_0_), channel_id=1, source_target_pairs={{0,8},{4,12},{8,0},{12,4},{16,24},{20,28},{24,16},{28,20},{1,9},{5... | collective-permute-start | bytes 49160 | tf_op jit(solution)/shard_map/share_vectors/ppermute | solution.py:29
  7.6 4.8 %collective-permute-start.2 = (f32[2,16,128]{2,1,0:T(8,128)S(1)}, f32[2,16,128]{2,1,0:T(8,128)S(1)}, u32[]{:S(2)}, u32[]{:S(2)}) collective-permute-start(f32[2,16,128]{2,1,0:T(8,128)S(1)} %get-tuple-element.51.near), channel_id=1, source_target_pairs={{0,2},{1,3},{2,0},{3,1},{4,6},{5,7},{6,4},{7,5},{8,10},{9,11},{10,... | collective-permute-start | bytes 49160 | tf_op jit(solution)/shard_map/share_vectors/ppermute | solution.py:29
  10.2 4.1 %collective-permute-start.4 = (f32[4,16,128]{2,1,0:T(8,128)S(1)}, f32[4,16,128]{2,1,0:T(8,128)S(1)}, u32[]{:S(2)}, u32[]{:S(2)}) collective-permute-start(f32[4,16,128]{2,1,0:T(8,128)S(1)} %join.3.near), channel_id=1, source_target_pairs={{0,16},{4,20},{8,24},{12,28},{16,0},{20,4},{24,8},{28,12},{1,17},{... | collective-permute-start | bytes 98312 | tf_op jit(solution)/shard_map/share_vectors/ppermute | solution.py:29
  12.4 0.7 %copy-start.1 = (s32[1,1,16]{2,1,0:T(1,128)S(1)}, s32[1,1,16]{2,1,0:T(1,128)}, u32[]{:S(2)}) copy-start(s32[1,1,16]{2,1,0:T(1,128)} %arow.3) | copy-start | bytes 196
  12.4 0.7 %copy-start.2 = (s32[1,1,16]{2,1,0:T(1,128)S(1)}, s32[1,1,16]{2,1,0:T(1,128)}, u32[]{:S(2)}) copy-start(s32[1,1,16]{2,1,0:T(1,128)} %bcol.3) | copy-start | bytes 196
  12.5 0.7 %copy-start.3 = (f32[128]{0:T(128)S(1)}, f32[128]{0:T(128)}, u32[]{:S(2)}) copy-start(f32[128]{0:T(128)} %param.9) | copy-start | bytes 1540
  15.8 1.7 %collective-permute-start.5 = (f32[4,16,128]{2,1,0:T(8,128)S(1)}, f32[4,16,128]{2,1,0:T(8,128)S(1)}, u32[]{:S(2)}, u32[]{:S(2)}) collective-permute-start(f32[4,16,128]{2,1,0:T(8,128)S(1)} %get-tuple-element.57), channel_id=1, source_target_pairs={{0,4},{4,0},{8,12},{12,8},{16,20},{20,16},{24,28},{28,24},{1,5},{5... | collective-permute-start | bytes 98312 | tf_op jit(solution)/shard_map/return_products/ppermute | solution.py:29
  15.9 3.8 %collective-permute-start.8 = (f32[2,16,128]{2,1,0:T(8,128)S(1)}, f32[2,16,128]{2,1,0:T(8,128)S(1)}, u32[]{:S(2)}, u32[]{:S(2)}) collective-permute-start(f32[2,16,128]{2,1,0:T(8,128)S(1)} %get-tuple-element.63), channel_id=1, source_target_pairs={{0,1},{1,0},{2,3},{3,2},{4,5},{5,4},{6,7},{7,6},{8,9},{9,8},{10,11... | collective-permute-start | bytes 49160 | tf_op jit(solution)/shard_map/return_products/ppermute | solution.py:29
  17.6 4.5 %collective-permute-start.6 = (f32[2,16,128]{2,1,0:T(8,128)S(1)}, f32[2,16,128]{2,1,0:T(8,128)S(1)}, u32[]{:S(2)}, u32[]{:S(2)}) collective-permute-start(f32[2,16,128]{2,1,0:T(8,128)S(1)} %get-tuple-element.59), channel_id=1, source_target_pairs={{0,8},{4,12},{8,0},{12,4},{16,24},{20,28},{24,16},{28,20},{1,9},{5... | collective-permute-start | bytes 49160 | tf_op jit(solution)/shard_map/return_products/ppermute | solution.py:29
  19.7 4.5 %collective-permute-start.9 = (f32[1,16,128]{2,1,0:T(8,128)S(1)}, f32[1,16,128]{2,1,0:T(8,128)S(1)}, u32[]{:S(2)}, u32[]{:S(2)}) collective-permute-start(f32[1,16,128]{2,1,0:T(8,128)S(1)} %get-tuple-element.65), channel_id=1, source_target_pairs={{0,2},{1,3},{2,0},{3,1},{4,6},{5,7},{6,4},{7,5},{8,10},{9,11},{10,... | collective-permute-start | bytes 24584 | tf_op jit(solution)/shard_map/return_products/ppermute | solution.py:29
  22.1 3.7 %collective-permute-start.7 = (f32[1,16,128]{2,1,0:T(8,128)S(1)}, f32[1,16,128]{2,1,0:T(8,128)S(1)}, u32[]{:S(2)}, u32[]{:S(2)}) collective-permute-start(f32[1,16,128]{2,1,0:T(8,128)S(1)} %get-tuple-element.61), channel_id=1, source_target_pairs={{0,16},{4,20},{8,24},{12,28},{16,0},{20,4},{24,8},{28,12},{1,17},{... | collective-permute-start | bytes 24584 | tf_op jit(solution)/shard_map/return_products/ppermute | solution.py:29

commit v15 on v14

--- a/solution.py
+++ b/solution.py
@@ -57,7 +57,9 @@
     for square in packed:
         spread = jnp.concatenate([jnp.broadcast_to(square[g : g + 1], (per, width)) for g in range(rows)], axis=0)
         wide.append(jnp.where(mask, spread, 0.0))
-    return mult(jnp.concatenate(wide, axis=0), (lane % nvec == column).astype(jnp.float32))
+    fold = (lane % nvec == column).astype(jnp.bfloat16)
+    pieces = [jnp.dot(part, fold, preferred_element_type=jnp.float32) for part in split(jnp.concatenate(wide, axis=0))]
+    return (pieces[2] + pieces[1]) + pieces[0]
 
 
 def split(value):
@@ -90,7 +92,10 @@
         out[half:] = other[...]
 
 
-def split_kernel(slots, tiles, *parts):
+def prepare_kernel(slots, tiles, *refs):
+    small, parts, copies = refs[:3], refs[3:6], refs[6:]
+    for array, copy in zip(small, copies):
+        copy[...] = array[...]
     for slot in range(slots):
         for part, piece in zip(parts, split(tiles[0, 0, slot])):
             part[slot] = piece
@@ -117,10 +122,14 @@
     part_blocks(sums, n_row, send, keep)
 
 
-def row_kernel(n_row, n_col, slots, place, arow, bcol, count, near, far, early, *refs):
-    *parts, late, send, keep, cols, sums = refs
+def hand_on_kernel(early, after, late):
+    del after
+    late[...] = early[...]
+
+
+def row_kernel(n_row, n_col, slots, place, arow, bcol, count, near, far, *refs):
+    *parts, send, keep, cols, sums = refs
     me_row, me_col = place[0], place[1]
-    late[...] = early[...]
     half = n_row // 2
     for flip in range(n_row):
         cols[flip] = stack_split(near[flip] if flip < half else far[flip - half])
@@ -237,16 +246,17 @@
             flip *= 2
         return keep, trade(send, axis, flip)
 
-    with jax.named_scope("split_tiles"):
-        parts = pl.pallas_call(
-            functools.partial(split_kernel, slots),
-            out_shape=[part] * 3,
-            in_specs=[VMEM],
-            out_specs=[VMEM] * 3,
+    with jax.named_scope("prepare"):
+        small = (tile_rows, tile_cols, energy)
+        *parts, arow, bcol, energy = pl.pallas_call(
+            functools.partial(prepare_kernel, slots),
+            out_shape=[part] * 3 + [jax.ShapeDtypeStruct(array.shape, array.dtype) for array in small],
+            in_specs=[VMEM] * 4,
+            out_specs=[VMEM] * 6,
             compiler_params=params,
             cost_estimate=pl.CostEstimate(flops=0, bytes_accessed=5 * slots * width * width, transcendentals=0),
-            name="split_tiles",
-        )(tiles)
+            name="prepare",
+        )(tiles, *small)
     with jax.named_scope("share_vectors"):
         x_row, x_col = gather(("row", "col"), parts[:1])
     with jax.named_scope("column_terms"):
@@ -262,13 +272,21 @@
             compiler_params=params,
             cost_estimate=cost,
             name="column_terms",
-        )(place, tile_rows, tile_cols, tile_count, energy, *x_col, *parts)
+        )(place, arow, bcol, tile_count, energy, *x_col, *parts)
+        col_send = pl.pallas_call(
+            hand_on_kernel,
+            out_shape=blocks(n_row // 2),
+            in_specs=[VMEM, pl.BlockSpec(memory_space=pl.ANY)],
+            out_specs=VMEM,
+            compiler_params=params,
+            name="hand_on",
+        )(col_send, x_row[1])
     with jax.named_scope("row_terms"):
-        col_send, row_send, row_keep = pl.pallas_call(
+        row_send, row_keep = pl.pallas_call(
             functools.partial(row_kernel, n_row, n_col, slots),
-            out_shape=[blocks(n_row // 2)] + [blocks(n_col // 2)] * 2,
-            in_specs=[SMEM] * 4 + [VMEM] * 6,
-            out_specs=[VMEM] * 3,
+            out_shape=[blocks(n_col // 2)] * 2,
+            in_specs=[SMEM] * 4 + [VMEM] * 5,
+            out_specs=[VMEM] * 2,
             scratch_shapes=[
                 pltpu.VMEM((n_row, 3 * nvec, width), jnp.bfloat16),
                 pltpu.VMEM((n_col + 1, nvec, width), jnp.float32),
@@ -276,7 +294,7 @@
             compiler_params=params,
             cost_estimate=cost,
             name="row_terms",
-        )(place, tile_rows, tile_cols, tile_count, *x_row, col_send, *parts)
+        )(place, arow, bcol, tile_count, *x_row, *parts)
     with jax.named_scope("return_products"):
         sums = halve(col_send, col_keep, "row") + halve(row_send, row_keep, "col")
     with jax.named_scope("product"):

time: 40.1 us -> 39.8 us (level)
  local copies, waits for them, and re-layouts: 1.97 us -> 1.33 us
  waiting for transfers between devices: 3.51 us -> 4.03 us
    unnamed x10, local copies, waits for them, and re-layouts: 1.97 us -> 1.33 us
    ppermute x10, waiting for transfers between devices: 3.51 us -> 4.03 us  [trade(): return lax.ppermute(value, axis, [(p, p ^ flip) for p in range(size)])]
  transfers between devices with their start and end apart: 10 -> 10, of which waited for: 4 -> 5; matrix products, arithmetic and copies ran while one was open for 0% -> 0% of each run, Pallas kernels for 3% -> 7%
where the time goes in v15:
time: 39.8 us; the launch traced here: 39.6 us
  starting transfers between devices  15.8 us (40%)
  blocking collectives  11.8 us (30%)
  Pallas kernels  4.4 us (11%)
  waiting for transfers between devices  4.03 us (10%)
  between operations  1.38 us (3%)
  local copies, waits for them, and re-layouts  1.33 us (3%)
  loops' own time  0.69 us (2%)
    ppermute x10, starting transfers between devices, trade(): return lax.ppermute(value, axis, [(p, p ^ flip) for p in range(size)])  15.8 us
    all_to_all x1, blocking collectives, swap(): return lax.all_to_all(blocks, axis, 0, 0, tiled=True)  11.8 us
    ppermute x10, waiting for transfers between devices, trade(): return lax.ppermute(value, axis, [(p, p ^ flip) for p in range(size)])  4.03 us
    pallas_call x1, Pallas kernels, per_device(): pl.pallas_call(functools.partial(row_kernel, n_row, n_col, slots), out_sh...  1.58 us
    unnamed x10, local copies, waits for them, and re-layouts  1.33 us
    pallas_call x1, Pallas kernels, per_device(): pl.pallas_call(functools.partial(result_kernel, scale), out_shape=[block,...  1.16 us
    pallas_call x1, Pallas kernels, per_device(): pl.pallas_call(functools.partial(column_kernel, n_row, n_col, slots), out...  1.1 us
  transfers between devices with their start and end apart: 10, of which 5 were waited for; matrix products, arithmetic and copies ran while one was open for 0% of the time, Pallas kernels for 7%

profile of v15, /device:TPU:0, one launch (start us, length us, event | category | flops | bytes accessed | tf_op | source)
XLA Modules:
  0.0 39.6 jit_solution(9472285127711552060)
XLA Ops:
  0.6 0.0 copy-start.1
  0.6 0.0 copy-start.2
  0.7 0.0 copy-start.3
  0.7 0.5 %collective-permute-start = (f32[1,16,128]{2,1,0:T(8,128)}, f32[1,16,128]{2,1,0:T(8,128)S(1)}, u32[]{:S(2)}, u32[]{:S(2)}) collective-permute-start(f32[1,16,128]{2,1,0:T(8,128)} %bitcast.6), channel_id=1, source_target_pairs={{0,4},{4,0},{8,12},{12,8},{16,20},{20,16},{24,28},{28,24},{1,5},{5... | collective-permute-start | bytes 24584 | tf_op jit(solution)/shard_map/share_vectors/ppermute | solution.py:29
  1.2 2.6 %collective-permute-start.1 = (f32[1,16,128]{2,1,0:T(8,128)}, f32[1,16,128]{2,1,0:T(8,128)S(1)}, u32[]{:S(2)}, u32[]{:S(2)}) collective-permute-start(f32[1,16,128]{2,1,0:T(8,128)} %bitcast.7), channel_id=1, source_target_pairs={{0,1},{1,0},{2,3},{3,2},{4,5},{5,4},{6,7},{7,6},{8,9},{9,8},{10,11... | collective-permute-start | bytes 24584 | tf_op jit(solution)/shard_map/share_vectors/ppermute | solution.py:29
  3.8 0.0 copy-done.1
  3.8 0.0 copy-done.2
  3.8 0.0 copy-done.3
  3.8 0.0 copy-start
  3.8 1.2 %copy-done = f32[1,1,16,128,128]{4,3,2,1,0:T(8,128)S(1)} copy-done((f32[1,1,16,128,128]{4,3,2,1,0:T(8,128)S(1)}, f32[1,1,16,128,128]{4,3,2,1,0:T(8,128)}, u32[]{:S(2)}) %copy-start) | copy-done | bytes 1048600
  5.1 0.0 copy-start.4
  5.1 0.2 prepare.1
  5.3 0.0 collective-permute-done.refs_1_
  5.3 0.4 %collective-permute-done.1.refs_3_ = f32[1,16,128]{2,1,0:T(8,128)S(1)} collective-permute-done((f32[1,16,128]{2,1,0:T(8,128)}, f32[1,16,128]{2,1,0:T(8,128)S(1)}, u32[]{:S(2)}, u32[]{:S(2)}) %collective-permute-start.1) | collective-permute-done | bytes 8224 | tf_op jit(solution)/shard_map/share_vectors/ppermute | solution.py:29
  5.7 0.1 copy-done.4
  5.8 1.8 %collective-permute-start.3 = (f32[2,16,128]{2,1,0:T(8,128)S(1)}, f32[2,16,128]{2,1,0:T(8,128)S(1)}, u32[]{:S(2)}, u32[]{:S(2)}) collective-permute-start(f32[2,16,128]{2,1,0:T(8,128)S(1)} %get-tuple-element.61.refs_0_), channel_id=1, source_target_pairs={{0,8},{4,12},{8,0},{12,4},{16,24},{20,28},{24,16},{28,20},{1,9},{5... | collective-permute-start | bytes 49160 | tf_op jit(solution)/shard_map/share_vectors/ppermute | solution.py:29
  7.6 2.6 %collective-permute-start.2 = (f32[2,16,128]{2,1,0:T(8,128)S(1)}, f32[2,16,128]{2,1,0:T(8,128)S(1)}, u32[]{:S(2)}, u32[]{:S(2)}) collective-permute-start(f32[2,16,128]{2,1,0:T(8,128)S(1)} %get-tuple-element.56.near), channel_id=1, source_target_pairs={{0,2},{1,3},{2,0},{3,1},{4,6},{5,7},{6,4},{7,5},{8,10},{9,11},{10,... | collective-permute-start | bytes 49160 | tf_op jit(solution)/shard_map/share_vectors/ppermute | solution.py:29
  10.2 0.0 collective-permute-done.3.refs_1_
  10.2 1.5 %collective-permute-start.4 = (f32[4,16,128]{2,1,0:T(8,128)S(1)}, f32[4,16,128]{2,1,0:T(8,128)S(1)}, u32[]{:S(2)}, u32[]{:S(2)}) collective-permute-start(f32[4,16,128]{2,1,0:T(8,128)S(1)} %join.3.near), channel_id=1, source_target_pairs={{0,16},{4,20},{8,24},{12,28},{16,0},{20,4},{24,8},{28,12},{1,17},{... | collective-permute-start | bytes 98312 | tf_op jit(solution)/shard_map/share_vectors/ppermute | solution.py:29
  11.7 0.1 pad_add_fusion.place
  12.5 0.0 collective-permute-done.2.far
  12.5 1.1 %column_terms.1 = (f32[4,16,128]{2,1,0:T(8,128)S(1)}, f32[4,16,128]{2,1,0:T(8,128)S(1)}) custom-call(s32[2]{0:T(128)S(1)} %pad_add_fusion.place, s32[1,1,16]{2,1,0:T(1,128)S(1)} %get-tuple-element.52.arow, s32[1,1,16]{2,1,0:T(1,128)S(1)} %get-tuple-element.53.bcol, s32[1,1]{1,0:T(1,128)S(6)} %copy.16.count, f32[1,128]{1,0:T(1,128)S(1)} %get-tuple-element.54.d_ref, ...), custom_call_target="tpu_custom_call" | custom-call | flops 50331648 | bytes 1048576 | tf_op jit(solution)/shard_map/column_terms/column_terms/pallas_call | solution.py:263
  13.6 0.5 %collective-permute-done.4.after.far = f32[4,16,128]{2,1,0:T(8,128)S(1)} collective-permute-done((f32[4,16,128]{2,1,0:T(8,128)S(1)}, f32[4,16,128]{2,1,0:T(8,128)S(1)}, u32[]{:S(2)}, u32[]{:S(2)}) %collective-permute-start.4) | collective-permute-done | bytes 32800 | tf_op jit(solution)/shard_map/share_vectors/ppermute | solution.py:29
  14.1 0.0 collective-permute-start.5
  14.1 1.6 %row_terms.1 = (f32[2,16,128]{2,1,0:T(8,128)S(1)}, f32[2,16,128]{2,1,0:T(8,128)S(1)}) custom-call(s32[2]{0:T(128)S(1)} %pad_add_fusion.place, s32[1,1,16]{2,1,0:T(1,128)S(1)} %get-tuple-element.52.arow, s32[1,1,16]{2,1,0:T(1,128)S(1)} %get-tuple-element.53.bcol, s32[1,1]{1,0:T(1,128)S(6)} %copy.16.count, f32[4,16,128]{2,1,0:T(8,128)S(1)} %join.3.near, ...), custom_call_target="tpu_custom_call" | custom-call | flops 50331648 | bytes 1048576 | tf_op jit(solution)/shard_map/row_terms/row_terms/pallas_call | solution.py:285
  15.7 1.6 %collective-permute-start.8 = (f32[2,16,128]{2,1,0:T(8,128)S(1)}, f32[2,16,128]{2,1,0:T(8,128)S(1)}, u32[]{:S(2)}, u32[]{:S(2)}) collective-permute-start(f32[2,16,128]{2,1,0:T(8,128)S(1)} %get-tuple-element.67), channel_id=1, source_target_pairs={{0,1},{1,0},{2,3},{3,2},{4,5},{5,4},{6,7},{7,6},{8,9},{9,8},{10,11... | collective-permute-start | bytes 49160 | tf_op jit(solution)/shard_map/return_products/ppermute | solution.py:29
  17.4 0.0 collective-permute-done.5.other
  17.4 1.2 %collective-permute-start.6 = (f32[2,16,128]{2,1,0:T(8,128)S(1)}, f32[2,16,128]{2,1,0:T(8,128)S(1)}, u32[]{:S(2)}, u32[]{:S(2)}) collective-permute-start(f32[2,16,128]{2,1,0:T(8,128)S(1)} %get-tuple-element.63), channel_id=1, source_target_pairs={{0,8},{4,12},{8,0},{12,4},{16,24},{20,28},{24,16},{28,20},{1,9},{5... | collective-permute-start | bytes 49160 | tf_op jit(solution)/shard_map/return_products/ppermute | solution.py:29
  18.6 0.9 %collective-permute-done.8.other = f32[2,16,128]{2,1,0:T(8,128)S(1)} collective-permute-done((f32[2,16,128]{2,1,0:T(8,128)S(1)}, f32[2,16,128]{2,1,0:T(8,128)S(1)}, u32[]{:S(2)}, u32[]{:S(2)}) %collective-permute-start.8) | collective-permute-done | bytes 16416 | tf_op jit(solution)/shard_map/return_products/ppermute | solution.py:29
  19.5 2.2 %collective-permute-start.9 = (f32[1,16,128]{2,1,0:T(8,128)S(1)}, f32[1,16,128]{2,1,0:T(8,128)S(1)}, u32[]{:S(2)}, u32[]{:S(2)}) collective-permute-start(f32[1,16,128]{2,1,0:T(8,128)S(1)} %get-tuple-element.69), channel_id=1, source_target_pairs={{0,2},{1,3},{2,0},{3,1},{4,6},{5,7},{6,4},{7,5},{8,10},{9,11},{10,... | collective-permute-start | bytes 24584 | tf_op jit(solution)/shard_map/return_products/ppermute | solution.py:29
  21.8 0.0 collective-permute-done.6.other
  21.8 1.6 %collective-permute-start.7 = (f32[1,16,128]{2,1,0:T(8,128)S(1)}, f32[1,16,128]{2,1,0:T(8,128)S(1)}, u32[]{:S(2)}, u32[]{:S(2)}) collective-permute-start(f32[1,16,128]{2,1,0:T(8,128)S(1)} %get-tuple-element.65), channel_id=1, source_target_pairs={{0,16},{4,20},{8,24},{12,28},{16,0},{20,4},{24,8},{28,12},{1,17},{... | collective-permute-start | bytes 24584 | tf_op jit(solution)/shard_map/return_products/ppermute | solution.py:29
  23.4 0.7 %collective-permute-done.9.refs_3_ = f32[1,16,128]{2,1,0:T(8,128)S(1)} collective-permute-done((f32[1,16,128]{2,1,0:T(8,128)S(1)}, f32[1,16,128]{2,1,0:T(8,128)S(1)}, u32[]{:S(2)}, u32[]{:S(2)}) %collective-permute-start.9) | collective-permute-done | bytes 8224 | tf_op jit(solution)/shard_map/return_products/ppermute | solution.py:29
  24.1 1.4 %collective-permute-done.7.refs_1_ = f32[1,16,128]{2,1,0:T(8,128)S(1)} collective-permute-done((f32[1,16,128]{2,1,0:T(8,128)S(1)}, f32[1,16,128]{2,1,0:T(8,128)S(1)}, u32[]{:S(2)}, u32[]{:S(2)}) %collective-permute-start.7) | collective-permute-done | bytes 8224 | tf_op jit(solution)/shard_map/return_products/ppermute | solution.py:29
  25.5 0.3 product.1
  25.8 11.8 %all_to_all.9.parts = f32[32,3,2,128]{3,2,1,0:T(2,128)S(1)} all-to-all(f32[32,3,2,128]{3,2,1,0:T(2,128)S(1)} %get-tuple-element.71), channel_id=1, replica_groups=mesh['row'=8,'col'=4] {'row','col'}, dimensions={0} | all-to-all | bytes 196608 | tf_op jit(solution)/shard_map/product/all_to_all | solution.py:24
  37.7 1.2 %results.1 = (f32[16,128]{1,0:T(8,128)}, f32[16,16]{1,0:T(8,128)}, f32[16,16]{1,0:T(8,128)}, s32[1,1]{1,0:T(1,128)}) custom-call(f32[16,128]{1,0:T(8,128)S(1)} %copy-done.4, f32[16,128]{1,0:T(8,128)S(1)} %get-tuple-element.95.product, f32[32,3,2,128]{3,2,1,0:T(2,128)S(1)} %all_to_all.9.parts), custom_call_target="tpu_custom_call" | custom-call | tf_op jit(solution)/shard_map/results/results/pallas_call | solution.py:311
  38.9 0.7 %while.9 = (s32[]{:T(128)}, f32[16,16]{1,0:T(8,128)}, f32[16,128]{1,0:T(8,128)S(1)}, f32[16,128]{1,0:T(8,128)S(1)}, f32[32,3,2,128]{3,2,1,0:T(2,128)S(1)}) while((s32[]{:T(128)}, f32[16,16]{1,0:T(8,128)}, f32[16,128]{1,0:T(8,128)S(1)}, f32[16,128]{1,0:T(8,128)S(1)}, f32[32,3,2,128]{3,2,1,0:T(2,128)S(1)}) %tuple.20), condition=%region_1.0_spmd, body=%region_0.0_spmd | while | flops 1 | bytes 98393 | solution.py:340
  (6 shorter events, 0.0 us)
Async XLA Ops:
  0.6 3.2 %copy-start.1 = (s32[1,1,16]{2,1,0:T(1,128)S(1)}, s32[1,1,16]{2,1,0:T(1,128)}, u32[]{:S(2)}) copy-start(s32[1,1,16]{2,1,0:T(1,128)} %refs_0_.1) | copy-start | bytes 196
  0.6 3.2 %copy-start.2 = (s32[1,1,16]{2,1,0:T(1,128)S(1)}, s32[1,1,16]{2,1,0:T(1,128)}, u32[]{:S(2)}) copy-start(s32[1,1,16]{2,1,0:T(1,128)} %refs_1_.1) | copy-start | bytes 196
  0.7 3.2 %copy-start.3 = (f32[128]{0:T(128)S(1)}, f32[128]{0:T(128)}, u32[]{:S(2)}) copy-start(f32[128]{0:T(128)} %param.9) | copy-start | bytes 1540
  0.7 4.6 %collective-permute-start = (f32[1,16,128]{2,1,0:T(8,128)}, f32[1,16,128]{2,1,0:T(8,128)S(1)}, u32[]{:S(2)}, u32[]{:S(2)}) collective-permute-start(f32[1,16,128]{2,1,0:T(8,128)} %bitcast.6), channel_id=1, source_target_pairs={{0,4},{4,0},{8,12},{12,8},{16,20},{20,16},{24,28},{28,24},{1,5},{5... | collective-permute-start | bytes 24584 | tf_op jit(solution)/shard_map/share_vectors/ppermute | solution.py:29
  1.2 4.5 %collective-permute-start.1 = (f32[1,16,128]{2,1,0:T(8,128)}, f32[1,16,128]{2,1,0:T(8,128)S(1)}, u32[]{:S(2)}, u32[]{:S(2)}) collective-permute-start(f32[1,16,128]{2,1,0:T(8,128)} %bitcast.7), channel_id=1, source_target_pairs={{0,1},{1,0},{2,3},{3,2},{4,5},{5,4},{6,7},{7,6},{8,9},{9,8},{10,11... | collective-permute-start | bytes 24584 | tf_op jit(solution)/shard_map/share_vectors/ppermute | solution.py:29
  3.8 1.2 %copy-start = (f32[1,1,16,128,128]{4,3,2,1,0:T(8,128)S(1)}, f32[1,1,16,128,128]{4,3,2,1,0:T(8,128)}, u32[]{:S(2)}) copy-start(f32[1,1,16,128,128]{4,3,2,1,0:T(8,128)} %tiles.1) | copy-start | bytes 3145732
  5.1 0.7 %copy-start.4 = (f32[16,128]{1,0:T(8,128)S(1)}, f32[16,128]{1,0:T(8,128)}, u32[]{:S(2)}) copy-start(f32[16,128]{1,0:T(8,128)} %x_ref.3) | copy-start | bytes 24580
  5.8 4.4 %collective-permute-start.3 = (f32[2,16,128]{2,1,0:T(8,128)S(1)}, f32[2,16,128]{2,1,0:T(8,128)S(1)}, u32[]{:S(2)}, u32[]{:S(2)}) collective-permute-start(f32[2,16,128]{2,1,0:T(8,128)S(1)} %get-tuple-element.61.refs_0_), channel_id=1, source_target_pairs={{0,8},{4,12},{8,0},{12,4},{16,24},{20,28},{24,16},{28,20},{1,9},{5... | collective-permute-start | bytes 49160 | tf_op jit(solution)/shard_map/share_vectors/ppermute | solution.py:29
  7.6 4.8 %collective-permute-start.2 = (f32[2,16,128]{2,1,0:T(8,128)S(1)}, f32[2,16,128]{2,1,0:T(8,128)S(1)}, u32[]{:S(2)}, u32[]{:S(2)}) collective-permute-start(f32[2,16,128]{2,1,0:T(8,128)S(1)} %get-tuple-element.56.near), channel_id=1, source_target_pairs={{0,2},{1,3},{2,0},{3,1},{4,6},{5,7},{6,4},{7,5},{8,10},{9,11},{10,... | collective-permute-start | bytes 49160 | tf_op jit(solution)/shard_map/share_vectors/ppermute | solution.py:29
  10.2 3.9 %collective-permute-start.4 = (f32[4,16,128]{2,1,0:T(8,128)S(1)}, f32[4,16,128]{2,1,0:T(8,128)S(1)}, u32[]{:S(2)}, u32[]{:S(2)}) collective-permute-start(f32[4,16,128]{2,1,0:T(8,128)S(1)} %join.3.near), channel_id=1, source_target_pairs={{0,16},{4,20},{8,24},{12,28},{16,0},{20,4},{24,8},{28,12},{1,17},{... | collective-permute-start | bytes 98312 | tf_op jit(solution)/shard_map/share_vectors/ppermute | solution.py:29
  14.1 3.2 %collective-permute-start.5 = (f32[4,16,128]{2,1,0:T(8,128)S(1)}, f32[4,16,128]{2,1,0:T(8,128)S(1)}, u32[]{:S(2)}, u32[]{:S(2)}) collective-permute-start(f32[4,16,128]{2,1,0:T(8,128)S(1)} %hand_on.1), channel_id=1, source_target_pairs={{0,4},{4,0},{8,12},{12,8},{16,20},{20,16},{24,28},{28,24},{1,5},{5... | collective-permute-start | bytes 98312 | tf_op jit(solution)/shard_map/return_products/ppermute | solution.py:29
  15.7 3.8 %collective-permute-start.8 = (f32[2,16,128]{2,1,0:T(8,128)S(1)}, f32[2,16,128]{2,1,0:T(8,128)S(1)}, u32[]{:S(2)}, u32[]{:S(2)}) collective-permute-start(f32[2,16,128]{2,1,0:T(8,128)S(1)} %get-tuple-element.67), channel_id=1, source_target_pairs={{0,1},{1,0},{2,3},{3,2},{4,5},{5,4},{6,7},{7,6},{8,9},{9,8},{10,11... | collective-permute-start | bytes 49160 | tf_op jit(solution)/shard_map/return_products/ppermute | solution.py:29
  17.4 4.4 %collective-permute-start.6 = (f32[2,16,128]{2,1,0:T(8,128)S(1)}, f32[2,16,128]{2,1,0:T(8,128)S(1)}, u32[]{:S(2)}, u32[]{:S(2)}) collective-permute-start(f32[2,16,128]{2,1,0:T(8,128)S(1)} %get-tuple-element.63), channel_id=1, source_target_pairs={{0,8},{4,12},{8,0},{12,4},{16,24},{20,28},{24,16},{28,20},{1,9},{5... | collective-permute-start | bytes 49160 | tf_op jit(solution)/shard_map/return_products/ppermute | solution.py:29
  19.5 4.5 %collective-permute-start.9 = (f32[1,16,128]{2,1,0:T(8,128)S(1)}, f32[1,16,128]{2,1,0:T(8,128)S(1)}, u32[]{:S(2)}, u32[]{:S(2)}) collective-permute-start(f32[1,16,128]{2,1,0:T(8,128)S(1)} %get-tuple-element.69), channel_id=1, source_target_pairs={{0,2},{1,3},{2,0},{3,1},{4,6},{5,7},{6,4},{7,5},{8,10},{9,11},{10,... | collective-permute-start | bytes 24584 | tf_op jit(solution)/shard_map/return_products/ppermute | solution.py:29
  21.8 3.7 %collective-permute-start.7 = (f32[1,16,128]{2,1,0:T(8,128)S(1)}, f32[1,16,128]{2,1,0:T(8,128)S(1)}, u32[]{:S(2)}, u32[]{:S(2)}) collective-permute-start(f32[1,16,128]{2,1,0:T(8,128)S(1)} %get-tuple-element.65), channel_id=1, source_target_pairs={{0,16},{4,20},{8,24},{12,28},{16,0},{20,4},{24,8},{28,12},{1,17},{... | collective-permute-start | bytes 24584 | tf_op jit(solution)/shard_map/return_products/ppermute | solution.py:29

commit v16 on v15

--- a/solution.py
+++ b/solution.py
@@ -73,15 +73,24 @@
     return jnp.concatenate(split(value), axis=0)
 
 
-def parts_product(stacked, parts, dims):
-    nvec = stacked.shape[0] // 3
-    total = None
-    for used, part in zip((1, 2, 3), parts[::-1]):
-        wide = lax.dot_general(stacked[: used * nvec], part, dims, preferred_element_type=jnp.float32)
-        for row in reversed(range(used)):
-            piece = wide[row * nvec : (row + 1) * nvec]
-            total = piece if total is None else total + piece
-    return total
+def pair_products(stacked, parts, transposed):
+    nvec, width = stacked[0].shape[0] // 3, stacked[0].shape[1]
+    dims = (((1,), (1 if transposed else 0,)), ((), ()))
+    axis = 0 if transposed else 1
+
+    def wide(left, pieces):
+        return lax.dot_general(left, jnp.concatenate(pieces, axis=axis), dims, preferred_element_type=jnp.float32)
+
+    last = wide(jnp.concatenate([value[:nvec] for value in stacked], axis=0), [part[2] for part in parts])
+    results = []
+    for which, (value, part) in enumerate(zip(stacked, parts)):
+        both = wide(value, part[:2])
+        first, second = both[:, :width], both[:, width:]
+        total = last[which * nvec : (which + 1) * nvec, which * width : (which + 1) * width]
+        total = (total + second[nvec : 2 * nvec]) + first[2 * nvec :]
+        total = (total + second[:nvec]) + first[nvec : 2 * nvec]
+        results.append(total + first[:nvec])
+    return results
 
 
 def join_kernel(axes, *refs):
@@ -115,10 +124,12 @@
         rows[flip] = stack_split(near[flip] if flip < half else far[flip - half])
     sums[...] = jnp.zeros_like(sums)
     sums[0] = d_ref[...] * near[0]
-    for slot in range(slots):
-        pieces = [part[slot] for part in parts]
-        block = jnp.where(slot < count[0, 0], bcol[0, 0, slot] ^ me_row, n_row)
-        sums[block] += parts_product(rows[arow[0, 0, slot] ^ me_col], pieces, (((1,), (0,)), ((), ())))
+    for pair in range(0, slots, 2):
+        pieces = [[part[slot] for part in parts] for slot in (pair, pair + 1)]
+        values = [rows[arow[0, 0, slot] ^ me_col] for slot in (pair, pair + 1)]
+        for slot, terms in zip((pair, pair + 1), pair_products(values, pieces, False)):
+            block = jnp.where(slot < count[0, 0], bcol[0, 0, slot] ^ me_row, n_row)
+            sums[block] += terms
     part_blocks(sums, n_row, send, keep)
 
 
@@ -134,10 +145,12 @@
     for flip in range(n_row):
         cols[flip] = stack_split(near[flip] if flip < half else far[flip - half])
     sums[...] = jnp.zeros_like(sums)
-    for slot in range(slots):
-        block = jnp.where(slot < count[0, 0], arow[0, 0, slot] ^ me_col, n_col)
-        pieces = [part[slot] for part in parts]
-        sums[block] += parts_product(cols[bcol[0, 0, slot] ^ me_row], pieces, (((1,), (1,)), ((), ())))
+    for pair in range(0, slots, 2):
+        pieces = [[part[slot] for part in parts] for slot in (pair, pair + 1)]
+        values = [cols[bcol[0, 0, slot] ^ me_row] for slot in (pair, pair + 1)]
+        for slot, terms in zip((pair, pair + 1), pair_products(values, pieces, True)):
+            block = jnp.where(slot < count[0, 0], arow[0, 0, slot] ^ me_col, n_col)
+            sums[block] += terms
     part_blocks(sums, n_col, send, keep)
 
 
@@ -175,8 +188,8 @@
     result = outer - (twice + twice.T) + lifted
     gram[...] = result
     diagonal = lax.broadcasted_iota(jnp.int32, (nvec, nvec), 0) == lax.broadcasted_iota(jnp.int32, (nvec, nvec), 1)
-    margin = jnp.sum(jnp.where(diagonal, 64.0 * result - (outer + lifted), 0.0))
-    sound[0, 0] = (margin >= 0.0).astype(jnp.int32)
+    margin = jnp.sum(jnp.where(diagonal, 64.0 * result - (outer + lifted), 0.0), keepdims=True)
+    sound[...] = (margin >= 0.0).astype(jnp.int32)
 
 
 def gram_parts_kernel(scale, x_ref, product, parts, out):
@@ -312,7 +325,7 @@
             functools.partial(result_kernel, scale),
             out_shape=[block, square, square, jax.ShapeDtypeStruct((1, 1), jnp.int32)],
             in_specs=[VMEM] * 3,
-            out_specs=[VMEM] * 3 + [SMEM],
+            out_specs=[VMEM] * 4,
             compiler_params=params,
             name="results",
         )(vectors, product, squares)

time: 39.8 us -> 39.5 us (level)
  Pallas kernels: 4.4 us -> 3.94 us
  transfers between devices with their start and end apart: 10 -> 10, of which waited for: 5 -> 5; matrix products, arithmetic and copies ran while one was open for 0% -> 0% of each run, Pallas kernels for 7% -> 6%
where the time goes in v16:
time: 39.5 us; the launch traced here: 39.2 us
  starting transfers between devices  15.8 us (40%)
  blocking collectives  11.8 us (30%)
  waiting for transfers between devices  4.21 us (11%)
  Pallas kernels  3.94 us (10%)
  between operations  1.36 us (3%)
  local copies, waits for them, and re-layouts  1.33 us (3%)
  loops' own time  0.69 us (2%)
    ppermute x10, starting transfers between devices, trade(): return lax.ppermute(value, axis, [(p, p ^ flip) for p in range(size)])  15.8 us
    all_to_all x1, blocking collectives, swap(): return lax.all_to_all(blocks, axis, 0, 0, tiled=True)  11.8 us
    ppermute x10, waiting for transfers between devices, trade(): return lax.ppermute(value, axis, [(p, p ^ flip) for p in range(size)])  4.21 us
    unnamed x10, local copies, waits for them, and re-layouts  1.33 us
    pallas_call x1, Pallas kernels, per_device(): pl.pallas_call(functools.partial(result_kernel, scale), out_shape=[block,...  1.24 us
    pallas_call x1, Pallas kernels, per_device(): pl.pallas_call(functools.partial(row_kernel, n_row, n_col, slots), out_sh...  1.2 us
    pallas_call x1, Pallas kernels, per_device(): pl.pallas_call(functools.partial(column_kernel, n_row, n_col, slots), out...  0.93 us
  transfers between devices with their start and end apart: 10, of which 5 were waited for; matrix products, arithmetic and copies ran while one was open for 0% of the time, Pallas kernels for 6%

profile of v16, /device:TPU:0, one launch (start us, length us, event | category | flops | bytes accessed | tf_op | source)
XLA Modules:
  0.0 39.2 jit_solution(12469192964782179237)
XLA Ops:
  0.6 0.0 copy-start.1
  0.6 0.0 copy-start.2
  0.7 0.0 copy-start.3
  0.7 0.5 %collective-permute-start = (f32[1,16,128]{2,1,0:T(8,128)}, f32[1,16,128]{2,1,0:T(8,128)S(1)}, u32[]{:S(2)}, u32[]{:S(2)}) collective-permute-start(f32[1,16,128]{2,1,0:T(8,128)} %bitcast.6), channel_id=1, source_target_pairs={{0,4},{4,0},{8,12},{12,8},{16,20},{20,16},{24,28},{28,24},{1,5},{5... | collective-permute-start | bytes 24584 | tf_op jit(solution)/shard_map/share_vectors/ppermute | solution.py:29
  1.2 2.6 %collective-permute-start.1 = (f32[1,16,128]{2,1,0:T(8,128)}, f32[1,16,128]{2,1,0:T(8,128)S(1)}, u32[]{:S(2)}, u32[]{:S(2)}) collective-permute-start(f32[1,16,128]{2,1,0:T(8,128)} %bitcast.7), channel_id=1, source_target_pairs={{0,1},{1,0},{2,3},{3,2},{4,5},{5,4},{6,7},{7,6},{8,9},{9,8},{10,11... | collective-permute-start | bytes 24584 | tf_op jit(solution)/shard_map/share_vectors/ppermute | solution.py:29
  3.8 0.0 copy-done.1
  3.8 0.0 copy-done.2
  3.8 0.0 copy-done.3
  3.8 0.0 copy-start
  3.8 1.2 %copy-done = f32[1,1,16,128,128]{4,3,2,1,0:T(8,128)S(1)} copy-done((f32[1,1,16,128,128]{4,3,2,1,0:T(8,128)S(1)}, f32[1,1,16,128,128]{4,3,2,1,0:T(8,128)}, u32[]{:S(2)}) %copy-start) | copy-done | bytes 1048600
  5.1 0.0 copy-start.4
  5.1 0.2 prepare.1
  5.3 0.0 collective-permute-done.refs_1_
  5.3 0.4 %collective-permute-done.1.refs_3_ = f32[1,16,128]{2,1,0:T(8,128)S(1)} collective-permute-done((f32[1,16,128]{2,1,0:T(8,128)}, f32[1,16,128]{2,1,0:T(8,128)S(1)}, u32[]{:S(2)}, u32[]{:S(2)}) %collective-permute-start.1) | collective-permute-done | bytes 8224 | tf_op jit(solution)/shard_map/share_vectors/ppermute | solution.py:29
  5.7 0.1 copy-done.4
  5.8 1.8 %collective-permute-start.3 = (f32[2,16,128]{2,1,0:T(8,128)S(1)}, f32[2,16,128]{2,1,0:T(8,128)S(1)}, u32[]{:S(2)}, u32[]{:S(2)}) collective-permute-start(f32[2,16,128]{2,1,0:T(8,128)S(1)} %get-tuple-element.61.refs_0_), channel_id=1, source_target_pairs={{0,8},{4,12},{8,0},{12,4},{16,24},{20,28},{24,16},{28,20},{1,9},{5... | collective-permute-start | bytes 49160 | tf_op jit(solution)/shard_map/share_vectors/ppermute | solution.py:29
  7.6 2.6 %collective-permute-start.2 = (f32[2,16,128]{2,1,0:T(8,128)S(1)}, f32[2,16,128]{2,1,0:T(8,128)S(1)}, u32[]{:S(2)}, u32[]{:S(2)}) collective-permute-start(f32[2,16,128]{2,1,0:T(8,128)S(1)} %get-tuple-element.56.near), channel_id=1, source_target_pairs={{0,2},{1,3},{2,0},{3,1},{4,6},{5,7},{6,4},{7,5},{8,10},{9,11},{10,... | collective-permute-start | bytes 49160 | tf_op jit(solution)/shard_map/share_vectors/ppermute | solution.py:29
  10.2 0.0 collective-permute-done.3.refs_1_
  10.2 1.5 %collective-permute-start.4 = (f32[4,16,128]{2,1,0:T(8,128)S(1)}, f32[4,16,128]{2,1,0:T(8,128)S(1)}, u32[]{:S(2)}, u32[]{:S(2)}) collective-permute-start(f32[4,16,128]{2,1,0:T(8,128)S(1)} %join.3.near), channel_id=1, source_target_pairs={{0,16},{4,20},{8,24},{12,28},{16,0},{20,4},{24,8},{28,12},{1,17},{... | collective-permute-start | bytes 98312 | tf_op jit(solution)/shard_map/share_vectors/ppermute | solution.py:29
  11.7 0.1 pad_add_fusion.place
  12.5 0.0 collective-permute-done.2.far
  12.5 0.9 %column_terms.1 = (f32[4,16,128]{2,1,0:T(8,128)S(1)}, f32[4,16,128]{2,1,0:T(8,128)S(1)}) custom-call(s32[2]{0:T(128)S(1)} %pad_add_fusion.place, s32[1,1,16]{2,1,0:T(1,128)S(1)} %get-tuple-element.52.arow, s32[1,1,16]{2,1,0:T(1,128)S(1)} %get-tuple-element.53.bcol, s32[1,1]{1,0:T(1,128)S(6)} %copy.16.count, f32[1,128]{1,0:T(1,128)S(1)} %get-tuple-element.54.d_ref, ...), custom_call_target="tpu_custom_call" | custom-call | flops 50331648 | bytes 1048576 | tf_op jit(solution)/shard_map/column_terms/column_terms/pallas_call | solution.py:276
  13.4 0.7 %collective-permute-done.4.after.far = f32[4,16,128]{2,1,0:T(8,128)S(1)} collective-permute-done((f32[4,16,128]{2,1,0:T(8,128)S(1)}, f32[4,16,128]{2,1,0:T(8,128)S(1)}, u32[]{:S(2)}, u32[]{:S(2)}) %collective-permute-start.4) | collective-permute-done | bytes 32800 | tf_op jit(solution)/shard_map/share_vectors/ppermute | solution.py:29
  14.1 0.0 collective-permute-start.5
  14.1 1.2 %row_terms.1 = (f32[2,16,128]{2,1,0:T(8,128)S(1)}, f32[2,16,128]{2,1,0:T(8,128)S(1)}) custom-call(s32[2]{0:T(128)S(1)} %pad_add_fusion.place, s32[1,1,16]{2,1,0:T(1,128)S(1)} %get-tuple-element.52.arow, s32[1,1,16]{2,1,0:T(1,128)S(1)} %get-tuple-element.53.bcol, s32[1,1]{1,0:T(1,128)S(6)} %copy.16.count, f32[4,16,128]{2,1,0:T(8,128)S(1)} %join.3.near, ...), custom_call_target="tpu_custom_call" | custom-call | flops 50331648 | bytes 1048576 | tf_op jit(solution)/shard_map/row_terms/row_terms/pallas_call | solution.py:298
  15.3 1.6 %collective-permute-start.8 = (f32[2,16,128]{2,1,0:T(8,128)S(1)}, f32[2,16,128]{2,1,0:T(8,128)S(1)}, u32[]{:S(2)}, u32[]{:S(2)}) collective-permute-start(f32[2,16,128]{2,1,0:T(8,128)S(1)} %get-tuple-element.67), channel_id=1, source_target_pairs={{0,1},{1,0},{2,3},{3,2},{4,5},{5,4},{6,7},{7,6},{8,9},{9,8},{10,11... | collective-permute-start | bytes 49160 | tf_op jit(solution)/shard_map/return_products/ppermute | solution.py:29
  17.0 0.0 collective-permute-done.5.other
  17.0 1.2 %collective-permute-start.6 = (f32[2,16,128]{2,1,0:T(8,128)S(1)}, f32[2,16,128]{2,1,0:T(8,128)S(1)}, u32[]{:S(2)}, u32[]{:S(2)}) collective-permute-start(f32[2,16,128]{2,1,0:T(8,128)S(1)} %get-tuple-element.63), channel_id=1, source_target_pairs={{0,8},{4,12},{8,0},{12,4},{16,24},{20,28},{24,16},{28,20},{1,9},{5... | collective-permute-start | bytes 49160 | tf_op jit(solution)/shard_map/return_products/ppermute | solution.py:29
  18.2 0.9 %collective-permute-done.8.other = f32[2,16,128]{2,1,0:T(8,128)S(1)} collective-permute-done((f32[2,16,128]{2,1,0:T(8,128)S(1)}, f32[2,16,128]{2,1,0:T(8,128)S(1)}, u32[]{:S(2)}, u32[]{:S(2)}) %collective-permute-start.8) | collective-permute-done | bytes 16416 | tf_op jit(solution)/shard_map/return_products/ppermute | solution.py:29
  19.1 2.2 %collective-permute-start.9 = (f32[1,16,128]{2,1,0:T(8,128)S(1)}, f32[1,16,128]{2,1,0:T(8,128)S(1)}, u32[]{:S(2)}, u32[]{:S(2)}) collective-permute-start(f32[1,16,128]{2,1,0:T(8,128)S(1)} %get-tuple-element.69), channel_id=1, source_target_pairs={{0,2},{1,3},{2,0},{3,1},{4,6},{5,7},{6,4},{7,5},{8,10},{9,11},{10,... | collective-permute-start | bytes 24584 | tf_op jit(solution)/shard_map/return_products/ppermute | solution.py:29
  21.4 0.0 collective-permute-done.6.other
  21.4 1.6 %collective-permute-start.7 = (f32[1,16,128]{2,1,0:T(8,128)S(1)}, f32[1,16,128]{2,1,0:T(8,128)S(1)}, u32[]{:S(2)}, u32[]{:S(2)}) collective-permute-start(f32[1,16,128]{2,1,0:T(8,128)S(1)} %get-tuple-element.65), channel_id=1, source_target_pairs={{0,16},{4,20},{8,24},{12,28},{16,0},{20,4},{24,8},{28,12},{1,17},{... | collective-permute-start | bytes 24584 | tf_op jit(solution)/shard_map/return_products/ppermute | solution.py:29
  23.0 0.7 %collective-permute-done.9.refs_3_ = f32[1,16,128]{2,1,0:T(8,128)S(1)} collective-permute-done((f32[1,16,128]{2,1,0:T(8,128)S(1)}, f32[1,16,128]{2,1,0:T(8,128)S(1)}, u32[]{:S(2)}, u32[]{:S(2)}) %collective-permute-start.9) | collective-permute-done | bytes 8224 | tf_op jit(solution)/shard_map/return_products/ppermute | solution.py:29
  23.7 1.4 %collective-permute-done.7.refs_1_ = f32[1,16,128]{2,1,0:T(8,128)S(1)} collective-permute-done((f32[1,16,128]{2,1,0:T(8,128)S(1)}, f32[1,16,128]{2,1,0:T(8,128)S(1)}, u32[]{:S(2)}, u32[]{:S(2)}) %collective-permute-start.7) | collective-permute-done | bytes 8224 | tf_op jit(solution)/shard_map/return_products/ppermute | solution.py:29
  25.1 0.3 product.1
  25.5 11.8 %all_to_all.9.parts = f32[32,3,2,128]{3,2,1,0:T(2,128)S(1)} all-to-all(f32[32,3,2,128]{3,2,1,0:T(2,128)S(1)} %get-tuple-element.71), channel_id=1, replica_groups=mesh['row'=8,'col'=4] {'row','col'}, dimensions={0} | all-to-all | bytes 196608 | tf_op jit(solution)/shard_map/product/all_to_all | solution.py:24
  37.3 1.2 %results.1 = (f32[16,128]{1,0:T(8,128)}, f32[16,16]{1,0:T(8,128)}, f32[16,16]{1,0:T(8,128)}, s32[1,1]{1,0:T(1,128)}) custom-call(f32[16,128]{1,0:T(8,128)S(1)} %copy-done.4, f32[16,128]{1,0:T(8,128)S(1)} %get-tuple-element.95.product, f32[32,3,2,128]{3,2,1,0:T(2,128)S(1)} %all_to_all.9.parts), custom_call_target="tpu_custom_call" | custom-call | tf_op jit(solution)/shard_map/results/results/pallas_call | solution.py:324
  38.6 0.7 %while.9 = (s32[]{:T(128)}, f32[16,16]{1,0:T(8,128)}, f32[16,128]{1,0:T(8,128)S(1)}, f32[16,128]{1,0:T(8,128)S(1)}, f32[32,3,2,128]{3,2,1,0:T(2,128)S(1)}) while((s32[]{:T(128)}, f32[16,16]{1,0:T(8,128)}, f32[16,128]{1,0:T(8,128)S(1)}, f32[16,128]{1,0:T(8,128)S(1)}, f32[32,3,2,128]{3,2,1,0:T(2,128)S(1)}) %tuple.20), condition=%region_1.0_spmd, body=%region_0.0_spmd | while | flops 1 | bytes 98393 | solution.py:353
  (6 shorter events, 0.0 us)
Async XLA Ops:
  0.6 3.2 %copy-start.1 = (s32[1,1,16]{2,1,0:T(1,128)S(1)}, s32[1,1,16]{2,1,0:T(1,128)}, u32[]{:S(2)}) copy-start(s32[1,1,16]{2,1,0:T(1,128)} %refs_0_.1) | copy-start | bytes 196
  0.6 3.2 %copy-start.2 = (s32[1,1,16]{2,1,0:T(1,128)S(1)}, s32[1,1,16]{2,1,0:T(1,128)}, u32[]{:S(2)}) copy-start(s32[1,1,16]{2,1,0:T(1,128)} %refs_1_.1) | copy-start | bytes 196
  0.7 3.2 %copy-start.3 = (f32[128]{0:T(128)S(1)}, f32[128]{0:T(128)}, u32[]{:S(2)}) copy-start(f32[128]{0:T(128)} %param.9) | copy-start | bytes 1540
  0.7 4.6 %collective-permute-start = (f32[1,16,128]{2,1,0:T(8,128)}, f32[1,16,128]{2,1,0:T(8,128)S(1)}, u32[]{:S(2)}, u32[]{:S(2)}) collective-permute-start(f32[1,16,128]{2,1,0:T(8,128)} %bitcast.6), channel_id=1, source_target_pairs={{0,4},{4,0},{8,12},{12,8},{16,20},{20,16},{24,28},{28,24},{1,5},{5... | collective-permute-start | bytes 24584 | tf_op jit(solution)/shard_map/share_vectors/ppermute | solution.py:29
  1.2 4.5 %collective-permute-start.1 = (f32[1,16,128]{2,1,0:T(8,128)}, f32[1,16,128]{2,1,0:T(8,128)S(1)}, u32[]{:S(2)}, u32[]{:S(2)}) collective-permute-start(f32[1,16,128]{2,1,0:T(8,128)} %bitcast.7), channel_id=1, source_target_pairs={{0,1},{1,0},{2,3},{3,2},{4,5},{5,4},{6,7},{7,6},{8,9},{9,8},{10,11... | collective-permute-start | bytes 24584 | tf_op jit(solution)/shard_map/share_vectors/ppermute | solution.py:29
  3.8 1.2 %copy-start = (f32[1,1,16,128,128]{4,3,2,1,0:T(8,128)S(1)}, f32[1,1,16,128,128]{4,3,2,1,0:T(8,128)}, u32[]{:S(2)}) copy-start(f32[1,1,16,128,128]{4,3,2,1,0:T(8,128)} %tiles.1) | copy-start | bytes 3145732
  5.1 0.7 %copy-start.4 = (f32[16,128]{1,0:T(8,128)S(1)}, f32[16,128]{1,0:T(8,128)}, u32[]{:S(2)}) copy-start(f32[16,128]{1,0:T(8,128)} %x_ref.3) | copy-start | bytes 24580
  5.8 4.4 %collective-permute-start.3 = (f32[2,16,128]{2,1,0:T(8,128)S(1)}, f32[2,16,128]{2,1,0:T(8,128)S(1)}, u32[]{:S(2)}, u32[]{:S(2)}) collective-permute-start(f32[2,16,128]{2,1,0:T(8,128)S(1)} %get-tuple-element.61.refs_0_), channel_id=1, source_target_pairs={{0,8},{4,12},{8,0},{12,4},{16,24},{20,28},{24,16},{28,20},{1,9},{5... | collective-permute-start | bytes 49160 | tf_op jit(solution)/shard_map/share_vectors/ppermute | solution.py:29
  7.6 4.8 %collective-permute-start.2 = (f32[2,16,128]{2,1,0:T(8,128)S(1)}, f32[2,16,128]{2,1,0:T(8,128)S(1)}, u32[]{:S(2)}, u32[]{:S(2)}) collective-permute-start(f32[2,16,128]{2,1,0:T(8,128)S(1)} %get-tuple-element.56.near), channel_id=1, source_target_pairs={{0,2},{1,3},{2,0},{3,1},{4,6},{5,7},{6,4},{7,5},{8,10},{9,11},{10,... | collective-permute-start | bytes 49160 | tf_op jit(solution)/shard_map/share_vectors/ppermute | solution.py:29
  10.2 3.9 %collective-permute-start.4 = (f32[4,16,128]{2,1,0:T(8,128)S(1)}, f32[4,16,128]{2,1,0:T(8,128)S(1)}, u32[]{:S(2)}, u32[]{:S(2)}) collective-permute-start(f32[4,16,128]{2,1,0:T(8,128)S(1)} %join.3.near), channel_id=1, source_target_pairs={{0,16},{4,20},{8,24},{12,28},{16,0},{20,4},{24,8},{28,12},{1,17},{... | collective-permute-start | bytes 98312 | tf_op jit(solution)/shard_map/share_vectors/ppermute | solution.py:29
  14.1 2.9 %collective-permute-start.5 = (f32[4,16,128]{2,1,0:T(8,128)S(1)}, f32[4,16,128]{2,1,0:T(8,128)S(1)}, u32[]{:S(2)}, u32[]{:S(2)}) collective-permute-start(f32[4,16,128]{2,1,0:T(8,128)S(1)} %hand_on.1), channel_id=1, source_target_pairs={{0,4},{4,0},{8,12},{12,8},{16,20},{20,16},{24,28},{28,24},{1,5},{5... | collective-permute-start | bytes 98312 | tf_op jit(solution)/shard_map/return_products/ppermute | solution.py:29
  15.3 3.8 %collective-permute-start.8 = (f32[2,16,128]{2,1,0:T(8,128)S(1)}, f32[2,16,128]{2,1,0:T(8,128)S(1)}, u32[]{:S(2)}, u32[]{:S(2)}) collective-permute-start(f32[2,16,128]{2,1,0:T(8,128)S(1)} %get-tuple-element.67), channel_id=1, source_target_pairs={{0,1},{1,0},{2,3},{3,2},{4,5},{5,4},{6,7},{7,6},{8,9},{9,8},{10,11... | collective-permute-start | bytes 49160 | tf_op jit(solution)/shard_map/return_products/ppermute | solution.py:29
  17.0 4.4 %collective-permute-start.6 = (f32[2,16,128]{2,1,0:T(8,128)S(1)}, f32[2,16,128]{2,1,0:T(8,128)S(1)}, u32[]{:S(2)}, u32[]{:S(2)}) collective-permute-start(f32[2,16,128]{2,1,0:T(8,128)S(1)} %get-tuple-element.63), channel_id=1, source_target_pairs={{0,8},{4,12},{8,0},{12,4},{16,24},{20,28},{24,16},{28,20},{1,9},{5... | collective-permute-start | bytes 49160 | tf_op jit(solution)/shard_map/return_products/ppermute | solution.py:29
  19.1 4.5 %collective-permute-start.9 = (f32[1,16,128]{2,1,0:T(8,128)S(1)}, f32[1,16,128]{2,1,0:T(8,128)S(1)}, u32[]{:S(2)}, u32[]{:S(2)}) collective-permute-start(f32[1,16,128]{2,1,0:T(8,128)S(1)} %get-tuple-element.69), channel_id=1, source_target_pairs={{0,2},{1,3},{2,0},{3,1},{4,6},{5,7},{6,4},{7,5},{8,10},{9,11},{10,... | collective-permute-start | bytes 24584 | tf_op jit(solution)/shard_map/return_products/ppermute | solution.py:29
  21.4 3.7 %collective-permute-start.7 = (f32[1,16,128]{2,1,0:T(8,128)S(1)}, f32[1,16,128]{2,1,0:T(8,128)S(1)}, u32[]{:S(2)}, u32[]{:S(2)}) collective-permute-start(f32[1,16,128]{2,1,0:T(8,128)S(1)} %get-tuple-element.65), channel_id=1, source_target_pairs={{0,16},{4,20},{8,24},{12,28},{16,0},{20,4},{24,8},{28,12},{1,17},{... | collective-permute-start | bytes 24584 | tf_op jit(solution)/shard_map/return_products/ppermute | solution.py:29

commit v17 on v16

--- a/solution.py
+++ b/solution.py
@@ -93,12 +93,10 @@
     return results
 
 
-def join_kernel(axes, *refs):
-    for which, out in enumerate(refs[-axes:]):
-        mine, other = refs[2 * which : 2 * which + 2]
-        half = mine.shape[0]
-        out[:half] = mine[...]
-        out[half:] = other[...]
+def pair_kernel(mine, other, after, out):
+    del after
+    out[0] = mine[...]
+    out[1] = other[...]
 
 
 def prepare_kernel(slots, tiles, *refs):
@@ -116,14 +114,13 @@
         send[block] = sums[2 * block + 1]
 
 
-def column_kernel(n_row, n_col, slots, place, arow, bcol, count, d_ref, near, far, *refs):
-    *parts, send, keep, rows, sums = refs
+def column_kernel(n_row, n_col, slots, place, arow, bcol, count, d_ref, *refs):
+    x_col, (*parts, send, keep, rows, sums) = refs[:n_col], refs[n_col:]
     me_row, me_col = place[0], place[1]
-    half = n_col // 2
     for flip in range(n_col):
-        rows[flip] = stack_split(near[flip] if flip < half else far[flip - half])
+        rows[flip] = stack_split(x_col[flip][...])
     sums[...] = jnp.zeros_like(sums)
-    sums[0] = d_ref[...] * near[0]
+    sums[0] = d_ref[...] * x_col[0][...]
     for pair in range(0, slots, 2):
         pieces = [[part[slot] for part in parts] for slot in (pair, pair + 1)]
         values = [rows[arow[0, 0, slot] ^ me_col] for slot in (pair, pair + 1)]
@@ -133,17 +130,16 @@
     part_blocks(sums, n_row, send, keep)
 
 
-def hand_on_kernel(early, after, late):
-    del after
+def hand_on_kernel(early, *refs):
+    late = refs[-1]
     late[...] = early[...]
 
 
-def row_kernel(n_row, n_col, slots, place, arow, bcol, count, near, far, *refs):
-    *parts, send, keep, cols, sums = refs
+def row_kernel(n_row, n_col, slots, place, arow, bcol, count, *refs):
+    x_pairs, (*parts, send, keep, cols, sums) = refs[: n_row // 2], refs[n_row // 2 :]
     me_row, me_col = place[0], place[1]
-    half = n_row // 2
     for flip in range(n_row):
-        cols[flip] = stack_split(near[flip] if flip < half else far[flip - half])
+        cols[flip] = stack_split(x_pairs[flip // 2][flip % 2])
     sums[...] = jnp.zeros_like(sums)
     for pair in range(0, slots, 2):
         pieces = [[part[slot] for part in parts] for slot in (pair, pair + 1)]
@@ -224,25 +220,8 @@
     def blocks(total):
         return jax.ShapeDtypeStruct((total, nvec, width), jnp.float32)
 
-    def gather(axes, after):
-        near = [vectors[None]] * len(axes)
-        far = [trade(vectors[None], axis, 1) for axis in axes]
-        reach = 2
-        while any(reach < lax.axis_size(axis) for axis in axes):
-            going = [which for which, axis in enumerate(axes) if reach < lax.axis_size(axis)]
-            joined = pl.pallas_call(
-                functools.partial(join_kernel, len(going)),
-                out_shape=[blocks(reach)] * len(going),
-                in_specs=[VMEM] * (2 * len(going)) + [pl.BlockSpec(memory_space=pl.ANY)] * len(after),
-                out_specs=[VMEM] * len(going),
-                compiler_params=params,
-                name="join",
-            )(*[half for which in going for half in (near[which], far[which])], *after)
-            for which, half in zip(going, joined):
-                near[which], far[which] = half, trade(half, axes[which], reach)
-            reach *= 2
-            after = ()
-        return list(zip(near, far))
+    def trades(value, axis, flips):
+        return [trade(value, axis, flip) for flip in reversed(flips)][::-1]
 
     def halve(send, keep, axis):
         flip = 1
@@ -271,12 +250,22 @@
             name="prepare",
         )(tiles, *small)
     with jax.named_scope("share_vectors"):
-        x_row, x_col = gather(("row", "col"), parts[:1])
+        other = trade(vectors, "row", 1)
+        x_col = [vectors] + trades(vectors, "col", range(1, n_col))
+        pair = pl.pallas_call(
+            pair_kernel,
+            out_shape=blocks(2),
+            in_specs=[VMEM] * 2 + [pl.BlockSpec(memory_space=pl.ANY)],
+            out_specs=VMEM,
+            compiler_params=params,
+            name="pair",
+        )(vectors, other, parts[0])
+        x_pairs = [pair] + trades(pair, "row", range(2, n_row, 2))
     with jax.named_scope("column_terms"):
         col_send, col_keep = pl.pallas_call(
             functools.partial(column_kernel, n_row, n_col, slots),
             out_shape=[blocks(n_row // 2)] * 2,
-            in_specs=[SMEM] * 4 + [VMEM] * 6,
+            in_specs=[SMEM] * 4 + [VMEM] * (n_col + 4),
             out_specs=[VMEM] * 2,
             scratch_shapes=[
                 pltpu.VMEM((n_col, 3 * nvec, width), jnp.bfloat16),
@@ -289,16 +278,16 @@
         col_send = pl.pallas_call(
             hand_on_kernel,
             out_shape=blocks(n_row // 2),
-            in_specs=[VMEM, pl.BlockSpec(memory_space=pl.ANY)],
+            in_specs=[VMEM] + [pl.BlockSpec(memory_space=pl.ANY)] * (n_row // 2 - 1),
             out_specs=VMEM,
             compiler_params=params,
             name="hand_on",
-        )(col_send, x_row[1])
+        )(col_send, *x_pairs[1:])
     with jax.named_scope("row_terms"):
         row_send, row_keep = pl.pallas_call(
             functools.partial(row_kernel, n_row, n_col, slots),
             out_shape=[blocks(n_col // 2)] * 2,
-            in_specs=[SMEM] * 4 + [VMEM] * 5,
+            in_specs=[SMEM] * 4 + [VMEM] * (n_row // 2 + 3),
             out_specs=[VMEM] * 2,
             scratch_shapes=[
                 pltpu.VMEM((n_row, 3 * nvec, width), jnp.bfloat16),
@@ -307,7 +296,7 @@
             compiler_params=params,
             cost_estimate=cost,
             name="row_terms",
-        )(place, arow, bcol, tile_count, *x_row, *parts)
+        )(place, arow, bcol, tile_count, *x_pairs, *parts)
     with jax.named_scope("return_products"):
         sums = halve(col_send, col_keep, "row") + halve(row_send, row_keep, "col")
     with jax.named_scope("product"):

time: 39.5 us -> 40.6 us (1.028)
  waiting for transfers between devices: 4.21 us -> 8.29 us
  starting transfers between devices: 15.8 us -> 13.3 us
  blocking collectives: 11.8 us -> 10.4 us
  local copies, waits for them, and re-layouts: 1.33 us -> 2.4 us
    ppermute x10 -> x12, waiting for transfers between devices: 4.21 us -> 8.29 us  [trade(): return lax.ppermute(value, axis, [(p, p ^ flip) for p in range(size)])]
    ppermute x10 -> x12, starting transfers between devices: 15.8 us -> 13.3 us  [trade(): return lax.ppermute(value, axis, [(p, p ^ flip) for p in range(size)])]
    all_to_all x1, blocking collectives: 11.8 us -> 10.4 us  [swap(): return lax.all_to_all(blocks, axis, 0, 0, tiled=True)]
    unnamed x10, local copies, waits for them, and re-layouts: 1.33 us -> 2.4 us
  transfers between devices with their start and end apart: 10 -> 12, of which waited for: 5 -> 5; matrix products, arithmetic and copies ran while one was open for 0% -> 0% of each run, Pallas kernels for 6% -> 6%
where the time goes in v17:
time: 40.6 us; the launch traced here: 40.4 us
  starting transfers between devices  13.3 us (33%)
  blocking collectives  10.4 us (26%)
  waiting for transfers between devices  8.29 us (20%)
  Pallas kernels  3.9 us (10%)
  local copies, waits for them, and re-layouts  2.4 us (6%)
  between operations  1.36 us (3%)
  loops' own time  0.64 us (2%)
    ppermute x12, starting transfers between devices, trade(): return lax.ppermute(value, axis, [(p, p ^ flip) for p in range(size)])  13.3 us
    all_to_all x1, blocking collectives, swap(): return lax.all_to_all(blocks, axis, 0, 0, tiled=True)  10.4 us
    ppermute x12, waiting for transfers between devices, trade(): return lax.ppermute(value, axis, [(p, p ^ flip) for p in range(size)])  8.29 us
    unnamed x10, local copies, waits for them, and re-layouts  2.4 us
    pallas_call x1, Pallas kernels, per_device(): pl.pallas_call(functools.partial(row_kernel, n_row, n_col, slots), out_sh...  1.22 us
    pallas_call x1, Pallas kernels, per_device(): pl.pallas_call(functools.partial(result_kernel, scale), out_shape=[block,...  1.18 us
    pallas_call x1, Pallas kernels, per_device(): pl.pallas_call(functools.partial(column_kernel, n_row, n_col, slots), out...  0.95 us
  transfers between devices with their start and end apart: 12, of which 5 were waited for; matrix products, arithmetic and copies ran while one was open for 0% of the time, Pallas kernels for 6%

profile of v17, /device:TPU:0, one launch (start us, length us, event | category | flops | bytes accessed | tf_op | source)
XLA Modules:
  0.0 40.4 jit_solution(11359033179029533672)
XLA Ops:
  0.6 0.5 %collective-permute-start.3 = (f32[16,128]{1,0:T(8,128)}, f32[16,128]{1,0:T(8,128)S(1)}, u32[]{:S(2)}, u32[]{:S(2)}) collective-permute-start(f32[16,128]{1,0:T(8,128)} %x_ref.3), channel_id=1, source_target_pairs={{0,4},{4,0},{8,12},{12,8},{16,20},{20,16},{24,28},{28,24},{1,5},{5... | collective-permute-start | bytes 24584 | tf_op jit(solution)/shard_map/share_vectors/ppermute | solution.py:29
  1.1 2.6 %collective-permute-start = (f32[16,128]{1,0:T(8,128)}, f32[16,128]{1,0:T(8,128)S(1)}, u32[]{:S(2)}, u32[]{:S(2)}) collective-permute-start(f32[16,128]{1,0:T(8,128)} %x_ref.3), channel_id=1, source_target_pairs={{0,1},{1,0},{2,3},{3,2},{4,5},{5,4},{6,7},{7,6},{8,9},{9,8},{10,11... | collective-permute-start | bytes 24584 | tf_op jit(solution)/shard_map/share_vectors/ppermute | solution.py:29
  3.8 2.6 %collective-permute-start.1 = (f32[16,128]{1,0:T(8,128)}, f32[16,128]{1,0:T(8,128)S(1)}, u32[]{:S(2)}, u32[]{:S(2)}) collective-permute-start(f32[16,128]{1,0:T(8,128)} %x_ref.3), channel_id=1, source_target_pairs={{0,2},{1,3},{2,0},{3,1},{4,6},{5,7},{6,4},{7,5},{8,10},{9,11},{10,... | collective-permute-start | bytes 24584 | tf_op jit(solution)/shard_map/share_vectors/ppermute | solution.py:29
  6.4 0.0 collective-permute-start.2
  6.4 0.0 copy-start.1
  6.4 0.0 copy-start.2
  6.4 0.0 copy-start.3
  6.4 0.6 %copy-done.1 = s32[1,1,16]{2,1,0:T(1,128)S(1)} copy-done((s32[1,1,16]{2,1,0:T(1,128)S(1)}, s32[1,1,16]{2,1,0:T(1,128)}, u32[]{:S(2)}) %copy-start.1) | copy-done | bytes 88
  7.0 0.0 copy-done.2
  7.1 0.0 copy-done.3
  7.1 0.0 copy-start
  7.1 1.2 %copy-done = f32[1,1,16,128,128]{4,3,2,1,0:T(8,128)S(1)} copy-done((f32[1,1,16,128,128]{4,3,2,1,0:T(8,128)S(1)}, f32[1,1,16,128,128]{4,3,2,1,0:T(8,128)}, u32[]{:S(2)}) %copy-start) | copy-done | bytes 1048600
  8.3 0.0 copy-start.4
  8.3 0.2 prepare.1
  8.5 0.0 collective-permute-done.3.other
  8.5 0.5 %copy-done.4 = f32[16,128]{1,0:T(8,128)S(1)} copy-done((f32[16,128]{1,0:T(8,128)S(1)}, f32[16,128]{1,0:T(8,128)}, u32[]{:S(2)}) %copy-start.4) | copy-done | bytes 8216
  9.0 1.7 %collective-permute-start.4 = (f32[2,16,128]{2,1,0:T(8,128)S(1)}, f32[2,16,128]{2,1,0:T(8,128)S(1)}, u32[]{:S(2)}, u32[]{:S(2)}) collective-permute-start(f32[2,16,128]{2,1,0:T(8,128)S(1)} %pair.1.refs_0_), channel_id=1, source_target_pairs={{0,8},{4,12},{8,0},{12,4},{16,24},{20,28},{24,16},{28,20},{1,9},{5... | collective-permute-start | bytes 49160 | tf_op jit(solution)/shard_map/share_vectors/ppermute | solution.py:29
  10.7 1.5 %collective-permute-start.5 = (f32[2,16,128]{2,1,0:T(8,128)S(1)}, f32[2,16,128]{2,1,0:T(8,128)S(1)}, u32[]{:S(2)}, u32[]{:S(2)}) collective-permute-start(f32[2,16,128]{2,1,0:T(8,128)S(1)} %pair.1.refs_0_), channel_id=1, source_target_pairs={{0,16},{4,20},{8,24},{12,28},{16,0},{20,4},{24,8},{28,12},{1,17},{... | collective-permute-start | bytes 49160 | tf_op jit(solution)/shard_map/share_vectors/ppermute | solution.py:29
  12.2 0.0 collective-permute-done.refs_1_
  12.2 0.3 collective-permute-start.6
  12.5 0.1 pad_add_fusion.place
  13.2 0.0 collective-permute-done.1.refs_2_
  13.2 0.0 collective-permute-done.2.refs_3_
  13.2 0.9 %column_terms.1 = (f32[4,16,128]{2,1,0:T(8,128)S(1)}, f32[4,16,128]{2,1,0:T(8,128)S(1)}) custom-call(s32[2]{0:T(128)S(1)} %pad_add_fusion.place, s32[1,1,16]{2,1,0:T(1,128)S(1)} %get-tuple-element.50.arow, s32[1,1,16]{2,1,0:T(1,128)S(1)} %get-tuple-element.51.bcol, s32[1,1]{1,0:T(1,128)S(6)} %copy.16.count, f32[1,128]{1,0:T(1,128)S(1)} %get-tuple-element.52.d_ref, ...), custom_call_target="tpu_custom_call" | custom-call | flops 50331648 | bytes 1048576 | tf_op jit(solution)/shard_map/column_terms/column_terms/pallas_call | solution.py:265
  14.2 0.0 collective-permute-done.4.refs_0_.refs_1_
  14.2 0.2 collective-permute-done.5.refs_1_.refs_2_
  14.5 2.4 %collective-permute-done.6.refs_2_.refs_3_ = f32[2,16,128]{2,1,0:T(8,128)S(1)} collective-permute-done((f32[2,16,128]{2,1,0:T(8,128)S(1)}, f32[2,16,128]{2,1,0:T(8,128)S(1)}, u32[]{:S(2)}, u32[]{:S(2)}) %collective-permute-start.6) | collective-permute-done | bytes 16416 | tf_op jit(solution)/shard_map/share_vectors/ppermute | solution.py:29
  16.9 0.0 collective-permute-start.7
  16.9 1.2 %row_terms.1 = (f32[2,16,128]{2,1,0:T(8,128)S(1)}, f32[2,16,128]{2,1,0:T(8,128)S(1)}) custom-call(s32[2]{0:T(128)S(1)} %pad_add_fusion.place, s32[1,1,16]{2,1,0:T(1,128)S(1)} %get-tuple-element.50.arow, s32[1,1,16]{2,1,0:T(1,128)S(1)} %get-tuple-element.51.bcol, s32[1,1]{1,0:T(1,128)S(6)} %copy.16.count, f32[2,16,128]{2,1,0:T(8,128)S(1)} %pair.1.refs_0_, ...), custom_call_target="tpu_custom_call" | custom-call | flops 50331648 | bytes 1048576 | tf_op jit(solution)/shard_map/row_terms/row_terms/pallas_call | solution.py:287
  18.1 0.7 %collective-permute-start.10 = (f32[2,16,128]{2,1,0:T(8,128)S(1)}, f32[2,16,128]{2,1,0:T(8,128)S(1)}, u32[]{:S(2)}, u32[]{:S(2)}) collective-permute-start(f32[2,16,128]{2,1,0:T(8,128)S(1)} %get-tuple-element.63), channel_id=1, source_target_pairs={{0,1},{1,0},{2,3},{3,2},{4,5},{5,4},{6,7},{7,6},{8,9},{9,8},{10,11... | collective-permute-start | bytes 49160 | tf_op jit(solution)/shard_map/return_products/ppermute | solution.py:29
  18.8 0.0 collective-permute-done.7.other
  18.9 0.6 %collective-permute-start.8 = (f32[2,16,128]{2,1,0:T(8,128)S(1)}, f32[2,16,128]{2,1,0:T(8,128)S(1)}, u32[]{:S(2)}, u32[]{:S(2)}) collective-permute-start(f32[2,16,128]{2,1,0:T(8,128)S(1)} %get-tuple-element.59), channel_id=1, source_target_pairs={{0,8},{4,12},{8,0},{12,4},{16,24},{20,28},{24,16},{28,20},{1,9},{5... | collective-permute-start | bytes 49160 | tf_op jit(solution)/shard_map/return_products/ppermute | solution.py:29
  19.5 2.5 %collective-permute-done.10.other = f32[2,16,128]{2,1,0:T(8,128)S(1)} collective-permute-done((f32[2,16,128]{2,1,0:T(8,128)S(1)}, f32[2,16,128]{2,1,0:T(8,128)S(1)}, u32[]{:S(2)}, u32[]{:S(2)}) %collective-permute-start.10) | collective-permute-done | bytes 16416 | tf_op jit(solution)/shard_map/return_products/ppermute | solution.py:29
  21.9 2.1 %collective-permute-start.11 = (f32[1,16,128]{2,1,0:T(8,128)S(1)}, f32[1,16,128]{2,1,0:T(8,128)S(1)}, u32[]{:S(2)}, u32[]{:S(2)}) collective-permute-start(f32[1,16,128]{2,1,0:T(8,128)S(1)} %get-tuple-element.65), channel_id=1, source_target_pairs={{0,2},{1,3},{2,0},{3,1},{4,6},{5,7},{6,4},{7,5},{8,10},{9,11},{10,... | collective-permute-start | bytes 24584 | tf_op jit(solution)/shard_map/return_products/ppermute | solution.py:29
  24.1 0.0 collective-permute-done.8.other
  24.1 0.6 %collective-permute-start.9 = (f32[1,16,128]{2,1,0:T(8,128)S(1)}, f32[1,16,128]{2,1,0:T(8,128)S(1)}, u32[]{:S(2)}, u32[]{:S(2)}) collective-permute-start(f32[1,16,128]{2,1,0:T(8,128)S(1)} %get-tuple-element.61), channel_id=1, source_target_pairs={{0,16},{4,20},{8,24},{12,28},{16,0},{20,4},{24,8},{28,12},{1,17},{... | collective-permute-start | bytes 24584 | tf_op jit(solution)/shard_map/return_products/ppermute | solution.py:29
  24.6 1.8 %collective-permute-done.11.refs_3_ = f32[1,16,128]{2,1,0:T(8,128)S(1)} collective-permute-done((f32[1,16,128]{2,1,0:T(8,128)S(1)}, f32[1,16,128]{2,1,0:T(8,128)S(1)}, u32[]{:S(2)}, u32[]{:S(2)}) %collective-permute-start.11) | collective-permute-done | bytes 8224 | tf_op jit(solution)/shard_map/return_products/ppermute | solution.py:29
  26.5 1.3 %collective-permute-done.9.refs_1_ = f32[1,16,128]{2,1,0:T(8,128)S(1)} collective-permute-done((f32[1,16,128]{2,1,0:T(8,128)S(1)}, f32[1,16,128]{2,1,0:T(8,128)S(1)}, u32[]{:S(2)}, u32[]{:S(2)}) %collective-permute-start.9) | collective-permute-done | bytes 8224 | tf_op jit(solution)/shard_map/return_products/ppermute | solution.py:29
  27.8 0.3 product.1
  28.1 10.4 %all_to_all.9.parts = f32[32,3,2,128]{3,2,1,0:T(2,128)S(1)} all-to-all(f32[32,3,2,128]{3,2,1,0:T(2,128)S(1)} %get-tuple-element.67), channel_id=1, replica_groups=mesh['row'=8,'col'=4] {'row','col'}, dimensions={0} | all-to-all | bytes 196608 | tf_op jit(solution)/shard_map/product/all_to_all | solution.py:24
  38.5 1.2 %results.1 = (f32[16,128]{1,0:T(8,128)}, f32[16,16]{1,0:T(8,128)}, f32[16,16]{1,0:T(8,128)}, s32[1,1]{1,0:T(1,128)}) custom-call(f32[16,128]{1,0:T(8,128)S(1)} %copy-done.4, f32[16,128]{1,0:T(8,128)S(1)} %get-tuple-element.91.product, f32[32,3,2,128]{3,2,1,0:T(2,128)S(1)} %all_to_all.9.parts), custom_call_target="tpu_custom_call" | custom-call | tf_op jit(solution)/shard_map/results/results/pallas_call | solution.py:313
  39.7 0.6 %while.9 = (s32[]{:T(128)}, f32[16,16]{1,0:T(8,128)}, f32[16,128]{1,0:T(8,128)S(1)}, f32[16,128]{1,0:T(8,128)S(1)}, f32[32,3,2,128]{3,2,1,0:T(2,128)S(1)}) while((s32[]{:T(128)}, f32[16,16]{1,0:T(8,128)}, f32[16,128]{1,0:T(8,128)S(1)}, f32[16,128]{1,0:T(8,128)S(1)}, f32[32,3,2,128]{3,2,1,0:T(2,128)S(1)}) %tuple.20), condition=%region_1.0_spmd, body=%region_0.0_spmd | while | flops 1 | bytes 98393 | solution.py:342
  (5 shorter events, 0.0 us)
Async XLA Ops:
  0.6 7.9 %collective-permute-start.3 = (f32[16,128]{1,0:T(8,128)}, f32[16,128]{1,0:T(8,128)S(1)}, u32[]{:S(2)}, u32[]{:S(2)}) collective-permute-start(f32[16,128]{1,0:T(8,128)} %x_ref.3), channel_id=1, source_target_pairs={{0,4},{4,0},{8,12},{12,8},{16,20},{20,16},{24,28},{28,24},{1,5},{5... | collective-permute-start | bytes 24584 | tf_op jit(solution)/shard_map/share_vectors/ppermute | solution.py:29
  1.1 11.1 %collective-permute-start = (f32[16,128]{1,0:T(8,128)}, f32[16,128]{1,0:T(8,128)S(1)}, u32[]{:S(2)}, u32[]{:S(2)}) collective-permute-start(f32[16,128]{1,0:T(8,128)} %x_ref.3), channel_id=1, source_target_pairs={{0,1},{1,0},{2,3},{3,2},{4,5},{5,4},{6,7},{7,6},{8,9},{9,8},{10,11... | collective-permute-start | bytes 24584 | tf_op jit(solution)/shard_map/share_vectors/ppermute | solution.py:29
  3.8 9.4 %collective-permute-start.1 = (f32[16,128]{1,0:T(8,128)}, f32[16,128]{1,0:T(8,128)S(1)}, u32[]{:S(2)}, u32[]{:S(2)}) collective-permute-start(f32[16,128]{1,0:T(8,128)} %x_ref.3), channel_id=1, source_target_pairs={{0,2},{1,3},{2,0},{3,1},{4,6},{5,7},{6,4},{7,5},{8,10},{9,11},{10,... | collective-permute-start | bytes 24584 | tf_op jit(solution)/shard_map/share_vectors/ppermute | solution.py:29
  6.4 6.8 %collective-permute-start.2 = (f32[16,128]{1,0:T(8,128)}, f32[16,128]{1,0:T(8,128)S(1)}, u32[]{:S(2)}, u32[]{:S(2)}) collective-permute-start(f32[16,128]{1,0:T(8,128)} %x_ref.3), channel_id=1, source_target_pairs={{0,3},{1,2},{2,1},{3,0},{4,7},{5,6},{6,5},{7,4},{8,11},{9,10},{10,... | collective-permute-start | bytes 24584 | tf_op jit(solution)/shard_map/share_vectors/ppermute | solution.py:29
  6.4 0.7 %copy-start.1 = (s32[1,1,16]{2,1,0:T(1,128)S(1)}, s32[1,1,16]{2,1,0:T(1,128)}, u32[]{:S(2)}) copy-start(s32[1,1,16]{2,1,0:T(1,128)} %refs_0_.2) | copy-start | bytes 196
  6.4 0.7 %copy-start.2 = (s32[1,1,16]{2,1,0:T(1,128)S(1)}, s32[1,1,16]{2,1,0:T(1,128)}, u32[]{:S(2)}) copy-start(s32[1,1,16]{2,1,0:T(1,128)} %refs_1_.1) | copy-start | bytes 196
  6.4 0.7 %copy-start.3 = (f32[128]{0:T(128)S(1)}, f32[128]{0:T(128)}, u32[]{:S(2)}) copy-start(f32[128]{0:T(128)} %param.9) | copy-start | bytes 1540
  7.1 1.2 %copy-start = (f32[1,1,16,128,128]{4,3,2,1,0:T(8,128)S(1)}, f32[1,1,16,128,128]{4,3,2,1,0:T(8,128)}, u32[]{:S(2)}) copy-start(f32[1,1,16,128,128]{4,3,2,1,0:T(8,128)} %tiles.1) | copy-start | bytes 3145732
  8.3 0.7 %copy-start.4 = (f32[16,128]{1,0:T(8,128)S(1)}, f32[16,128]{1,0:T(8,128)}, u32[]{:S(2)}) copy-start(f32[16,128]{1,0:T(8,128)} %x_ref.3) | copy-start | bytes 24580
  9.0 5.2 %collective-permute-start.4 = (f32[2,16,128]{2,1,0:T(8,128)S(1)}, f32[2,16,128]{2,1,0:T(8,128)S(1)}, u32[]{:S(2)}, u32[]{:S(2)}) collective-permute-start(f32[2,16,128]{2,1,0:T(8,128)S(1)} %pair.1.refs_0_), channel_id=1, source_target_pairs={{0,8},{4,12},{8,0},{12,4},{16,24},{20,28},{24,16},{28,20},{1,9},{5... | collective-permute-start | bytes 49160 | tf_op jit(solution)/shard_map/share_vectors/ppermute | solution.py:29
  10.7 3.7 %collective-permute-start.5 = (f32[2,16,128]{2,1,0:T(8,128)S(1)}, f32[2,16,128]{2,1,0:T(8,128)S(1)}, u32[]{:S(2)}, u32[]{:S(2)}) collective-permute-start(f32[2,16,128]{2,1,0:T(8,128)S(1)} %pair.1.refs_0_), channel_id=1, source_target_pairs={{0,16},{4,20},{8,24},{12,28},{16,0},{20,4},{24,8},{28,12},{1,17},{... | collective-permute-start | bytes 49160 | tf_op jit(solution)/shard_map/share_vectors/ppermute | solution.py:29
  12.2 4.6 %collective-permute-start.6 = (f32[2,16,128]{2,1,0:T(8,128)S(1)}, f32[2,16,128]{2,1,0:T(8,128)S(1)}, u32[]{:S(2)}, u32[]{:S(2)}) collective-permute-start(f32[2,16,128]{2,1,0:T(8,128)S(1)} %pair.1.refs_0_), channel_id=1, source_target_pairs={{0,24},{4,28},{8,16},{12,20},{16,8},{20,12},{24,0},{28,4},{1,25},{... | collective-permute-start | bytes 49160 | tf_op jit(solution)/shard_map/share_vectors/ppermute | solution.py:29
  16.9 2.0 %collective-permute-start.7 = (f32[4,16,128]{2,1,0:T(8,128)S(1)}, f32[4,16,128]{2,1,0:T(8,128)S(1)}, u32[]{:S(2)}, u32[]{:S(2)}) collective-permute-start(f32[4,16,128]{2,1,0:T(8,128)S(1)} %hand_on.1), channel_id=1, source_target_pairs={{0,4},{4,0},{8,12},{12,8},{16,20},{20,16},{24,28},{28,24},{1,5},{5... | collective-permute-start | bytes 98312 | tf_op jit(solution)/shard_map/return_products/ppermute | solution.py:29
  18.1 3.8 %collective-permute-start.10 = (f32[2,16,128]{2,1,0:T(8,128)S(1)}, f32[2,16,128]{2,1,0:T(8,128)S(1)}, u32[]{:S(2)}, u32[]{:S(2)}) collective-permute-start(f32[2,16,128]{2,1,0:T(8,128)S(1)} %get-tuple-element.63), channel_id=1, source_target_pairs={{0,1},{1,0},{2,3},{3,2},{4,5},{5,4},{6,7},{7,6},{8,9},{9,8},{10,11... | collective-permute-start | bytes 49160 | tf_op jit(solution)/shard_map/return_products/ppermute | solution.py:29
  18.9 5.2 %collective-permute-start.8 = (f32[2,16,128]{2,1,0:T(8,128)S(1)}, f32[2,16,128]{2,1,0:T(8,128)S(1)}, u32[]{:S(2)}, u32[]{:S(2)}) collective-permute-start(f32[2,16,128]{2,1,0:T(8,128)S(1)} %get-tuple-element.59), channel_id=1, source_target_pairs={{0,8},{4,12},{8,0},{12,4},{16,24},{20,28},{24,16},{28,20},{1,9},{5... | collective-permute-start | bytes 49160 | tf_op jit(solution)/shard_map/return_products/ppermute | solution.py:29
  21.9 4.5 %collective-permute-start.11 = (f32[1,16,128]{2,1,0:T(8,128)S(1)}, f32[1,16,128]{2,1,0:T(8,128)S(1)}, u32[]{:S(2)}, u32[]{:S(2)}) collective-permute-start(f32[1,16,128]{2,1,0:T(8,128)S(1)} %get-tuple-element.65), channel_id=1, source_target_pairs={{0,2},{1,3},{2,0},{3,1},{4,6},{5,7},{6,4},{7,5},{8,10},{9,11},{10,... | collective-permute-start | bytes 24584 | tf_op jit(solution)/shard_map/return_products/ppermute | solution.py:29
  24.1 3.7 %collective-permute-start.9 = (f32[1,16,128]{2,1,0:T(8,128)S(1)}, f32[1,16,128]{2,1,0:T(8,128)S(1)}, u32[]{:S(2)}, u32[]{:S(2)}) collective-permute-start(f32[1,16,128]{2,1,0:T(8,128)S(1)} %get-tuple-element.61), channel_id=1, source_target_pairs={{0,16},{4,20},{8,24},{12,28},{16,0},{20,4},{24,8},{28,12},{1,17},{... | collective-permute-start | bytes 24584 | tf_op jit(solution)/shard_map/return_products/ppermute | solution.py:29

commit v18 on v17

--- a/solution.py
+++ b/solution.py
@@ -93,10 +93,11 @@
     return results
 
 
-def pair_kernel(mine, other, after, out):
-    del after
-    out[0] = mine[...]
-    out[1] = other[...]
+def join_kernel(mine, other, *refs):
+    out = refs[-1]
+    half = mine.shape[0]
+    out[:half] = mine[...]
+    out[half:] = other[...]
 
 
 def prepare_kernel(slots, tiles, *refs):
@@ -114,13 +115,14 @@
         send[block] = sums[2 * block + 1]
 
 
-def column_kernel(n_row, n_col, slots, place, arow, bcol, count, d_ref, *refs):
-    x_col, (*parts, send, keep, rows, sums) = refs[:n_col], refs[n_col:]
+def column_kernel(n_row, n_col, slots, place, arow, bcol, count, d_ref, near, far, *refs):
+    *parts, _, send, keep, rows, sums = refs
     me_row, me_col = place[0], place[1]
+    half = n_col // 2
     for flip in range(n_col):
-        rows[flip] = stack_split(x_col[flip][...])
+        rows[flip] = stack_split(near[flip] if flip < half else far[flip - half])
     sums[...] = jnp.zeros_like(sums)
-    sums[0] = d_ref[...] * x_col[0][...]
+    sums[0] = d_ref[...] * near[0]
     for pair in range(0, slots, 2):
         pieces = [[part[slot] for part in parts] for slot in (pair, pair + 1)]
         values = [rows[arow[0, 0, slot] ^ me_col] for slot in (pair, pair + 1)]
@@ -128,11 +130,6 @@
             block = jnp.where(slot < count[0, 0], bcol[0, 0, slot] ^ me_row, n_row)
             sums[block] += terms
     part_blocks(sums, n_row, send, keep)
-
-
-def hand_on_kernel(early, *refs):
-    late = refs[-1]
-    late[...] = early[...]
 
 
 def row_kernel(n_row, n_col, slots, place, arow, bcol, count, *refs):
@@ -152,6 +149,11 @@
 
 def halve_kernel(mine, other, send, keep):
     part_blocks([mine[block] + other[block] for block in range(mine.shape[0])], mine.shape[0], send, keep)
+
+
+def chip_kernel(mine, other, *outs):
+    for chip, out in enumerate(outs):
+        out[0] = mine[chip] + other[chip]
 
 
 def product_kernel(x_ref, *refs):
@@ -249,40 +251,27 @@
             cost_estimate=pl.CostEstimate(flops=0, bytes_accessed=5 * slots * width * width, transcendentals=0),
             name="prepare",
         )(tiles, *small)
+    def join(mine, other, *after):
+        return pl.pallas_call(
+            join_kernel,
+            out_shape=blocks(2 * mine.shape[0]),
+            in_specs=[VMEM] * 2 + [pl.BlockSpec(memory_space=pl.ANY)] * len(after),
+            out_specs=VMEM,
+            compiler_params=params,
+            name="join",
+        )(mine, other, *after)
+
     with jax.named_scope("share_vectors"):
-        other = trade(vectors, "row", 1)
-        x_col = [vectors] + trades(vectors, "col", range(1, n_col))
-        pair = pl.pallas_call(
-            pair_kernel,
-            out_shape=blocks(2),
-            in_specs=[VMEM] * 2 + [pl.BlockSpec(memory_space=pl.ANY)],
-            out_specs=VMEM,
-            compiler_params=params,
-            name="pair",
-        )(vectors, other, parts[0])
+        own = vectors[None]
+        other = trade(own, "row", 1)
+        near, far = own, trade(own, "col", 1)
+        pair = join(own, other, parts[0])
         x_pairs = [pair] + trades(pair, "row", range(2, n_row, 2))
-    with jax.named_scope("column_terms"):
-        col_send, col_keep = pl.pallas_call(
-            functools.partial(column_kernel, n_row, n_col, slots),
-            out_shape=[blocks(n_row // 2)] * 2,
-            in_specs=[SMEM] * 4 + [VMEM] * (n_col + 4),
-            out_specs=[VMEM] * 2,
-            scratch_shapes=[
-                pltpu.VMEM((n_col, 3 * nvec, width), jnp.bfloat16),
-                pltpu.VMEM((n_row + 1, nvec, width), jnp.float32),
-            ],
-            compiler_params=params,
-            cost_estimate=cost,
-            name="column_terms",
-        )(place, arow, bcol, tile_count, energy, *x_col, *parts)
-        col_send = pl.pallas_call(
-            hand_on_kernel,
-            out_shape=blocks(n_row // 2),
-            in_specs=[VMEM] + [pl.BlockSpec(memory_space=pl.ANY)] * (n_row // 2 - 1),
-            out_specs=VMEM,
-            compiler_params=params,
-            name="hand_on",
-        )(col_send, *x_pairs[1:])
+        reach = 2
+        while reach < n_col:
+            near = join(near, far)
+            far = trade(near, "col", reach)
+            reach *= 2
     with jax.named_scope("row_terms"):
         row_send, row_keep = pl.pallas_call(
             functools.partial(row_kernel, n_row, n_col, slots),
@@ -297,13 +286,36 @@
             cost_estimate=cost,
             name="row_terms",
         )(place, arow, bcol, tile_count, *x_pairs, *parts)
+    with jax.named_scope("column_terms"):
+        col_send, col_keep = pl.pallas_call(
+            functools.partial(column_kernel, n_row, n_col, slots),
+            out_shape=[blocks(n_row // 2)] * 2,
+            in_specs=[SMEM] * 4 + [VMEM] * 6 + [pl.BlockSpec(memory_space=pl.ANY)],
+            out_specs=[VMEM] * 2,
+            scratch_shapes=[
+                pltpu.VMEM((n_col, 3 * nvec, width), jnp.bfloat16),
+                pltpu.VMEM((n_row + 1, nvec, width), jnp.float32),
+            ],
+            compiler_params=params,
+            cost_estimate=cost,
+            name="column_terms",
+        )(place, arow, bcol, tile_count, energy, near, far, *parts, row_send)
     with jax.named_scope("return_products"):
-        sums = halve(col_send, col_keep, "row") + halve(row_send, row_keep, "col")
+        sums = halve(row_send, row_keep, "col")
+        chips = pl.pallas_call(
+            chip_kernel,
+            out_shape=[blocks(1)] * (n_row // 2),
+            in_specs=[VMEM] * 2,
+            out_specs=[VMEM] * (n_row // 2),
+            compiler_params=params,
+            name="chip_sum",
+        )(col_keep, trade(col_send, "row", 1))
+        sums += (chips[0], *[trade(chips[chip], "row", 2 * chip) for chip in range(1, n_row // 2)])
     with jax.named_scope("product"):
         product, squares = pl.pallas_call(
             product_kernel,
             out_shape=[block, jax.ShapeDtypeStruct((devices, 3, packed_rows, width), jnp.float32)],
-            in_specs=[VMEM] * 5,
+            in_specs=[VMEM] * (1 + len(sums)),
             out_specs=[VMEM] * 2,
             compiler_params=params,
             name="product",

time: 40.6 us -> 41.8 us (1.030)
  starting transfers between devices: 13.3 us -> 16 us
  waiting for transfers between devices: 8.29 us -> 7.44 us
  blocking collectives: 10.4 us -> 9.64 us
    ppermute x12, starting transfers between devices: 13.3 us -> 16 us  [trade(): return lax.ppermute(value, axis, [(p, p ^ flip) for p in range(size)])]
    ppermute x12, waiting for transfers between devices: 8.29 us -> 7.44 us  [trade(): return lax.ppermute(value, axis, [(p, p ^ flip) for p in range(size)])]
    all_to_all x1, blocking collectives: 10.4 us -> 9.64 us  [swap(): return lax.all_to_all(blocks, axis, 0, 0, tiled=True)]
  transfers between devices with their start and end apart: 12 -> 12, of which waited for: 5 -> 5; matrix products, arithmetic and copies ran while one was open for 0% -> 0% of each run, Pallas kernels for 6% -> 3%
where the time goes in v18:
time: 41.8 us; the launch traced here: 41.5 us
  starting transfers between devices  16 us (38%)
  blocking collectives  9.64 us (23%)
  waiting for transfers between devices  7.44 us (18%)
  Pallas kernels  3.94 us (9%)
  local copies, waits for them, and re-layouts  2.4 us (6%)
  between operations  1.36 us (3%)
  loops' own time  0.69 us (2%)
    ppermute x12, starting transfers between devices, trade(): return lax.ppermute(value, axis, [(p, p ^ flip) for p in range(size)])  16 us
    all_to_all x1, blocking collectives, swap(): return lax.all_to_all(blocks, axis, 0, 0, tiled=True)  9.64 us
    ppermute x12, waiting for transfers between devices, trade(): return lax.ppermute(value, axis, [(p, p ^ flip) for p in range(size)])  7.44 us
    unnamed x10, local copies, waits for them, and re-layouts  2.4 us
    pallas_call x1, Pallas kernels, per_device(): pl.pallas_call(functools.partial(result_kernel, scale), out_shape=[block,...  1.24 us
    pallas_call x1, Pallas kernels, per_device(): pl.pallas_call(functools.partial(row_kernel, n_row, n_col, slots), out_sh...  1.21 us
    pallas_call x1, Pallas kernels, per_device(): pl.pallas_call(functools.partial(column_kernel, n_row, n_col, slots), out...  0.94 us
  transfers between devices with their start and end apart: 12, of which 5 were waited for; matrix products, arithmetic and copies ran while one was open for 0% of the time, Pallas kernels for 3%

profile of v18, /device:TPU:0, one launch (start us, length us, event | category | flops | bytes accessed | tf_op | source)
XLA Modules:
  0.0 41.5 jit_solution(5383058548484991878)
XLA Ops:
  0.6 0.5 %collective-permute-start = (f32[1,16,128]{2,1,0:T(8,128)}, f32[1,16,128]{2,1,0:T(8,128)S(1)}, u32[]{:S(2)}, u32[]{:S(2)}) collective-permute-start(f32[1,16,128]{2,1,0:T(8,128)} %bitcast.6), channel_id=1, source_target_pairs={{0,4},{4,0},{8,12},{12,8},{16,20},{20,16},{24,28},{28,24},{1,5},{5... | collective-permute-start | bytes 24584 | tf_op jit(solution)/shard_map/share_vectors/ppermute | solution.py:29
  1.1 2.6 %collective-permute-start.6 = (f32[1,16,128]{2,1,0:T(8,128)}, f32[1,16,128]{2,1,0:T(8,128)S(1)}, u32[]{:S(2)}, u32[]{:S(2)}) collective-permute-start(f32[1,16,128]{2,1,0:T(8,128)} %bitcast.7), channel_id=1, source_target_pairs={{0,1},{1,0},{2,3},{3,2},{4,5},{5,4},{6,7},{7,6},{8,9},{9,8},{10,11... | collective-permute-start | bytes 24584 | tf_op jit(solution)/shard_map/share_vectors/ppermute | solution.py:29
  3.8 0.0 copy-start.1
  3.8 0.0 copy-start.2
  3.8 0.0 copy-start.3
  3.8 0.6 %copy-done.1 = s32[1,1,16]{2,1,0:T(1,128)S(1)} copy-done((s32[1,1,16]{2,1,0:T(1,128)S(1)}, s32[1,1,16]{2,1,0:T(1,128)}, u32[]{:S(2)}) %copy-start.1) | copy-done | bytes 88
  4.5 0.0 copy-done.2
  4.5 0.0 copy-done.3
  4.5 0.0 copy-start
  4.5 1.2 %copy-done = f32[1,1,16,128,128]{4,3,2,1,0:T(8,128)S(1)} copy-done((f32[1,1,16,128,128]{4,3,2,1,0:T(8,128)S(1)}, f32[1,1,16,128,128]{4,3,2,1,0:T(8,128)}, u32[]{:S(2)}) %copy-start) | copy-done | bytes 1048600
  5.7 0.0 copy-start.4
  5.7 0.2 prepare.1
  5.9 0.0 collective-permute-done.other
  5.9 0.5 %copy-done.4 = f32[16,128]{1,0:T(8,128)S(1)} copy-done((f32[16,128]{1,0:T(8,128)S(1)}, f32[16,128]{1,0:T(8,128)}, u32[]{:S(2)}) %copy-start.4) | copy-done | bytes 8216
  6.4 1.5 %collective-permute-start.1 = (f32[2,16,128]{2,1,0:T(8,128)S(1)}, f32[2,16,128]{2,1,0:T(8,128)S(1)}, u32[]{:S(2)}, u32[]{:S(2)}) collective-permute-start(f32[2,16,128]{2,1,0:T(8,128)S(1)} %join.2.refs_0_), channel_id=1, source_target_pairs={{0,8},{4,12},{8,0},{12,4},{16,24},{20,28},{24,16},{28,20},{1,9},{5... | collective-permute-start | bytes 49160 | tf_op jit(solution)/shard_map/share_vectors/ppermute | solution.py:29
  7.9 1.5 %collective-permute-start.2 = (f32[2,16,128]{2,1,0:T(8,128)S(1)}, f32[2,16,128]{2,1,0:T(8,128)S(1)}, u32[]{:S(2)}, u32[]{:S(2)}) collective-permute-start(f32[2,16,128]{2,1,0:T(8,128)S(1)} %join.2.refs_0_), channel_id=1, source_target_pairs={{0,16},{4,20},{8,24},{12,28},{16,0},{20,4},{24,8},{28,12},{1,17},{... | collective-permute-start | bytes 49160 | tf_op jit(solution)/shard_map/share_vectors/ppermute | solution.py:29
  9.4 0.5 %collective-permute-start.3 = (f32[2,16,128]{2,1,0:T(8,128)S(1)}, f32[2,16,128]{2,1,0:T(8,128)S(1)}, u32[]{:S(2)}, u32[]{:S(2)}) collective-permute-start(f32[2,16,128]{2,1,0:T(8,128)S(1)} %join.2.refs_0_), channel_id=1, source_target_pairs={{0,24},{4,28},{8,16},{12,20},{16,8},{20,12},{24,0},{28,4},{1,25},{... | collective-permute-start | bytes 49160 | tf_op jit(solution)/shard_map/share_vectors/ppermute | solution.py:29
  9.9 0.0 collective-permute-done.6.other
  9.9 2.6 %collective-permute-start.7 = (f32[2,16,128]{2,1,0:T(8,128)S(1)}, f32[2,16,128]{2,1,0:T(8,128)S(1)}, u32[]{:S(2)}, u32[]{:S(2)}) collective-permute-start(f32[2,16,128]{2,1,0:T(8,128)S(1)} %join.3.near), channel_id=1, source_target_pairs={{0,2},{1,3},{2,0},{3,1},{4,6},{5,7},{6,4},{7,5},{8,10},{9,11},{10,... | collective-permute-start | bytes 49160 | tf_op jit(solution)/shard_map/share_vectors/ppermute | solution.py:29
  12.5 0.1 pad_add_fusion.place
  13.2 0.0 collective-permute-done.1.refs_1_
  13.2 0.0 collective-permute-done.2.refs_2_
  13.2 0.8 %collective-permute-done.3.refs_3_ = f32[2,16,128]{2,1,0:T(8,128)S(1)} collective-permute-done((f32[2,16,128]{2,1,0:T(8,128)S(1)}, f32[2,16,128]{2,1,0:T(8,128)S(1)}, u32[]{:S(2)}, u32[]{:S(2)}) %collective-permute-start.3) | collective-permute-done | bytes 16416 | tf_op jit(solution)/shard_map/share_vectors/ppermute | solution.py:29
  14.1 1.2 %row_terms.1 = (f32[2,16,128]{2,1,0:T(8,128)S(1)}, f32[2,16,128]{2,1,0:T(8,128)S(1)}) custom-call(s32[2]{0:T(128)S(1)} %pad_add_fusion.place, s32[1,1,16]{2,1,0:T(1,128)S(1)} %get-tuple-element.50.arow, s32[1,1,16]{2,1,0:T(1,128)S(1)} %get-tuple-element.51.bcol, s32[1,1]{1,0:T(1,128)S(6)} %copy.16.count, f32[2,16,128]{2,1,0:T(8,128)S(1)} %join.2.refs_0_, ...), custom_call_target="tpu_custom_call" | custom-call | flops 50331648 | bytes 1048576 | tf_op jit(solution)/shard_map/row_terms/row_terms/pallas_call | solution.py:276
  15.3 0.0 collective-permute-done.7.far
  15.3 0.9 %column_terms.1 = (f32[4,16,128]{2,1,0:T(8,128)S(1)}, f32[4,16,128]{2,1,0:T(8,128)S(1)}) custom-call(s32[2]{0:T(128)S(1)} %pad_add_fusion.place, s32[1,1,16]{2,1,0:T(1,128)S(1)} %get-tuple-element.50.arow, s32[1,1,16]{2,1,0:T(1,128)S(1)} %get-tuple-element.51.bcol, s32[1,1]{1,0:T(1,128)S(6)} %copy.16.count, f32[1,128]{1,0:T(1,128)S(1)} %get-tuple-element.59.d_ref, ...), custom_call_target="tpu_custom_call" | custom-call | flops 50331648 | bytes 1048576 | tf_op jit(solution)/shard_map/column_terms/column_terms/pallas_call | solution.py:290
  16.2 0.1 collective-permute-start.8
  16.3 0.5 %collective-permute-start.4 = (f32[2,16,128]{2,1,0:T(8,128)S(1)}, f32[2,16,128]{2,1,0:T(8,128)S(1)}, u32[]{:S(2)}, u32[]{:S(2)}) collective-permute-start(f32[2,16,128]{2,1,0:T(8,128)S(1)} %get-tuple-element.56.refs_3_), channel_id=1, source_target_pairs={{0,1},{1,0},{2,3},{3,2},{4,5},{5,4},{6,7},{7,6},{8,9},{9,8},{10,11... | collective-permute-start | bytes 49160 | tf_op jit(solution)/shard_map/return_products/ppermute | solution.py:29
  16.8 3.3 %collective-permute-done.4.other = f32[2,16,128]{2,1,0:T(8,128)S(1)} collective-permute-done((f32[2,16,128]{2,1,0:T(8,128)S(1)}, f32[2,16,128]{2,1,0:T(8,128)S(1)}, u32[]{:S(2)}, u32[]{:S(2)}) %collective-permute-start.4) | collective-permute-done | bytes 16416 | tf_op jit(solution)/shard_map/return_products/ppermute | solution.py:29
  20.1 2.6 %collective-permute-start.5 = (f32[1,16,128]{2,1,0:T(8,128)S(1)}, f32[1,16,128]{2,1,0:T(8,128)S(1)}, u32[]{:S(2)}, u32[]{:S(2)}) collective-permute-start(f32[1,16,128]{2,1,0:T(8,128)S(1)} %get-tuple-element.58), channel_id=1, source_target_pairs={{0,2},{1,3},{2,0},{3,1},{4,6},{5,7},{6,4},{7,5},{8,10},{9,11},{10,... | collective-permute-start | bytes 24584 | tf_op jit(solution)/shard_map/return_products/ppermute | solution.py:29
  22.7 0.0 collective-permute-done.8.other
  22.7 0.8 %collective-permute-start.9 = (f32[1,16,128]{2,1,0:T(8,128)S(1)}, f32[1,16,128]{2,1,0:T(8,128)S(1)}, u32[]{:S(2)}, u32[]{:S(2)}) collective-permute-start(f32[1,16,128]{2,1,0:T(8,128)S(1)} %get-tuple-element.63), channel_id=1, source_target_pairs={{0,8},{4,12},{8,0},{12,4},{16,24},{20,28},{24,16},{28,20},{1,9},{5... | collective-permute-start | bytes 24584 | tf_op jit(solution)/shard_map/return_products/ppermute | solution.py:29
  23.5 1.5 %collective-permute-start.10 = (f32[1,16,128]{2,1,0:T(8,128)S(1)}, f32[1,16,128]{2,1,0:T(8,128)S(1)}, u32[]{:S(2)}, u32[]{:S(2)}) collective-permute-start(f32[1,16,128]{2,1,0:T(8,128)S(1)} %get-tuple-element.64), channel_id=1, source_target_pairs={{0,16},{4,20},{8,24},{12,28},{16,0},{20,4},{24,8},{28,12},{1,17},{... | collective-permute-start | bytes 24584 | tf_op jit(solution)/shard_map/return_products/ppermute | solution.py:29
  25.0 1.2 %collective-permute-start.11 = (f32[1,16,128]{2,1,0:T(8,128)S(1)}, f32[1,16,128]{2,1,0:T(8,128)S(1)}, u32[]{:S(2)}, u32[]{:S(2)}) collective-permute-start(f32[1,16,128]{2,1,0:T(8,128)S(1)} %get-tuple-element.65), channel_id=1, source_target_pairs={{0,24},{4,28},{8,16},{12,20},{16,8},{20,12},{24,0},{28,4},{1,25},{... | collective-permute-start | bytes 24584 | tf_op jit(solution)/shard_map/return_products/ppermute | solution.py:29
  26.3 0.0 collective-permute-done.5.refs_1_
  26.3 0.2 collective-permute-done.9.refs_3_
  26.4 0.7 %collective-permute-done.10.refs_4_ = f32[1,16,128]{2,1,0:T(8,128)S(1)} collective-permute-done((f32[1,16,128]{2,1,0:T(8,128)S(1)}, f32[1,16,128]{2,1,0:T(8,128)S(1)}, u32[]{:S(2)}, u32[]{:S(2)}) %collective-permute-start.10) | collective-permute-done | bytes 8224 | tf_op jit(solution)/shard_map/return_products/ppermute | solution.py:29
  27.2 2.4 %collective-permute-done.11.refs_5_ = f32[1,16,128]{2,1,0:T(8,128)S(1)} collective-permute-done((f32[1,16,128]{2,1,0:T(8,128)S(1)}, f32[1,16,128]{2,1,0:T(8,128)S(1)}, u32[]{:S(2)}, u32[]{:S(2)}) %collective-permute-start.11) | collective-permute-done | bytes 8224 | tf_op jit(solution)/shard_map/return_products/ppermute | solution.py:29
  29.6 0.3 product.1
  30.0 9.6 %all_to_all.9.parts = f32[32,3,2,128]{3,2,1,0:T(2,128)S(1)} all-to-all(f32[32,3,2,128]{3,2,1,0:T(2,128)S(1)} %get-tuple-element.67), channel_id=1, replica_groups=mesh['row'=8,'col'=4] {'row','col'}, dimensions={0} | all-to-all | bytes 196608 | tf_op jit(solution)/shard_map/product/all_to_all | solution.py:24
  39.6 1.2 %results.1 = (f32[16,128]{1,0:T(8,128)}, f32[16,16]{1,0:T(8,128)}, f32[16,16]{1,0:T(8,128)}, s32[1,1]{1,0:T(1,128)}) custom-call(f32[16,128]{1,0:T(8,128)S(1)} %copy-done.4, f32[16,128]{1,0:T(8,128)S(1)} %get-tuple-element.91.product, f32[32,3,2,128]{3,2,1,0:T(2,128)S(1)} %all_to_all.9.parts), custom_call_target="tpu_custom_call" | custom-call | tf_op jit(solution)/shard_map/results/results/pallas_call | solution.py:325
  40.8 0.7 %while.9 = (s32[]{:T(128)}, f32[16,16]{1,0:T(8,128)}, f32[16,128]{1,0:T(8,128)S(1)}, f32[16,128]{1,0:T(8,128)S(1)}, f32[32,3,2,128]{3,2,1,0:T(2,128)S(1)}) while((s32[]{:T(128)}, f32[16,16]{1,0:T(8,128)}, f32[16,128]{1,0:T(8,128)S(1)}, f32[16,128]{1,0:T(8,128)S(1)}, f32[32,3,2,128]{3,2,1,0:T(2,128)S(1)}) %tuple.20), condition=%region_1.0_spmd, body=%region_0.0_spmd | while | flops 1 | bytes 98393 | solution.py:354
  (4 shorter events, 0.0 us)
Async XLA Ops:
  0.6 5.3 %collective-permute-start = (f32[1,16,128]{2,1,0:T(8,128)}, f32[1,16,128]{2,1,0:T(8,128)S(1)}, u32[]{:S(2)}, u32[]{:S(2)}) collective-permute-start(f32[1,16,128]{2,1,0:T(8,128)} %bitcast.6), channel_id=1, source_target_pairs={{0,4},{4,0},{8,12},{12,8},{16,20},{20,16},{24,28},{28,24},{1,5},{5... | collective-permute-start | bytes 24584 | tf_op jit(solution)/shard_map/share_vectors/ppermute | solution.py:29
  1.1 8.8 %collective-permute-start.6 = (f32[1,16,128]{2,1,0:T(8,128)}, f32[1,16,128]{2,1,0:T(8,128)S(1)}, u32[]{:S(2)}, u32[]{:S(2)}) collective-permute-start(f32[1,16,128]{2,1,0:T(8,128)} %bitcast.7), channel_id=1, source_target_pairs={{0,1},{1,0},{2,3},{3,2},{4,5},{5,4},{6,7},{7,6},{8,9},{9,8},{10,11... | collective-permute-start | bytes 24584 | tf_op jit(solution)/shard_map/share_vectors/ppermute | solution.py:29
  3.8 0.7 %copy-start.1 = (s32[1,1,16]{2,1,0:T(1,128)S(1)}, s32[1,1,16]{2,1,0:T(1,128)}, u32[]{:S(2)}) copy-start(s32[1,1,16]{2,1,0:T(1,128)} %refs_0_.1) | copy-start | bytes 196
  3.8 0.7 %copy-start.2 = (s32[1,1,16]{2,1,0:T(1,128)S(1)}, s32[1,1,16]{2,1,0:T(1,128)}, u32[]{:S(2)}) copy-start(s32[1,1,16]{2,1,0:T(1,128)} %refs_1_.1) | copy-start | bytes 196
  3.8 0.7 %copy-start.3 = (f32[128]{0:T(128)S(1)}, f32[128]{0:T(128)}, u32[]{:S(2)}) copy-start(f32[128]{0:T(128)} %param.9) | copy-start | bytes 1540
  4.5 1.2 %copy-start = (f32[1,1,16,128,128]{4,3,2,1,0:T(8,128)S(1)}, f32[1,1,16,128,128]{4,3,2,1,0:T(8,128)}, u32[]{:S(2)}) copy-start(f32[1,1,16,128,128]{4,3,2,1,0:T(8,128)} %tiles.1) | copy-start | bytes 3145732
  5.7 0.7 %copy-start.4 = (f32[16,128]{1,0:T(8,128)S(1)}, f32[16,128]{1,0:T(8,128)}, u32[]{:S(2)}) copy-start(f32[16,128]{1,0:T(8,128)} %x_ref.3) | copy-start | bytes 24580
  6.4 6.8 %collective-permute-start.1 = (f32[2,16,128]{2,1,0:T(8,128)S(1)}, f32[2,16,128]{2,1,0:T(8,128)S(1)}, u32[]{:S(2)}, u32[]{:S(2)}) collective-permute-start(f32[2,16,128]{2,1,0:T(8,128)S(1)} %join.2.refs_0_), channel_id=1, source_target_pairs={{0,8},{4,12},{8,0},{12,4},{16,24},{20,28},{24,16},{28,20},{1,9},{5... | collective-permute-start | bytes 49160 | tf_op jit(solution)/shard_map/share_vectors/ppermute | solution.py:29
  7.9 5.3 %collective-permute-start.2 = (f32[2,16,128]{2,1,0:T(8,128)S(1)}, f32[2,16,128]{2,1,0:T(8,128)S(1)}, u32[]{:S(2)}, u32[]{:S(2)}) collective-permute-start(f32[2,16,128]{2,1,0:T(8,128)S(1)} %join.2.refs_0_), channel_id=1, source_target_pairs={{0,16},{4,20},{8,24},{12,28},{16,0},{20,4},{24,8},{28,12},{1,17},{... | collective-permute-start | bytes 49160 | tf_op jit(solution)/shard_map/share_vectors/ppermute | solution.py:29
  9.4 4.6 %collective-permute-start.3 = (f32[2,16,128]{2,1,0:T(8,128)S(1)}, f32[2,16,128]{2,1,0:T(8,128)S(1)}, u32[]{:S(2)}, u32[]{:S(2)}) collective-permute-start(f32[2,16,128]{2,1,0:T(8,128)S(1)} %join.2.refs_0_), channel_id=1, source_target_pairs={{0,24},{4,28},{8,16},{12,20},{16,8},{20,12},{24,0},{28,4},{1,25},{... | collective-permute-start | bytes 49160 | tf_op jit(solution)/shard_map/share_vectors/ppermute | solution.py:29
  9.9 5.4 %collective-permute-start.7 = (f32[2,16,128]{2,1,0:T(8,128)S(1)}, f32[2,16,128]{2,1,0:T(8,128)S(1)}, u32[]{:S(2)}, u32[]{:S(2)}) collective-permute-start(f32[2,16,128]{2,1,0:T(8,128)S(1)} %join.3.near), channel_id=1, source_target_pairs={{0,2},{1,3},{2,0},{3,1},{4,6},{5,7},{6,4},{7,5},{8,10},{9,11},{10,... | collective-permute-start | bytes 49160 | tf_op jit(solution)/shard_map/share_vectors/ppermute | solution.py:29
  16.2 6.5 %collective-permute-start.8 = (f32[4,16,128]{2,1,0:T(8,128)S(1)}, f32[4,16,128]{2,1,0:T(8,128)S(1)}, u32[]{:S(2)}, u32[]{:S(2)}) collective-permute-start(f32[4,16,128]{2,1,0:T(8,128)S(1)} %get-tuple-element.61), channel_id=1, source_target_pairs={{0,4},{4,0},{8,12},{12,8},{16,20},{20,16},{24,28},{28,24},{1,5},{5... | collective-permute-start | bytes 98312 | tf_op jit(solution)/shard_map/return_products/ppermute | solution.py:29
  16.3 3.8 %collective-permute-start.4 = (f32[2,16,128]{2,1,0:T(8,128)S(1)}, f32[2,16,128]{2,1,0:T(8,128)S(1)}, u32[]{:S(2)}, u32[]{:S(2)}) collective-permute-start(f32[2,16,128]{2,1,0:T(8,128)S(1)} %get-tuple-element.56.refs_3_), channel_id=1, source_target_pairs={{0,1},{1,0},{2,3},{3,2},{4,5},{5,4},{6,7},{7,6},{8,9},{9,8},{10,11... | collective-permute-start | bytes 49160 | tf_op jit(solution)/shard_map/return_products/ppermute | solution.py:29
  20.1 6.2 %collective-permute-start.5 = (f32[1,16,128]{2,1,0:T(8,128)S(1)}, f32[1,16,128]{2,1,0:T(8,128)S(1)}, u32[]{:S(2)}, u32[]{:S(2)}) collective-permute-start(f32[1,16,128]{2,1,0:T(8,128)S(1)} %get-tuple-element.58), channel_id=1, source_target_pairs={{0,2},{1,3},{2,0},{3,1},{4,6},{5,7},{6,4},{7,5},{8,10},{9,11},{10,... | collective-permute-start | bytes 24584 | tf_op jit(solution)/shard_map/return_products/ppermute | solution.py:29
  22.7 3.7 %collective-permute-start.9 = (f32[1,16,128]{2,1,0:T(8,128)S(1)}, f32[1,16,128]{2,1,0:T(8,128)S(1)}, u32[]{:S(2)}, u32[]{:S(2)}) collective-permute-start(f32[1,16,128]{2,1,0:T(8,128)S(1)} %get-tuple-element.63), channel_id=1, source_target_pairs={{0,8},{4,12},{8,0},{12,4},{16,24},{20,28},{24,16},{28,20},{1,9},{5... | collective-permute-start | bytes 24584 | tf_op jit(solution)/shard_map/return_products/ppermute | solution.py:29
  23.5 3.7 %collective-permute-start.10 = (f32[1,16,128]{2,1,0:T(8,128)S(1)}, f32[1,16,128]{2,1,0:T(8,128)S(1)}, u32[]{:S(2)}, u32[]{:S(2)}) collective-permute-start(f32[1,16,128]{2,1,0:T(8,128)S(1)} %get-tuple-element.64), channel_id=1, source_target_pairs={{0,16},{4,20},{8,24},{12,28},{16,0},{20,4},{24,8},{28,12},{1,17},{... | collective-permute-start | bytes 24584 | tf_op jit(solution)/shard_map/return_products/ppermute | solution.py:29
  25.0 4.5 %collective-permute-start.11 = (f32[1,16,128]{2,1,0:T(8,128)S(1)}, f32[1,16,128]{2,1,0:T(8,128)S(1)}, u32[]{:S(2)}, u32[]{:S(2)}) collective-permute-start(f32[1,16,128]{2,1,0:T(8,128)S(1)} %get-tuple-element.65), channel_id=1, source_target_pairs={{0,24},{4,28},{8,16},{12,20},{16,8},{20,12},{24,0},{28,4},{1,25},{... | collective-permute-start | bytes 24584 | tf_op jit(solution)/shard_map/return_products/ppermute | solution.py:29

commit v19 on v16

--- a/solution.py
+++ b/solution.py
@@ -93,12 +93,11 @@
     return results
 
 
-def join_kernel(axes, *refs):
-    for which, out in enumerate(refs[-axes:]):
-        mine, other = refs[2 * which : 2 * which + 2]
-        half = mine.shape[0]
-        out[:half] = mine[...]
-        out[half:] = other[...]
+def join_kernel(mine, other, *refs):
+    out = refs[-1]
+    half = mine.shape[0]
+    out[:half] = mine[...]
+    out[half:] = other[...]
 
 
 def prepare_kernel(slots, tiles, *refs):
@@ -224,25 +223,23 @@
     def blocks(total):
         return jax.ShapeDtypeStruct((total, nvec, width), jnp.float32)
 
-    def gather(axes, after):
-        near = [vectors[None]] * len(axes)
-        far = [trade(vectors[None], axis, 1) for axis in axes]
+    def gather(axis, *after):
+        near = vectors[None]
+        far = trade(near, axis, 1)
         reach = 2
-        while any(reach < lax.axis_size(axis) for axis in axes):
-            going = [which for which, axis in enumerate(axes) if reach < lax.axis_size(axis)]
-            joined = pl.pallas_call(
-                functools.partial(join_kernel, len(going)),
-                out_shape=[blocks(reach)] * len(going),
-                in_specs=[VMEM] * (2 * len(going)) + [pl.BlockSpec(memory_space=pl.ANY)] * len(after),
-                out_specs=[VMEM] * len(going),
+        while reach < lax.axis_size(axis):
+            near = pl.pallas_call(
+                join_kernel,
+                out_shape=blocks(reach),
+                in_specs=[VMEM] * 2 + [pl.BlockSpec(memory_space=pl.ANY)] * len(after),
+                out_specs=VMEM,
                 compiler_params=params,
-                name="join",
-            )(*[half for which in going for half in (near[which], far[which])], *after)
-            for which, half in zip(going, joined):
-                near[which], far[which] = half, trade(half, axes[which], reach)
+                name="join_" + axis,
+            )(near, far, *after)
+            far = trade(near, axis, reach)
             reach *= 2
             after = ()
-        return list(zip(near, far))
+        return near, far
 
     def halve(send, keep, axis):
         flip = 1
@@ -271,7 +268,8 @@
             name="prepare",
         )(tiles, *small)
     with jax.named_scope("share_vectors"):
-        x_row, x_col = gather(("row", "col"), parts[:1])
+        x_row = gather("row", parts[0])
+        x_col = gather("col")
     with jax.named_scope("column_terms"):
         col_send, col_keep = pl.pallas_call(
             functools.partial(column_kernel, n_row, n_col, slots),

time: 39.5 us -> 40.6 us (1.028)
  waiting for transfers between devices: 4.21 us -> 6.51 us
  starting transfers between devices: 15.8 us -> 14.7 us
  local copies, waits for them, and re-layouts: 1.33 us -> 1.86 us
  blocking collectives: 11.8 us -> 11.3 us
    ppermute x10, waiting for transfers between devices: 4.21 us -> 6.51 us  [trade(): return lax.ppermute(value, axis, [(p, p ^ flip) for p in range(size)])]
    ppermute x10, starting transfers between devices: 15.8 us -> 14.7 us  [trade(): return lax.ppermute(value, axis, [(p, p ^ flip) for p in range(size)])]
    all_to_all x1, blocking collectives: 11.8 us -> 11.3 us  [swap(): return lax.all_to_all(blocks, axis, 0, 0, tiled=True)]
    unnamed x10, local copies, waits for them, and re-layouts: 1.33 us -> 1.86 us
where the time goes in v19:
time: 40.6 us; the launch traced here: 40.4 us
  starting transfers between devices  14.7 us (36%)
  blocking collectives  11.3 us (28%)
  waiting for transfers between devices  6.51 us (16%)
  Pallas kernels  3.92 us (10%)
  local copies, waits for them, and re-layouts  1.86 us (5%)
  between operations  1.36 us (3%)
  loops' own time  0.68 us (2%)
    ppermute x10, starting transfers between devices, trade(): return lax.ppermute(value, axis, [(p, p ^ flip) for p in range(size)])  14.7 us
    all_to_all x1, blocking collectives, swap(): return lax.all_to_all(blocks, axis, 0, 0, tiled=True)  11.3 us
    ppermute x10, waiting for transfers between devices, trade(): return lax.ppermute(value, axis, [(p, p ^ flip) for p in range(size)])  6.51 us
    unnamed x10, local copies, waits for them, and re-layouts  1.86 us
    pallas_call x1, Pallas kernels, per_device(): pl.pallas_call(functools.partial(result_kernel, scale), out_shape=[block,...  1.22 us
    pallas_call x1, Pallas kernels, per_device(): pl.pallas_call(functools.partial(row_kernel, n_row, n_col, slots), out_sh...  1.21 us
    pallas_call x1, Pallas kernels, per_device(): pl.pallas_call(functools.partial(column_kernel, n_row, n_col, slots), out...  0.93 us
  transfers between devices with their start and end apart: 10, of which 5 were waited for; matrix products, arithmetic and copies ran while one was open for 0% of the time, Pallas kernels for 6%

profile of v19, /device:TPU:0, one launch (start us, length us, event | category | flops | bytes accessed | tf_op | source)
XLA Modules:
  0.0 40.4 jit_solution(7486568397977937289)
XLA Ops:
  0.6 0.0 copy-start.1
  0.6 0.0 copy-start.2
  0.7 0.0 copy-start.3
  0.7 0.5 %collective-permute-start.2 = (f32[1,16,128]{2,1,0:T(8,128)}, f32[1,16,128]{2,1,0:T(8,128)S(1)}, u32[]{:S(2)}, u32[]{:S(2)}) collective-permute-start(f32[1,16,128]{2,1,0:T(8,128)} %bitcast.6), channel_id=1, source_target_pairs={{0,4},{4,0},{8,12},{12,8},{16,20},{20,16},{24,28},{28,24},{1,5},{5... | collective-permute-start | bytes 24584 | tf_op jit(solution)/shard_map/share_vectors/ppermute | solution.py:29
  1.2 0.1 copy-done.1
  1.3 0.0 copy-done.2
  1.3 0.0 copy-done.3
  1.3 0.0 copy-start
  1.3 1.2 %copy-done = f32[1,1,16,128,128]{4,3,2,1,0:T(8,128)S(1)} copy-done((f32[1,1,16,128,128]{4,3,2,1,0:T(8,128)S(1)}, f32[1,1,16,128,128]{4,3,2,1,0:T(8,128)}, u32[]{:S(2)}) %copy-start) | copy-done | bytes 1048600
  2.5 0.0 copy-start.4
  2.5 0.2 prepare.1
  2.7 0.0 collective-permute-done.2.other
  2.8 0.5 %copy-done.4 = f32[16,128]{1,0:T(8,128)S(1)} copy-done((f32[16,128]{1,0:T(8,128)S(1)}, f32[16,128]{1,0:T(8,128)}, u32[]{:S(2)}) %copy-start.4) | copy-done | bytes 8216
  3.2 2.9 %collective-permute-start.3 = (f32[2,16,128]{2,1,0:T(8,128)S(1)}, f32[2,16,128]{2,1,0:T(8,128)S(1)}, u32[]{:S(2)}, u32[]{:S(2)}) collective-permute-start(f32[2,16,128]{2,1,0:T(8,128)S(1)} %join_row.2.mine), channel_id=1, source_target_pairs={{0,8},{4,12},{8,0},{12,4},{16,24},{20,28},{24,16},{28,20},{1,9},{5... | collective-permute-start | bytes 49160 | tf_op jit(solution)/shard_map/share_vectors/ppermute | solution.py:29
  6.2 1.6 %collective-permute-start = (f32[1,16,128]{2,1,0:T(8,128)S(1)}, f32[1,16,128]{2,1,0:T(8,128)S(1)}, u32[]{:S(2)}, u32[]{:S(2)}) collective-permute-start(f32[1,16,128]{2,1,0:T(8,128)S(1)} %bitcast.8), channel_id=1, source_target_pairs={{0,1},{1,0},{2,3},{3,2},{4,5},{5,4},{6,7},{7,6},{8,9},{9,8},{10,11... | collective-permute-start | bytes 24584 | tf_op jit(solution)/shard_map/share_vectors/ppermute | solution.py:29
  7.8 2.1 %collective-permute-done.other = f32[1,16,128]{2,1,0:T(8,128)S(1)} collective-permute-done((f32[1,16,128]{2,1,0:T(8,128)S(1)}, f32[1,16,128]{2,1,0:T(8,128)S(1)}, u32[]{:S(2)}, u32[]{:S(2)}) %collective-permute-start) | collective-permute-done | bytes 8224 | tf_op jit(solution)/shard_map/share_vectors/ppermute | solution.py:29
  9.8 2.6 %collective-permute-start.1 = (f32[2,16,128]{2,1,0:T(8,128)S(1)}, f32[2,16,128]{2,1,0:T(8,128)S(1)}, u32[]{:S(2)}, u32[]{:S(2)}) collective-permute-start(f32[2,16,128]{2,1,0:T(8,128)S(1)} %join_col.1.near), channel_id=1, source_target_pairs={{0,2},{1,3},{2,0},{3,1},{4,6},{5,7},{6,4},{7,5},{8,10},{9,11},{10,... | collective-permute-start | bytes 49160 | tf_op jit(solution)/shard_map/share_vectors/ppermute | solution.py:29
  12.4 0.0 collective-permute-done.3.other
  12.4 1.5 %collective-permute-start.4 = (f32[4,16,128]{2,1,0:T(8,128)S(1)}, f32[4,16,128]{2,1,0:T(8,128)S(1)}, u32[]{:S(2)}, u32[]{:S(2)}) collective-permute-start(f32[4,16,128]{2,1,0:T(8,128)S(1)} %join_row.3.near), channel_id=1, source_target_pairs={{0,16},{4,20},{8,24},{12,28},{16,0},{20,4},{24,8},{28,12},{1,17},{... | collective-permute-start | bytes 98312 | tf_op jit(solution)/shard_map/share_vectors/ppermute | solution.py:29
  14.0 0.1 pad_add_fusion.place
  14.7 0.0 collective-permute-done.1.far
  14.7 0.9 %column_terms.1 = (f32[4,16,128]{2,1,0:T(8,128)S(1)}, f32[4,16,128]{2,1,0:T(8,128)S(1)}) custom-call(s32[2]{0:T(128)S(1)} %pad_add_fusion.place, s32[1,1,16]{2,1,0:T(1,128)S(1)} %get-tuple-element.50.arow, s32[1,1,16]{2,1,0:T(1,128)S(1)} %get-tuple-element.51.bcol, s32[1,1]{1,0:T(1,128)S(6)} %copy.16.count, f32[1,128]{1,0:T(1,128)S(1)} %get-tuple-element.52.d_ref, ...), custom_call_target="tpu_custom_call" | custom-call | flops 50331648 | bytes 1048576 | tf_op jit(solution)/shard_map/column_terms/column_terms/pallas_call | solution.py:274
  15.6 0.7 %collective-permute-done.4.after.far = f32[4,16,128]{2,1,0:T(8,128)S(1)} collective-permute-done((f32[4,16,128]{2,1,0:T(8,128)S(1)}, f32[4,16,128]{2,1,0:T(8,128)S(1)}, u32[]{:S(2)}, u32[]{:S(2)}) %collective-permute-start.4) | collective-permute-done | bytes 32800 | tf_op jit(solution)/shard_map/share_vectors/ppermute | solution.py:29
  16.4 0.0 collective-permute-start.5
  16.4 1.2 %row_terms.1 = (f32[2,16,128]{2,1,0:T(8,128)S(1)}, f32[2,16,128]{2,1,0:T(8,128)S(1)}) custom-call(s32[2]{0:T(128)S(1)} %pad_add_fusion.place, s32[1,1,16]{2,1,0:T(1,128)S(1)} %get-tuple-element.50.arow, s32[1,1,16]{2,1,0:T(1,128)S(1)} %get-tuple-element.51.bcol, s32[1,1]{1,0:T(1,128)S(6)} %copy.16.count, f32[4,16,128]{2,1,0:T(8,128)S(1)} %join_row.3.near, ...), custom_call_target="tpu_custom_call" | custom-call | flops 50331648 | bytes 1048576 | tf_op jit(solution)/shard_map/row_terms/row_terms/pallas_call | solution.py:296
  17.6 1.6 %collective-permute-start.8 = (f32[2,16,128]{2,1,0:T(8,128)S(1)}, f32[2,16,128]{2,1,0:T(8,128)S(1)}, u32[]{:S(2)}, u32[]{:S(2)}) collective-permute-start(f32[2,16,128]{2,1,0:T(8,128)S(1)} %get-tuple-element.63), channel_id=1, source_target_pairs={{0,1},{1,0},{2,3},{3,2},{4,5},{5,4},{6,7},{7,6},{8,9},{9,8},{10,11... | collective-permute-start | bytes 49160 | tf_op jit(solution)/shard_map/return_products/ppermute | solution.py:29
  19.2 0.0 collective-permute-done.5.other
  19.2 0.6 %collective-permute-start.6 = (f32[2,16,128]{2,1,0:T(8,128)S(1)}, f32[2,16,128]{2,1,0:T(8,128)S(1)}, u32[]{:S(2)}, u32[]{:S(2)}) collective-permute-start(f32[2,16,128]{2,1,0:T(8,128)S(1)} %get-tuple-element.59), channel_id=1, source_target_pairs={{0,8},{4,12},{8,0},{12,4},{16,24},{20,28},{24,16},{28,20},{1,9},{5... | collective-permute-start | bytes 49160 | tf_op jit(solution)/shard_map/return_products/ppermute | solution.py:29
  19.8 1.6 %collective-permute-done.8.other = f32[2,16,128]{2,1,0:T(8,128)S(1)} collective-permute-done((f32[2,16,128]{2,1,0:T(8,128)S(1)}, f32[2,16,128]{2,1,0:T(8,128)S(1)}, u32[]{:S(2)}, u32[]{:S(2)}) %collective-permute-start.8) | collective-permute-done | bytes 16416 | tf_op jit(solution)/shard_map/return_products/ppermute | solution.py:29
  21.4 1.8 %collective-permute-start.9 = (f32[1,16,128]{2,1,0:T(8,128)S(1)}, f32[1,16,128]{2,1,0:T(8,128)S(1)}, u32[]{:S(2)}, u32[]{:S(2)}) collective-permute-start(f32[1,16,128]{2,1,0:T(8,128)S(1)} %get-tuple-element.65), channel_id=1, source_target_pairs={{0,2},{1,3},{2,0},{3,1},{4,6},{5,7},{6,4},{7,5},{8,10},{9,11},{10,... | collective-permute-start | bytes 24584 | tf_op jit(solution)/shard_map/return_products/ppermute | solution.py:29
  23.1 0.0 collective-permute-done.6.other
  23.1 1.6 %collective-permute-start.7 = (f32[1,16,128]{2,1,0:T(8,128)S(1)}, f32[1,16,128]{2,1,0:T(8,128)S(1)}, u32[]{:S(2)}, u32[]{:S(2)}) collective-permute-start(f32[1,16,128]{2,1,0:T(8,128)S(1)} %get-tuple-element.61), channel_id=1, source_target_pairs={{0,16},{4,20},{8,24},{12,28},{16,0},{20,4},{24,8},{28,12},{1,17},{... | collective-permute-start | bytes 24584 | tf_op jit(solution)/shard_map/return_products/ppermute | solution.py:29
  24.7 1.2 %collective-permute-done.9.refs_3_ = f32[1,16,128]{2,1,0:T(8,128)S(1)} collective-permute-done((f32[1,16,128]{2,1,0:T(8,128)S(1)}, f32[1,16,128]{2,1,0:T(8,128)S(1)}, u32[]{:S(2)}, u32[]{:S(2)}) %collective-permute-start.9) | collective-permute-done | bytes 8224 | tf_op jit(solution)/shard_map/return_products/ppermute | solution.py:29
  25.9 0.9 %collective-permute-done.7.refs_1_ = f32[1,16,128]{2,1,0:T(8,128)S(1)} collective-permute-done((f32[1,16,128]{2,1,0:T(8,128)S(1)}, f32[1,16,128]{2,1,0:T(8,128)S(1)}, u32[]{:S(2)}, u32[]{:S(2)}) %collective-permute-start.7) | collective-permute-done | bytes 8224 | tf_op jit(solution)/shard_map/return_products/ppermute | solution.py:29
  26.9 0.3 product.1
  27.2 11.3 %all_to_all.9.parts = f32[32,3,2,128]{3,2,1,0:T(2,128)S(1)} all-to-all(f32[32,3,2,128]{3,2,1,0:T(2,128)S(1)} %get-tuple-element.67), channel_id=1, replica_groups=mesh['row'=8,'col'=4] {'row','col'}, dimensions={0} | all-to-all | bytes 196608 | tf_op jit(solution)/shard_map/product/all_to_all | solution.py:24
  38.5 1.2 %results.1 = (f32[16,128]{1,0:T(8,128)}, f32[16,16]{1,0:T(8,128)}, f32[16,16]{1,0:T(8,128)}, s32[1,1]{1,0:T(1,128)}) custom-call(f32[16,128]{1,0:T(8,128)S(1)} %copy-done.4, f32[16,128]{1,0:T(8,128)S(1)} %get-tuple-element.91.product, f32[32,3,2,128]{3,2,1,0:T(2,128)S(1)} %all_to_all.9.parts), custom_call_target="tpu_custom_call" | custom-call | tf_op jit(solution)/shard_map/results/results/pallas_call | solution.py:322
  39.7 0.7 %while.9 = (s32[]{:T(128)}, f32[16,16]{1,0:T(8,128)}, f32[16,128]{1,0:T(8,128)S(1)}, f32[16,128]{1,0:T(8,128)S(1)}, f32[32,3,2,128]{3,2,1,0:T(2,128)S(1)}) while((s32[]{:T(128)}, f32[16,16]{1,0:T(8,128)}, f32[16,128]{1,0:T(8,128)S(1)}, f32[16,128]{1,0:T(8,128)S(1)}, f32[32,3,2,128]{3,2,1,0:T(2,128)S(1)}) %tuple.20), condition=%region_1.0_spmd, body=%region_0.0_spmd | while | flops 1 | bytes 98393 | solution.py:351
  (7 shorter events, 0.0 us)
Async XLA Ops:
  0.6 0.7 %copy-start.1 = (s32[1,1,16]{2,1,0:T(1,128)S(1)}, s32[1,1,16]{2,1,0:T(1,128)}, u32[]{:S(2)}) copy-start(s32[1,1,16]{2,1,0:T(1,128)} %refs_0_.1) | copy-start | bytes 196
  0.6 0.7 %copy-start.2 = (s32[1,1,16]{2,1,0:T(1,128)S(1)}, s32[1,1,16]{2,1,0:T(1,128)}, u32[]{:S(2)}) copy-start(s32[1,1,16]{2,1,0:T(1,128)} %refs_1_.1) | copy-start | bytes 196
  0.7 0.7 %copy-start.3 = (f32[128]{0:T(128)S(1)}, f32[128]{0:T(128)}, u32[]{:S(2)}) copy-start(f32[128]{0:T(128)} %param.9) | copy-start | bytes 1540
  0.7 2.1 %collective-permute-start.2 = (f32[1,16,128]{2,1,0:T(8,128)}, f32[1,16,128]{2,1,0:T(8,128)S(1)}, u32[]{:S(2)}, u32[]{:S(2)}) collective-permute-start(f32[1,16,128]{2,1,0:T(8,128)} %bitcast.6), channel_id=1, source_target_pairs={{0,4},{4,0},{8,12},{12,8},{16,20},{20,16},{24,28},{28,24},{1,5},{5... | collective-permute-start | bytes 24584 | tf_op jit(solution)/shard_map/share_vectors/ppermute | solution.py:29
  1.3 1.2 %copy-start = (f32[1,1,16,128,128]{4,3,2,1,0:T(8,128)S(1)}, f32[1,1,16,128,128]{4,3,2,1,0:T(8,128)}, u32[]{:S(2)}) copy-start(f32[1,1,16,128,128]{4,3,2,1,0:T(8,128)} %tiles.1) | copy-start | bytes 3145732
  2.5 0.7 %copy-start.4 = (f32[16,128]{1,0:T(8,128)S(1)}, f32[16,128]{1,0:T(8,128)}, u32[]{:S(2)}) copy-start(f32[16,128]{1,0:T(8,128)} %x_ref.3) | copy-start | bytes 24580
  3.2 9.2 %collective-permute-start.3 = (f32[2,16,128]{2,1,0:T(8,128)S(1)}, f32[2,16,128]{2,1,0:T(8,128)S(1)}, u32[]{:S(2)}, u32[]{:S(2)}) collective-permute-start(f32[2,16,128]{2,1,0:T(8,128)S(1)} %join_row.2.mine), channel_id=1, source_target_pairs={{0,8},{4,12},{8,0},{12,4},{16,24},{20,28},{24,16},{28,20},{1,9},{5... | collective-permute-start | bytes 49160 | tf_op jit(solution)/shard_map/share_vectors/ppermute | solution.py:29
  6.2 3.7 %collective-permute-start = (f32[1,16,128]{2,1,0:T(8,128)S(1)}, f32[1,16,128]{2,1,0:T(8,128)S(1)}, u32[]{:S(2)}, u32[]{:S(2)}) collective-permute-start(f32[1,16,128]{2,1,0:T(8,128)S(1)} %bitcast.8), channel_id=1, source_target_pairs={{0,1},{1,0},{2,3},{3,2},{4,5},{5,4},{6,7},{7,6},{8,9},{9,8},{10,11... | collective-permute-start | bytes 24584 | tf_op jit(solution)/shard_map/share_vectors/ppermute | solution.py:29
  9.8 4.8 %collective-permute-start.1 = (f32[2,16,128]{2,1,0:T(8,128)S(1)}, f32[2,16,128]{2,1,0:T(8,128)S(1)}, u32[]{:S(2)}, u32[]{:S(2)}) collective-permute-start(f32[2,16,128]{2,1,0:T(8,128)S(1)} %join_col.1.near), channel_id=1, source_target_pairs={{0,2},{1,3},{2,0},{3,1},{4,6},{5,7},{6,4},{7,5},{8,10},{9,11},{10,... | collective-permute-start | bytes 49160 | tf_op jit(solution)/shard_map/share_vectors/ppermute | solution.py:29
  12.4 3.9 %collective-permute-start.4 = (f32[4,16,128]{2,1,0:T(8,128)S(1)}, f32[4,16,128]{2,1,0:T(8,128)S(1)}, u32[]{:S(2)}, u32[]{:S(2)}) collective-permute-start(f32[4,16,128]{2,1,0:T(8,128)S(1)} %join_row.3.near), channel_id=1, source_target_pairs={{0,16},{4,20},{8,24},{12,28},{16,0},{20,4},{24,8},{28,12},{1,17},{... | collective-permute-start | bytes 98312 | tf_op jit(solution)/shard_map/share_vectors/ppermute | solution.py:29
  16.4 2.9 %collective-permute-start.5 = (f32[4,16,128]{2,1,0:T(8,128)S(1)}, f32[4,16,128]{2,1,0:T(8,128)S(1)}, u32[]{:S(2)}, u32[]{:S(2)}) collective-permute-start(f32[4,16,128]{2,1,0:T(8,128)S(1)} %hand_on.1), channel_id=1, source_target_pairs={{0,4},{4,0},{8,12},{12,8},{16,20},{20,16},{24,28},{28,24},{1,5},{5... | collective-permute-start | bytes 98312 | tf_op jit(solution)/shard_map/return_products/ppermute | solution.py:29
  17.6 3.8 %collective-permute-start.8 = (f32[2,16,128]{2,1,0:T(8,128)S(1)}, f32[2,16,128]{2,1,0:T(8,128)S(1)}, u32[]{:S(2)}, u32[]{:S(2)}) collective-permute-start(f32[2,16,128]{2,1,0:T(8,128)S(1)} %get-tuple-element.63), channel_id=1, source_target_pairs={{0,1},{1,0},{2,3},{3,2},{4,5},{5,4},{6,7},{7,6},{8,9},{9,8},{10,11... | collective-permute-start | bytes 49160 | tf_op jit(solution)/shard_map/return_products/ppermute | solution.py:29
  19.2 3.9 %collective-permute-start.6 = (f32[2,16,128]{2,1,0:T(8,128)S(1)}, f32[2,16,128]{2,1,0:T(8,128)S(1)}, u32[]{:S(2)}, u32[]{:S(2)}) collective-permute-start(f32[2,16,128]{2,1,0:T(8,128)S(1)} %get-tuple-element.59), channel_id=1, source_target_pairs={{0,8},{4,12},{8,0},{12,4},{16,24},{20,28},{24,16},{28,20},{1,9},{5... | collective-permute-start | bytes 49160 | tf_op jit(solution)/shard_map/return_products/ppermute | solution.py:29
  21.4 4.5 %collective-permute-start.9 = (f32[1,16,128]{2,1,0:T(8,128)S(1)}, f32[1,16,128]{2,1,0:T(8,128)S(1)}, u32[]{:S(2)}, u32[]{:S(2)}) collective-permute-start(f32[1,16,128]{2,1,0:T(8,128)S(1)} %get-tuple-element.65), channel_id=1, source_target_pairs={{0,2},{1,3},{2,0},{3,1},{4,6},{5,7},{6,4},{7,5},{8,10},{9,11},{10,... | collective-permute-start | bytes 24584 | tf_op jit(solution)/shard_map/return_products/ppermute | solution.py:29
  23.1 3.7 %collective-permute-start.7 = (f32[1,16,128]{2,1,0:T(8,128)S(1)}, f32[1,16,128]{2,1,0:T(8,128)S(1)}, u32[]{:S(2)}, u32[]{:S(2)}) collective-permute-start(f32[1,16,128]{2,1,0:T(8,128)S(1)} %get-tuple-element.61), channel_id=1, source_target_pairs={{0,16},{4,20},{8,24},{12,28},{16,0},{20,4},{24,8},{28,12},{1,17},{... | collective-permute-start | bytes 24584 | tf_op jit(solution)/shard_map/return_products/ppermute | solution.py:29

commit v20 on v16

--- a/solution.py
+++ b/solution.py
@@ -141,9 +141,9 @@
 def row_kernel(n_row, n_col, slots, place, arow, bcol, count, near, far, *refs):
     *parts, send, keep, cols, sums = refs
     me_row, me_col = place[0], place[1]
-    half = n_row // 2
-    for flip in range(n_row):
-        cols[flip] = stack_split(near[flip] if flip < half else far[flip - half])
+    for pair in range(n_row // 2):
+        cols[2 * pair] = stack_split(near[pair])
+        cols[2 * pair + 1] = stack_split(far[pair])
     sums[...] = jnp.zeros_like(sums)
     for pair in range(0, slots, 2):
         pieces = [[part[slot] for part in parts] for slot in (pair, pair + 1)]
@@ -224,23 +224,24 @@
     def blocks(total):
         return jax.ShapeDtypeStruct((total, nvec, width), jnp.float32)
 
-    def gather(axes, after):
+    def gather(after, **flips):
+        axes = list(flips)
         near = [vectors[None]] * len(axes)
-        far = [trade(vectors[None], axis, 1) for axis in axes]
-        reach = 2
-        while any(reach < lax.axis_size(axis) for axis in axes):
-            going = [which for which, axis in enumerate(axes) if reach < lax.axis_size(axis)]
+        far = [trade(vectors[None], axis, flips[axis][0]) for axis in axes]
+        step = 1
+        while any(step < len(flips[axis]) for axis in axes):
+            going = [which for which, axis in enumerate(axes) if step < len(flips[axis])]
             joined = pl.pallas_call(
                 functools.partial(join_kernel, len(going)),
-                out_shape=[blocks(reach)] * len(going),
+                out_shape=[blocks(2**step)] * len(going),
                 in_specs=[VMEM] * (2 * len(going)) + [pl.BlockSpec(memory_space=pl.ANY)] * len(after),
                 out_specs=[VMEM] * len(going),
                 compiler_params=params,
                 name="join",
             )(*[half for which in going for half in (near[which], far[which])], *after)
             for which, half in zip(going, joined):
-                near[which], far[which] = half, trade(half, axes[which], reach)
-            reach *= 2
+                near[which], far[which] = half, trade(half, axes[which], flips[axes[which]][step])
+            step += 1
             after = ()
         return list(zip(near, far))
 
@@ -271,7 +272,8 @@
             name="prepare",
         )(tiles, *small)
     with jax.named_scope("share_vectors"):
-        x_row, x_col = gather(("row", "col"), parts[:1])
+        bits = [1 << bit for bit in range(n_row.bit_length() - 1)]
+        x_row, x_col = gather(parts[:1], row=bits[1:] + bits[:1], col=[1 << bit for bit in range(n_col.bit_length() - 1)])
     with jax.named_scope("column_terms"):
         col_send, col_keep = pl.pallas_call(
             functools.partial(column_kernel, n_row, n_col, slots),

time: 39.5 us -> 38.6 us (0.977)
  waiting for transfers between devices: 4.21 us -> 6.87 us
  blocking collectives: 11.8 us -> 10 us
  starting transfers between devices: 15.8 us -> 14.2 us
    ppermute x10, waiting for transfers between devices: 4.21 us -> 6.87 us  [trade(): return lax.ppermute(value, axis, [(p, p ^ flip) for p in range(size)])]
    all_to_all x1, blocking collectives: 11.8 us -> 10 us  [swap(): return lax.all_to_all(blocks, axis, 0, 0, tiled=True)]
    ppermute x10, starting transfers between devices: 15.8 us -> 14.2 us  [trade(): return lax.ppermute(value, axis, [(p, p ^ flip) for p in range(size)])]
where the time goes in v20:
time: 38.6 us; the launch traced here: 38.4 us
  starting transfers between devices  14.2 us (37%)
  blocking collectives  10 us (26%)
  waiting for transfers between devices  6.87 us (18%)
  Pallas kernels  3.94 us (10%)
  between operations  1.38 us (4%)
  local copies, waits for them, and re-layouts  1.24 us (3%)
  loops' own time  0.69 us (2%)
    ppermute x10, starting transfers between devices, trade(): return lax.ppermute(value, axis, [(p, p ^ flip) for p in range(size)])  14.2 us
    all_to_all x1, blocking collectives, swap(): return lax.all_to_all(blocks, axis, 0, 0, tiled=True)  10 us
    ppermute x10, waiting for transfers between devices, trade(): return lax.ppermute(value, axis, [(p, p ^ flip) for p in range(size)])  6.87 us
    unnamed x10, local copies, waits for them, and re-layouts  1.24 us
    pallas_call x1, Pallas kernels, per_device(): pl.pallas_call(functools.partial(result_kernel, scale), out_shape=[block,...  1.24 us
    pallas_call x1, Pallas kernels, per_device(): pl.pallas_call(functools.partial(row_kernel, n_row, n_col, slots), out_sh...  1.21 us
    pallas_call x1, Pallas kernels, per_device(): pl.pallas_call(functools.partial(column_kernel, n_row, n_col, slots), out...  0.93 us
  transfers between devices with their start and end apart: 10, of which 5 were waited for; matrix products, arithmetic and copies ran while one was open for 0% of the time, Pallas kernels for 6%

profile of v20, /device:TPU:0, one launch (start us, length us, event | category | flops | bytes accessed | tf_op | source)
XLA Modules:
  0.0 38.4 jit_solution(14394959015513828635)
XLA Ops:
  0.6 0.0 copy-start.1
  0.6 0.0 copy-start.2
  0.7 0.0 copy-start.3
  0.7 3.0 %collective-permute-start = (f32[1,16,128]{2,1,0:T(8,128)}, f32[1,16,128]{2,1,0:T(8,128)S(1)}, u32[]{:S(2)}, u32[]{:S(2)}) collective-permute-start(f32[1,16,128]{2,1,0:T(8,128)} %bitcast.6), channel_id=1, source_target_pairs={{0,8},{4,12},{8,0},{12,4},{16,24},{20,28},{24,16},{28,20},{1,9},{5... | collective-permute-start | bytes 24584 | tf_op jit(solution)/shard_map/share_vectors/ppermute | solution.py:29
  3.7 1.6 %collective-permute-start.1 = (f32[1,16,128]{2,1,0:T(8,128)}, f32[1,16,128]{2,1,0:T(8,128)S(1)}, u32[]{:S(2)}, u32[]{:S(2)}) collective-permute-start(f32[1,16,128]{2,1,0:T(8,128)} %bitcast.7), channel_id=1, source_target_pairs={{0,1},{1,0},{2,3},{3,2},{4,5},{5,4},{6,7},{7,6},{8,9},{9,8},{10,11... | collective-permute-start | bytes 24584 | tf_op jit(solution)/shard_map/share_vectors/ppermute | solution.py:29
  5.2 0.0 copy-done.1
  5.2 0.0 copy-done.2
  5.2 0.0 copy-done.3
  5.2 0.0 copy-start
  5.3 1.2 %copy-done = f32[1,1,16,128,128]{4,3,2,1,0:T(8,128)S(1)} copy-done((f32[1,1,16,128,128]{4,3,2,1,0:T(8,128)S(1)}, f32[1,1,16,128,128]{4,3,2,1,0:T(8,128)}, u32[]{:S(2)}) %copy-start) | copy-done | bytes 1048600
  6.5 0.0 copy-start.4
  6.5 0.2 prepare.1
  6.7 0.0 collective-permute-done.refs_1_
  6.7 0.8 %collective-permute-done.1.refs_3_ = f32[1,16,128]{2,1,0:T(8,128)S(1)} collective-permute-done((f32[1,16,128]{2,1,0:T(8,128)}, f32[1,16,128]{2,1,0:T(8,128)S(1)}, u32[]{:S(2)}, u32[]{:S(2)}) %collective-permute-start.1) | collective-permute-done | bytes 8224 | tf_op jit(solution)/shard_map/share_vectors/ppermute | solution.py:29
  7.5 0.0 copy-done.4
  7.5 1.5 %collective-permute-start.3 = (f32[2,16,128]{2,1,0:T(8,128)S(1)}, f32[2,16,128]{2,1,0:T(8,128)S(1)}, u32[]{:S(2)}, u32[]{:S(2)}) collective-permute-start(f32[2,16,128]{2,1,0:T(8,128)S(1)} %get-tuple-element.61.refs_0_), channel_id=1, source_target_pairs={{0,16},{4,20},{8,24},{12,28},{16,0},{20,4},{24,8},{28,12},{1,17},{... | collective-permute-start | bytes 49160 | tf_op jit(solution)/shard_map/share_vectors/ppermute | solution.py:29
  9.1 2.6 %collective-permute-start.2 = (f32[2,16,128]{2,1,0:T(8,128)S(1)}, f32[2,16,128]{2,1,0:T(8,128)S(1)}, u32[]{:S(2)}, u32[]{:S(2)}) collective-permute-start(f32[2,16,128]{2,1,0:T(8,128)S(1)} %get-tuple-element.56.near), channel_id=1, source_target_pairs={{0,2},{1,3},{2,0},{3,1},{4,6},{5,7},{6,4},{7,5},{8,10},{9,11},{10,... | collective-permute-start | bytes 49160 | tf_op jit(solution)/shard_map/share_vectors/ppermute | solution.py:29
  11.6 0.0 collective-permute-done.3.refs_1_
  11.7 0.0 collective-permute-start.4
  11.7 0.1 pad_add_fusion.place
  12.4 1.3 %collective-permute-done.2.far = f32[2,16,128]{2,1,0:T(8,128)S(1)} collective-permute-done((f32[2,16,128]{2,1,0:T(8,128)S(1)}, f32[2,16,128]{2,1,0:T(8,128)S(1)}, u32[]{:S(2)}, u32[]{:S(2)}) %collective-permute-start.2) | collective-permute-done | bytes 16416 | tf_op jit(solution)/shard_map/share_vectors/ppermute | solution.py:29
  13.7 0.9 %column_terms.1 = (f32[4,16,128]{2,1,0:T(8,128)S(1)}, f32[4,16,128]{2,1,0:T(8,128)S(1)}) custom-call(s32[2]{0:T(128)S(1)} %pad_add_fusion.place, s32[1,1,16]{2,1,0:T(1,128)S(1)} %get-tuple-element.52.arow, s32[1,1,16]{2,1,0:T(1,128)S(1)} %get-tuple-element.53.bcol, s32[1,1]{1,0:T(1,128)S(6)} %copy.16.count, f32[1,128]{1,0:T(1,128)S(1)} %get-tuple-element.54.d_ref, ...), custom_call_target="tpu_custom_call" | custom-call | flops 50331648 | bytes 1048576 | tf_op jit(solution)/shard_map/column_terms/column_terms/pallas_call | solution.py:278
  14.6 0.0 collective-permute-done.4.after.far
  14.6 0.1 collective-permute-start.5
  14.7 1.2 %row_terms.1 = (f32[2,16,128]{2,1,0:T(8,128)S(1)}, f32[2,16,128]{2,1,0:T(8,128)S(1)}) custom-call(s32[2]{0:T(128)S(1)} %pad_add_fusion.place, s32[1,1,16]{2,1,0:T(1,128)S(1)} %get-tuple-element.52.arow, s32[1,1,16]{2,1,0:T(1,128)S(1)} %get-tuple-element.53.bcol, s32[1,1]{1,0:T(1,128)S(6)} %copy.16.count, f32[4,16,128]{2,1,0:T(8,128)S(1)} %join.3.near, ...), custom_call_target="tpu_custom_call" | custom-call | flops 50331648 | bytes 1048576 | tf_op jit(solution)/shard_map/row_terms/row_terms/pallas_call | solution.py:300
  15.9 1.6 %collective-permute-start.8 = (f32[2,16,128]{2,1,0:T(8,128)S(1)}, f32[2,16,128]{2,1,0:T(8,128)S(1)}, u32[]{:S(2)}, u32[]{:S(2)}) collective-permute-start(f32[2,16,128]{2,1,0:T(8,128)S(1)} %get-tuple-element.67), channel_id=1, source_target_pairs={{0,1},{1,0},{2,3},{3,2},{4,5},{5,4},{6,7},{7,6},{8,9},{9,8},{10,11... | collective-permute-start | bytes 49160 | tf_op jit(solution)/shard_map/return_products/ppermute | solution.py:29
  17.6 0.0 collective-permute-done.5.other
  17.6 0.6 %collective-permute-start.6 = (f32[2,16,128]{2,1,0:T(8,128)S(1)}, f32[2,16,128]{2,1,0:T(8,128)S(1)}, u32[]{:S(2)}, u32[]{:S(2)}) collective-permute-start(f32[2,16,128]{2,1,0:T(8,128)S(1)} %get-tuple-element.63), channel_id=1, source_target_pairs={{0,8},{4,12},{8,0},{12,4},{16,24},{20,28},{24,16},{28,20},{1,9},{5... | collective-permute-start | bytes 49160 | tf_op jit(solution)/shard_map/return_products/ppermute | solution.py:29
  18.2 1.6 %collective-permute-done.8.other = f32[2,16,128]{2,1,0:T(8,128)S(1)} collective-permute-done((f32[2,16,128]{2,1,0:T(8,128)S(1)}, f32[2,16,128]{2,1,0:T(8,128)S(1)}, u32[]{:S(2)}, u32[]{:S(2)}) %collective-permute-start.8) | collective-permute-done | bytes 16416 | tf_op jit(solution)/shard_map/return_products/ppermute | solution.py:29
  19.7 2.6 %collective-permute-start.9 = (f32[1,16,128]{2,1,0:T(8,128)S(1)}, f32[1,16,128]{2,1,0:T(8,128)S(1)}, u32[]{:S(2)}, u32[]{:S(2)}) collective-permute-start(f32[1,16,128]{2,1,0:T(8,128)S(1)} %get-tuple-element.69), channel_id=1, source_target_pairs={{0,2},{1,3},{2,0},{3,1},{4,6},{5,7},{6,4},{7,5},{8,10},{9,11},{10,... | collective-permute-start | bytes 24584 | tf_op jit(solution)/shard_map/return_products/ppermute | solution.py:29
  22.4 0.0 collective-permute-done.6.other
  22.4 0.6 %collective-permute-start.7 = (f32[1,16,128]{2,1,0:T(8,128)S(1)}, f32[1,16,128]{2,1,0:T(8,128)S(1)}, u32[]{:S(2)}, u32[]{:S(2)}) collective-permute-start(f32[1,16,128]{2,1,0:T(8,128)S(1)} %get-tuple-element.65), channel_id=1, source_target_pairs={{0,16},{4,20},{8,24},{12,28},{16,0},{20,4},{24,8},{28,12},{1,17},{... | collective-permute-start | bytes 24584 | tf_op jit(solution)/shard_map/return_products/ppermute | solution.py:29
  22.9 1.4 %collective-permute-done.9.refs_3_ = f32[1,16,128]{2,1,0:T(8,128)S(1)} collective-permute-done((f32[1,16,128]{2,1,0:T(8,128)S(1)}, f32[1,16,128]{2,1,0:T(8,128)S(1)}, u32[]{:S(2)}, u32[]{:S(2)}) %collective-permute-start.9) | collective-permute-done | bytes 8224 | tf_op jit(solution)/shard_map/return_products/ppermute | solution.py:29
  24.3 1.8 %collective-permute-done.7.refs_1_ = f32[1,16,128]{2,1,0:T(8,128)S(1)} collective-permute-done((f32[1,16,128]{2,1,0:T(8,128)S(1)}, f32[1,16,128]{2,1,0:T(8,128)S(1)}, u32[]{:S(2)}, u32[]{:S(2)}) %collective-permute-start.7) | collective-permute-done | bytes 8224 | tf_op jit(solution)/shard_map/return_products/ppermute | solution.py:29
  26.1 0.3 product.1
  26.4 10.0 %all_to_all.9.parts = f32[32,3,2,128]{3,2,1,0:T(2,128)S(1)} all-to-all(f32[32,3,2,128]{3,2,1,0:T(2,128)S(1)} %get-tuple-element.71), channel_id=1, replica_groups=mesh['row'=8,'col'=4] {'row','col'}, dimensions={0} | all-to-all | bytes 196608 | tf_op jit(solution)/shard_map/product/all_to_all | solution.py:24
  36.4 1.2 %results.1 = (f32[16,128]{1,0:T(8,128)}, f32[16,16]{1,0:T(8,128)}, f32[16,16]{1,0:T(8,128)}, s32[1,1]{1,0:T(1,128)}) custom-call(f32[16,128]{1,0:T(8,128)S(1)} %copy-done.4, f32[16,128]{1,0:T(8,128)S(1)} %get-tuple-element.95.product, f32[32,3,2,128]{3,2,1,0:T(2,128)S(1)} %all_to_all.9.parts), custom_call_target="tpu_custom_call" | custom-call | tf_op jit(solution)/shard_map/results/results/pallas_call | solution.py:326
  37.7 0.7 %while.9 = (s32[]{:T(128)}, f32[16,16]{1,0:T(8,128)}, f32[16,128]{1,0:T(8,128)S(1)}, f32[16,128]{1,0:T(8,128)S(1)}, f32[32,3,2,128]{3,2,1,0:T(2,128)S(1)}) while((s32[]{:T(128)}, f32[16,16]{1,0:T(8,128)}, f32[16,128]{1,0:T(8,128)S(1)}, f32[16,128]{1,0:T(8,128)S(1)}, f32[32,3,2,128]{3,2,1,0:T(2,128)S(1)}) %tuple.20), condition=%region_1.0_spmd, body=%region_0.0_spmd | while | flops 1 | bytes 98393 | solution.py:355
  (6 shorter events, 0.0 us)
Async XLA Ops:
  0.6 4.6 %copy-start.1 = (s32[1,1,16]{2,1,0:T(1,128)S(1)}, s32[1,1,16]{2,1,0:T(1,128)}, u32[]{:S(2)}) copy-start(s32[1,1,16]{2,1,0:T(1,128)} %refs_0_.1) | copy-start | bytes 196
  0.6 4.6 %copy-start.2 = (s32[1,1,16]{2,1,0:T(1,128)S(1)}, s32[1,1,16]{2,1,0:T(1,128)}, u32[]{:S(2)}) copy-start(s32[1,1,16]{2,1,0:T(1,128)} %refs_1_.1) | copy-start | bytes 196
  0.7 4.6 %copy-start.3 = (f32[128]{0:T(128)S(1)}, f32[128]{0:T(128)}, u32[]{:S(2)}) copy-start(f32[128]{0:T(128)} %param.9) | copy-start | bytes 1540
  0.7 6.0 %collective-permute-start = (f32[1,16,128]{2,1,0:T(8,128)}, f32[1,16,128]{2,1,0:T(8,128)S(1)}, u32[]{:S(2)}, u32[]{:S(2)}) collective-permute-start(f32[1,16,128]{2,1,0:T(8,128)} %bitcast.6), channel_id=1, source_target_pairs={{0,8},{4,12},{8,0},{12,4},{16,24},{20,28},{24,16},{28,20},{1,9},{5... | collective-permute-start | bytes 24584 | tf_op jit(solution)/shard_map/share_vectors/ppermute | solution.py:29
  3.7 3.9 %collective-permute-start.1 = (f32[1,16,128]{2,1,0:T(8,128)}, f32[1,16,128]{2,1,0:T(8,128)S(1)}, u32[]{:S(2)}, u32[]{:S(2)}) collective-permute-start(f32[1,16,128]{2,1,0:T(8,128)} %bitcast.7), channel_id=1, source_target_pairs={{0,1},{1,0},{2,3},{3,2},{4,5},{5,4},{6,7},{7,6},{8,9},{9,8},{10,11... | collective-permute-start | bytes 24584 | tf_op jit(solution)/shard_map/share_vectors/ppermute | solution.py:29
  5.2 1.2 %copy-start = (f32[1,1,16,128,128]{4,3,2,1,0:T(8,128)S(1)}, f32[1,1,16,128,128]{4,3,2,1,0:T(8,128)}, u32[]{:S(2)}) copy-start(f32[1,1,16,128,128]{4,3,2,1,0:T(8,128)} %tiles.1) | copy-start | bytes 3145732
  6.5 1.1 %copy-start.4 = (f32[16,128]{1,0:T(8,128)S(1)}, f32[16,128]{1,0:T(8,128)}, u32[]{:S(2)}) copy-start(f32[16,128]{1,0:T(8,128)} %x_ref.3) | copy-start | bytes 24580
  7.5 4.1 %collective-permute-start.3 = (f32[2,16,128]{2,1,0:T(8,128)S(1)}, f32[2,16,128]{2,1,0:T(8,128)S(1)}, u32[]{:S(2)}, u32[]{:S(2)}) collective-permute-start(f32[2,16,128]{2,1,0:T(8,128)S(1)} %get-tuple-element.61.refs_0_), channel_id=1, source_target_pairs={{0,16},{4,20},{8,24},{12,28},{16,0},{20,4},{24,8},{28,12},{1,17},{... | collective-permute-start | bytes 49160 | tf_op jit(solution)/shard_map/share_vectors/ppermute | solution.py:29
  9.1 4.6 %collective-permute-start.2 = (f32[2,16,128]{2,1,0:T(8,128)S(1)}, f32[2,16,128]{2,1,0:T(8,128)S(1)}, u32[]{:S(2)}, u32[]{:S(2)}) collective-permute-start(f32[2,16,128]{2,1,0:T(8,128)S(1)} %get-tuple-element.56.near), channel_id=1, source_target_pairs={{0,2},{1,3},{2,0},{3,1},{4,6},{5,7},{6,4},{7,5},{8,10},{9,11},{10,... | collective-permute-start | bytes 49160 | tf_op jit(solution)/shard_map/share_vectors/ppermute | solution.py:29
  11.7 3.0 %collective-permute-start.4 = (f32[4,16,128]{2,1,0:T(8,128)S(1)}, f32[4,16,128]{2,1,0:T(8,128)S(1)}, u32[]{:S(2)}, u32[]{:S(2)}) collective-permute-start(f32[4,16,128]{2,1,0:T(8,128)S(1)} %join.3.near), channel_id=1, source_target_pairs={{0,4},{4,0},{8,12},{12,8},{16,20},{20,16},{24,28},{28,24},{1,5},{5... | collective-permute-start | bytes 98312 | tf_op jit(solution)/shard_map/share_vectors/ppermute | solution.py:29
  14.6 2.9 %collective-permute-start.5 = (f32[4,16,128]{2,1,0:T(8,128)S(1)}, f32[4,16,128]{2,1,0:T(8,128)S(1)}, u32[]{:S(2)}, u32[]{:S(2)}) collective-permute-start(f32[4,16,128]{2,1,0:T(8,128)S(1)} %hand_on.1), channel_id=1, source_target_pairs={{0,4},{4,0},{8,12},{12,8},{16,20},{20,16},{24,28},{28,24},{1,5},{5... | collective-permute-start | bytes 98312 | tf_op jit(solution)/shard_map/return_products/ppermute | solution.py:29
  15.9 3.8 %collective-permute-start.8 = (f32[2,16,128]{2,1,0:T(8,128)S(1)}, f32[2,16,128]{2,1,0:T(8,128)S(1)}, u32[]{:S(2)}, u32[]{:S(2)}) collective-permute-start(f32[2,16,128]{2,1,0:T(8,128)S(1)} %get-tuple-element.67), channel_id=1, source_target_pairs={{0,1},{1,0},{2,3},{3,2},{4,5},{5,4},{6,7},{7,6},{8,9},{9,8},{10,11... | collective-permute-start | bytes 49160 | tf_op jit(solution)/shard_map/return_products/ppermute | solution.py:29
  17.6 4.8 %collective-permute-start.6 = (f32[2,16,128]{2,1,0:T(8,128)S(1)}, f32[2,16,128]{2,1,0:T(8,128)S(1)}, u32[]{:S(2)}, u32[]{:S(2)}) collective-permute-start(f32[2,16,128]{2,1,0:T(8,128)S(1)} %get-tuple-element.63), channel_id=1, source_target_pairs={{0,8},{4,12},{8,0},{12,4},{16,24},{20,28},{24,16},{28,20},{1,9},{5... | collective-permute-start | bytes 49160 | tf_op jit(solution)/shard_map/return_products/ppermute | solution.py:29
  19.7 4.5 %collective-permute-start.9 = (f32[1,16,128]{2,1,0:T(8,128)S(1)}, f32[1,16,128]{2,1,0:T(8,128)S(1)}, u32[]{:S(2)}, u32[]{:S(2)}) collective-permute-start(f32[1,16,128]{2,1,0:T(8,128)S(1)} %get-tuple-element.69), channel_id=1, source_target_pairs={{0,2},{1,3},{2,0},{3,1},{4,6},{5,7},{6,4},{7,5},{8,10},{9,11},{10,... | collective-permute-start | bytes 24584 | tf_op jit(solution)/shard_map/return_products/ppermute | solution.py:29
  22.4 3.7 %collective-permute-start.7 = (f32[1,16,128]{2,1,0:T(8,128)S(1)}, f32[1,16,128]{2,1,0:T(8,128)S(1)}, u32[]{:S(2)}, u32[]{:S(2)}) collective-permute-start(f32[1,16,128]{2,1,0:T(8,128)S(1)} %get-tuple-element.65), channel_id=1, source_target_pairs={{0,16},{4,20},{8,24},{12,28},{16,0},{20,4},{24,8},{28,12},{1,17},{... | collective-permute-start | bytes 24584 | tf_op jit(solution)/shard_map/return_products/ppermute | solution.py:29

commit v21 on v20

--- a/solution.py
+++ b/solution.py
@@ -273,7 +273,7 @@
         )(tiles, *small)
     with jax.named_scope("share_vectors"):
         bits = [1 << bit for bit in range(n_row.bit_length() - 1)]
-        x_row, x_col = gather(parts[:1], row=bits[1:] + bits[:1], col=[1 << bit for bit in range(n_col.bit_length() - 1)])
+        x_col, x_row = gather(parts[:1], col=[1 << bit for bit in range(n_col.bit_length() - 1)], row=bits[1:] + bits[:1])
     with jax.named_scope("column_terms"):
         col_send, col_keep = pl.pallas_call(
             functools.partial(column_kernel, n_row, n_col, slots),

time: 38.6 us -> 39.1 us (1.013)
  blocking collectives: 10 us -> 10.5 us
    all_to_all x1, blocking collectives: 10 us -> 10.5 us  [swap(): return lax.all_to_all(blocks, axis, 0, 0, tiled=True)]
where the time goes in v21:
time: 39.1 us; the launch traced here: 38.9 us
  starting transfers between devices  13.9 us (36%)
  blocking collectives  10.5 us (27%)
  waiting for transfers between devices  7.24 us (19%)
  Pallas kernels  3.94 us (10%)
  between operations  1.38 us (4%)
  local copies, waits for them, and re-layouts  1.24 us (3%)
  loops' own time  0.69 us (2%)
    ppermute x10, starting transfers between devices, trade(): return lax.ppermute(value, axis, [(p, p ^ flip) for p in range(size)])  13.9 us
    all_to_all x1, blocking collectives, swap(): return lax.all_to_all(blocks, axis, 0, 0, tiled=True)  10.5 us
    ppermute x10, waiting for transfers between devices, trade(): return lax.ppermute(value, axis, [(p, p ^ flip) for p in range(size)])  7.24 us
    unnamed x10, local copies, waits for them, and re-layouts  1.24 us
    pallas_call x1, Pallas kernels, per_device(): pl.pallas_call(functools.partial(result_kernel, scale), out_shape=[block,...  1.24 us
    pallas_call x1, Pallas kernels, per_device(): pl.pallas_call(functools.partial(row_kernel, n_row, n_col, slots), out_sh...  1.21 us
    pallas_call x1, Pallas kernels, per_device(): pl.pallas_call(functools.partial(column_kernel, n_row, n_col, slots), out...  0.93 us
  transfers between devices with their start and end apart: 10, of which 5 were waited for; matrix products, arithmetic and copies ran while one was open for 0% of the time, Pallas kernels for 6%

profile of v21, /device:TPU:0, one launch (start us, length us, event | category | flops | bytes accessed | tf_op | source)
XLA Modules:
  0.0 38.9 jit_solution(4078336904862503065)
XLA Ops:
  0.6 0.0 copy-start.1
  0.6 0.0 copy-start.2
  0.7 0.0 copy-start.3
  0.7 3.1 %collective-permute-start = (f32[1,16,128]{2,1,0:T(8,128)}, f32[1,16,128]{2,1,0:T(8,128)S(1)}, u32[]{:S(2)}, u32[]{:S(2)}) collective-permute-start(f32[1,16,128]{2,1,0:T(8,128)} %bitcast.6), channel_id=1, source_target_pairs={{0,1},{1,0},{2,3},{3,2},{4,5},{5,4},{6,7},{7,6},{8,9},{9,8},{10,11... | collective-permute-start | bytes 24584 | tf_op jit(solution)/shard_map/share_vectors/ppermute | solution.py:29
  3.8 1.5 %collective-permute-start.1 = (f32[1,16,128]{2,1,0:T(8,128)}, f32[1,16,128]{2,1,0:T(8,128)S(1)}, u32[]{:S(2)}, u32[]{:S(2)}) collective-permute-start(f32[1,16,128]{2,1,0:T(8,128)} %bitcast.7), channel_id=1, source_target_pairs={{0,8},{4,12},{8,0},{12,4},{16,24},{20,28},{24,16},{28,20},{1,9},{5... | collective-permute-start | bytes 24584 | tf_op jit(solution)/shard_map/share_vectors/ppermute | solution.py:29
  5.2 0.0 copy-done.1
  5.2 0.0 copy-done.2
  5.2 0.0 copy-done.3
  5.2 0.0 copy-start
  5.3 1.2 %copy-done = f32[1,1,16,128,128]{4,3,2,1,0:T(8,128)S(1)} copy-done((f32[1,1,16,128,128]{4,3,2,1,0:T(8,128)S(1)}, f32[1,1,16,128,128]{4,3,2,1,0:T(8,128)}, u32[]{:S(2)}) %copy-start) | copy-done | bytes 1048600
  6.5 0.0 copy-start.4
  6.5 0.2 prepare.1
  6.7 0.0 collective-permute-done.refs_1_
  6.7 0.9 %collective-permute-done.1.refs_3_ = f32[1,16,128]{2,1,0:T(8,128)S(1)} collective-permute-done((f32[1,16,128]{2,1,0:T(8,128)}, f32[1,16,128]{2,1,0:T(8,128)S(1)}, u32[]{:S(2)}, u32[]{:S(2)}) %collective-permute-start.1) | collective-permute-done | bytes 8224 | tf_op jit(solution)/shard_map/share_vectors/ppermute | solution.py:29
  7.6 0.0 copy-done.4
  7.6 1.5 %collective-permute-start.3 = (f32[2,16,128]{2,1,0:T(8,128)S(1)}, f32[2,16,128]{2,1,0:T(8,128)S(1)}, u32[]{:S(2)}, u32[]{:S(2)}) collective-permute-start(f32[2,16,128]{2,1,0:T(8,128)S(1)} %get-tuple-element.61.refs_0_), channel_id=1, source_target_pairs={{0,16},{4,20},{8,24},{12,28},{16,0},{20,4},{24,8},{28,12},{1,17},{... | collective-permute-start | bytes 49160 | tf_op jit(solution)/shard_map/share_vectors/ppermute | solution.py:29
  9.1 2.6 %collective-permute-start.2 = (f32[2,16,128]{2,1,0:T(8,128)S(1)}, f32[2,16,128]{2,1,0:T(8,128)S(1)}, u32[]{:S(2)}, u32[]{:S(2)}) collective-permute-start(f32[2,16,128]{2,1,0:T(8,128)S(1)} %get-tuple-element.56.near), channel_id=1, source_target_pairs={{0,2},{1,3},{2,0},{3,1},{4,6},{5,7},{6,4},{7,5},{8,10},{9,11},{10,... | collective-permute-start | bytes 49160 | tf_op jit(solution)/shard_map/share_vectors/ppermute | solution.py:29
  11.7 0.0 collective-permute-done.3.refs_1_
  11.7 0.0 collective-permute-start.4
  11.7 0.1 pad_add_fusion.place
  12.5 1.4 %collective-permute-done.2.far = f32[2,16,128]{2,1,0:T(8,128)S(1)} collective-permute-done((f32[2,16,128]{2,1,0:T(8,128)S(1)}, f32[2,16,128]{2,1,0:T(8,128)S(1)}, u32[]{:S(2)}, u32[]{:S(2)}) %collective-permute-start.2) | collective-permute-done | bytes 16416 | tf_op jit(solution)/shard_map/share_vectors/ppermute | solution.py:29
  13.8 0.9 %column_terms.1 = (f32[4,16,128]{2,1,0:T(8,128)S(1)}, f32[4,16,128]{2,1,0:T(8,128)S(1)}) custom-call(s32[2]{0:T(128)S(1)} %pad_add_fusion.place, s32[1,1,16]{2,1,0:T(1,128)S(1)} %get-tuple-element.52.arow, s32[1,1,16]{2,1,0:T(1,128)S(1)} %get-tuple-element.53.bcol, s32[1,1]{1,0:T(1,128)S(6)} %copy.16.count, f32[1,128]{1,0:T(1,128)S(1)} %get-tuple-element.54.d_ref, ...), custom_call_target="tpu_custom_call" | custom-call | flops 50331648 | bytes 1048576 | tf_op jit(solution)/shard_map/column_terms/column_terms/pallas_call | solution.py:278
  14.8 0.0 collective-permute-done.4.after.far
  14.8 0.1 collective-permute-start.5
  14.9 1.2 %row_terms.1 = (f32[2,16,128]{2,1,0:T(8,128)S(1)}, f32[2,16,128]{2,1,0:T(8,128)S(1)}) custom-call(s32[2]{0:T(128)S(1)} %pad_add_fusion.place, s32[1,1,16]{2,1,0:T(1,128)S(1)} %get-tuple-element.52.arow, s32[1,1,16]{2,1,0:T(1,128)S(1)} %get-tuple-element.53.bcol, s32[1,1]{1,0:T(1,128)S(6)} %copy.16.count, f32[4,16,128]{2,1,0:T(8,128)S(1)} %join.3.near, ...), custom_call_target="tpu_custom_call" | custom-call | flops 50331648 | bytes 1048576 | tf_op jit(solution)/shard_map/row_terms/row_terms/pallas_call | solution.py:300
  16.1 0.5 %collective-permute-start.8 = (f32[2,16,128]{2,1,0:T(8,128)S(1)}, f32[2,16,128]{2,1,0:T(8,128)S(1)}, u32[]{:S(2)}, u32[]{:S(2)}) collective-permute-start(f32[2,16,128]{2,1,0:T(8,128)S(1)} %get-tuple-element.67), channel_id=1, source_target_pairs={{0,1},{1,0},{2,3},{3,2},{4,5},{5,4},{6,7},{7,6},{8,9},{9,8},{10,11... | collective-permute-start | bytes 49160 | tf_op jit(solution)/shard_map/return_products/ppermute | solution.py:29
  16.5 0.0 collective-permute-done.5.other
  16.6 1.6 %collective-permute-start.6 = (f32[2,16,128]{2,1,0:T(8,128)S(1)}, f32[2,16,128]{2,1,0:T(8,128)S(1)}, u32[]{:S(2)}, u32[]{:S(2)}) collective-permute-start(f32[2,16,128]{2,1,0:T(8,128)S(1)} %get-tuple-element.63), channel_id=1, source_target_pairs={{0,8},{4,12},{8,0},{12,4},{16,24},{20,28},{24,16},{28,20},{1,9},{5... | collective-permute-start | bytes 49160 | tf_op jit(solution)/shard_map/return_products/ppermute | solution.py:29
  18.1 1.8 %collective-permute-done.8.other = f32[2,16,128]{2,1,0:T(8,128)S(1)} collective-permute-done((f32[2,16,128]{2,1,0:T(8,128)S(1)}, f32[2,16,128]{2,1,0:T(8,128)S(1)}, u32[]{:S(2)}, u32[]{:S(2)}) %collective-permute-start.8) | collective-permute-done | bytes 16416 | tf_op jit(solution)/shard_map/return_products/ppermute | solution.py:29
  19.9 2.5 %collective-permute-start.9 = (f32[1,16,128]{2,1,0:T(8,128)S(1)}, f32[1,16,128]{2,1,0:T(8,128)S(1)}, u32[]{:S(2)}, u32[]{:S(2)}) collective-permute-start(f32[1,16,128]{2,1,0:T(8,128)S(1)} %get-tuple-element.69), channel_id=1, source_target_pairs={{0,2},{1,3},{2,0},{3,1},{4,6},{5,7},{6,4},{7,5},{8,10},{9,11},{10,... | collective-permute-start | bytes 24584 | tf_op jit(solution)/shard_map/return_products/ppermute | solution.py:29
  22.4 0.0 collective-permute-done.6.other
  22.4 0.6 %collective-permute-start.7 = (f32[1,16,128]{2,1,0:T(8,128)S(1)}, f32[1,16,128]{2,1,0:T(8,128)S(1)}, u32[]{:S(2)}, u32[]{:S(2)}) collective-permute-start(f32[1,16,128]{2,1,0:T(8,128)S(1)} %get-tuple-element.65), channel_id=1, source_target_pairs={{0,16},{4,20},{8,24},{12,28},{16,0},{20,4},{24,8},{28,12},{1,17},{... | collective-permute-start | bytes 24584 | tf_op jit(solution)/shard_map/return_products/ppermute | solution.py:29
  23.0 1.5 %collective-permute-done.9.refs_3_ = f32[1,16,128]{2,1,0:T(8,128)S(1)} collective-permute-done((f32[1,16,128]{2,1,0:T(8,128)S(1)}, f32[1,16,128]{2,1,0:T(8,128)S(1)}, u32[]{:S(2)}, u32[]{:S(2)}) %collective-permute-start.9) | collective-permute-done | bytes 8224 | tf_op jit(solution)/shard_map/return_products/ppermute | solution.py:29
  24.4 1.7 %collective-permute-done.7.refs_1_ = f32[1,16,128]{2,1,0:T(8,128)S(1)} collective-permute-done((f32[1,16,128]{2,1,0:T(8,128)S(1)}, f32[1,16,128]{2,1,0:T(8,128)S(1)}, u32[]{:S(2)}, u32[]{:S(2)}) %collective-permute-start.7) | collective-permute-done | bytes 8224 | tf_op jit(solution)/shard_map/return_products/ppermute | solution.py:29
  26.1 0.3 product.1
  26.5 10.5 %all_to_all.9.parts = f32[32,3,2,128]{3,2,1,0:T(2,128)S(1)} all-to-all(f32[32,3,2,128]{3,2,1,0:T(2,128)S(1)} %get-tuple-element.71), channel_id=1, replica_groups=mesh['row'=8,'col'=4] {'row','col'}, dimensions={0} | all-to-all | bytes 196608 | tf_op jit(solution)/shard_map/product/all_to_all | solution.py:24
  37.0 1.2 %results.1 = (f32[16,128]{1,0:T(8,128)}, f32[16,16]{1,0:T(8,128)}, f32[16,16]{1,0:T(8,128)}, s32[1,1]{1,0:T(1,128)}) custom-call(f32[16,128]{1,0:T(8,128)S(1)} %copy-done.4, f32[16,128]{1,0:T(8,128)S(1)} %get-tuple-element.95.product, f32[32,3,2,128]{3,2,1,0:T(2,128)S(1)} %all_to_all.9.parts), custom_call_target="tpu_custom_call" | custom-call | tf_op jit(solution)/shard_map/results/results/pallas_call | solution.py:326
  38.2 0.7 %while.9 = (s32[]{:T(128)}, f32[16,16]{1,0:T(8,128)}, f32[16,128]{1,0:T(8,128)S(1)}, f32[16,128]{1,0:T(8,128)S(1)}, f32[32,3,2,128]{3,2,1,0:T(2,128)S(1)}) while((s32[]{:T(128)}, f32[16,16]{1,0:T(8,128)}, f32[16,128]{1,0:T(8,128)S(1)}, f32[16,128]{1,0:T(8,128)S(1)}, f32[32,3,2,128]{3,2,1,0:T(2,128)S(1)}) %tuple.20), condition=%region_1.0_spmd, body=%region_0.0_spmd | while | flops 1 | bytes 98393 | solution.py:355
  (6 shorter events, 0.0 us)
Async XLA Ops:
  0.6 4.6 %copy-start.1 = (s32[1,1,16]{2,1,0:T(1,128)S(1)}, s32[1,1,16]{2,1,0:T(1,128)}, u32[]{:S(2)}) copy-start(s32[1,1,16]{2,1,0:T(1,128)} %refs_0_.1) | copy-start | bytes 196
  0.6 4.6 %copy-start.2 = (s32[1,1,16]{2,1,0:T(1,128)S(1)}, s32[1,1,16]{2,1,0:T(1,128)}, u32[]{:S(2)}) copy-start(s32[1,1,16]{2,1,0:T(1,128)} %refs_1_.1) | copy-start | bytes 196
  0.7 4.6 %copy-start.3 = (f32[128]{0:T(128)S(1)}, f32[128]{0:T(128)}, u32[]{:S(2)}) copy-start(f32[128]{0:T(128)} %param.9) | copy-start | bytes 1540
  0.7 6.0 %collective-permute-start = (f32[1,16,128]{2,1,0:T(8,128)}, f32[1,16,128]{2,1,0:T(8,128)S(1)}, u32[]{:S(2)}, u32[]{:S(2)}) collective-permute-start(f32[1,16,128]{2,1,0:T(8,128)} %bitcast.6), channel_id=1, source_target_pairs={{0,1},{1,0},{2,3},{3,2},{4,5},{5,4},{6,7},{7,6},{8,9},{9,8},{10,11... | collective-permute-start | bytes 24584 | tf_op jit(solution)/shard_map/share_vectors/ppermute | solution.py:29
  3.8 3.9 %collective-permute-start.1 = (f32[1,16,128]{2,1,0:T(8,128)}, f32[1,16,128]{2,1,0:T(8,128)S(1)}, u32[]{:S(2)}, u32[]{:S(2)}) collective-permute-start(f32[1,16,128]{2,1,0:T(8,128)} %bitcast.7), channel_id=1, source_target_pairs={{0,8},{4,12},{8,0},{12,4},{16,24},{20,28},{24,16},{28,20},{1,9},{5... | collective-permute-start | bytes 24584 | tf_op jit(solution)/shard_map/share_vectors/ppermute | solution.py:29
  5.2 1.2 %copy-start = (f32[1,1,16,128,128]{4,3,2,1,0:T(8,128)S(1)}, f32[1,1,16,128,128]{4,3,2,1,0:T(8,128)}, u32[]{:S(2)}) copy-start(f32[1,1,16,128,128]{4,3,2,1,0:T(8,128)} %tiles.1) | copy-start | bytes 3145732
  6.5 1.1 %copy-start.4 = (f32[16,128]{1,0:T(8,128)S(1)}, f32[16,128]{1,0:T(8,128)}, u32[]{:S(2)}) copy-start(f32[16,128]{1,0:T(8,128)} %x_ref.3) | copy-start | bytes 24580
  7.6 4.1 %collective-permute-start.3 = (f32[2,16,128]{2,1,0:T(8,128)S(1)}, f32[2,16,128]{2,1,0:T(8,128)S(1)}, u32[]{:S(2)}, u32[]{:S(2)}) collective-permute-start(f32[2,16,128]{2,1,0:T(8,128)S(1)} %get-tuple-element.61.refs_0_), channel_id=1, source_target_pairs={{0,16},{4,20},{8,24},{12,28},{16,0},{20,4},{24,8},{28,12},{1,17},{... | collective-permute-start | bytes 49160 | tf_op jit(solution)/shard_map/share_vectors/ppermute | solution.py:29
  9.1 4.7 %collective-permute-start.2 = (f32[2,16,128]{2,1,0:T(8,128)S(1)}, f32[2,16,128]{2,1,0:T(8,128)S(1)}, u32[]{:S(2)}, u32[]{:S(2)}) collective-permute-start(f32[2,16,128]{2,1,0:T(8,128)S(1)} %get-tuple-element.56.near), channel_id=1, source_target_pairs={{0,2},{1,3},{2,0},{3,1},{4,6},{5,7},{6,4},{7,5},{8,10},{9,11},{10,... | collective-permute-start | bytes 49160 | tf_op jit(solution)/shard_map/share_vectors/ppermute | solution.py:29
  11.7 3.0 %collective-permute-start.4 = (f32[4,16,128]{2,1,0:T(8,128)S(1)}, f32[4,16,128]{2,1,0:T(8,128)S(1)}, u32[]{:S(2)}, u32[]{:S(2)}) collective-permute-start(f32[4,16,128]{2,1,0:T(8,128)S(1)} %join.3.near), channel_id=1, source_target_pairs={{0,4},{4,0},{8,12},{12,8},{16,20},{20,16},{24,28},{28,24},{1,5},{5... | collective-permute-start | bytes 98312 | tf_op jit(solution)/shard_map/share_vectors/ppermute | solution.py:29
  14.8 1.8 %collective-permute-start.5 = (f32[4,16,128]{2,1,0:T(8,128)S(1)}, f32[4,16,128]{2,1,0:T(8,128)S(1)}, u32[]{:S(2)}, u32[]{:S(2)}) collective-permute-start(f32[4,16,128]{2,1,0:T(8,128)S(1)} %hand_on.1), channel_id=1, source_target_pairs={{0,4},{4,0},{8,12},{12,8},{16,20},{20,16},{24,28},{28,24},{1,5},{5... | collective-permute-start | bytes 98312 | tf_op jit(solution)/shard_map/return_products/ppermute | solution.py:29
  16.1 3.8 %collective-permute-start.8 = (f32[2,16,128]{2,1,0:T(8,128)S(1)}, f32[2,16,128]{2,1,0:T(8,128)S(1)}, u32[]{:S(2)}, u32[]{:S(2)}) collective-permute-start(f32[2,16,128]{2,1,0:T(8,128)S(1)} %get-tuple-element.67), channel_id=1, source_target_pairs={{0,1},{1,0},{2,3},{3,2},{4,5},{5,4},{6,7},{7,6},{8,9},{9,8},{10,11... | collective-permute-start | bytes 49160 | tf_op jit(solution)/shard_map/return_products/ppermute | solution.py:29
  16.6 5.9 %collective-permute-start.6 = (f32[2,16,128]{2,1,0:T(8,128)S(1)}, f32[2,16,128]{2,1,0:T(8,128)S(1)}, u32[]{:S(2)}, u32[]{:S(2)}) collective-permute-start(f32[2,16,128]{2,1,0:T(8,128)S(1)} %get-tuple-element.63), channel_id=1, source_target_pairs={{0,8},{4,12},{8,0},{12,4},{16,24},{20,28},{24,16},{28,20},{1,9},{5... | collective-permute-start | bytes 49160 | tf_op jit(solution)/shard_map/return_products/ppermute | solution.py:29
  19.9 4.5 %collective-permute-start.9 = (f32[1,16,128]{2,1,0:T(8,128)S(1)}, f32[1,16,128]{2,1,0:T(8,128)S(1)}, u32[]{:S(2)}, u32[]{:S(2)}) collective-permute-start(f32[1,16,128]{2,1,0:T(8,128)S(1)} %get-tuple-element.69), channel_id=1, source_target_pairs={{0,2},{1,3},{2,0},{3,1},{4,6},{5,7},{6,4},{7,5},{8,10},{9,11},{10,... | collective-permute-start | bytes 24584 | tf_op jit(solution)/shard_map/return_products/ppermute | solution.py:29
  22.4 3.7 %collective-permute-start.7 = (f32[1,16,128]{2,1,0:T(8,128)S(1)}, f32[1,16,128]{2,1,0:T(8,128)S(1)}, u32[]{:S(2)}, u32[]{:S(2)}) collective-permute-start(f32[1,16,128]{2,1,0:T(8,128)S(1)} %get-tuple-element.65), channel_id=1, source_target_pairs={{0,16},{4,20},{8,24},{12,28},{16,0},{20,4},{24,8},{28,12},{1,17},{... | collective-permute-start | bytes 24584 | tf_op jit(solution)/shard_map/return_products/ppermute | solution.py:29

commit v22 on v20

--- a/solution.py
+++ b/solution.py
@@ -182,9 +182,12 @@
     nvec = own.shape[0]
     ray, outer, inner = summed_squares(scale, parts, nvec)
     rayleigh[...] = ray
-    residual[...] = product[...] - mult(ray, own)
-    twice = mult(ray, ray)
-    lifted = mult_last(mult(ray, inner), ray)
+    width = own.shape[1]
+    blank = jnp.zeros((nvec, width - nvec), jnp.float32)
+    wide = mult(ray, jnp.concatenate([own, ray, blank, inner, blank], axis=1))
+    residual[...] = product[...] - wide[:, :width]
+    twice = wide[:, width : width + nvec]
+    lifted = mult_last(wide[:, 2 * width : 2 * width + nvec], ray)
     result = outer - (twice + twice.T) + lifted
     gram[...] = result
     diagonal = lax.broadcasted_iota(jnp.int32, (nvec, nvec), 0) == lax.broadcasted_iota(jnp.int32, (nvec, nvec), 1)

time: 38.6 us -> 38.6 us (level)
  no operation moved by 1% of the time
where the time goes in v22:
time: 38.6 us; the launch traced here: 38.4 us
  starting transfers between devices  14.2 us (37%)
  blocking collectives  10 us (26%)
  waiting for transfers between devices  6.87 us (18%)
  Pallas kernels  3.93 us (10%)
  between operations  1.38 us (4%)
  local copies, waits for them, and re-layouts  1.24 us (3%)
  loops' own time  0.69 us (2%)
    ppermute x10, starting transfers between devices, trade(): return lax.ppermute(value, axis, [(p, p ^ flip) for p in range(size)])  14.2 us
    all_to_all x1, blocking collectives, swap(): return lax.all_to_all(blocks, axis, 0, 0, tiled=True)  10 us
    ppermute x10, waiting for transfers between devices, trade(): return lax.ppermute(value, axis, [(p, p ^ flip) for p in range(size)])  6.87 us
    unnamed x10, local copies, waits for them, and re-layouts  1.24 us
    pallas_call x1, Pallas kernels, per_device(): pl.pallas_call(functools.partial(result_kernel, scale), out_shape=[block,...  1.23 us
    pallas_call x1, Pallas kernels, per_device(): pl.pallas_call(functools.partial(row_kernel, n_row, n_col, slots), out_sh...  1.21 us
    pallas_call x1, Pallas kernels, per_device(): pl.pallas_call(functools.partial(column_kernel, n_row, n_col, slots), out...  0.93 us
  transfers between devices with their start and end apart: 10, of which 5 were waited for; matrix products, arithmetic and copies ran while one was open for 0% of the time, Pallas kernels for 6%

profile of v22, /device:TPU:0, one launch (start us, length us, event | category | flops | bytes accessed | tf_op | source)
XLA Modules:
  0.0 38.4 jit_solution(6231292384987527523)
XLA Ops:
  0.6 0.0 copy-start.1
  0.6 0.0 copy-start.2
  0.7 0.0 copy-start.3
  0.7 3.0 %collective-permute-start = (f32[1,16,128]{2,1,0:T(8,128)}, f32[1,16,128]{2,1,0:T(8,128)S(1)}, u32[]{:S(2)}, u32[]{:S(2)}) collective-permute-start(f32[1,16,128]{2,1,0:T(8,128)} %bitcast.6), channel_id=1, source_target_pairs={{0,8},{4,12},{8,0},{12,4},{16,24},{20,28},{24,16},{28,20},{1,9},{5... | collective-permute-start | bytes 24584 | tf_op jit(solution)/shard_map/share_vectors/ppermute | solution.py:29
  3.7 1.6 %collective-permute-start.1 = (f32[1,16,128]{2,1,0:T(8,128)}, f32[1,16,128]{2,1,0:T(8,128)S(1)}, u32[]{:S(2)}, u32[]{:S(2)}) collective-permute-start(f32[1,16,128]{2,1,0:T(8,128)} %bitcast.7), channel_id=1, source_target_pairs={{0,1},{1,0},{2,3},{3,2},{4,5},{5,4},{6,7},{7,6},{8,9},{9,8},{10,11... | collective-permute-start | bytes 24584 | tf_op jit(solution)/shard_map/share_vectors/ppermute | solution.py:29
  5.2 0.0 copy-done.1
  5.2 0.0 copy-done.2
  5.2 0.0 copy-done.3
  5.2 0.0 copy-start
  5.3 1.2 %copy-done = f32[1,1,16,128,128]{4,3,2,1,0:T(8,128)S(1)} copy-done((f32[1,1,16,128,128]{4,3,2,1,0:T(8,128)S(1)}, f32[1,1,16,128,128]{4,3,2,1,0:T(8,128)}, u32[]{:S(2)}) %copy-start) | copy-done | bytes 1048600
  6.5 0.0 copy-start.4
  6.5 0.2 prepare.1
  6.7 0.0 collective-permute-done.refs_1_
  6.7 0.8 %collective-permute-done.1.refs_3_ = f32[1,16,128]{2,1,0:T(8,128)S(1)} collective-permute-done((f32[1,16,128]{2,1,0:T(8,128)}, f32[1,16,128]{2,1,0:T(8,128)S(1)}, u32[]{:S(2)}, u32[]{:S(2)}) %collective-permute-start.1) | collective-permute-done | bytes 8224 | tf_op jit(solution)/shard_map/share_vectors/ppermute | solution.py:29
  7.5 0.0 copy-done.4
  7.5 1.5 %collective-permute-start.3 = (f32[2,16,128]{2,1,0:T(8,128)S(1)}, f32[2,16,128]{2,1,0:T(8,128)S(1)}, u32[]{:S(2)}, u32[]{:S(2)}) collective-permute-start(f32[2,16,128]{2,1,0:T(8,128)S(1)} %get-tuple-element.61.refs_0_), channel_id=1, source_target_pairs={{0,16},{4,20},{8,24},{12,28},{16,0},{20,4},{24,8},{28,12},{1,17},{... | collective-permute-start | bytes 49160 | tf_op jit(solution)/shard_map/share_vectors/ppermute | solution.py:29
  9.1 2.6 %collective-permute-start.2 = (f32[2,16,128]{2,1,0:T(8,128)S(1)}, f32[2,16,128]{2,1,0:T(8,128)S(1)}, u32[]{:S(2)}, u32[]{:S(2)}) collective-permute-start(f32[2,16,128]{2,1,0:T(8,128)S(1)} %get-tuple-element.56.near), channel_id=1, source_target_pairs={{0,2},{1,3},{2,0},{3,1},{4,6},{5,7},{6,4},{7,5},{8,10},{9,11},{10,... | collective-permute-start | bytes 49160 | tf_op jit(solution)/shard_map/share_vectors/ppermute | solution.py:29
  11.6 0.0 collective-permute-done.3.refs_1_
  11.7 0.0 collective-permute-start.4
  11.7 0.1 pad_add_fusion.place
  12.4 1.3 %collective-permute-done.2.far = f32[2,16,128]{2,1,0:T(8,128)S(1)} collective-permute-done((f32[2,16,128]{2,1,0:T(8,128)S(1)}, f32[2,16,128]{2,1,0:T(8,128)S(1)}, u32[]{:S(2)}, u32[]{:S(2)}) %collective-permute-start.2) | collective-permute-done | bytes 16416 | tf_op jit(solution)/shard_map/share_vectors/ppermute | solution.py:29
  13.7 0.9 %column_terms.1 = (f32[4,16,128]{2,1,0:T(8,128)S(1)}, f32[4,16,128]{2,1,0:T(8,128)S(1)}) custom-call(s32[2]{0:T(128)S(1)} %pad_add_fusion.place, s32[1,1,16]{2,1,0:T(1,128)S(1)} %get-tuple-element.52.arow, s32[1,1,16]{2,1,0:T(1,128)S(1)} %get-tuple-element.53.bcol, s32[1,1]{1,0:T(1,128)S(6)} %copy.16.count, f32[1,128]{1,0:T(1,128)S(1)} %get-tuple-element.54.d_ref, ...), custom_call_target="tpu_custom_call" | custom-call | flops 50331648 | bytes 1048576 | tf_op jit(solution)/shard_map/column_terms/column_terms/pallas_call | solution.py:281
  14.6 0.0 collective-permute-done.4.after.far
  14.6 0.1 collective-permute-start.5
  14.7 1.2 %row_terms.1 = (f32[2,16,128]{2,1,0:T(8,128)S(1)}, f32[2,16,128]{2,1,0:T(8,128)S(1)}) custom-call(s32[2]{0:T(128)S(1)} %pad_add_fusion.place, s32[1,1,16]{2,1,0:T(1,128)S(1)} %get-tuple-element.52.arow, s32[1,1,16]{2,1,0:T(1,128)S(1)} %get-tuple-element.53.bcol, s32[1,1]{1,0:T(1,128)S(6)} %copy.16.count, f32[4,16,128]{2,1,0:T(8,128)S(1)} %join.3.near, ...), custom_call_target="tpu_custom_call" | custom-call | flops 50331648 | bytes 1048576 | tf_op jit(solution)/shard_map/row_terms/row_terms/pallas_call | solution.py:303
  15.9 1.6 %collective-permute-start.8 = (f32[2,16,128]{2,1,0:T(8,128)S(1)}, f32[2,16,128]{2,1,0:T(8,128)S(1)}, u32[]{:S(2)}, u32[]{:S(2)}) collective-permute-start(f32[2,16,128]{2,1,0:T(8,128)S(1)} %get-tuple-element.67), channel_id=1, source_target_pairs={{0,1},{1,0},{2,3},{3,2},{4,5},{5,4},{6,7},{7,6},{8,9},{9,8},{10,11... | collective-permute-start | bytes 49160 | tf_op jit(solution)/shard_map/return_products/ppermute | solution.py:29
  17.6 0.0 collective-permute-done.5.other
  17.6 0.6 %collective-permute-start.6 = (f32[2,16,128]{2,1,0:T(8,128)S(1)}, f32[2,16,128]{2,1,0:T(8,128)S(1)}, u32[]{:S(2)}, u32[]{:S(2)}) collective-permute-start(f32[2,16,128]{2,1,0:T(8,128)S(1)} %get-tuple-element.63), channel_id=1, source_target_pairs={{0,8},{4,12},{8,0},{12,4},{16,24},{20,28},{24,16},{28,20},{1,9},{5... | collective-permute-start | bytes 49160 | tf_op jit(solution)/shard_map/return_products/ppermute | solution.py:29
  18.2 1.6 %collective-permute-done.8.other = f32[2,16,128]{2,1,0:T(8,128)S(1)} collective-permute-done((f32[2,16,128]{2,1,0:T(8,128)S(1)}, f32[2,16,128]{2,1,0:T(8,128)S(1)}, u32[]{:S(2)}, u32[]{:S(2)}) %collective-permute-start.8) | collective-permute-done | bytes 16416 | tf_op jit(solution)/shard_map/return_products/ppermute | solution.py:29
  19.8 2.6 %collective-permute-start.9 = (f32[1,16,128]{2,1,0:T(8,128)S(1)}, f32[1,16,128]{2,1,0:T(8,128)S(1)}, u32[]{:S(2)}, u32[]{:S(2)}) collective-permute-start(f32[1,16,128]{2,1,0:T(8,128)S(1)} %get-tuple-element.69), channel_id=1, source_target_pairs={{0,2},{1,3},{2,0},{3,1},{4,6},{5,7},{6,4},{7,5},{8,10},{9,11},{10,... | collective-permute-start | bytes 24584 | tf_op jit(solution)/shard_map/return_products/ppermute | solution.py:29
  22.4 0.0 collective-permute-done.6.other
  22.4 0.6 %collective-permute-start.7 = (f32[1,16,128]{2,1,0:T(8,128)S(1)}, f32[1,16,128]{2,1,0:T(8,128)S(1)}, u32[]{:S(2)}, u32[]{:S(2)}) collective-permute-start(f32[1,16,128]{2,1,0:T(8,128)S(1)} %get-tuple-element.65), channel_id=1, source_target_pairs={{0,16},{4,20},{8,24},{12,28},{16,0},{20,4},{24,8},{28,12},{1,17},{... | collective-permute-start | bytes 24584 | tf_op jit(solution)/shard_map/return_products/ppermute | solution.py:29
  22.9 1.4 %collective-permute-done.9.refs_3_ = f32[1,16,128]{2,1,0:T(8,128)S(1)} collective-permute-done((f32[1,16,128]{2,1,0:T(8,128)S(1)}, f32[1,16,128]{2,1,0:T(8,128)S(1)}, u32[]{:S(2)}, u32[]{:S(2)}) %collective-permute-start.9) | collective-permute-done | bytes 8224 | tf_op jit(solution)/shard_map/return_products/ppermute | solution.py:29
  24.3 1.8 %collective-permute-done.7.refs_1_ = f32[1,16,128]{2,1,0:T(8,128)S(1)} collective-permute-done((f32[1,16,128]{2,1,0:T(8,128)S(1)}, f32[1,16,128]{2,1,0:T(8,128)S(1)}, u32[]{:S(2)}, u32[]{:S(2)}) %collective-permute-start.7) | collective-permute-done | bytes 8224 | tf_op jit(solution)/shard_map/return_products/ppermute | solution.py:29
  26.1 0.3 product.1
  26.4 10.0 %all_to_all.9.parts = f32[32,3,2,128]{3,2,1,0:T(2,128)S(1)} all-to-all(f32[32,3,2,128]{3,2,1,0:T(2,128)S(1)} %get-tuple-element.71), channel_id=1, replica_groups=mesh['row'=8,'col'=4] {'row','col'}, dimensions={0} | all-to-all | bytes 196608 | tf_op jit(solution)/shard_map/product/all_to_all | solution.py:24
  36.4 1.2 %results.1 = (f32[16,128]{1,0:T(8,128)}, f32[16,16]{1,0:T(8,128)}, f32[16,16]{1,0:T(8,128)}, s32[1,1]{1,0:T(1,128)}) custom-call(f32[16,128]{1,0:T(8,128)S(1)} %copy-done.4, f32[16,128]{1,0:T(8,128)S(1)} %get-tuple-element.95.product, f32[32,3,2,128]{3,2,1,0:T(2,128)S(1)} %all_to_all.9.parts), custom_call_target="tpu_custom_call" | custom-call | tf_op jit(solution)/shard_map/results/results/pallas_call | solution.py:329
  37.7 0.7 %while.9 = (s32[]{:T(128)}, f32[16,16]{1,0:T(8,128)}, f32[16,128]{1,0:T(8,128)S(1)}, f32[16,128]{1,0:T(8,128)S(1)}, f32[32,3,2,128]{3,2,1,0:T(2,128)S(1)}) while((s32[]{:T(128)}, f32[16,16]{1,0:T(8,128)}, f32[16,128]{1,0:T(8,128)S(1)}, f32[16,128]{1,0:T(8,128)S(1)}, f32[32,3,2,128]{3,2,1,0:T(2,128)S(1)}) %tuple.20), condition=%region_1.0_spmd, body=%region_0.0_spmd | while | flops 1 | bytes 98393 | solution.py:358
  (6 shorter events, 0.0 us)
Async XLA Ops:
  0.6 4.6 %copy-start.1 = (s32[1,1,16]{2,1,0:T(1,128)S(1)}, s32[1,1,16]{2,1,0:T(1,128)}, u32[]{:S(2)}) copy-start(s32[1,1,16]{2,1,0:T(1,128)} %refs_0_.1) | copy-start | bytes 196
  0.6 4.6 %copy-start.2 = (s32[1,1,16]{2,1,0:T(1,128)S(1)}, s32[1,1,16]{2,1,0:T(1,128)}, u32[]{:S(2)}) copy-start(s32[1,1,16]{2,1,0:T(1,128)} %refs_1_.1) | copy-start | bytes 196
  0.7 4.6 %copy-start.3 = (f32[128]{0:T(128)S(1)}, f32[128]{0:T(128)}, u32[]{:S(2)}) copy-start(f32[128]{0:T(128)} %param.9) | copy-start | bytes 1540
  0.7 6.0 %collective-permute-start = (f32[1,16,128]{2,1,0:T(8,128)}, f32[1,16,128]{2,1,0:T(8,128)S(1)}, u32[]{:S(2)}, u32[]{:S(2)}) collective-permute-start(f32[1,16,128]{2,1,0:T(8,128)} %bitcast.6), channel_id=1, source_target_pairs={{0,8},{4,12},{8,0},{12,4},{16,24},{20,28},{24,16},{28,20},{1,9},{5... | collective-permute-start | bytes 24584 | tf_op jit(solution)/shard_map/share_vectors/ppermute | solution.py:29
  3.7 3.9 %collective-permute-start.1 = (f32[1,16,128]{2,1,0:T(8,128)}, f32[1,16,128]{2,1,0:T(8,128)S(1)}, u32[]{:S(2)}, u32[]{:S(2)}) collective-permute-start(f32[1,16,128]{2,1,0:T(8,128)} %bitcast.7), channel_id=1, source_target_pairs={{0,1},{1,0},{2,3},{3,2},{4,5},{5,4},{6,7},{7,6},{8,9},{9,8},{10,11... | collective-permute-start | bytes 24584 | tf_op jit(solution)/shard_map/share_vectors/ppermute | solution.py:29
  5.2 1.2 %copy-start = (f32[1,1,16,128,128]{4,3,2,1,0:T(8,128)S(1)}, f32[1,1,16,128,128]{4,3,2,1,0:T(8,128)}, u32[]{:S(2)}) copy-start(f32[1,1,16,128,128]{4,3,2,1,0:T(8,128)} %tiles.1) | copy-start | bytes 3145732
  6.5 1.1 %copy-start.4 = (f32[16,128]{1,0:T(8,128)S(1)}, f32[16,128]{1,0:T(8,128)}, u32[]{:S(2)}) copy-start(f32[16,128]{1,0:T(8,128)} %x_ref.3) | copy-start | bytes 24580
  7.5 4.1 %collective-permute-start.3 = (f32[2,16,128]{2,1,0:T(8,128)S(1)}, f32[2,16,128]{2,1,0:T(8,128)S(1)}, u32[]{:S(2)}, u32[]{:S(2)}) collective-permute-start(f32[2,16,128]{2,1,0:T(8,128)S(1)} %get-tuple-element.61.refs_0_), channel_id=1, source_target_pairs={{0,16},{4,20},{8,24},{12,28},{16,0},{20,4},{24,8},{28,12},{1,17},{... | collective-permute-start | bytes 49160 | tf_op jit(solution)/shard_map/share_vectors/ppermute | solution.py:29
  9.1 4.6 %collective-permute-start.2 = (f32[2,16,128]{2,1,0:T(8,128)S(1)}, f32[2,16,128]{2,1,0:T(8,128)S(1)}, u32[]{:S(2)}, u32[]{:S(2)}) collective-permute-start(f32[2,16,128]{2,1,0:T(8,128)S(1)} %get-tuple-element.56.near), channel_id=1, source_target_pairs={{0,2},{1,3},{2,0},{3,1},{4,6},{5,7},{6,4},{7,5},{8,10},{9,11},{10,... | collective-permute-start | bytes 49160 | tf_op jit(solution)/shard_map/share_vectors/ppermute | solution.py:29
  11.7 3.0 %collective-permute-start.4 = (f32[4,16,128]{2,1,0:T(8,128)S(1)}, f32[4,16,128]{2,1,0:T(8,128)S(1)}, u32[]{:S(2)}, u32[]{:S(2)}) collective-permute-start(f32[4,16,128]{2,1,0:T(8,128)S(1)} %join.3.near), channel_id=1, source_target_pairs={{0,4},{4,0},{8,12},{12,8},{16,20},{20,16},{24,28},{28,24},{1,5},{5... | collective-permute-start | bytes 98312 | tf_op jit(solution)/shard_map/share_vectors/ppermute | solution.py:29
  14.6 2.9 %collective-permute-start.5 = (f32[4,16,128]{2,1,0:T(8,128)S(1)}, f32[4,16,128]{2,1,0:T(8,128)S(1)}, u32[]{:S(2)}, u32[]{:S(2)}) collective-permute-start(f32[4,16,128]{2,1,0:T(8,128)S(1)} %hand_on.1), channel_id=1, source_target_pairs={{0,4},{4,0},{8,12},{12,8},{16,20},{20,16},{24,28},{28,24},{1,5},{5... | collective-permute-start | bytes 98312 | tf_op jit(solution)/shard_map/return_products/ppermute | solution.py:29
  15.9 3.8 %collective-permute-start.8 = (f32[2,16,128]{2,1,0:T(8,128)S(1)}, f32[2,16,128]{2,1,0:T(8,128)S(1)}, u32[]{:S(2)}, u32[]{:S(2)}) collective-permute-start(f32[2,16,128]{2,1,0:T(8,128)S(1)} %get-tuple-element.67), channel_id=1, source_target_pairs={{0,1},{1,0},{2,3},{3,2},{4,5},{5,4},{6,7},{7,6},{8,9},{9,8},{10,11... | collective-permute-start | bytes 49160 | tf_op jit(solution)/shard_map/return_products/ppermute | solution.py:29
  17.6 4.8 %collective-permute-start.6 = (f32[2,16,128]{2,1,0:T(8,128)S(1)}, f32[2,16,128]{2,1,0:T(8,128)S(1)}, u32[]{:S(2)}, u32[]{:S(2)}) collective-permute-start(f32[2,16,128]{2,1,0:T(8,128)S(1)} %get-tuple-element.63), channel_id=1, source_target_pairs={{0,8},{4,12},{8,0},{12,4},{16,24},{20,28},{24,16},{28,20},{1,9},{5... | collective-permute-start | bytes 49160 | tf_op jit(solution)/shard_map/return_products/ppermute | solution.py:29
  19.8 4.5 %collective-permute-start.9 = (f32[1,16,128]{2,1,0:T(8,128)S(1)}, f32[1,16,128]{2,1,0:T(8,128)S(1)}, u32[]{:S(2)}, u32[]{:S(2)}) collective-permute-start(f32[1,16,128]{2,1,0:T(8,128)S(1)} %get-tuple-element.69), channel_id=1, source_target_pairs={{0,2},{1,3},{2,0},{3,1},{4,6},{5,7},{6,4},{7,5},{8,10},{9,11},{10,... | collective-permute-start | bytes 24584 | tf_op jit(solution)/shard_map/return_products/ppermute | solution.py:29
  22.4 3.7 %collective-permute-start.7 = (f32[1,16,128]{2,1,0:T(8,128)S(1)}, f32[1,16,128]{2,1,0:T(8,128)S(1)}, u32[]{:S(2)}, u32[]{:S(2)}) collective-permute-start(f32[1,16,128]{2,1,0:T(8,128)S(1)} %get-tuple-element.65), channel_id=1, source_target_pairs={{0,16},{4,20},{8,24},{12,28},{16,0},{20,4},{24,8},{28,12},{1,17},{... | collective-permute-start | bytes 24584 | tf_op jit(solution)/shard_map/return_products/ppermute | solution.py:29

commit v23 on v20

--- a/solution.py
+++ b/solution.py
@@ -295,7 +295,7 @@
             out_specs=VMEM,
             compiler_params=params,
             name="hand_on",
-        )(col_send, x_row[1])
+        )(col_send, x_row[0])
     with jax.named_scope("row_terms"):
         row_send, row_keep = pl.pallas_call(
             functools.partial(row_kernel, n_row, n_col, slots),

time: 38.6 us -> 39.9 us (1.034)
  waiting for transfers between devices: 6.87 us -> 7.87 us
  local copies, waits for them, and re-layouts: 1.24 us -> 2.15 us
  starting transfers between devices: 14.2 us -> 13.4 us
    ppermute x10, waiting for transfers between devices: 6.87 us -> 7.87 us  [trade(): return lax.ppermute(value, axis, [(p, p ^ flip) for p in range(size)])]
    unnamed x10, local copies, waits for them, and re-layouts: 1.24 us -> 2.15 us
    ppermute x10, starting transfers between devices: 14.2 us -> 13.4 us  [trade(): return lax.ppermute(value, axis, [(p, p ^ flip) for p in range(size)])]
  transfers between devices with their start and end apart: 10 -> 10, of which waited for: 5 -> 7; matrix products, arithmetic and copies ran while one was open for 0% -> 0% of each run, Pallas kernels for 6% -> 4%
where the time goes in v23:
time: 39.9 us; the launch traced here: 39.7 us
  starting transfers between devices  13.4 us (34%)
  blocking collectives  10.2 us (26%)
  waiting for transfers between devices  7.87 us (20%)
  Pallas kernels  3.95 us (10%)
  local copies, waits for them, and re-layouts  2.15 us (5%)
  between operations  1.34 us (3%)
  loops' own time  0.69 us (2%)
    ppermute x10, starting transfers between devices, trade(): return lax.ppermute(value, axis, [(p, p ^ flip) for p in range(size)])  13.4 us
    all_to_all x1, blocking collectives, swap(): return lax.all_to_all(blocks, axis, 0, 0, tiled=True)  10.2 us
    ppermute x10, waiting for transfers between devices, trade(): return lax.ppermute(value, axis, [(p, p ^ flip) for p in range(size)])  7.87 us
    unnamed x10, local copies, waits for them, and re-layouts  2.15 us
    pallas_call x1, Pallas kernels, per_device(): pl.pallas_call(functools.partial(result_kernel, scale), out_shape=[block,...  1.24 us
    pallas_call x1, Pallas kernels, per_device(): pl.pallas_call(functools.partial(row_kernel, n_row, n_col, slots), out_sh...  1.21 us
    pallas_call x1, Pallas kernels, per_device(): pl.pallas_call(functools.partial(column_kernel, n_row, n_col, slots), out...  0.94 us
  transfers between devices with their start and end apart: 10, of which 7 were waited for; matrix products, arithmetic and copies ran while one was open for 0% of the time, Pallas kernels for 4%

profile of v23, /device:TPU:0, one launch (start us, length us, event | category | flops | bytes accessed | tf_op | source)
XLA Modules:
  0.0 39.7 jit_solution(18229162666499680504)
XLA Ops:
  0.6 3.1 %collective-permute-start.1 = (f32[1,16,128]{2,1,0:T(8,128)}, f32[1,16,128]{2,1,0:T(8,128)S(1)}, u32[]{:S(2)}, u32[]{:S(2)}) collective-permute-start(f32[1,16,128]{2,1,0:T(8,128)} %bitcast.6), channel_id=1, source_target_pairs={{0,1},{1,0},{2,3},{3,2},{4,5},{5,4},{6,7},{7,6},{8,9},{9,8},{10,11... | collective-permute-start | bytes 24584 | tf_op jit(solution)/shard_map/share_vectors/ppermute | solution.py:29
  3.7 1.5 %collective-permute-start = (f32[1,16,128]{2,1,0:T(8,128)}, f32[1,16,128]{2,1,0:T(8,128)S(1)}, u32[]{:S(2)}, u32[]{:S(2)}) collective-permute-start(f32[1,16,128]{2,1,0:T(8,128)} %bitcast.7), channel_id=1, source_target_pairs={{0,8},{4,12},{8,0},{12,4},{16,24},{20,28},{24,16},{28,20},{1,9},{5... | collective-permute-start | bytes 24584 | tf_op jit(solution)/shard_map/share_vectors/ppermute | solution.py:29
  5.2 0.0 copy-start.1
  5.2 0.0 copy-start.2
  5.2 0.0 copy-start.3
  5.2 0.6 %copy-done.1 = s32[1,1,16]{2,1,0:T(1,128)S(1)} copy-done((s32[1,1,16]{2,1,0:T(1,128)S(1)}, s32[1,1,16]{2,1,0:T(1,128)}, u32[]{:S(2)}) %copy-start.1) | copy-done | bytes 88
  5.9 0.0 copy-done.2
  5.9 0.0 copy-done.3
  5.9 0.0 copy-start
  5.9 1.2 %copy-done = f32[1,1,16,128,128]{4,3,2,1,0:T(8,128)S(1)} copy-done((f32[1,1,16,128,128]{4,3,2,1,0:T(8,128)S(1)}, f32[1,1,16,128,128]{4,3,2,1,0:T(8,128)}, u32[]{:S(2)}) %copy-start) | copy-done | bytes 1048600
  7.1 0.0 copy-start.4
  7.1 0.2 prepare.1
  7.3 0.0 collective-permute-done.1.refs_3_
  7.3 0.3 collective-permute-done.refs_1_
  7.6 0.2 copy-done.4
  7.8 2.6 %collective-permute-start.2 = (f32[2,16,128]{2,1,0:T(8,128)S(1)}, f32[2,16,128]{2,1,0:T(8,128)S(1)}, u32[]{:S(2)}, u32[]{:S(2)}) collective-permute-start(f32[2,16,128]{2,1,0:T(8,128)S(1)} %get-tuple-element.56.near), channel_id=1, source_target_pairs={{0,2},{1,3},{2,0},{3,1},{4,6},{5,7},{6,4},{7,5},{8,10},{9,11},{10,... | collective-permute-start | bytes 49160 | tf_op jit(solution)/shard_map/share_vectors/ppermute | solution.py:29
  10.4 1.5 %collective-permute-start.3 = (f32[2,16,128]{2,1,0:T(8,128)S(1)}, f32[2,16,128]{2,1,0:T(8,128)S(1)}, u32[]{:S(2)}, u32[]{:S(2)}) collective-permute-start(f32[2,16,128]{2,1,0:T(8,128)S(1)} %get-tuple-element.61.refs_0_), channel_id=1, source_target_pairs={{0,16},{4,20},{8,24},{12,28},{16,0},{20,4},{24,8},{28,12},{1,17},{... | collective-permute-start | bytes 49160 | tf_op jit(solution)/shard_map/share_vectors/ppermute | solution.py:29
  11.9 0.1 pad_add_fusion.place
  12.7 1.5 %collective-permute-done.3.refs_1_ = f32[2,16,128]{2,1,0:T(8,128)S(1)} collective-permute-done((f32[2,16,128]{2,1,0:T(8,128)S(1)}, f32[2,16,128]{2,1,0:T(8,128)S(1)}, u32[]{:S(2)}, u32[]{:S(2)}) %collective-permute-start.3) | collective-permute-done | bytes 16416 | tf_op jit(solution)/shard_map/share_vectors/ppermute | solution.py:29
  14.2 0.0 collective-permute-done.2.far
  14.2 0.9 %column_terms.1 = (f32[4,16,128]{2,1,0:T(8,128)S(1)}, f32[4,16,128]{2,1,0:T(8,128)S(1)}) custom-call(s32[2]{0:T(128)S(1)} %pad_add_fusion.place, s32[1,1,16]{2,1,0:T(1,128)S(1)} %get-tuple-element.52.arow, s32[1,1,16]{2,1,0:T(1,128)S(1)} %get-tuple-element.53.bcol, s32[1,1]{1,0:T(1,128)S(6)} %copy.16.count, f32[1,128]{1,0:T(1,128)S(1)} %get-tuple-element.54.d_ref, ...), custom_call_target="tpu_custom_call" | custom-call | flops 50331648 | bytes 1048576 | tf_op jit(solution)/shard_map/column_terms/column_terms/pallas_call | solution.py:278
  15.1 0.1 collective-permute-start.4
  15.2 0.5 %collective-permute-start.7 = (f32[4,16,128]{2,1,0:T(8,128)S(1)}, f32[4,16,128]{2,1,0:T(8,128)S(1)}, u32[]{:S(2)}, u32[]{:S(2)}) collective-permute-start(f32[4,16,128]{2,1,0:T(8,128)S(1)} %join.3.after.near), channel_id=1, source_target_pairs={{0,4},{4,0},{8,12},{12,8},{16,20},{20,16},{24,28},{28,24},{1,5},{5... | collective-permute-start | bytes 98312 | tf_op jit(solution)/shard_map/share_vectors/ppermute | solution.py:29
  15.7 0.7 %collective-permute-done.4.other = f32[4,16,128]{2,1,0:T(8,128)S(1)} collective-permute-done((f32[4,16,128]{2,1,0:T(8,128)S(1)}, f32[4,16,128]{2,1,0:T(8,128)S(1)}, u32[]{:S(2)}, u32[]{:S(2)}) %collective-permute-start.4) | collective-permute-done | bytes 32800 | tf_op jit(solution)/shard_map/return_products/ppermute | solution.py:29
  16.4 1.3 %collective-permute-start.5 = (f32[2,16,128]{2,1,0:T(8,128)S(1)}, f32[2,16,128]{2,1,0:T(8,128)S(1)}, u32[]{:S(2)}, u32[]{:S(2)}) collective-permute-start(f32[2,16,128]{2,1,0:T(8,128)S(1)} %get-tuple-element.63), channel_id=1, source_target_pairs={{0,8},{4,12},{8,0},{12,4},{16,24},{20,28},{24,16},{28,20},{1,9},{5... | collective-permute-start | bytes 49160 | tf_op jit(solution)/shard_map/return_products/ppermute | solution.py:29
  17.6 0.0 collective-permute-done.7.far
  17.7 1.2 %row_terms.1 = (f32[2,16,128]{2,1,0:T(8,128)S(1)}, f32[2,16,128]{2,1,0:T(8,128)S(1)}) custom-call(s32[2]{0:T(128)S(1)} %pad_add_fusion.place, s32[1,1,16]{2,1,0:T(1,128)S(1)} %get-tuple-element.52.arow, s32[1,1,16]{2,1,0:T(1,128)S(1)} %get-tuple-element.53.bcol, s32[1,1]{1,0:T(1,128)S(6)} %copy.16.count, f32[4,16,128]{2,1,0:T(8,128)S(1)} %join.3.after.near, ...), custom_call_target="tpu_custom_call" | custom-call | flops 50331648 | bytes 1048576 | tf_op jit(solution)/shard_map/row_terms/row_terms/pallas_call | solution.py:300
  18.9 0.5 %collective-permute-start.8 = (f32[2,16,128]{2,1,0:T(8,128)S(1)}, f32[2,16,128]{2,1,0:T(8,128)S(1)}, u32[]{:S(2)}, u32[]{:S(2)}) collective-permute-start(f32[2,16,128]{2,1,0:T(8,128)S(1)} %get-tuple-element.67), channel_id=1, source_target_pairs={{0,1},{1,0},{2,3},{3,2},{4,5},{5,4},{6,7},{7,6},{8,9},{9,8},{10,11... | collective-permute-start | bytes 49160 | tf_op jit(solution)/shard_map/return_products/ppermute | solution.py:29
  19.4 0.8 %collective-permute-done.5.other = f32[2,16,128]{2,1,0:T(8,128)S(1)} collective-permute-done((f32[2,16,128]{2,1,0:T(8,128)S(1)}, f32[2,16,128]{2,1,0:T(8,128)S(1)}, u32[]{:S(2)}, u32[]{:S(2)}) %collective-permute-start.5) | collective-permute-done | bytes 16416 | tf_op jit(solution)/shard_map/return_products/ppermute | solution.py:29
  20.1 1.5 %collective-permute-start.6 = (f32[1,16,128]{2,1,0:T(8,128)S(1)}, f32[1,16,128]{2,1,0:T(8,128)S(1)}, u32[]{:S(2)}, u32[]{:S(2)}) collective-permute-start(f32[1,16,128]{2,1,0:T(8,128)S(1)} %get-tuple-element.65), channel_id=1, source_target_pairs={{0,16},{4,20},{8,24},{12,28},{16,0},{20,4},{24,8},{28,12},{1,17},{... | collective-permute-start | bytes 24584 | tf_op jit(solution)/shard_map/return_products/ppermute | solution.py:29
  21.7 1.0 %collective-permute-done.8.other = f32[2,16,128]{2,1,0:T(8,128)S(1)} collective-permute-done((f32[2,16,128]{2,1,0:T(8,128)S(1)}, f32[2,16,128]{2,1,0:T(8,128)S(1)}, u32[]{:S(2)}, u32[]{:S(2)}) %collective-permute-start.8) | collective-permute-done | bytes 16416 | tf_op jit(solution)/shard_map/return_products/ppermute | solution.py:29
  22.7 0.9 %collective-permute-start.9 = (f32[1,16,128]{2,1,0:T(8,128)S(1)}, f32[1,16,128]{2,1,0:T(8,128)S(1)}, u32[]{:S(2)}, u32[]{:S(2)}) collective-permute-start(f32[1,16,128]{2,1,0:T(8,128)S(1)} %get-tuple-element.69), channel_id=1, source_target_pairs={{0,2},{1,3},{2,0},{3,1},{4,6},{5,7},{6,4},{7,5},{8,10},{9,11},{10,... | collective-permute-start | bytes 24584 | tf_op jit(solution)/shard_map/return_products/ppermute | solution.py:29
  23.6 0.2 collective-permute-done.6.refs_1_
  23.8 3.4 %collective-permute-done.9.refs_3_ = f32[1,16,128]{2,1,0:T(8,128)S(1)} collective-permute-done((f32[1,16,128]{2,1,0:T(8,128)S(1)}, f32[1,16,128]{2,1,0:T(8,128)S(1)}, u32[]{:S(2)}, u32[]{:S(2)}) %collective-permute-start.9) | collective-permute-done | bytes 8224 | tf_op jit(solution)/shard_map/return_products/ppermute | solution.py:29
  27.2 0.3 product.1
  27.6 10.2 %all_to_all.9.parts = f32[32,3,2,128]{3,2,1,0:T(2,128)S(1)} all-to-all(f32[32,3,2,128]{3,2,1,0:T(2,128)S(1)} %get-tuple-element.71), channel_id=1, replica_groups=mesh['row'=8,'col'=4] {'row','col'}, dimensions={0} | all-to-all | bytes 196608 | tf_op jit(solution)/shard_map/product/all_to_all | solution.py:24
  37.7 1.2 %results.1 = (f32[16,128]{1,0:T(8,128)}, f32[16,16]{1,0:T(8,128)}, f32[16,16]{1,0:T(8,128)}, s32[1,1]{1,0:T(1,128)}) custom-call(f32[16,128]{1,0:T(8,128)S(1)} %copy-done.4, f32[16,128]{1,0:T(8,128)S(1)} %get-tuple-element.95.product, f32[32,3,2,128]{3,2,1,0:T(2,128)S(1)} %all_to_all.9.parts), custom_call_target="tpu_custom_call" | custom-call | tf_op jit(solution)/shard_map/results/results/pallas_call | solution.py:326
  39.0 0.7 %while.9 = (s32[]{:T(128)}, f32[16,16]{1,0:T(8,128)}, f32[16,128]{1,0:T(8,128)S(1)}, f32[16,128]{1,0:T(8,128)S(1)}, f32[32,3,2,128]{3,2,1,0:T(2,128)S(1)}) while((s32[]{:T(128)}, f32[16,16]{1,0:T(8,128)}, f32[16,128]{1,0:T(8,128)S(1)}, f32[16,128]{1,0:T(8,128)S(1)}, f32[32,3,2,128]{3,2,1,0:T(2,128)S(1)}) %tuple.20), condition=%region_1.0_spmd, body=%region_0.0_spmd | while | flops 1 | bytes 98393 | solution.py:355
  (6 shorter events, 0.0 us)
Async XLA Ops:
  0.6 6.7 %collective-permute-start.1 = (f32[1,16,128]{2,1,0:T(8,128)}, f32[1,16,128]{2,1,0:T(8,128)S(1)}, u32[]{:S(2)}, u32[]{:S(2)}) collective-permute-start(f32[1,16,128]{2,1,0:T(8,128)} %bitcast.6), channel_id=1, source_target_pairs={{0,1},{1,0},{2,3},{3,2},{4,5},{5,4},{6,7},{7,6},{8,9},{9,8},{10,11... | collective-permute-start | bytes 24584 | tf_op jit(solution)/shard_map/share_vectors/ppermute | solution.py:29
  3.7 3.9 %collective-permute-start = (f32[1,16,128]{2,1,0:T(8,128)}, f32[1,16,128]{2,1,0:T(8,128)S(1)}, u32[]{:S(2)}, u32[]{:S(2)}) collective-permute-start(f32[1,16,128]{2,1,0:T(8,128)} %bitcast.7), channel_id=1, source_target_pairs={{0,8},{4,12},{8,0},{12,4},{16,24},{20,28},{24,16},{28,20},{1,9},{5... | collective-permute-start | bytes 24584 | tf_op jit(solution)/shard_map/share_vectors/ppermute | solution.py:29
  5.2 0.7 %copy-start.1 = (s32[1,1,16]{2,1,0:T(1,128)S(1)}, s32[1,1,16]{2,1,0:T(1,128)}, u32[]{:S(2)}) copy-start(s32[1,1,16]{2,1,0:T(1,128)} %refs_0_.1) | copy-start | bytes 196
  5.2 0.7 %copy-start.2 = (s32[1,1,16]{2,1,0:T(1,128)S(1)}, s32[1,1,16]{2,1,0:T(1,128)}, u32[]{:S(2)}) copy-start(s32[1,1,16]{2,1,0:T(1,128)} %refs_1_.1) | copy-start | bytes 196
  5.2 0.7 %copy-start.3 = (f32[128]{0:T(128)S(1)}, f32[128]{0:T(128)}, u32[]{:S(2)}) copy-start(f32[128]{0:T(128)} %param.9) | copy-start | bytes 1540
  5.9 1.2 %copy-start = (f32[1,1,16,128,128]{4,3,2,1,0:T(8,128)S(1)}, f32[1,1,16,128,128]{4,3,2,1,0:T(8,128)}, u32[]{:S(2)}) copy-start(f32[1,1,16,128,128]{4,3,2,1,0:T(8,128)} %tiles.1) | copy-start | bytes 3145732
  7.1 0.7 %copy-start.4 = (f32[16,128]{1,0:T(8,128)S(1)}, f32[16,128]{1,0:T(8,128)}, u32[]{:S(2)}) copy-start(f32[16,128]{1,0:T(8,128)} %x_ref.3) | copy-start | bytes 24580
  7.8 6.3 %collective-permute-start.2 = (f32[2,16,128]{2,1,0:T(8,128)S(1)}, f32[2,16,128]{2,1,0:T(8,128)S(1)}, u32[]{:S(2)}, u32[]{:S(2)}) collective-permute-start(f32[2,16,128]{2,1,0:T(8,128)S(1)} %get-tuple-element.56.near), channel_id=1, source_target_pairs={{0,2},{1,3},{2,0},{3,1},{4,6},{5,7},{6,4},{7,5},{8,10},{9,11},{10,... | collective-permute-start | bytes 49160 | tf_op jit(solution)/shard_map/share_vectors/ppermute | solution.py:29
  10.4 3.7 %collective-permute-start.3 = (f32[2,16,128]{2,1,0:T(8,128)S(1)}, f32[2,16,128]{2,1,0:T(8,128)S(1)}, u32[]{:S(2)}, u32[]{:S(2)}) collective-permute-start(f32[2,16,128]{2,1,0:T(8,128)S(1)} %get-tuple-element.61.refs_0_), channel_id=1, source_target_pairs={{0,16},{4,20},{8,24},{12,28},{16,0},{20,4},{24,8},{28,12},{1,17},{... | collective-permute-start | bytes 49160 | tf_op jit(solution)/shard_map/share_vectors/ppermute | solution.py:29
  15.1 1.3 %collective-permute-start.4 = (f32[4,16,128]{2,1,0:T(8,128)S(1)}, f32[4,16,128]{2,1,0:T(8,128)S(1)}, u32[]{:S(2)}, u32[]{:S(2)}) collective-permute-start(f32[4,16,128]{2,1,0:T(8,128)S(1)} %hand_on.1), channel_id=1, source_target_pairs={{0,4},{4,0},{8,12},{12,8},{16,20},{20,16},{24,28},{28,24},{1,5},{5... | collective-permute-start | bytes 98312 | tf_op jit(solution)/shard_map/return_products/ppermute | solution.py:29
  15.2 2.5 %collective-permute-start.7 = (f32[4,16,128]{2,1,0:T(8,128)S(1)}, f32[4,16,128]{2,1,0:T(8,128)S(1)}, u32[]{:S(2)}, u32[]{:S(2)}) collective-permute-start(f32[4,16,128]{2,1,0:T(8,128)S(1)} %join.3.after.near), channel_id=1, source_target_pairs={{0,4},{4,0},{8,12},{12,8},{16,20},{20,16},{24,28},{28,24},{1,5},{5... | collective-permute-start | bytes 98312 | tf_op jit(solution)/shard_map/share_vectors/ppermute | solution.py:29
  16.4 3.7 %collective-permute-start.5 = (f32[2,16,128]{2,1,0:T(8,128)S(1)}, f32[2,16,128]{2,1,0:T(8,128)S(1)}, u32[]{:S(2)}, u32[]{:S(2)}) collective-permute-start(f32[2,16,128]{2,1,0:T(8,128)S(1)} %get-tuple-element.63), channel_id=1, source_target_pairs={{0,8},{4,12},{8,0},{12,4},{16,24},{20,28},{24,16},{28,20},{1,9},{5... | collective-permute-start | bytes 49160 | tf_op jit(solution)/shard_map/return_products/ppermute | solution.py:29
  18.9 3.8 %collective-permute-start.8 = (f32[2,16,128]{2,1,0:T(8,128)S(1)}, f32[2,16,128]{2,1,0:T(8,128)S(1)}, u32[]{:S(2)}, u32[]{:S(2)}) collective-permute-start(f32[2,16,128]{2,1,0:T(8,128)S(1)} %get-tuple-element.67), channel_id=1, source_target_pairs={{0,1},{1,0},{2,3},{3,2},{4,5},{5,4},{6,7},{7,6},{8,9},{9,8},{10,11... | collective-permute-start | bytes 49160 | tf_op jit(solution)/shard_map/return_products/ppermute | solution.py:29
  20.1 3.7 %collective-permute-start.6 = (f32[1,16,128]{2,1,0:T(8,128)S(1)}, f32[1,16,128]{2,1,0:T(8,128)S(1)}, u32[]{:S(2)}, u32[]{:S(2)}) collective-permute-start(f32[1,16,128]{2,1,0:T(8,128)S(1)} %get-tuple-element.65), channel_id=1, source_target_pairs={{0,16},{4,20},{8,24},{12,28},{16,0},{20,4},{24,8},{28,12},{1,17},{... | collective-permute-start | bytes 24584 | tf_op jit(solution)/shard_map/return_products/ppermute | solution.py:29
  22.7 4.5 %collective-permute-start.9 = (f32[1,16,128]{2,1,0:T(8,128)S(1)}, f32[1,16,128]{2,1,0:T(8,128)S(1)}, u32[]{:S(2)}, u32[]{:S(2)}) collective-permute-start(f32[1,16,128]{2,1,0:T(8,128)S(1)} %get-tuple-element.69), channel_id=1, source_target_pairs={{0,2},{1,3},{2,0},{3,1},{4,6},{5,7},{6,4},{7,5},{8,10},{9,11},{10,... | collective-permute-start | bytes 24584 | tf_op jit(solution)/shard_map/return_products/ppermute | solution.py:29
